TPU v7x, 32 devices: a whole 2x2x4 slice. The times are simulated.
32 devices in a mesh: blk: 8 (over z, y), sub: 4 (over x, core).
Axes of the slice: x: 2, y: 2, z: 4, core: 2. Of those that a mesh axis runs over, the one named last changes fastest.
Arguments:
- node_input: float32 [512, 16384], P(('blk', 'sub')), may hold values from -6 to 6
- edge_input: bfloat16 [147456, 512], P(('blk', 'sub')), may hold values from -6 to 6
- senders: int32 [147456], P(('blk', 'sub')), may hold values from 0 to 16383, as said below
- receivers: int32 [147456], P(('blk', 'sub')), may hold values from 0 to 16383, as said below
- edge_count: int32 [32], P(('blk', 'sub')), may hold values from 1 to 4608, 110592 in all
- edge_w_one: bfloat16 [1536, 512], replicated, may hold values from -0.15625 to 0.15625
- edge_b_one: float32 [512], replicated, may hold values from -3 to 3
- edge_w_two: bfloat16 [512, 512], replicated, may hold values from -0.25 to 0.25
- edge_b_two: float32 [512], replicated, may hold values from -3 to 3
- edge_gain: float32 [512], replicated, may hold values from 0.1 to 1.9
- edge_shift: float32 [512], replicated, may hold values from -2 to 2
- node_w_one: bfloat16 [1024, 512], replicated, may hold values from -0.1875 to 0.1875
- node_b_one: float32 [512], replicated, may hold values from -3 to 3
- node_w_two: bfloat16 [512, 512], replicated, may hold values from -0.25 to 0.25
- node_b_two: float32 [512], replicated, may hold values from -3 to 3
- node_gain: float32 [512], replicated, may hold values from 0.1 to 1.9
- node_shift: float32 [512], replicated, may hold values from -2 to 2
- node_cotangent: float32 [512, 16384], P(('blk', 'sub')), may hold values from -6 to 6
- edge_cotangent: bfloat16 [147456, 512], P(('blk', 'sub')), may hold values from -6 to 6
Outputs:
- node_out: float32 [512, 16384], P(('blk', 'sub'))
- edge_out: float32 [147456, 512], P(('blk', 'sub'))
- node_grad: float32 [512, 16384], P(('blk', 'sub'))
- edge_grad: float32 [147456, 512], P(('blk', 'sub'))
- grad_edge_w_one: float32 [1536, 512], replicated
- grad_edge_b_one: float32 [512], replicated
- grad_edge_w_two: float32 [512, 512], replicated
- grad_edge_b_two: float32 [512], replicated
- grad_edge_gain: float32 [512], replicated
- grad_edge_shift: float32 [512], replicated
- grad_node_w_one: float32 [1024, 512], replicated
- grad_node_b_one: float32 [512], replicated
- grad_node_w_two: float32 [512, 512], replicated
- grad_node_b_two: float32 [512], replicated
- grad_node_gain: float32 [512], replicated
- grad_node_shift: float32 [512], replicated
Inputs may be any that keep to these rules, and one draw needn't show every extreme that they name: `senders`: an edge slot of device d (slots d * 4608 to d * 4608 + 4607) has its sender among nodes d * 512 to d * 512 + 511. `receivers`: with device d = g * 4 + s, an edge slot of device d has its receiver in node group g - 1, g or g + 1 modulo 8, where group k holds nodes k * 4 * 512 to (k + 1) * 4 * 512 - 1.
All inputs are finite; a program needn't handle non-finite values. No bound on the sum of `edge_count` on one device may be relied on, other than what follows from the above.
Results may differ from a plain program's by a relative error of at most 0.0079.
Values may be sent and summed in bfloat16 or wider, within the bound.
A program may use at most 256 MiB of HBM per device.

v0:
```python
import jax
import jax.numpy as jnp
from jax import lax
from jax.sharding import PartitionSpec as P

EPSILON = 1e-05


def shifted(block, axis, distance):
    devices = range(lax.axis_size(axis))
    route = [((i - distance) % len(devices), i) for i in devices]
    return lax.ppermute(block, axis, route)


def extended(cells, sides, width):
    for axis, dim in sides:
        count = lax.axis_size(axis)
        head = lax.slice_in_dim(cells, 0, width, axis=dim)
        tail = lax.slice_in_dim(cells, cells.shape[dim] - width, cells.shape[dim], axis=dim)
        cells = jnp.concatenate(
            [
                lax.ppermute(tail, axis, [(i, (i + 1) % count) for i in range(count)]),
                cells,
                lax.ppermute(head, axis, [((i + 1) % count, i) for i in range(count)]),
            ],
            axis=dim,
        )
    return cells


def norm_apply(values, gain, shift):
    average = jnp.mean(values, -1, keepdims=True)
    centred = values - average
    variance = jnp.mean(centred * centred, -1, keepdims=True)
    return centred * lax.rsqrt(variance + EPSILON) * gain + shift


def silu_slope(values):
    logistic = jax.nn.sigmoid(values)
    return logistic * (1.0 + values * (1.0 - logistic))


def matmul(left, right):
    return jnp.dot(left, right, preferred_element_type=jnp.float32)


def left_matmul(left, right):
    return lax.dot_general(
        left, right, (((0,), (0,)), ((), ())), preferred_element_type=jnp.float32
    )


def right_matmul(left, right):
    return lax.dot_general(
        left, right, (((1,), (1,)), ((), ())), preferred_element_type=jnp.float32
    )


def to_nodes(channels, cotangent):
    moved = (
        lax.all_to_all(channels, ("blk", "sub"), split_axis=1, concat_axis=0, tiled=True),
        lax.all_to_all(cotangent, ("blk", "sub"), split_axis=1, concat_axis=0, tiled=True),
    )
    return (moved[0], moved[1])


def to_channels(values, gradient):
    moved = (
        lax.all_to_all(
            values.astype(jnp.bfloat16), ("blk", "sub"), split_axis=0, concat_axis=1, tiled=True
        ).astype(values.dtype),
        lax.all_to_all(
            gradient.astype(jnp.bfloat16), ("blk", "sub"), split_axis=0, concat_axis=1, tiled=True
        ).astype(gradient.dtype),
    )
    return (moved[0], moved[1])


def combine_sums(wide_sums, per_group):
    lower_part = wide_sums[:per_group]
    middle_part = wide_sums[per_group : 2 * per_group]
    upper_part = wide_sums[2 * per_group :]
    from_above = shifted(lower_part, "blk", -1)
    from_below = shifted(upper_part, "blk", 1)
    return lax.psum_scatter(
        middle_part + from_above + from_below, "sub", scatter_dimension=0, tiled=True
    )


def shards(
    node_input,
    edge_input,
    senders,
    receivers,
    edge_count,
    edge_w_one,
    edge_b_one,
    edge_w_two,
    edge_b_two,
    edge_gain,
    edge_shift,
    node_w_one,
    node_b_one,
    node_w_two,
    node_b_two,
    node_gain,
    node_shift,
    node_cotangent,
    edge_cotangent,
):
    groups = lax.axis_size("blk")
    sub_count = lax.axis_size("sub")
    block_index = lax.axis_index("blk")
    sub_index = lax.axis_index("sub")
    width = edge_input.shape[1]
    node_cols, cot_cols = to_nodes(node_input, node_cotangent)
    node_rows = node_cols.T
    node_upstream = cot_cols.T
    per_device = node_rows.shape[0]
    per_group = per_device * sub_count
    my_start = (block_index * sub_count + sub_index) * per_device
    send_local = senders - my_start
    relative = (receivers // per_group - block_index + 1 + groups) % groups
    recv_wide = relative * per_group + receivers % per_group
    slot_index = jnp.arange(edge_input.shape[0], dtype=jnp.int32)
    live = jnp.where(slot_index < edge_count[0], 1.0, 0.0).astype(jnp.float32)[:, None]
    node_low = node_rows.astype(jnp.bfloat16)
    group_low = lax.all_gather(node_low, "sub", axis=0, tiled=True)
    wide_low = extended(group_low, (("blk", 0),), per_group)
    stacked = jnp.concatenate(
        [edge_input, jnp.take(node_low, send_local, axis=0), jnp.take(wide_low, recv_wide, axis=0)],
        axis=1,
    )
    first_pre = matmul(stacked, edge_w_one) + edge_b_one
    first_act = jax.nn.silu(first_pre).astype(jnp.bfloat16)
    second_pre = matmul(first_act, edge_w_two) + edge_b_two
    edge_branch, edge_norm_back = jax.vjp(norm_apply, second_pre, edge_gain, edge_shift)
    edge_result = edge_input.astype(jnp.float32) + live * edge_branch
    wide_sums = jax.ops.segment_sum(live * edge_result, recv_wide, num_segments=3 * per_group)
    gathered = combine_sums(wide_sums, per_group)
    joined = jnp.concatenate([node_low, gathered.astype(jnp.bfloat16)], axis=1)
    third_pre = matmul(joined, node_w_one) + node_b_one
    third_act = jax.nn.silu(third_pre).astype(jnp.bfloat16)
    fourth_pre = matmul(third_act, node_w_two) + node_b_two
    node_branch, node_norm_back = jax.vjp(norm_apply, fourth_pre, node_gain, node_shift)
    node_result = node_rows + node_branch
    grad_fourth, grad_node_gain, grad_node_shift = node_norm_back(node_upstream)
    fourth_low = grad_fourth.astype(jnp.bfloat16)
    grad_node_w_two = left_matmul(third_act, fourth_low)
    grad_node_b_two = jnp.sum(fourth_low.astype(jnp.float32), 0)
    grad_third = right_matmul(fourth_low, node_w_two) * silu_slope(third_pre)
    third_low = grad_third.astype(jnp.bfloat16)
    grad_node_w_one = left_matmul(joined, third_low)
    grad_node_b_one = jnp.sum(third_low.astype(jnp.float32), 0)
    grad_joined = right_matmul(third_low, node_w_one)
    grad_nodes = node_upstream + grad_joined[:, :width]
    grad_gathered = grad_joined[:, width:]
    group_grad = lax.all_gather(
        grad_gathered.astype(jnp.bfloat16), "sub", axis=0, tiled=True
    ).astype(grad_gathered.dtype)
    wide_grad = extended(group_grad.astype(jnp.bfloat16), (("blk", 0),), per_group).astype(
        group_grad.dtype
    )
    edge_total = edge_cotangent.astype(jnp.float32) + live * jnp.take(wide_grad, recv_wide, axis=0)
    grad_second, grad_edge_gain, grad_edge_shift = edge_norm_back(live * edge_total)
    second_low = grad_second.astype(jnp.bfloat16)
    grad_edge_w_two = left_matmul(first_act, second_low)
    grad_edge_b_two = jnp.sum(second_low.astype(jnp.float32), 0)
    grad_first = right_matmul(second_low, edge_w_two) * silu_slope(first_pre)
    first_low = grad_first.astype(jnp.bfloat16)
    grad_edge_w_one = left_matmul(stacked, first_low)
    grad_edge_b_one = jnp.sum(first_low.astype(jnp.float32), 0)
    grad_stacked = right_matmul(first_low, edge_w_one)
    edge_grad = edge_total + grad_stacked[:, :width]
    sender_grad = jax.ops.segment_sum(
        grad_stacked[:, width : 2 * width], send_local, num_segments=per_device
    )
    receiver_wide = jax.ops.segment_sum(
        grad_stacked[:, 2 * width :], recv_wide, num_segments=3 * per_group
    )
    receiver_grad = combine_sums(receiver_wide, per_group)
    node_total = grad_nodes + sender_grad + receiver_grad
    summed = lax.psum(
        (
            grad_edge_w_one,
            grad_edge_b_one,
            grad_edge_w_two,
            grad_edge_b_two,
            grad_edge_gain,
            grad_edge_shift,
            grad_node_w_one,
            grad_node_b_one,
            grad_node_w_two,
            grad_node_b_two,
            grad_node_gain,
            grad_node_shift,
        ),
        ("blk", "sub"),
    )
    node_out, node_grad = to_channels(node_result.T, node_total.T)
    return (
        node_out,
        edge_result,
        node_grad,
        edge_grad,
        summed[0],
        summed[1],
        summed[2],
        summed[3],
        summed[4],
        summed[5],
        summed[6],
        summed[7],
        summed[8],
        summed[9],
        summed[10],
        summed[11],
    )


def solution(mesh):
    placed = (
        P(("blk", "sub"), None),
        P(("blk", "sub"), None),
        P(("blk", "sub")),
        P(("blk", "sub")),
        P(("blk", "sub")),
        P(),
        P(),
        P(),
        P(),
        P(),
        P(),
        P(),
        P(),
        P(),
        P(),
        P(),
        P(),
        P(("blk", "sub"), None),
        P(("blk", "sub"), None),
    )
    return jax.shard_map(
        shards,
        mesh=mesh,
        in_specs=placed,
        out_specs=(
            P(("blk", "sub"), None),
            P(("blk", "sub"), None),
            P(("blk", "sub"), None),
            P(("blk", "sub"), None),
            P(),
            P(),
            P(),
            P(),
            P(),
            P(),
            P(),
            P(),
            P(),
            P(),
            P(),
            P(),
        ),
        check_vma=False,
    )
```

profile of v0, /device:TPU:0, one launch (start us, length us, event | category | flops | bytes accessed | tf_op | source)
XLA Modules:
  0.0 1247.0 jit_solution(12306203952096527585)
XLA Ops:
  8.7 33.3 %all_to_all.64 = f32[16,32,512]{2,0,1:T(8,128)S(1)} all-to-all(f32[16,32,512]{2,0,1:T(8,128)S(1)} %bitcast.79), channel_id=1, replica_groups=mesh['blk'=8,'sub'=4] {'blk','sub'}, dimensions={1} | all-to-all | bytes 2097152 | tf_op jit(solution)/shard_map/all_to_all | solution.py:61
  43.9 21.7 %all-gather.3.cloned.1.call-done = bf16[2048,512]{0,1:T(8,128)(2,1)} async-done(((bf16[512,512]{0,1:T(8,128)(2,1)}), bf16[2048,512]{0,1:T(8,128)(2,1)}) %all-gather.3.cloned.1.call-update) | async-done | bytes 2097168 | tf_op jit(solution)/shard_map/all_gather | solution.py:128
  65.6 4.2 collective-permute-start.1
  70.5 6.7 copy.78
  78.2 13.8 %gather_fusion = bf16[4608,512]{1,0:T(8,128)(2,1)} fusion(bf16[512,512]{1,0:T(8,128)(2,1)S(1)} %copy.79, s32[5120]{0:T(1024)S(1)} %pad_clamp_fusion.1), kind=kCustom, calls=%fused_computation | custom fusion | bytes 9455616 | tf_op jit(solution)/shard_map/jit(_take)/gather | solution.py:131
  92.0 6.7 copy.80
  98.7 60.0 %collective-permute-done.1 = bf16[2048,512]{0,1:T(8,128)(2,1)} collective-permute-done((bf16[2048,512]{0,1:T(8,128)(2,1)}, bf16[2048,512]{0,1:T(8,128)(2,1)}, u32[]{:S(2)}, u32[]{:S(2)}) %collective-permute-start.1) | collective-permute-done | bytes 2097184 | tf_op jit(solution)/shard_map/ppermute | solution.py:24
  158.7 6.4 pad_maximum_fusion.1
  165.1 8.6 copy.81
  173.7 17.6 %gather_fusion.1 = bf16[4608,512]{1,0:T(8,128)(2,1)} fusion(bf16[6144,512]{1,0:T(8,128)(2,1)} %copy.81, s32[5120]{0:T(1024)S(1)} %pad_clamp_fusion), kind=kCustom, calls=%fused_computation.1 | custom fusion | bytes 9455616 | tf_op jit(solution)/shard_map/jit(_take)/gather | solution.py:131
  191.3 6.6 copy.82
  197.9 8.3 broadcast_select_fusion
  206.2 15.2 %multiply_convert_fusion.1 = (bf16[4608,512]{1,0:T(8,128)(2,1)}, f32[4608,512]{1,0:T(8,128)}) fusion(f32[512]{0:T(512)S(1)} %copy-done.40, bf16[1536,512]{1,0:T(8,128)(2,1)S(1)} %copy-done, bf16[4608,512]{0,1:T(8,128)(2,1)} %get-tuple-element.114, bf16[4608,512]{0,1:T(8,128)(2,1)} %get-tuple-element.115, bf16[4608,512]{0,1:T(8,128)(2,1)} %copy.78), kind=kOutput, calls=%fused_computation.21 | convolution fusion | flops 7304380416 | bytes 29886464 | tf_op jit(solution)/shard_map/dot_general | solution.py:44
  221.5 5.1 add_reduce_fusion
  228.5 3.5 slice-done
  232.3 8.5 broadcast_multiply_fusion
  240.9 9.6 copy.84
  250.5 33.5 %scatter_custom_fusion = f32[6144,512]{1,0:T(8,128)} fusion(s32[4608]{0:T(1024)S(1)} %get-tuple-element.95, f32[4608,512]{1,0:T(8,128)} %copy.84, f32[]{:T(128)} %constant.103.clone.1), kind=kCustom, calls=%fused_computation.29 | custom fusion | flops 2359296 | bytes 12583424 | tf_op jit(solution)/shard_map/scatter-add | solution.py:139
  284.0 9.8 fusion.32
  293.7 5.5 copy.103
  299.2 5.3 copy.104
  309.3 6.0 copy.102
  315.3 171.9 %collective-permute-done.3 = f32[2048,512]{0,1:T(8,128)} collective-permute-done((f32[2048,512]{0,1:T(8,128)}, f32[2048,512]{0,1:T(8,128)}, u32[]{:S(2)}, u32[]{:S(2)}) %collective-permute-start.3) | collective-permute-done | bytes 4194336 | tf_op jit(solution)/shard_map/ppermute | solution.py:12
  489.4 8.4 add_add_fusion.2
  498.9 2.6 all-to-all-start.2
  501.6 41.0 %reduce-scatter.3.cloned.1.call-done = f32[512,512]{0,1:T(8,128)} async-done(((f32[2048,512]{0,1:T(8,128)}), f32[512,512]{0,1:T(8,128)}) %reduce-scatter.3.cloned.1.call-update) | async-done | bytes 1048592 | tf_op jit(solution)/shard_map/reduce_scatter | solution.py:85
  546.1 3.0 fusion.33
  555.8 2.9 convert_reduce_fusion.3
  562.6 22.7 %all-gather.5.cloned.1.call-done = bf16[2048,512]{1,0:T(8,128)(2,1)} async-done(((bf16[512,512]{1,0:T(8,128)(2,1)}), bf16[2048,512]{1,0:T(8,128)(2,1)}) %all-gather.5.cloned.1.call-update) | async-done | bytes 2097168 | tf_op jit(solution)/shard_map/all_gather | solution.py:158
  585.3 4.2 collective-permute-start.5
  589.6 6.8 copy.91
  596.4 81.9 %collective-permute-done.5 = bf16[2048,512]{1,0:T(8,128)(2,1)} collective-permute-done((bf16[2048,512]{1,0:T(8,128)(2,1)}, bf16[2048,512]{1,0:T(8,128)(2,1)}, u32[]{:S(2)}, u32[]{:S(2)}) %collective-permute-start.5) | collective-permute-done | bytes 2097184 | tf_op jit(solution)/shard_map/ppermute | solution.py:24
  678.4 9.2 maximum_convert_fusion
  687.5 19.1 %gather_fusion.2 = f32[4608,512]{1,0:T(8,128)} fusion(f32[6144,512]{1,0:T(8,128)} %maximum_convert_fusion, s32[5120]{0:T(1024)S(1)} %pad_clamp_fusion), kind=kCustom, calls=%fused_computation.2 | custom fusion | bytes 18892800 | tf_op jit(solution)/shard_map/jit(_take)/gather | solution.py:164
  706.7 9.7 copy.92
  716.3 10.8 multiply_reduce_fusion
  727.2 9.1 fusion.29
  737.9 9.2 convert_reduce_fusion.1
  749.3 13.1 %fusion.35 = f32[4608,1536]{1,0:T(8,128)} fusion(bf16[4608,512]{1,0:T(8,128)(2,1)S(1)} %get-tuple-element.111, bf16[1536,512]{1,0:T(8,128)(2,1)S(1)} %copy-done), kind=kOutput, calls=%fused_computation.112 | convolution fusion | flops 7247757312 | bytes 34603008 | tf_op jit(solution)/shard_map/dot_general | solution.py:54
  762.4 34.0 %scatter_custom_fusion.1 = f32[6144,512]{1,0:T(8,128)} fusion(s32[4608]{0:T(1024)S(1)} %get-tuple-element.95, f32[4608,1536]{1,0:T(8,128)} %fusion.35, f32[]{:T(128)} %constant.103.clone.1), kind=kCustom, calls=%fused_computation.10 | custom fusion | flops 2359296 | bytes 22020608 | tf_op jit(solution)/shard_map/scatter-add | solution.py:178
  796.4 9.6 fusion.31
  806.0 5.4 copy.107
  811.4 5.4 copy.108
  821.5 5.4 copy.106
  826.9 172.5 %collective-permute-done.7 = f32[2048,512]{0,1:T(8,128)} collective-permute-done((f32[2048,512]{0,1:T(8,128)}, f32[2048,512]{0,1:T(8,128)}, u32[]{:S(2)}, u32[]{:S(2)}) %collective-permute-start.7) | collective-permute-done | bytes 4194336 | tf_op jit(solution)/shard_map/ppermute | solution.py:12
  1001.6 8.4 add_add_fusion.1
  1012.6 2.9 fusion.28
  1015.6 8.2 fusion.36
  1023.8 16.4 %fusion.7 = f32[1536,512]{1,0:T(8,128)} fusion(bf16[4608,512]{1,0:T(8,128)(2,1)} %copy-done.42, bf16[4608,512]{0,1:T(8,128)(2,1)} %get-tuple-element.114, bf16[4608,512]{0,1:T(8,128)(2,1)} %get-tuple-element.115, bf16[4608,512]{0,1:T(8,128)(2,1)} %copy.78), kind=kOutput, calls=%fused_computation.31 | convolution fusion | flops 7290224640 | bytes 22020096 | tf_op jit(solution)/shard_map/dot_general | solution.py:48
  1040.3 2.7 fusion.12
  1042.9 2.6 all-to-all-start.1
  1047.9 2.5 copy.105
  1050.4 5.7 reduce-scatter.5.cloned.1.call-done
  1056.1 2.8 fusion.10
  1061.4 31.1 %scatter_custom_fusion.2 = f32[512,512]{1,0:T(8,128)} fusion(f32[512,512]{1,0:T(8,128)} %copy.96, s32[4608]{0:T(1024)} %copy-done.20, f32[4608,1536]{1,0:T(8,128)} %fusion.35), kind=kCustom, calls=%fused_computation.8 | custom fusion | flops 2359296 | bytes 10485760 | tf_op jit(solution)/shard_map/scatter-add | solution.py:175
  1097.4 5.0 all-to-all-start.3
  1102.7 9.7 copy.100
  1113.6 8.5 slice.61
  1122.1 9.7 copy.109
  1131.8 11.9 add.247
  1143.7 9.6 copy.101
  1153.4 41.1 %all-reduce = (f32[512]{0:T(512)}, f32[512]{0:T(512)}, f32[512]{0:T(512)}, f32[512]{0:T(512)}, f32[512]{0:T(512)}, /*index=5*/f32[512]{0:T(512)}, f32[512]{0:T(512)}, f32[512]{0:T(512)}) all-reduce(f32[512]{0:T(512)S(1)} %get-tuple-element.110, f32[512]{0:T(512)S(1)} %get-tuple-element.85, ...), channel_id=1, replica_groups=mesh['blk'=8,'sub'=4] {'blk','sub'}, use_global_device_ids=true, to_apply=%region_15.16 | all-reduce | flops 4096 | bytes 32768 | tf_op jit(solution)/shard_map/psum | solution.py:183
  1195.6 36.1 %all-reduce.4.cloned.1.call-done = (f32[1536,512]{1,0:T(8,128)}, f32[512,512]{1,0:T(8,128)}, f32[1024,512]{1,0:T(8,128)}, f32[512,512]{1,0:T(8,128)}) async-done(((f32[1536,512]{1,0:T(8,128)}, f32[512,512]{1,0:T(8,128)}, f32[1024,512]{1,0:T(8,128)}, f32[512,512]{1,0:T(8,128)}), (f32[1536,512]{1,0:T(8,128)}, f32[512,512]{1,0:T(8,128)}, f32[1024,512]{1,0:T(8,128)}, ...) | async-done | bytes 7340048 | tf_op jit(solution)/shard_map/psum | solution.py:183
  1231.7 4.0 copy.124
  (154 shorter events, 58.8 us)
Async XLA Ops:
  7.2 199.0 %copy-start = (bf16[1536,512]{1,0:T(8,128)(2,1)S(1)}, bf16[1536,512]{1,0:T(8,128)(2,1)}, u32[]{:S(2)}) copy-start(bf16[1536,512]{1,0:T(8,128)(2,1)} %param.24) | copy-start | bytes 4718596
  7.2 70.1 %copy-start.28 = (s32[4608]{0:T(1024)S(1)}, s32[4608]{0:T(1024)}, u32[]{:S(2)}) copy-start(s32[4608]{0:T(1024)} %param.21) | copy-start | bytes 55300
  7.2 70.7 %copy-start.29 = (s32[4608]{0:T(1024)S(1)}, s32[4608]{0:T(1024)}, u32[]{:S(2)}) copy-start(s32[4608]{0:T(1024)} %param.22) | copy-start | bytes 55300
  7.2 58.4 %all-gather.3.cloned.1.call-start = ((), (), s32[]{:S(2)}) async-start(), calls=%async_computation.6 | async-start | bytes 2621440 | tf_op jit(solution)/shard_map/all_gather | solution.py:128
  42.0 1.0 copy-start.5
  43.8 34.1 %copy-start.6 = (bf16[512,512]{1,0:T(8,128)(2,1)S(1)}, bf16[512,512]{1,0:T(8,128)(2,1)}, u32[]{:S(2)}) copy-start(bf16[512,512]{1,0:T(8,128)(2,1)} %bitcast_convert_fusion) | copy-start | bytes 1572868
  43.9 498.7 %reduce-scatter.3.cloned.1.call-start = ((), (), s32[]{:S(2)}) async-start(), calls=%async_computation.7 | async-start | bytes 5242880 | tf_op jit(solution)/shard_map/reduce_scatter | solution.py:85
  65.6 93.0 %collective-permute-start.1 = (bf16[2048,512]{0,1:T(8,128)(2,1)}, bf16[2048,512]{0,1:T(8,128)(2,1)}, u32[]{:S(2)}, u32[]{:S(2)}) collective-permute-start(bf16[2048,512]{0,1:T(8,128)(2,1)} %all-gather.3.cloned.1.call-done), channel_id=1, source_target_pairs={{4,0},{8,4},{12,8},{16,12},{20,16},{24,20},{28,24},{0,28},{5,1},{9... | collective-permute-start | bytes 6291464 | tf_op jit(solution)/shard_map/ppermute | solution.py:24
  69.9 88.8 %collective-permute-start = (bf16[2048,512]{0,1:T(8,128)(2,1)}, bf16[2048,512]{0,1:T(8,128)(2,1)}, u32[]{:S(2)}, u32[]{:S(2)}) collective-permute-start(bf16[2048,512]{0,1:T(8,128)(2,1)} %all-gather.3.cloned.1.call-done), channel_id=1, source_target_pairs={{0,4},{4,8},{8,12},{12,16},{16,20},{20,24},{24,28},{28,0},{1,5},{5... | collective-permute-start | bytes 6291464 | tf_op jit(solution)/shard_map/ppermute | solution.py:22
  77.3 0.6 copy-start.20
  197.9 8.3 copy-start.40
  206.2 15.3 %copy-start.23 = (f32[512]{0:T(512)S(1)}, f32[512]{0:T(512)}, u32[]{:S(2)}) copy-start(f32[512]{0:T(512)} %param.27) | copy-start | bytes 6148
  206.2 15.3 %copy-start.36 = (bf16[512,512]{1,0:T(8,128)(2,1)S(1)}, bf16[512,512]{1,0:T(8,128)(2,1)}, u32[]{:S(2)}) copy-start(bf16[512,512]{1,0:T(8,128)(2,1)} %param.26) | copy-start | bytes 1572868
  226.6 14.3 %copy-start.1 = (f32[4608,512]{0,1:T(8,128)}, f32[4608,512]{0,1:T(8,128)S(1)}, u32[]{:S(2)}) copy-start(f32[4608,512]{0,1:T(8,128)S(1)} %get-tuple-element.107) | copy-start | bytes 28311556
  226.6 5.3 slice-start
  226.6 5.3 copy-start.30
  226.6 5.3 copy-start.33
  226.6 5.7 slice-start.1
  304.6 182.6 %collective-permute-start.3 = (f32[2048,512]{0,1:T(8,128)}, f32[2048,512]{0,1:T(8,128)}, u32[]{:S(2)}, u32[]{:S(2)}) collective-permute-start(f32[2048,512]{0,1:T(8,128)} %copy.104), channel_id=1, source_target_pairs={{28,0},{0,4},{4,8},{8,12},{12,16},{16,20},{20,24},{24,28},{29,1},{... | collective-permute-start | bytes 12582920 | tf_op jit(solution)/shard_map/ppermute | solution.py:12
  307.0 182.4 %collective-permute-start.2 = (f32[2048,512]{0,1:T(8,128)}, f32[2048,512]{0,1:T(8,128)}, u32[]{:S(2)}, u32[]{:S(2)}) collective-permute-start(f32[2048,512]{0,1:T(8,128)} %copy.103), channel_id=1, source_target_pairs={{4,0},{8,4},{12,8},{16,12},{20,16},{24,20},{28,24},{0,28},{5,1},{9... | collective-permute-start | bytes 12582920 | tf_op jit(solution)/shard_map/ppermute | solution.py:12
  315.3 182.5 %copy-start.17 = (f32[16,16384]{1,0:T(8,128)S(1)}, f32[16,16384]{1,0:T(8,128)}, u32[]{:S(2)}) copy-start(f32[16,16384]{1,0:T(8,128)} %param.36) | copy-start | bytes 3145732
  315.3 228.6 %copy-start.38 = (f32[512]{0:T(512)S(1)}, f32[512]{0:T(512)}, u32[]{:S(2)}) copy-start(f32[512]{0:T(512)} %param.31) | copy-start | bytes 6148
  497.8 48.3 %copy-start.39 = (f32[512]{0:T(512)S(1)}, f32[512]{0:T(512)}, u32[]{:S(2)}) copy-start(f32[512]{0:T(512)} %param.33) | copy-start | bytes 6148
  497.8 51.3 %copy-start.26 = (f32[512]{0:T(512)S(1)}, f32[512]{0:T(512)}, u32[]{:S(2)}) copy-start(f32[512]{0:T(512)} %param.34) | copy-start | bytes 6148
  498.9 50.2 %all-to-all-start.2 = ((f32[16,32,512]{2,0,1:T(8,128)}), f32[16,32,512]{2,0,1:T(8,128)S(1)}, u32[]{:S(2)}, u32[]{:S(2)}) async-start(f32[16,32,512]{2,0,1:T(8,128)} %bitcast.78), calls=%async_computation.3 | async-start | bytes 2097152 | tf_op jit(solution)/shard_map/all_to_all | solution.py:62
  501.6 83.8 %all-gather.5.cloned.1.call-start = ((), (), s32[]{:S(2)}) async-start(), calls=%async_computation.8 | async-start | bytes 2621440 | tf_op jit(solution)/shard_map/all_gather | solution.py:158
  543.9 5.2 copy-start.9
  546.1 3.0 copy-start.41
  549.1 13.5 %copy-start.21 = (f32[512]{0:T(512)}, f32[512]{0:T(512)S(1)}, u32[]{:S(2)}) copy-start(f32[512]{0:T(512)S(1)} %broadcast_multiply_fusion.2) | copy-start | bytes 6148
  549.1 13.5 %copy-start.3 = (f32[16,32,512]{2,0,1:T(8,128)}, f32[16,32,512]{2,0,1:T(8,128)S(1)}, u32[]{:S(2)}) copy-start(f32[16,32,512]{2,0,1:T(8,128)S(1)} %all-to-all-done.2) | copy-start | bytes 3145732
  549.1 10.5 copy-start.16
  551.2 7.5 copy-start.24
  555.8 4.5 copy-start.19
  558.7 0.9 copy-start.11
  560.3 1.3 copy-start.7
  562.6 493.6 %reduce-scatter.5.cloned.1.call-start = ((), (), s32[]{:S(2)}) async-start(), calls=%async_computation.9 | async-start | bytes 5242880 | tf_op jit(solution)/shard_map/reduce_scatter | solution.py:85
  585.3 93.0 %collective-permute-start.5 = (bf16[2048,512]{1,0:T(8,128)(2,1)}, bf16[2048,512]{1,0:T(8,128)(2,1)}, u32[]{:S(2)}, u32[]{:S(2)}) collective-permute-start(bf16[2048,512]{1,0:T(8,128)(2,1)} %all-gather.5.cloned.1.call-done), channel_id=1, source_target_pairs={{4,0},{8,4},{12,8},{16,12},{20,16},{24,20},{28,24},{0,28},{5,1},{9... | collective-permute-start | bytes 6291464 | tf_op jit(solution)/shard_map/ppermute | solution.py:24
  589.6 88.8 %collective-permute-start.4 = (bf16[2048,512]{1,0:T(8,128)(2,1)}, bf16[2048,512]{1,0:T(8,128)(2,1)}, u32[]{:S(2)}, u32[]{:S(2)}) collective-permute-start(bf16[2048,512]{1,0:T(8,128)(2,1)} %all-gather.5.cloned.1.call-done), channel_id=1, source_target_pairs={{0,4},{4,8},{8,12},{12,16},{16,20},{20,24},{24,28},{28,0},{1,5},{5... | collective-permute-start | bytes 6291464 | tf_op jit(solution)/shard_map/ppermute | solution.py:22
  727.2 9.2 copy-start.2
  736.3 1.5 copy-start.37
  737.9 9.2 copy-start.8
  747.1 2.2 copy-start.42
  816.8 182.6 %collective-permute-start.7 = (f32[2048,512]{0,1:T(8,128)}, f32[2048,512]{0,1:T(8,128)}, u32[]{:S(2)}, u32[]{:S(2)}) collective-permute-start(f32[2048,512]{0,1:T(8,128)} %copy.108), channel_id=1, source_target_pairs={{28,0},{0,4},{4,8},{8,12},{12,16},{16,20},{20,24},{24,28},{29,1},{... | collective-permute-start | bytes 12582920 | tf_op jit(solution)/shard_map/ppermute | solution.py:12
  819.2 182.4 %collective-permute-start.6 = (f32[2048,512]{0,1:T(8,128)}, f32[2048,512]{0,1:T(8,128)}, u32[]{:S(2)}, u32[]{:S(2)}) collective-permute-start(f32[2048,512]{0,1:T(8,128)} %copy.107), channel_id=1, source_target_pairs={{4,0},{8,4},{12,8},{16,12},{20,16},{24,20},{28,24},{0,28},{5,1},{9... | collective-permute-start | bytes 12582920 | tf_op jit(solution)/shard_map/ppermute | solution.py:12
  826.9 183.5 %copy-start.10 = (bf16[512,512]{0,1:T(8,128)(2,1)S(1)}, bf16[512,512]{0,1:T(8,128)(2,1)}, u32[]{:S(2)}) copy-start(bf16[512,512]{0,1:T(8,128)(2,1)} %copy-done.9) | copy-start | bytes 1572868
  826.9 183.5 %copy-start.12 = (bf16[512,512]{1,0:T(8,128)(2,1)S(1)}, bf16[512,512]{1,0:T(8,128)(2,1)}, u32[]{:S(2)}) copy-start(bf16[512,512]{1,0:T(8,128)(2,1)} %copy-done.11) | copy-start | bytes 1572868
  1010.0 221.7 %all-reduce.4.cloned.1.call-start = ((), (), s32[]{:S(2)}) async-start(), calls=%async_computation.10 | async-start | bytes 14680064 | tf_op jit(solution)/shard_map/psum | solution.py:183
  1023.8 16.4 %copy-start.22 = (f32[512]{0:T(512)S(1)}, f32[512]{0:T(512)}, u32[]{:S(2)}) copy-start(f32[512]{0:T(512)} %copy-done.21) | copy-start | bytes 6148
  1023.8 16.4 %copy-start.25 = (f32[512]{0:T(512)S(1)}, f32[512]{0:T(512)}, u32[]{:S(2)}) copy-start(f32[512]{0:T(512)} %copy-done.24) | copy-start | bytes 6148
  1023.8 16.4 %copy-start.27 = (f32[512]{0:T(512)S(1)}, f32[512]{0:T(512)}, u32[]{:S(2)}) copy-start(f32[512]{0:T(512)} %param.34) | copy-start | bytes 6148
  1023.8 16.4 %copy-start.34 = (f32[512]{0:T(512)S(1)}, f32[512]{0:T(512)}, u32[]{:S(2)}) copy-start(f32[512]{0:T(512)} %param.35) | copy-start | bytes 6148
  1040.2 15.9 %copy-start.4 = (f32[16,32,512]{2,0,1:T(8,128)S(1)}, f32[16,32,512]{2,0,1:T(8,128)}, u32[]{:S(2)}) copy-start(f32[16,32,512]{2,0,1:T(8,128)} %copy-done.3) | copy-start | bytes 3145732
  1042.9 53.7 %all-to-all-start.1 = ((bf16[32,16,512]{2,1,0:T(8,128)(2,1)}), bf16[32,16,512]{2,1,0:T(8,128)(2,1)S(1)}, u32[]{:S(2)}, u32[]{:S(2)}) async-start(bf16[32,16,512]{2,1,0:T(8,128)(2,1)} %bitcast.80), calls=%async_computation.2 | async-start | bytes 1048576 | tf_op jit(solution)/shard_map/all_to_all | solution.py:69
  1096.6 0.8 copy-start.13
  1097.4 97.0 %all-to-all-start.3 = ((bf16[32,16,512]{2,1,0:T(8,128)(2,1)}), bf16[32,16,512]{2,1,0:T(8,128)(2,1)S(1)}, u32[]{:S(2)}, u32[]{:S(2)}) async-start(bf16[32,16,512]{2,1,0:T(8,128)(2,1)} %bitcast.81), calls=%async_computation.5 | async-start | bytes 1048576 | tf_op jit(solution)/shard_map/all_to_all | solution.py:72
  1102.7 9.7 copy-start.14
  1143.7 9.6 copy-start.31
  1143.7 9.6 copy-start.32
  1143.7 9.6 copy-start.35
  1231.7 6.3 copy-start.15
  1231.7 7.6 copy-start.18
Sparse Core Ops, SparseCore 0:
  44.0 21.5 all-gather.2
  497.9 44.6 reduce-scatter.2
  562.7 22.6 all-gather.4
  1010.1 45.9 reduce-scatter.4
  1062.7 168.9 all-reduce.3
where the time goes:
time: 1260 us; the launch traced here: 1250 us
  waiting for transfers between devices  618 us (49%)
  local copies, waits for them, and re-layouts  230 us (18%)
  other arithmetic  200 us (16%)
  matrix products  81.1 us (6%)
  blocking collectives  74.4 us (6%)
  starting transfers between devices  28.8 us (2%)
  between operations  15.2 us (1%)
    ppermute x4, waiting for transfers between devices, shifted(): return lax.ppermute(block, axis, route)  349 us
    ppermute x2, waiting for transfers between devices, extended(): lax.ppermute(head, axis, [((i + 1) % count, i) for i in range(count)])  142 us
    unnamed x106, local copies, waits for them, and re-layouts  97.5 us
    reduce_scatter x2, waiting for transfers between devices, combine_sums(): lax.psum_scatter(middle_part + from_above + from_below, 'sub', scatter_di...  46.7 us
    psum x1, blocking collectives, shards(): lax.psum((grad_edge_w_one, grad_edge_b_one, grad_edge_w_two, grad_edge_b_...  41.1 us
    psum x1, waiting for transfers between devices, shards(): lax.psum((grad_edge_w_one, grad_edge_b_one, grad_edge_w_two, grad_edge_b_...  36.1 us
    scatter-add x1, other arithmetic, shards(): jax.ops.segment_sum(grad_stacked[:, 2 * width:], recv_wide, num_segments=...  34 us
    scatter-add x1, other arithmetic, shards(): jax.ops.segment_sum(live * edge_result, recv_wide, num_segments=3 * per_g...  33.5 us
  transfers between devices with their start and end apart: 16, of which 11 were waited for; matrix products, arithmetic and copies ran while one was open for 15% of the time, Pallas kernels for 0%

commit v1 on v0

v1 whole, which is shorter than its diff:
```python
import jax
import jax.numpy as jnp
from jax import lax
from jax.sharding import PartitionSpec as P

EPSILON = 1e-05


def shifted(block, axis, distance):
    devices = range(lax.axis_size(axis))
    route = [((i - distance) % len(devices), i) for i in devices]
    return lax.ppermute(block, axis, route)


def norm_apply(values, gain, shift):
    average = jnp.mean(values, -1, keepdims=True)
    centred = values - average
    variance = jnp.mean(centred * centred, -1, keepdims=True)
    return centred * lax.rsqrt(variance + EPSILON) * gain + shift


def silu_slope(values):
    logistic = jax.nn.sigmoid(values)
    return logistic * (1.0 + values * (1.0 - logistic))


def matmul(left, right):
    return jnp.dot(left, right, preferred_element_type=jnp.float32)


def left_matmul(left, right):
    return lax.dot_general(
        left, right, (((0,), (0,)), ((), ())), preferred_element_type=jnp.float32
    )


def right_matmul(left, right):
    return lax.dot_general(
        left, right, (((1,), (1,)), ((), ())), preferred_element_type=jnp.float32
    )


def to_nodes(channels):
    return lax.all_to_all(
        channels.astype(jnp.bfloat16), ("blk", "sub"), split_axis=1, concat_axis=0, tiled=True
    )


def to_channels(values):
    return lax.all_to_all(
        values.astype(jnp.bfloat16), ("blk", "sub"), split_axis=0, concat_axis=1, tiled=True
    ).astype(jnp.float32)


def widened(rows):
    below = shifted(rows, "blk", 1)
    above = shifted(rows, "blk", -1)
    return lax.all_gather(jnp.concatenate([below, rows, above], 0), "sub", axis=0, tiled=True)


def combine_sums(wide_sums, per_device):
    mine = lax.psum_scatter(
        wide_sums.astype(jnp.bfloat16), "sub", scatter_dimension=0, tiled=True
    )
    from_above = shifted(mine[:per_device], "blk", -1)
    from_below = shifted(mine[2 * per_device :], "blk", 1)
    return (
        mine[per_device : 2 * per_device].astype(jnp.float32)
        + from_above.astype(jnp.float32)
        + from_below.astype(jnp.float32)
    )


def shards(
    node_input,
    edge_input,
    senders,
    receivers,
    edge_count,
    edge_w_one,
    edge_b_one,
    edge_w_two,
    edge_b_two,
    edge_gain,
    edge_shift,
    node_w_one,
    node_b_one,
    node_w_two,
    node_b_two,
    node_gain,
    node_shift,
    node_cotangent,
    edge_cotangent,
):
    groups = lax.axis_size("blk")
    sub_count = lax.axis_size("sub")
    block_index = lax.axis_index("blk")
    sub_index = lax.axis_index("sub")
    width = edge_input.shape[1]
    node_low = to_nodes(node_input).T
    node_upstream = to_nodes(node_cotangent).T.astype(jnp.float32)
    per_device = node_low.shape[0]
    per_group = per_device * sub_count
    my_start = (block_index * sub_count + sub_index) * per_device
    send_local = senders - my_start
    relative = (receivers // per_group - block_index + 1 + groups) % groups
    recv_sub = receivers % per_group // per_device
    recv_wide = (recv_sub * 3 + relative) * per_device + receivers % per_device
    slot_index = jnp.arange(edge_input.shape[0], dtype=jnp.int32)
    live = jnp.where(slot_index < edge_count[0], 1.0, 0.0).astype(jnp.float32)[:, None]
    wide_low = widened(node_low)
    stacked = jnp.concatenate(
        [edge_input, jnp.take(node_low, send_local, axis=0), jnp.take(wide_low, recv_wide, axis=0)],
        axis=1,
    )
    first_pre = matmul(stacked, edge_w_one) + edge_b_one
    first_act = jax.nn.silu(first_pre).astype(jnp.bfloat16)
    second_pre = matmul(first_act, edge_w_two) + edge_b_two
    edge_branch, edge_norm_back = jax.vjp(norm_apply, second_pre, edge_gain, edge_shift)
    edge_result = edge_input.astype(jnp.float32) + live * edge_branch
    wide_sums = jax.ops.segment_sum(live * edge_result, recv_wide, num_segments=3 * per_group)
    gathered = combine_sums(wide_sums, per_device)
    joined = jnp.concatenate([node_low, gathered.astype(jnp.bfloat16)], axis=1)
    third_pre = matmul(joined, node_w_one) + node_b_one
    third_act = jax.nn.silu(third_pre).astype(jnp.bfloat16)
    fourth_pre = matmul(third_act, node_w_two) + node_b_two
    node_branch, node_norm_back = jax.vjp(norm_apply, fourth_pre, node_gain, node_shift)
    grad_fourth, grad_node_gain, grad_node_shift = node_norm_back(node_upstream)
    fourth_low = grad_fourth.astype(jnp.bfloat16)
    grad_node_w_two = left_matmul(third_act, fourth_low)
    grad_node_b_two = jnp.sum(fourth_low.astype(jnp.float32), 0)
    grad_third = right_matmul(fourth_low, node_w_two) * silu_slope(third_pre)
    third_low = grad_third.astype(jnp.bfloat16)
    grad_node_w_one = left_matmul(joined, third_low)
    grad_node_b_one = jnp.sum(third_low.astype(jnp.float32), 0)
    grad_joined = right_matmul(third_low, node_w_one)
    grad_nodes = grad_joined[:, :width]
    grad_gathered = grad_joined[:, width:]
    wide_grad = widened(grad_gathered.astype(jnp.bfloat16))
    node_summed = lax.psum(
        (grad_node_w_one, grad_node_b_one, grad_node_w_two, grad_node_b_two, grad_node_gain, grad_node_shift),
        ("blk", "sub"),
    )
    node_out = node_input + to_channels(node_branch.T)
    edge_total = edge_cotangent.astype(jnp.float32) + live * jnp.take(wide_grad, recv_wide, axis=0).astype(jnp.float32)
    grad_second, grad_edge_gain, grad_edge_shift = edge_norm_back(live * edge_total)
    second_low = grad_second.astype(jnp.bfloat16)
    grad_edge_w_two = left_matmul(first_act, second_low)
    grad_edge_b_two = jnp.sum(second_low.astype(jnp.float32), 0)
    grad_first = right_matmul(second_low, edge_w_two) * silu_slope(first_pre)
    first_low = grad_first.astype(jnp.bfloat16)
    grad_edge_w_one = left_matmul(stacked, first_low)
    grad_edge_b_one = jnp.sum(first_low.astype(jnp.float32), 0)
    grad_stacked = right_matmul(first_low, edge_w_one)
    edge_grad = edge_total + grad_stacked[:, :width]
    sender_grad = jax.ops.segment_sum(
        grad_stacked[:, width : 2 * width], send_local, num_segments=per_device
    )
    receiver_wide = jax.ops.segment_sum(
        grad_stacked[:, 2 * width :], recv_wide, num_segments=3 * per_group
    )
    receiver_grad = combine_sums(receiver_wide, per_device)
    node_total = grad_nodes + sender_grad + receiver_grad
    summed = lax.psum(
        (
            grad_edge_w_one,
            grad_edge_b_one,
            grad_edge_w_two,
            grad_edge_b_two,
            grad_edge_gain,
            grad_edge_shift,
        ),
        ("blk", "sub"),
    )
    node_grad = node_cotangent + to_channels(node_total.T)
    return (
        node_out,
        edge_result,
        node_grad,
        edge_grad,
        summed[0],
        summed[1],
        summed[2],
        summed[3],
        summed[4],
        summed[5],
        node_summed[0],
        node_summed[1],
        node_summed[2],
        node_summed[3],
        node_summed[4],
        node_summed[5],
    )


def solution(mesh):
    placed = (
        P(("blk", "sub"), None),
        P(("blk", "sub"), None),
        P(("blk", "sub")),
        P(("blk", "sub")),
        P(("blk", "sub")),
        P(),
        P(),
        P(),
        P(),
        P(),
        P(),
        P(),
        P(),
        P(),
        P(),
        P(),
        P(),
        P(("blk", "sub"), None),
        P(("blk", "sub"), None),
    )
    return jax.shard_map(
        shards,
        mesh=mesh,
        in_specs=placed,
        out_specs=(
            P(("blk", "sub"), None),
            P(("blk", "sub"), None),
            P(("blk", "sub"), None),
            P(("blk", "sub"), None),
            P(),
            P(),
            P(),
            P(),
            P(),
            P(),
            P(),
            P(),
            P(),
            P(),
            P(),
            P(),
        ),
        check_vma=False,
    )
```

time: 1260 us -> 781 us (0.62)
  waiting for transfers between devices: 618 us -> 243 us
  local copies, waits for them, and re-layouts: 230 us -> 140 us
    ppermute x4 -> x8, waiting for transfers between devices: 349 us -> 62.9 us  [shifted(): return lax.ppermute(block, axis, route)]
    ppermute x4 -> x0, waiting for transfers between devices: 142 us -> none  [the longest x2 142 us: extended(): lax.ppermute(head, axis, [((i + 1) % count, i) for i in range(count)])]
    unnamed x106 -> x91, local copies, waits for them, and re-layouts: 97.5 us -> 59.4 us
    reduce_scatter x2, waiting for transfers between devices: 46.7 us -> 82.9 us  [combine_sums(): lax.psum_scatter(wide_sums.astype(jnp.bfloat16), 'sub', scatter_dimension...]
    slice x3 -> x2, local copies, waits for them, and re-layouts: 21.7 us -> 4.47 us  [combine_sums(): from_above = shifted(mine[:per_device], 'blk', -1)]
    add x2, other arithmetic: 16.8 us -> 2.15 us  [the longest x1 1.08 us: shards(): node_grad = node_cotangent + to_channels(node_total.T)]
  transfers between devices with their start and end apart: 16 -> 16, of which waited for: 11 -> 11; matrix products, arithmetic and copies ran while one was open for 15% -> 21% of each run, Pallas kernels for 0% -> 0%
where the time goes in v1:
time: 781 us; the launch traced here: 770 us
  waiting for transfers between devices  243 us (31%)
  other arithmetic  192 us (25%)
  local copies, waits for them, and re-layouts  140 us (18%)
  matrix products  80.4 us (10%)
  blocking collectives  63.6 us (8%)
  starting transfers between devices  34.6 us (4%)
  between operations  15.4 us (2%)
    reduce_scatter x2, waiting for transfers between devices, combine_sums(): lax.psum_scatter(wide_sums.astype(jnp.bfloat16), 'sub', scatter_dimension...  82.9 us
    ppermute x8, waiting for transfers between devices, shifted(): return lax.ppermute(block, axis, route)  62.9 us
    unnamed x91, local copies, waits for them, and re-layouts  59.4 us
    all_gather x2, waiting for transfers between devices, widened(): lax.all_gather(jnp.concatenate([below, rows, above], 0), 'sub', axis=0, t...  51.8 us
    psum x1, waiting for transfers between devices, shards(): lax.psum((grad_edge_w_one, grad_edge_b_one, grad_edge_w_two, grad_edge_b_...  45.8 us
    psum x1, blocking collectives, shards(): lax.psum((grad_edge_w_one, grad_edge_b_one, grad_edge_w_two, grad_edge_b_...  40.9 us
    scatter-add x1, other arithmetic, shards(): jax.ops.segment_sum(grad_stacked[:, 2 * width:], recv_wide, num_segments=...  34 us
    scatter-add x1, other arithmetic, shards(): jax.ops.segment_sum(live * edge_result, recv_wide, num_segments=3 * per_g...  33.5 us
  transfers between devices with their start and end apart: 16, of which 11 were waited for; matrix products, arithmetic and copies ran while one was open for 21% of the time, Pallas kernels for 0%

profile of v1, /device:TPU:0, one launch (start us, length us, event | category | flops | bytes accessed | tf_op | source)
XLA Modules:
  0.0 769.8 jit_solution(18369747307095065011)
XLA Ops:
  8.7 22.7 %all_to_all.58 = bf16[16,32,512]{2,0,1:T(8,128)(2,1)S(1)} all-to-all(bf16[16,32,512]{2,0,1:T(8,128)(2,1)S(1)} %bitcast.85), channel_id=1, replica_groups=mesh['blk'=8,'sub'=4] {'blk','sub'}, dimensions={1} | all-to-all | bytes 1048576 | tf_op jit(solution)/shard_map/all_to_all | solution.py:44
  32.9 3.5 collective-permute-start.1
  36.4 18.6 %collective-permute-done = bf16[512,512]{1,0:T(8,128)(2,1)S(1)} collective-permute-done((bf16[512,512]{1,0:T(8,128)(2,1)S(1)}, bf16[512,512]{1,0:T(8,128)(2,1)S(1)}, u32[]{:S(2)}, u32[]{:S(2)}) %collective-permute-start) | collective-permute-done | bytes 524320 | tf_op jit(solution)/shard_map/ppermute | solution.py:12
  55.0 2.2 collective-permute-done.1
  59.2 6.7 copy.71
  66.6 13.8 %gather_fusion = bf16[4608,512]{1,0:T(8,128)(2,1)} fusion(bf16[512,512]{1,0:T(8,128)(2,1)S(1)} %bitcast.74, s32[5120]{0:T(1024)S(1)} %pad_clamp_fusion.1), kind=kCustom, calls=%fused_computation.2 | custom fusion | bytes 9455616 | tf_op jit(solution)/shard_map/jit(_take)/gather | solution.py:113
  80.4 6.7 broadcast_select_fusion.1
  87.1 15.7 %all-gather.3.cloned.1.call-done = bf16[6144,512]{1,0:T(8,128)(2,1)} async-done(((bf16[1536,512]{1,0:T(8,128)(2,1)}), bf16[6144,512]{1,0:T(8,128)(2,1)}) %all-gather.3.cloned.1.call-update) | async-done | bytes 6291472 | tf_op jit(solution)/shard_map/all_gather | solution.py:58
  102.8 17.6 %gather_fusion.1 = bf16[4608,512]{1,0:T(8,128)(2,1)} fusion(bf16[6144,512]{1,0:T(8,128)(2,1)} %all-gather.3.cloned.1.call-done, s32[5120]{0:T(1024)S(1)} %pad_clamp_fusion), kind=kCustom, calls=%fused_computation.clone | custom fusion | bytes 9455616 | tf_op jit(solution)/shard_map/jit(_take)/gather | solution.py:113
  120.4 6.7 broadcast_select_fusion
  127.1 15.1 %multiply_convert_fusion.1 = (bf16[4608,512]{1,0:T(8,128)(2,1)}, f32[4608,512]{1,0:T(8,128)}) fusion(f32[512]{0:T(512)S(1)} %copy-done.33, bf16[1536,512]{1,0:T(8,128)(2,1)S(1)} %copy-done, bf16[4608,512]{1,0:T(8,128)(2,1)} %broadcast_select_fusion, bf16[4608,512]{1,0:T(8,128)(2,1)} %broadcast_select_fusion.1, bf16[4608,512]{1,0:T(8,128)(2,1)} %param.22), kind=kOutput, calls=%fused_computation.21 | convolution fusion | flops 7304380416 | bytes 29886464 | tf_op jit(solution)/shard_map/dot_general | solution.py:28
  142.3 4.8 add_reduce_fusion
  147.2 1.8 multiply_reduce_fusion.2
  149.0 3.5 slice-done.3
  152.8 8.8 %broadcast_multiply_fusion = (f32[4608,512]{0,1:T(8,128)}, f32[4608,512]{0,1:T(8,128)}) fusion(f32[4608]{0:T(1024)S(1)} %get-tuple-element.129, f32[512]{0:T(512)S(1)} %copy-done.26, f32[512]{0:T(512)S(1)} %copy-done.22, f32[4608]{0:T(1024)S(1)} %get-tuple-element.130, f32[4608]{0:T(1024)S(1)} %broadcast_multiply_fusion.1, ...), kind=kLoop, calls=%fused_computation.32 | loop fusion | flops 21233664 | bytes 33091584 | tf_op jit(solution)/shard_map/mul | solution.py:121
  161.6 9.6 %copy.72 = f32[4608,512]{1,0:T(8,128)} copy(f32[4608,512]{0,1:T(8,128)} %get-tuple-element.106) | data formatting | bytes 18874368 | tf_op jit(solution)/shard_map/mul | solution.py:121
  171.2 33.5 %scatter_custom_fusion = f32[6144,512]{1,0:T(8,128)} fusion(s32[4608]{0:T(1024)S(1)} %get-tuple-element.111, f32[4608,512]{1,0:T(8,128)} %copy.72, f32[]{:T(128)} %constant.106.clone.1), kind=kCustom, calls=%fused_computation.28 | custom fusion | flops 2359296 | bytes 12583424 | tf_op jit(solution)/shard_map/scatter-add | solution.py:121
  204.7 8.2 %convert_element_type.115 = bf16[6144,512]{1,0:T(8,128)(2,1)} convert(f32[6144,512]{1,0:T(8,128)} %scatter_custom_fusion) | non-fusion elementwise | flops 3145728 | bytes 18874368 | tf_op jit(solution)/shard_map/convert_element_type | solution.py:63
  212.9 58.5 %reduce-scatter.3.cloned.1.call-done = bf16[1536,512]{1,0:T(8,128)(2,1)} async-done(((bf16[6144,512]{1,0:T(8,128)(2,1)}), bf16[1536,512]{1,0:T(8,128)(2,1)}) %reduce-scatter.3.cloned.1.call-update) | async-done | bytes 1572880 | tf_op jit(solution)/shard_map/reduce_scatter | solution.py:62
  271.4 2.2 fusion.42
  273.6 4.2 collective-permute-start.2
  278.8 5.1 all-to-all-start.2
  284.0 19.6 %collective-permute-done.2 = bf16[512,512]{1,0:T(8,128)(2,1)} collective-permute-done((bf16[512,512]{1,0:T(8,128)(2,1)}, bf16[512,512]{1,0:T(8,128)(2,1)}, u32[]{:S(2)}, u32[]{:S(2)}) %collective-permute-start.2) | collective-permute-done | bytes 524320 | tf_op jit(solution)/shard_map/ppermute | solution.py:12
  305.4 2.1 convolution_add_fusion.1
  307.5 3.0 fusion.43
  312.2 2.3 fusion.17
  314.6 3.1 convert_reduce_fusion.2
  317.7 2.9 convert_reduce_fusion.3
  322.7 2.5 collective-permute-start.4
  325.2 2.5 collective-permute-start.5
  327.7 20.1 %collective-permute-done.4 = bf16[512,512]{1,0:T(8,128)(2,1)S(1)} collective-permute-done((bf16[512,512]{1,0:T(8,128)(2,1)S(1)}, bf16[512,512]{1,0:T(8,128)(2,1)S(1)}, u32[]{:S(2)}, u32[]{:S(2)}) %collective-permute-start.4) | collective-permute-done | bytes 524320 | tf_op jit(solution)/shard_map/ppermute | solution.py:12
  347.8 2.2 collective-permute-done.5
  351.7 6.8 copy.75
  358.5 36.1 %all-gather.5.cloned.1.call-done = bf16[6144,512]{1,0:T(8,128)(2,1)} async-done(((bf16[1536,512]{1,0:T(8,128)(2,1)}), bf16[6144,512]{1,0:T(8,128)(2,1)}) %all-gather.5.cloned.1.call-update) | async-done | bytes 6291472 | tf_op jit(solution)/shard_map/all_gather | solution.py:58
  394.6 17.6 %gather_fusion.2 = bf16[4608,512]{1,0:T(8,128)(2,1)} fusion(bf16[6144,512]{1,0:T(8,128)(2,1)} %all-gather.5.cloned.1.call-done, s32[5120]{0:T(1024)S(1)} %pad_clamp_fusion), kind=kCustom, calls=%fused_computation.1.clone | custom fusion | bytes 9455616 | tf_op jit(solution)/shard_map/jit(_take)/gather | solution.py:145
  412.2 6.8 copy.76
  419.0 10.3 %multiply_reduce_fusion = (f32[512]{0:T(512)S(1)}, f32[4608]{0:T(1024)S(1)}, f32[512]{0:T(512)S(1)}) fusion(f32[4608,512]{0,1:T(8,128)} %copy-done.1, f32[4608]{0:T(1024)S(1)} %get-tuple-element.130, f32[4608]{0:T(1024)S(1)} %broadcast_multiply_fusion.1, f32[512]{0:T(512)S(1)} %copy-done.19, bf16[4608,512]{0,1:T(8,128)(2,1)} %copy.75, ...), kind=kLoop, calls=%fused_computation.12 | loop fusion | flops 35383808 | bytes 18960896 | tf_op jit(solution)/shard_map/transpose(jvp())/reduce_sum | solution.py:19
  429.4 8.9 %fusion.39 = (f32[4608]{0:T(1024)S(1)}, f32[4608,512]{0,1:T(8,128)}) fusion(f32[4608]{0:T(1024)S(1)} %multiply_multiply_fusion, f32[4608]{0:T(1024)S(1)} %broadcast_multiply_fusion.1, f32[4608,512]{0,1:T(8,128)S(1)} %bitcast.78, f32[512]{0:T(512)S(1)} %copy-done.19, f32[4608]{0:T(1024)S(1)} %get-tuple-element.130, f32[512]{0:T(512)S(1)} %copy-done.22, ...), kind=kLoop, calls=%fused_computation.121 | loop fusion | flops 33025536 | bytes 28412416 | tf_op jit(solution)/shard_map/transpose(jvp())/reduce_sum | solution.py:17
  438.3 5.3 convert_reduce_fusion
  443.6 9.2 %convert_reduce_fusion.1 = (f32[512]{0:T(512)S(1)}, bf16[4608,512]{1,0:T(8,128)(2,1)S(1)}) fusion(f32[4608,512]{1,0:T(8,128)} %get-tuple-element.120, f32[512]{0:T(512)S(1)} %copy-done.33, bf16[4608,512]{0,1:T(8,128)(2,1)S(1)} %get-tuple-element.103, bf16[512,512]{1,0:T(8,128)(2,1)S(1)} %copy-done.30), kind=kOutput, calls=%fused_computation.14 | convolution fusion | flops 2444230144 | bytes 19402752 | tf_op jit(solution)/shard_map/dot_general | solution.py:38
  452.8 2.2 copy-done.35
  455.0 13.5 %fusion.45 = f32[4608,1536]{1,0:T(8,128)} fusion(bf16[4608,512]{1,0:T(8,128)(2,1)S(1)} %get-tuple-element.126, bf16[1536,512]{1,0:T(8,128)(2,1)S(1)} %copy-done), kind=kOutput, calls=%fused_computation.126 | convolution fusion | flops 7247757312 | bytes 34603008 | tf_op jit(solution)/shard_map/dot_general | solution.py:38
  468.4 34.0 %scatter_custom_fusion.1 = f32[6144,512]{1,0:T(8,128)} fusion(s32[4608]{0:T(1024)S(1)} %get-tuple-element.111, f32[4608,1536]{1,0:T(8,128)} %fusion.45, f32[]{:T(128)} %constant.106.clone.1), kind=kCustom, calls=%fused_computation.10 | custom fusion | flops 2359296 | bytes 22020608 | tf_op jit(solution)/shard_map/scatter-add | solution.py:159
  502.4 8.2 %convert_element_type.136 = bf16[6144,512]{1,0:T(8,128)(2,1)} convert(f32[6144,512]{1,0:T(8,128)} %scatter_custom_fusion.1) | non-fusion elementwise | flops 3145728 | bytes 18874368 | tf_op jit(solution)/shard_map/convert_element_type | solution.py:63
  510.6 4.7 all-to-all-start.1
  515.7 2.2 fusion.18
  517.9 3.2 fusion.38
  521.0 16.3 %fusion.9 = f32[1536,512]{1,0:T(8,128)} fusion(bf16[4608,512]{1,0:T(8,128)(2,1)} %copy-done.35, bf16[4608,512]{1,0:T(8,128)(2,1)} %broadcast_select_fusion, bf16[4608,512]{1,0:T(8,128)(2,1)} %broadcast_select_fusion.1, bf16[4608,512]{1,0:T(8,128)(2,1)} %param.22), kind=kOutput, calls=%fused_computation.30 | convolution fusion | flops 7290224640 | bytes 22020096 | tf_op jit(solution)/shard_map/dot_general | solution.py:32
  537.4 7.4 fusion.46
  544.8 24.4 %reduce-scatter.5.cloned.1.call-done = bf16[1536,512]{1,0:T(8,128)(2,1)} async-done(((bf16[6144,512]{1,0:T(8,128)(2,1)}), bf16[1536,512]{1,0:T(8,128)(2,1)}) %reduce-scatter.5.cloned.1.call-update) | async-done | bytes 1572880 | tf_op jit(solution)/shard_map/reduce_scatter | solution.py:62
  569.2 2.2 fusion.41
  571.4 4.2 collective-permute-start.6
  576.2 9.8 %copy.80 = f32[4608,512]{1,0:T(8,128)} copy(f32[4608,512]{0,1:T(8,128)} %get-tuple-element.107) | data formatting | bytes 18874368
  588.3 8.5 %slice.61 = f32[4608,512]{1,0:T(8,128)} slice(f32[4608,1536]{1,0:T(8,128)} %fusion.45), slice={[0:4608], [0:512]} | slice | bytes 18874368 | tf_op jit(solution)/shard_map/slice | solution.py:155
  596.8 9.6 %copy.82 = f32[4608,512]{0,1:T(8,128)} copy(f32[4608,512]{1,0:T(8,128)} %slice.61) | data formatting | bytes 18874368
  606.5 2.0 slice_add_fusion
  608.5 29.2 %scatter_custom_fusion.2 = f32[512,512]{1,0:T(8,128)S(1)} fusion(f32[512,512]{1,0:T(8,128)S(1)} %slice_add_fusion, s32[4608]{0:T(1024)} %copy-done.18, f32[4608,1536]{1,0:T(8,128)} %fusion.45), kind=kCustom, calls=%fused_computation.8 | custom fusion | flops 2359296 | bytes 10485760 | tf_op jit(solution)/shard_map/scatter-add | solution.py:156
  638.8 5.4 all-to-all-start.3
  644.3 12.3 %fusion.4 = f32[4608,512]{0,1:T(8,128)} fusion(f32[4608,512]{0,1:T(8,128)} %copy.82, bf16[4608,512]{0,1:T(8,128)(2,1)} %copy.75, f32[4608]{0:T(1024)S(1)} %get-tuple-element.129, bf16[4608,512]{0,1:T(8,128)(2,1)} %copy.76, pred[4608]{0:T(1024)(128)(4,1)S(1)} %get-tuple-element.110), kind=kLoop, calls=%fused_computation.25 | loop fusion | flops 14155776 | bytes 28334592 | tf_op jit(solution)/shard_map/add | solution.py:155
  656.6 9.7 %copy.81 = f32[4608,512]{1,0:T(8,128)} copy(f32[4608,512]{0,1:T(8,128)} %fusion.4) | data formatting | bytes 18874368
  666.3 40.9 %all-reduce = (f32[512]{0:T(512)}, f32[512]{0:T(512)}, f32[512]{0:T(512)}, f32[512]{0:T(512)}, f32[512]{0:T(512)}, /*index=5*/f32[512]{0:T(512)}, f32[512]{0:T(512)}, f32[512]{0:T(512)}) all-reduce(f32[512]{0:T(512)S(1)} %get-tuple-element.125, f32[512]{0:T(512)S(1)} %get-tuple-element.102, ...), channel_id=1, replica_groups=mesh['blk'=8,'sub'=4] {'blk','sub'}, use_global_device_ids=true, to_apply=%region_15.17 | all-reduce | flops 4096 | bytes 32768 | tf_op jit(solution)/shard_map/psum | solution.py:164
  708.5 45.8 %all-reduce.4.cloned.1.call-done = (f32[1536,512]{1,0:T(8,128)}, f32[512,512]{1,0:T(8,128)}, f32[1024,512]{1,0:T(8,128)}, f32[512,512]{1,0:T(8,128)}) async-done(((f32[1536,512]{1,0:T(8,128)}, f32[512,512]{1,0:T(8,128)}, f32[1024,512]{1,0:T(8,128)}, f32[512,512]{1,0:T(8,128)}), (f32[1536,512]{1,0:T(8,128)}, f32[512,512]{1,0:T(8,128)}, f32[1024,512]{1,0:T(8,128)}, ...) | async-done | bytes 7340048 | tf_op jit(solution)/shard_map/psum | solution.py:164
  754.3 4.0 copy.97
  758.3 2.3 copy.98
  (137 shorter events, 21.6 us)
Async XLA Ops:
  7.2 119.9 %copy-start = (bf16[1536,512]{1,0:T(8,128)(2,1)S(1)}, bf16[1536,512]{1,0:T(8,128)(2,1)}, u32[]{:S(2)}) copy-start(bf16[1536,512]{1,0:T(8,128)(2,1)} %param.26) | copy-start | bytes 4718596
  7.2 58.7 %copy-start.20 = (s32[4608]{0:T(1024)S(1)}, s32[4608]{0:T(1024)}, u32[]{:S(2)}) copy-start(s32[4608]{0:T(1024)} %param.24) | copy-start | bytes 55300
  7.2 58.8 %copy-start.21 = (s32[4608]{0:T(1024)S(1)}, s32[4608]{0:T(1024)}, u32[]{:S(2)}) copy-start(s32[4608]{0:T(1024)} %param.23) | copy-start | bytes 55300
  7.2 95.6 %all-gather.3.cloned.1.call-start = ((), (), s32[]{:S(2)}) async-start(), calls=%async_computation.6 | async-start | bytes 7864320 | tf_op jit(solution)/shard_map/all_gather | solution.py:58
  31.6 23.4 %collective-permute-start = (bf16[512,512]{1,0:T(8,128)(2,1)S(1)}, bf16[512,512]{1,0:T(8,128)(2,1)S(1)}, u32[]{:S(2)}, u32[]{:S(2)}) collective-permute-start(bf16[512,512]{1,0:T(8,128)(2,1)S(1)} %bitcast.71), channel_id=1, source_target_pairs={{28,0},{0,4},{4,8},{8,12},{12,16},{16,20},{20,24},{24,28},{29,1},{... | collective-permute-start | bytes 1572872 | tf_op jit(solution)/shard_map/ppermute | solution.py:12
  32.9 24.3 %collective-permute-start.1 = (bf16[512,512]{1,0:T(8,128)(2,1)S(1)}, bf16[512,512]{1,0:T(8,128)(2,1)S(1)}, u32[]{:S(2)}, u32[]{:S(2)}) collective-permute-start(bf16[512,512]{1,0:T(8,128)(2,1)S(1)} %bitcast.72), channel_id=1, source_target_pairs={{4,0},{8,4},{12,8},{16,12},{20,16},{24,20},{28,24},{0,28},{5,1},{9... | collective-permute-start | bytes 1572872 | tf_op jit(solution)/shard_map/ppermute | solution.py:12
  58.5 213.0 %reduce-scatter.3.cloned.1.call-start = ((), (), s32[]{:S(2)}) async-start(), calls=%async_computation.7 | async-start | bytes 7864320 | tf_op jit(solution)/shard_map/reduce_scatter | solution.py:62
  66.0 0.6 copy-start.18
  120.4 6.7 copy-start.33
  127.1 15.1 %copy-start.19 = (f32[512]{0:T(512)S(1)}, f32[512]{0:T(512)}, u32[]{:S(2)}) copy-start(f32[512]{0:T(512)} %param.29) | copy-start | bytes 6148
  127.1 15.1 %copy-start.29 = (bf16[512,512]{1,0:T(8,128)(2,1)S(1)}, bf16[512,512]{1,0:T(8,128)(2,1)}, u32[]{:S(2)}) copy-start(bf16[512,512]{1,0:T(8,128)(2,1)} %param.28) | copy-start | bytes 1572868
  147.1 14.5 %copy-start.1 = (f32[4608,512]{0,1:T(8,128)}, f32[4608,512]{0,1:T(8,128)S(1)}, u32[]{:S(2)}) copy-start(f32[4608,512]{0,1:T(8,128)S(1)} %get-tuple-element.122) | copy-start | bytes 28311556
  147.1 5.3 slice-start.3
  147.1 5.3 copy-start.22
  147.1 5.3 copy-start.26
  147.1 5.7 slice-start.4
  204.7 73.2 %copy-start.8 = (f32[16,16384]{1,0:T(8,128)S(1)}, f32[16,16384]{1,0:T(8,128)}, u32[]{:S(2)}) copy-start(f32[16,16384]{1,0:T(8,128)} %param.38) | copy-start | bytes 3145732
  212.9 92.5 %copy-start.31 = (f32[512]{0:T(512)S(1)}, f32[512]{0:T(512)}, u32[]{:S(2)}) copy-start(f32[512]{0:T(512)} %param.33) | copy-start | bytes 6148
  212.9 94.6 %copy-start.32 = (f32[512]{0:T(512)S(1)}, f32[512]{0:T(512)}, u32[]{:S(2)}) copy-start(f32[512]{0:T(512)} %param.35) | copy-start | bytes 6148
  212.9 97.6 %copy-start.23 = (f32[512]{0:T(512)S(1)}, f32[512]{0:T(512)}, u32[]{:S(2)}) copy-start(f32[512]{0:T(512)} %param.36) | copy-start | bytes 6148
  273.6 30.0 %collective-permute-start.2 = (bf16[512,512]{1,0:T(8,128)(2,1)}, bf16[512,512]{1,0:T(8,128)(2,1)}, u32[]{:S(2)}, u32[]{:S(2)}) collective-permute-start(bf16[512,512]{1,0:T(8,128)(2,1)} %get-tuple-element.114), channel_id=1, source_target_pairs={{4,0},{8,4},{12,8},{16,12},{20,16},{24,20},{28,24},{0,28},{5,1},{9... | collective-permute-start | bytes 1572872 | tf_op jit(solution)/shard_map/ppermute | solution.py:12
  277.9 36.7 %copy-start.28 = (f32[512]{0:T(512)S(1)}, f32[512]{0:T(512)}, u32[]{:S(2)}) copy-start(f32[512]{0:T(512)} %param.37) | copy-start | bytes 6148
  277.9 25.9 %collective-permute-start.3 = (bf16[512,512]{1,0:T(8,128)(2,1)}, bf16[512,512]{1,0:T(8,128)(2,1)}, u32[]{:S(2)}, u32[]{:S(2)}) collective-permute-start(bf16[512,512]{1,0:T(8,128)(2,1)} %get-tuple-element.115), channel_id=1, source_target_pairs={{28,0},{0,4},{4,8},{8,12},{12,16},{16,20},{20,24},{24,28},{29,1},{... | collective-permute-start | bytes 1572872 | tf_op jit(solution)/shard_map/ppermute | solution.py:12
  278.8 31.7 %all-to-all-start.2 = ((bf16[16,32,512]{2,0,1:T(8,128)(2,1)}), bf16[16,32,512]{2,0,1:T(8,128)(2,1)S(1)}, u32[]{:S(2)}, u32[]{:S(2)}) async-start(bf16[16,32,512]{2,0,1:T(8,128)(2,1)} %bitcast.68), calls=%async_computation.3 | async-start | bytes 1048576 | tf_op jit(solution)/shard_map/all_to_all | solution.py:44
  283.9 110.7 %all-gather.5.cloned.1.call-start = ((), (), s32[]{:S(2)}) async-start(), calls=%async_computation.8 | async-start | bytes 7864320 | tf_op jit(solution)/shard_map/all_gather | solution.py:58
  305.3 5.1 copy-start.15
  307.5 3.0 copy-start.34
  310.5 40.7 %copy-start.3 = (bf16[16,32,512]{2,0,1:T(8,128)(2,1)}, bf16[16,32,512]{2,0,1:T(8,128)(2,1)S(1)}, u32[]{:S(2)}) copy-start(bf16[16,32,512]{2,0,1:T(8,128)(2,1)S(1)} %all-to-all-done.2) | copy-start | bytes 1572868
  310.5 10.1 %copy-start.11 = (bf16[1024,512]{1,0:T(8,128)(2,1)S(1)}, bf16[1024,512]{1,0:T(8,128)(2,1)}, u32[]{:S(2)}) copy-start(bf16[1024,512]{1,0:T(8,128)(2,1)} %param.32) | copy-start | bytes 3145732
  317.7 30.1 %copy-start.17 = (bf16[512,512]{0,1:T(8,128)(2,1)}, bf16[512,512]{0,1:T(8,128)(2,1)S(1)}, u32[]{:S(2)}) copy-start(bf16[512,512]{0,1:T(8,128)(2,1)S(1)} %get-tuple-element.101) | copy-start | bytes 1572868
  320.6 27.2 %copy-start.13 = (bf16[512,512]{1,0:T(8,128)(2,1)}, bf16[512,512]{1,0:T(8,128)(2,1)S(1)}, u32[]{:S(2)}) copy-start(bf16[512,512]{1,0:T(8,128)(2,1)S(1)} %get-tuple-element.128) | copy-start | bytes 1572868
  321.3 1.3 copy-start.5
  322.7 25.0 %collective-permute-start.4 = (bf16[512,512]{1,0:T(8,128)(2,1)S(1)}, bf16[512,512]{1,0:T(8,128)(2,1)S(1)}, u32[]{:S(2)}, u32[]{:S(2)}) collective-permute-start(bf16[512,512]{1,0:T(8,128)(2,1)S(1)} %slice.70), channel_id=1, source_target_pairs={{28,0},{0,4},{4,8},{8,12},{12,16},{16,20},{20,24},{24,28},{29,1},{... | collective-permute-start | bytes 1572872 | tf_op jit(solution)/shard_map/ppermute | solution.py:12
  325.2 24.7 %collective-permute-start.5 = (bf16[512,512]{1,0:T(8,128)(2,1)S(1)}, bf16[512,512]{1,0:T(8,128)(2,1)S(1)}, u32[]{:S(2)}, u32[]{:S(2)}) collective-permute-start(bf16[512,512]{1,0:T(8,128)(2,1)S(1)} %slice.70), channel_id=1, source_target_pairs={{4,0},{8,4},{12,8},{16,12},{20,16},{24,20},{28,24},{0,28},{5,1},{9... | collective-permute-start | bytes 1572872 | tf_op jit(solution)/shard_map/ppermute | solution.py:12
  351.2 218.0 %reduce-scatter.5.cloned.1.call-start = ((), (), s32[]{:S(2)}) async-start(), calls=%async_computation.9 | async-start | bytes 7864320 | tf_op jit(solution)/shard_map/reduce_scatter | solution.py:62
  412.2 17.2 %slice-start = ((s8[9437184]{0:T(1024)(128)(4,1)}), s8[1048576]{0:T(1024)(128)(4,1)S(1)}, s32[]{:S(2)}) async-start(s8[9437184]{0:T(1024)(128)(4,1)} %bitcast.77), calls=%async_computation.11 | async-start | bytes 2097152
  419.0 10.3 %slice-start.1 = ((s8[9437184]{0:T(1024)(128)(4,1)}), s8[4194304]{0:T(1024)(128)(4,1)S(1)}, s32[]{:S(2)}) async-start(s8[9437184]{0:T(1024)(128)(4,1)} %bitcast.77), calls=%async_computation.12 | async-start | bytes 8388608
  419.0 10.4 %slice-start.2 = ((s8[9437184]{0:T(1024)(128)(4,1)}), s8[4194304]{0:T(1024)(128)(4,1)S(1)}, s32[]{:S(2)}) async-start(s8[9437184]{0:T(1024)(128)(4,1)} %bitcast.77), calls=%async_computation.13 | async-start | bytes 8388608
  419.0 10.4 %copy-start.2 = (bf16[4608,512]{0,1:T(8,128)(2,1)S(1)}, bf16[4608,512]{0,1:T(8,128)(2,1)}, u32[]{:S(2)}) copy-start(bf16[4608,512]{0,1:T(8,128)(2,1)} %copy.76) | copy-start | bytes 14155780
  438.3 5.3 copy-start.30
  443.6 9.2 %copy-start.6 = (bf16[4608,512]{0,1:T(8,128)(2,1)}, bf16[4608,512]{0,1:T(8,128)(2,1)S(1)}, u32[]{:S(2)}) copy-start(bf16[4608,512]{0,1:T(8,128)(2,1)S(1)} %get-tuple-element.103) | copy-start | bytes 14155780
  452.8 2.2 copy-start.35
  502.4 13.2 %copy-start.14 = (bf16[512,512]{1,0:T(8,128)(2,1)S(1)}, bf16[512,512]{1,0:T(8,128)(2,1)}, u32[]{:S(2)}) copy-start(bf16[512,512]{1,0:T(8,128)(2,1)} %copy-done.13) | copy-start | bytes 1572868
  502.4 13.2 %copy-start.16 = (bf16[512,512]{1,0:T(8,128)(2,1)S(1)}, bf16[512,512]{1,0:T(8,128)(2,1)}, u32[]{:S(2)}) copy-start(bf16[512,512]{1,0:T(8,128)(2,1)} %copy-done.15) | copy-start | bytes 1572868
  510.6 75.3 %all-to-all-start.1 = ((bf16[32,16,512]{2,1,0:T(8,128)(2,1)}), bf16[32,16,512]{2,1,0:T(8,128)(2,1)}, u32[]{:S(2)}, u32[]{:S(2)}) async-start(bf16[32,16,512]{2,1,0:T(8,128)(2,1)} %bitcast.5), calls=%async_computation.2 | async-start | bytes 1048576 | tf_op jit(solution)/shard_map/all_to_all | solution.py:50
  515.4 238.9 %all-reduce.4.cloned.1.call-start = ((), (), s32[]{:S(2)}) async-start(), calls=%async_computation.10 | async-start | bytes 14680064 | tf_op jit(solution)/shard_map/psum | solution.py:164
  537.4 38.6 %copy-start.4 = (bf16[16,32,512]{2,0,1:T(8,128)(2,1)S(1)}, bf16[16,32,512]{2,0,1:T(8,128)(2,1)}, u32[]{:S(2)}) copy-start(bf16[16,32,512]{2,0,1:T(8,128)(2,1)} %copy-done.3) | copy-start | bytes 1572868
  571.4 35.0 %collective-permute-start.6 = (bf16[512,512]{1,0:T(8,128)(2,1)}, bf16[512,512]{1,0:T(8,128)(2,1)}, u32[]{:S(2)}, u32[]{:S(2)}) collective-permute-start(bf16[512,512]{1,0:T(8,128)(2,1)} %get-tuple-element.112), channel_id=1, source_target_pairs={{4,0},{8,4},{12,8},{16,12},{20,16},{24,20},{28,24},{0,28},{5,1},{9... | collective-permute-start | bytes 1572872 | tf_op jit(solution)/shard_map/ppermute | solution.py:12
  575.7 30.8 %collective-permute-start.7 = (bf16[512,512]{1,0:T(8,128)(2,1)}, bf16[512,512]{1,0:T(8,128)(2,1)}, u32[]{:S(2)}, u32[]{:S(2)}) collective-permute-start(bf16[512,512]{1,0:T(8,128)(2,1)} %get-tuple-element.113), channel_id=1, source_target_pairs={{28,0},{0,4},{4,8},{8,12},{12,16},{16,20},{20,24},{24,28},{29,1},{... | collective-permute-start | bytes 1572872 | tf_op jit(solution)/shard_map/ppermute | solution.py:12
  576.1 11.1 %copy-start.7 = (f32[16,16384]{1,0:T(8,128)S(1)}, f32[16,16384]{1,0:T(8,128)}, u32[]{:S(2)}) copy-start(f32[16,16384]{1,0:T(8,128)} %param.21) | copy-start | bytes 3145732
  638.8 68.3 %all-to-all-start.3 = ((bf16[32,16,512]{2,1,0:T(8,128)(2,1)}), bf16[32,16,512]{2,1,0:T(8,128)(2,1)S(1)}, u32[]{:S(2)}, u32[]{:S(2)}) async-start(bf16[32,16,512]{2,1,0:T(8,128)(2,1)} %bitcast.11), calls=%async_computation.5 | async-start | bytes 1048576 | tf_op jit(solution)/shard_map/all_to_all | solution.py:50
  656.6 9.7 %copy-start.24 = (f32[512]{0:T(512)S(1)}, f32[512]{0:T(512)}, u32[]{:S(2)}) copy-start(f32[512]{0:T(512)} %get-tuple-element.84) | copy-start | bytes 6148
  656.6 9.7 %copy-start.25 = (f32[512]{0:T(512)S(1)}, f32[512]{0:T(512)}, u32[]{:S(2)}) copy-start(f32[512]{0:T(512)} %get-tuple-element.100) | copy-start | bytes 6148
  656.6 9.7 %copy-start.27 = (f32[512]{0:T(512)S(1)}, f32[512]{0:T(512)}, u32[]{:S(2)}) copy-start(f32[512]{0:T(512)} %get-tuple-element.127) | copy-start | bytes 6148
  656.6 50.8 %copy-start.9 = (f32[16,16384]{1,0:T(8,128)S(1)}, f32[16,16384]{1,0:T(8,128)}, u32[]{:S(2)}) copy-start(f32[16,16384]{1,0:T(8,128)} %param.38) | copy-start | bytes 3145732
  754.3 6.3 copy-start.10
  754.3 7.6 copy-start.12
Sparse Core Ops, SparseCore 0:
  58.6 44.1 all-gather.2
  213.0 58.3 reduce-scatter.2
  351.3 43.2 all-gather.4
  510.8 58.3 reduce-scatter.4
  576.3 177.9 all-reduce.3

commit v2 on v1

--- a/solution.py
+++ b/solution.py
@@ -1,6 +1,8 @@
 import jax
 import jax.numpy as jnp
 from jax import lax
+from jax.experimental import pallas as pl
+from jax.experimental.pallas import tpu as pltpu
 from jax.sharding import PartitionSpec as P
 
 EPSILON = 1e-05
@@ -69,6 +71,332 @@
         + from_above.astype(jnp.float32)
         + from_below.astype(jnp.float32)
     )
+
+
+TILE = 512
+CHUNK = 512
+LANES = 128
+VMEM_BYTES = 60 * 2**20
+
+
+def dot(left, right):
+    return jnp.dot(left, right, preferred_element_type=jnp.float32)
+
+
+def dot_left(left, right):
+    return lax.dot_general(
+        left, right, (((0,), (0,)), ((), ())), preferred_element_type=jnp.float32
+    )
+
+
+def split_low(values):
+    high = values.astype(jnp.bfloat16)
+    return high, (values - high.astype(jnp.float32)).astype(jnp.bfloat16)
+
+
+def lay_rows(target, start, values):
+    count, width = values.shape
+    parts = width // LANES
+    for j in range(parts):
+        target[pl.ds(start * parts + j, count, stride=parts), :] = values[:, j * LANES : (j + 1) * LANES]
+
+
+def read_rows(source, start, count, parts):
+    return jnp.concatenate(
+        [source[pl.ds(start * parts + j, count, stride=parts), :] for j in range(parts)], axis=1
+    )
+
+
+def load_table(wide, table, stage, sems):
+    steps = wide.shape[0] // CHUNK
+
+    def fetch(i, slot):
+        return pltpu.make_async_copy(wide.at[pl.ds(i * CHUNK, CHUNK)], stage.at[slot], sems.at[slot])
+
+    fetch(0, 0).start()
+
+    def body(i, carry):
+        slot = lax.rem(i, 2)
+
+        @pl.when(i + 1 < steps)
+        def _():
+            fetch(i + 1, 1 - slot).start()
+
+        fetch(i, slot).wait()
+
+        def piece(k, carry):
+            values = stage[slot, pl.ds(k * 64, 64), :].astype(jnp.float32)
+            lay_rows(table, i * CHUNK + k * 64, values)
+            return carry
+
+        return lax.fori_loop(0, CHUNK // 64, piece, carry)
+
+    lax.fori_loop(0, steps, body, 0)
+
+
+def store_table(table, wide, stage, sems):
+    steps = wide.shape[0] // CHUNK
+    parts = wide.shape[1] // LANES
+
+    def send(i, slot):
+        return pltpu.make_async_copy(stage.at[slot], wide.at[pl.ds(i * CHUNK, CHUNK)], sems.at[slot])
+
+    def body(i, carry):
+        slot = lax.rem(i, 2)
+
+        @pl.when(i >= 2)
+        def _():
+            send(i - 2, slot).wait()
+
+        def piece(k, carry):
+            values = read_rows(table, i * CHUNK + k * 64, 64, parts)
+            stage[slot, pl.ds(k * 64, 64), :] = values.astype(jnp.bfloat16)
+            return carry
+
+        lax.fori_loop(0, CHUNK // 64, piece, 0)
+        send(i, slot).start()
+        return carry
+
+    lax.fori_loop(0, steps, body, 0)
+    for i in (steps - 2, steps - 1):
+        send(i, i % 2).wait()
+
+
+def clear(table):
+    def body(i, carry):
+        table[pl.ds(i * 512, 512), :] = jnp.zeros((512, LANES), table.dtype)
+        return carry
+
+    lax.fori_loop(0, table.shape[0] // 512, body, 0)
+
+
+def gather_rows(index, base, table, rows, parts):
+    count = rows.shape[0] // parts
+
+    def body(i, carry):
+        for u in range(16):
+            slot = i * 16 + u
+            place = index[base + slot]
+            rows[pl.ds(pl.multiple_of(slot * parts, parts), parts), :] = table[
+                pl.ds(pl.multiple_of(place * parts, parts), parts), :
+            ]
+        return carry
+
+    lax.fori_loop(0, count // 16, body, 0)
+
+
+def add_rows(index, base, rows, table, parts):
+    count = rows.shape[0] // parts
+
+    def body(i, carry):
+        for u in range(0, 16, 2):
+            slot = i * 16 + u
+            one, two = index[base + slot], index[base + slot + 1]
+            at_one = pl.ds(pl.multiple_of(one * parts, parts), parts)
+            at_two = pl.ds(pl.multiple_of(two * parts, parts), parts)
+            held_one, held_two = table[at_one, :], table[at_two, :]
+            sum_one = held_one + rows[pl.ds(pl.multiple_of(slot * parts, parts), parts), :]
+            held_two = jnp.where(one == two, sum_one, held_two)
+            sum_two = held_two + rows[pl.ds(pl.multiple_of((slot + 1) * parts, parts), parts), :]
+            table[at_one, :] = sum_one
+            table[at_two, :] = sum_two
+        return carry
+
+    lax.fori_loop(0, count // 16, body, 0)
+
+
+def row_normal(values):
+    average = jnp.mean(values, -1, keepdims=True)
+    centred = values - average
+    variance = jnp.mean(centred * centred, -1, keepdims=True)
+    scale = lax.rsqrt(variance + EPSILON)
+    return centred * scale, scale
+
+
+def forward_kernel(
+    count, recv, send, edge, wide, nodes, w_one, b_one, w_two, b_two, gain, shift,
+    result, first, second, received, sums,
+    table, total, rows, stage, sems,
+):
+    step = pl.program_id(0)
+    base = step * TILE
+    width = nodes.shape[1]
+    parts = width // LANES
+
+    @pl.when(step == 0)
+    def _():
+        load_table(wide, table, stage, sems)
+        clear(total)
+
+    gather_rows(recv, base, table, rows, parts)
+    from_recv = read_rows(rows, 0, TILE, parts).astype(jnp.bfloat16)
+    received[...] = from_recv
+    column = jnp.broadcast_to(send[0], (LANES, TILE)).T
+    lane = lax.broadcasted_iota(jnp.int32, (TILE, LANES), 1)
+    chosen = jnp.concatenate(
+        [
+            jnp.where(column == lane + j * LANES, 1.0, 0.0).astype(jnp.bfloat16)
+            for j in range(nodes.shape[0] // LANES)
+        ],
+        axis=1,
+    )
+    from_send = dot(chosen, nodes[...]).astype(jnp.bfloat16)
+    pre = (
+        dot(edge[...], w_one[:width])
+        + dot(from_send, w_one[width : 2 * width])
+        + dot(from_recv, w_one[2 * width :])
+        + b_one[...]
+    )
+    first[...] = pre
+    act = (pre * jax.nn.sigmoid(pre)).astype(jnp.bfloat16)
+    post = dot(act, w_two[...]) + b_two[...]
+    second[...] = post
+    normal, _ = row_normal(post)
+    branch = normal * gain[...] + shift[...]
+    live = base + lax.broadcasted_iota(jnp.int32, (TILE, 1), 0) < count[0]
+    outcome = edge[...].astype(jnp.float32) + jnp.where(live, branch, 0.0)
+    result[...] = outcome
+    lay_rows(rows, 0, jnp.where(live, outcome, 0.0))
+    add_rows(recv, base, rows, total, parts)
+
+    @pl.when(step == pl.num_programs(0) - 1)
+    def _():
+        store_table(total, sums, stage, sems)
+
+
+def edge_forward(count, recv, send, edge, wide, nodes, w_one, b_one, w_two, b_two, gain, shift):
+    edges, width = edge.shape
+    steps = edges // TILE
+    parts = width // LANES
+    hold = pl.BlockSpec(memory_space=pltpu.VMEM)
+    scalar = pl.BlockSpec(memory_space=pltpu.SMEM)
+    tile = pl.BlockSpec((TILE, width), lambda i: (i, 0))
+    return pl.pallas_call(
+        forward_kernel,
+        grid=(steps,),
+        in_specs=[
+            scalar, scalar, pl.BlockSpec((1, 1, TILE), lambda i: (i, 0, 0)), tile,
+            pl.BlockSpec(memory_space=pl.ANY), hold, hold, hold, hold, hold, hold, hold,
+        ],
+        out_specs=[tile, tile, tile, tile, pl.BlockSpec(memory_space=pl.ANY)],
+        out_shape=[
+            jax.ShapeDtypeStruct((edges, width), jnp.float32),
+            jax.ShapeDtypeStruct((edges, width), jnp.float32),
+            jax.ShapeDtypeStruct((edges, width), jnp.float32),
+            jax.ShapeDtypeStruct((edges, width), jnp.bfloat16),
+            jax.ShapeDtypeStruct(wide.shape, jnp.bfloat16),
+        ],
+        scratch_shapes=[
+            pltpu.VMEM((wide.shape[0] * parts, LANES), jnp.float32),
+            pltpu.VMEM((wide.shape[0] * parts, LANES), jnp.float32),
+            pltpu.VMEM((TILE * parts, LANES), jnp.float32),
+            pltpu.VMEM((2, CHUNK, width), jnp.bfloat16),
+            pltpu.SemaphoreType.DMA((2,)),
+        ],
+        compiler_params=pltpu.CompilerParams(vmem_limit_bytes=VMEM_BYTES),
+        name="edge_forward",
+    )(count, recv, send.reshape(steps, 1, TILE), edge, wide, nodes, w_one, b_one, w_two, b_two, gain, shift)
+
+
+def backward_kernel(
+    count, recv, send, cotangent, edge, received, first, second, wide, nodes, w_one_t, w_two_t, gain,
+    grad, sums, grad_one, grad_two, vectors, sender_grad,
+    table, total, rows, stage, sems, by_sender,
+):
+    step = pl.program_id(0)
+    base = step * TILE
+    width = nodes.shape[1]
+    parts = width // LANES
+
+    @pl.when(step == 0)
+    def _():
+        load_table(wide, table, stage, sems)
+        clear(total)
+        grad_one[...] = jnp.zeros_like(grad_one)
+        grad_two[...] = jnp.zeros_like(grad_two)
+        vectors[...] = jnp.zeros_like(vectors)
+        by_sender[...] = jnp.zeros_like(by_sender)
+
+    gather_rows(recv, base, table, rows, parts)
+    live = base + lax.broadcasted_iota(jnp.int32, (TILE, 1), 0) < count[0]
+    upstream = cotangent[...].astype(jnp.float32) + jnp.where(live, read_rows(rows, 0, TILE, parts), 0.0)
+    masked = jnp.where(live, upstream, 0.0)
+    normal, scale = row_normal(second[...])
+    vectors[2:3, :] += jnp.sum(masked * normal, 0, keepdims=True)
+    vectors[3:4, :] += jnp.sum(masked, 0, keepdims=True)
+    scaled = masked * gain[...]
+    slope = jnp.mean(scaled * normal, -1, keepdims=True)
+    grad_second = scale * (scaled - jnp.mean(scaled, -1, keepdims=True) - normal * slope)
+    second_low = grad_second.astype(jnp.bfloat16)
+    vectors[1:2, :] += jnp.sum(second_low.astype(jnp.float32), 0, keepdims=True)
+    pre = first[...]
+    logistic = jax.nn.sigmoid(pre)
+    act = (pre * logistic).astype(jnp.bfloat16)
+    grad_two[...] += dot_left(act, second_low)
+    grad_first = dot(second_low, w_two_t[...]) * (logistic * (1.0 + pre * (1.0 - logistic)))
+    first_low = grad_first.astype(jnp.bfloat16)
+    first_wide = first_low.astype(jnp.float32)
+    vectors[0:1, :] += jnp.sum(first_wide, 0, keepdims=True)
+    grad_one[:width] += dot_left(edge[...], first_low)
+    grad_one[2 * width :] += dot_left(received[...], first_low)
+    node = lax.broadcasted_iota(jnp.int32, (nodes.shape[0], TILE), 0)
+    chosen = jnp.where(node == send[0], 1.0, 0.0).astype(jnp.bfloat16)
+    by_sender[...] += dot(chosen, first_low)
+    grad[...] = upstream + dot(first_low, w_one_t[:, :width])
+    lay_rows(rows, 0, first_wide)
+    add_rows(recv, base, rows, total, parts)
+
+    @pl.when(step == pl.num_programs(0) - 1)
+    def _():
+        high, rest = split_low(by_sender[...])
+        grad_one[width : 2 * width] = dot_left(nodes[...], high) + dot_left(nodes[...], rest)
+        middle = w_one_t[:, width : 2 * width]
+        sender_grad[...] = dot(high, middle) + dot(rest, middle)
+        store_table(total, sums, stage, sems)
+
+
+def edge_backward(count, recv, send, cotangent, edge, received, first, second, wide, nodes, w_one_t, w_two_t, gain):
+    edges, width = edge.shape
+    steps = edges // TILE
+    parts = width // LANES
+    per_device = nodes.shape[0]
+    hold = pl.BlockSpec(memory_space=pltpu.VMEM)
+    scalar = pl.BlockSpec(memory_space=pltpu.SMEM)
+    tile = pl.BlockSpec((TILE, width), lambda i: (i, 0))
+
+    def whole(rows):
+        return pl.BlockSpec((rows, width), lambda i: (0, 0))
+
+    return pl.pallas_call(
+        backward_kernel,
+        grid=(steps,),
+        in_specs=[
+            scalar, scalar, pl.BlockSpec((1, 1, TILE), lambda i: (i, 0, 0)), tile, tile, tile, tile, tile,
+            pl.BlockSpec(memory_space=pl.ANY), hold, hold, hold, hold,
+        ],
+        out_specs=[
+            tile, pl.BlockSpec(memory_space=pl.ANY),
+            whole(3 * width), whole(width), whole(8), whole(per_device),
+        ],
+        out_shape=[
+            jax.ShapeDtypeStruct((edges, width), jnp.float32),
+            jax.ShapeDtypeStruct(wide.shape, jnp.bfloat16),
+            jax.ShapeDtypeStruct((3 * width, width), jnp.float32),
+            jax.ShapeDtypeStruct((width, width), jnp.float32),
+            jax.ShapeDtypeStruct((8, width), jnp.float32),
+            jax.ShapeDtypeStruct((per_device, width), jnp.float32),
+        ],
+        scratch_shapes=[
+            pltpu.VMEM((wide.shape[0] * parts, LANES), jnp.float32),
+            pltpu.VMEM((wide.shape[0] * parts, LANES), jnp.float32),
+            pltpu.VMEM((TILE * parts, LANES), jnp.float32),
+            pltpu.VMEM((2, CHUNK, width), jnp.bfloat16),
+            pltpu.SemaphoreType.DMA((2,)),
+            pltpu.VMEM((per_device, width), jnp.float32),
+        ],
+        compiler_params=pltpu.CompilerParams(vmem_limit_bytes=VMEM_BYTES),
+        name="edge_backward",
+    )(count, recv, send.reshape(steps, 1, TILE), cotangent, edge, received, first, second, wide, nodes, w_one_t, w_two_t, gain)
 
 
 def shards(
@@ -106,19 +434,11 @@
     relative = (receivers // per_group - block_index + 1 + groups) % groups
     recv_sub = receivers % per_group // per_device
     recv_wide = (recv_sub * 3 + relative) * per_device + receivers % per_device
-    slot_index = jnp.arange(edge_input.shape[0], dtype=jnp.int32)
-    live = jnp.where(slot_index < edge_count[0], 1.0, 0.0).astype(jnp.float32)[:, None]
     wide_low = widened(node_low)
-    stacked = jnp.concatenate(
-        [edge_input, jnp.take(node_low, send_local, axis=0), jnp.take(wide_low, recv_wide, axis=0)],
-        axis=1,
-    )
-    first_pre = matmul(stacked, edge_w_one) + edge_b_one
-    first_act = jax.nn.silu(first_pre).astype(jnp.bfloat16)
-    second_pre = matmul(first_act, edge_w_two) + edge_b_two
-    edge_branch, edge_norm_back = jax.vjp(norm_apply, second_pre, edge_gain, edge_shift)
-    edge_result = edge_input.astype(jnp.float32) + live * edge_branch
-    wide_sums = jax.ops.segment_sum(live * edge_result, recv_wide, num_segments=3 * per_group)
+    edge_result, first_pre, second_pre, received, wide_sums = edge_forward(
+        edge_count, recv_wide, send_local, edge_input, wide_low, node_low,
+        edge_w_one, edge_b_one[None], edge_w_two, edge_b_two[None], edge_gain[None], edge_shift[None],
+    )
     gathered = combine_sums(wide_sums, per_device)
     joined = jnp.concatenate([node_low, gathered.astype(jnp.bfloat16)], axis=1)
     third_pre = matmul(joined, node_w_one) + node_b_one
@@ -142,24 +462,14 @@
         ("blk", "sub"),
     )
     node_out = node_input + to_channels(node_branch.T)
-    edge_total = edge_cotangent.astype(jnp.float32) + live * jnp.take(wide_grad, recv_wide, axis=0).astype(jnp.float32)
-    grad_second, grad_edge_gain, grad_edge_shift = edge_norm_back(live * edge_total)
-    second_low = grad_second.astype(jnp.bfloat16)
-    grad_edge_w_two = left_matmul(first_act, second_low)
-    grad_edge_b_two = jnp.sum(second_low.astype(jnp.float32), 0)
-    grad_first = right_matmul(second_low, edge_w_two) * silu_slope(first_pre)
-    first_low = grad_first.astype(jnp.bfloat16)
-    grad_edge_w_one = left_matmul(stacked, first_low)
-    grad_edge_b_one = jnp.sum(first_low.astype(jnp.float32), 0)
-    grad_stacked = right_matmul(first_low, edge_w_one)
-    edge_grad = edge_total + grad_stacked[:, :width]
-    sender_grad = jax.ops.segment_sum(
-        grad_stacked[:, width : 2 * width], send_local, num_segments=per_device
-    )
-    receiver_wide = jax.ops.segment_sum(
-        grad_stacked[:, 2 * width :], recv_wide, num_segments=3 * per_group
-    )
-    receiver_grad = combine_sums(receiver_wide, per_device)
+    edge_grad, receiver_wide, grad_edge_w_one, grad_edge_w_two, vectors, sender_grad = edge_backward(
+        edge_count, recv_wide, send_local, edge_cotangent, edge_input, received, first_pre, second_pre,
+        wide_grad, node_low, edge_w_one.T, edge_w_two.T, edge_gain[None],
+    )
+    grad_edge_b_one, grad_edge_b_two, grad_edge_gain, grad_edge_shift = (vectors[i] for i in range(4))
+    high, rest = split_low(combine_sums(receiver_wide, per_device))
+    receiver_weight = edge_w_one[2 * width :]
+    receiver_grad = right_matmul(high, receiver_weight) + right_matmul(rest, receiver_weight)
     node_total = grad_nodes + sender_grad + receiver_grad
     summed = lax.psum(
         (

time: 781 us -> 675 us (0.86); the launches traced: 770 us -> 674 us
  other arithmetic: 192 us -> 11.8 us
  waiting for transfers between devices: 243 us -> 389 us
  Pallas kernels: 0 us -> 124 us
  local copies, waits for them, and re-layouts: 140 us -> 23.9 us
  matrix products: 80.4 us -> 12.3 us
    pallas_call x0 -> x2, Pallas kernels: none -> 124 us  [the longest x1 68.4 us: edge_backward(): pl.pallas_call(backward_kernel, grid=(steps,), in_specs=[scalar, scalar,...]
    scatter-add x3 -> x0, other arithmetic: 96.7 us -> none  [the longest x1 34 us: shards(): jax.ops.segment_sum(grad_stacked[:, 2 * width:], recv_wide, num_segments=...]
    psum x1, waiting for transfers between devices: 45.8 us -> 103 us  [shards(): lax.psum((grad_edge_w_one, grad_edge_b_one, grad_edge_w_two, grad_edge_b_...]
    gather x4 -> x0, local copies, waits for them, and re-layouts: 55.8 us -> none  [the longest x2 24.4 us: shards(): jnp.take(wide_grad, recv_wide, axis=0).astype(jnp.float32)]
    unnamed x91 -> x74, local copies, waits for them, and re-layouts: 59.4 us -> 15.7 us
    all_gather x2, waiting for transfers between devices: 51.8 us -> 82.8 us  [widened(): lax.all_gather(jnp.concatenate([below, rows, above], 0), 'sub', axis=0, t...]
    ppermute x8, waiting for transfers between devices: 62.9 us -> 92.7 us  [shifted(): return lax.ppermute(block, axis, route)]
    reduce_scatter x2, waiting for transfers between devices: 82.9 us -> 111 us  [combine_sums(): lax.psum_scatter(wide_sums.astype(jnp.bfloat16), 'sub', scatter_dimension...]
  transfers between devices with their start and end apart: 16 -> 16, of which waited for: 11 -> 13; matrix products, arithmetic and copies ran while one was open for 21% -> 4% of each run, Pallas kernels for 0% -> 0%
where the time goes in v2:
time: 675 us; the launch traced here: 674 us
  waiting for transfers between devices  389 us (58%)
  Pallas kernels  124 us (18%)
  blocking collectives  64.2 us (10%)
  starting transfers between devices  33.9 us (5%)
  local copies, waits for them, and re-layouts  23.9 us (4%)
  between operations  14.9 us (2%)
  matrix products  12.3 us (2%)
  other arithmetic  11.8 us (2%)
    reduce_scatter x2, waiting for transfers between devices, combine_sums(): lax.psum_scatter(wide_sums.astype(jnp.bfloat16), 'sub', scatter_dimension...  111 us
    psum x1, waiting for transfers between devices, shards(): lax.psum((grad_edge_w_one, grad_edge_b_one, grad_edge_w_two, grad_edge_b_...  103 us
    ppermute x8, waiting for transfers between devices, shifted(): return lax.ppermute(block, axis, route)  92.7 us
    all_gather x2, waiting for transfers between devices, widened(): lax.all_gather(jnp.concatenate([below, rows, above], 0), 'sub', axis=0, t...  82.8 us
    pallas_call x1, Pallas kernels, edge_backward(): pl.pallas_call(backward_kernel, grid=(steps,), in_specs=[scalar, scalar,...  68.4 us
    pallas_call x1, Pallas kernels, edge_forward(): pl.pallas_call(forward_kernel, grid=(steps,), in_specs=[scalar, scalar, p...  55.7 us
    psum x1, blocking collectives, shards(): lax.psum((grad_edge_w_one, grad_edge_b_one, grad_edge_w_two, grad_edge_b_...  41.6 us
    all_to_all x1, blocking collectives, to_nodes(): lax.all_to_all(channels.astype(jnp.bfloat16), ('blk', 'sub'), split_axis=...  22.7 us
  transfers between devices with their start and end apart: 16, of which 13 were waited for; matrix products, arithmetic and copies ran while one was open for 4% of the time, Pallas kernels for 0%

profile of v2, /device:TPU:0, one launch (start us, length us, event | category | flops | bytes accessed | tf_op | source)
XLA Modules:
  0.0 674.4 jit_solution(10058561703206390434)
XLA Ops:
  7.2 1.4 convert_element_type.91
  8.7 22.7 %all_to_all.58 = bf16[16,32,512]{2,0,1:T(8,128)(2,1)S(1)} all-to-all(bf16[16,32,512]{2,0,1:T(8,128)(2,1)S(1)} %bitcast.82), channel_id=1, replica_groups=mesh['blk'=8,'sub'=4] {'blk','sub'}, dimensions={1} | all-to-all | bytes 1048576 | tf_op jit(solution)/shard_map/all_to_all | solution.py:46
  31.3 0.2 copy.62
  31.6 1.3 collective-permute-start
  32.9 3.5 collective-permute-start.1
  36.3 18.6 %collective-permute-done = bf16[512,512]{1,0:T(8,128)(2,1)S(1)} collective-permute-done((bf16[512,512]{1,0:T(8,128)(2,1)S(1)}, bf16[512,512]{1,0:T(8,128)(2,1)S(1)}, u32[]{:S(2)}, u32[]{:S(2)}) %collective-permute-start) | collective-permute-done | bytes 524320 | tf_op jit(solution)/shard_map/ppermute | solution.py:14
  55.0 2.2 collective-permute-done.1
  57.2 1.2 pad_maximum_fusion
  58.5 0.6 reshape.88.send
  59.8 0.7 fusion.26.recv
  60.5 42.3 %all-gather.3.cloned.1.call-done.wide = bf16[6144,512]{1,0:T(8,128)(2,1)} async-done(((bf16[1536,512]{1,0:T(8,128)(2,1)}), bf16[6144,512]{1,0:T(8,128)(2,1)}) %all-gather.3.cloned.1.call-update) | async-done | bytes 6291472 | tf_op jit(solution)/shard_map/all_gather | solution.py:60
  102.8 55.7 %edge_forward.1 = (f32[4608,512]{1,0:T(8,128)}, f32[4608,512]{1,0:T(8,128)}, f32[4608,512]{1,0:T(8,128)}, bf16[4608,512]{1,0:T(8,128)(2,1)}, bf16[6144,512]{1,0:T(8,128)(2,1)}) custom-call(s32[1]{0:T(128)S(6)} %copy.85.count, s32[4608]{0:T(1024)} %fusion.26.recv, s32[9,1,512]{2,1,0:T(1,128)} %reshape.88.send, bf16[4608,512]{1,0:T(8,128)(2,1)} %edge.3, ...), custom_call_target="tpu_custom_call" | custom-call | tf_op jit(solution)/shard_map/edge_forward/pallas_call | solution.py:274
  158.5 58.5 %reduce-scatter.3.cloned.1.call-done = bf16[1536,512]{1,0:T(8,128)(2,1)} async-done(((bf16[6144,512]{1,0:T(8,128)(2,1)}), bf16[1536,512]{1,0:T(8,128)(2,1)}) %reduce-scatter.3.cloned.1.call-update) | async-done | bytes 1572880 | tf_op jit(solution)/shard_map/reduce_scatter | solution.py:64
  217.0 2.1 fusion.38
  219.1 4.2 collective-permute-start.2
  223.4 0.9 copy.79
  224.3 5.1 all-to-all-start.2
  229.4 19.5 %collective-permute-done.2 = bf16[512,512]{1,0:T(8,128)(2,1)S(1)} collective-permute-done((bf16[512,512]{1,0:T(8,128)(2,1)}, bf16[512,512]{1,0:T(8,128)(2,1)S(1)}, u32[]{:S(2)}, u32[]{:S(2)}) %collective-permute-start.2) | collective-permute-done | bytes 524320 | tf_op jit(solution)/shard_map/ppermute | solution.py:14
  249.1 1.4 add_convert_fusion.2
  250.6 0.7 convolution_add_fusion.2
  251.3 0.5 copy-done.27
  251.8 0.6 fusion.40
  252.4 0.4 copy-done.31
  252.8 0.3 fusion.5
  253.1 0.6 fusion.7
  253.7 1.3 convert_reduce_fusion
  255.0 0.7 convert_reduce_fusion.1
  255.8 0.7 fusion.41
  256.5 1.3 copy-done.6
  257.9 2.6 collective-permute-start.4
  260.6 2.2 collective-permute-start.5
  262.8 20.3 %collective-permute-done.4 = bf16[512,512]{1,0:T(8,128)(2,1)S(1)} collective-permute-done((bf16[512,512]{1,0:T(8,128)(2,1)S(1)}, bf16[512,512]{1,0:T(8,128)(2,1)S(1)}, u32[]{:S(2)}, u32[]{:S(2)}) %collective-permute-start.4) | collective-permute-done | bytes 524320 | tf_op jit(solution)/shard_map/ppermute | solution.py:14
  283.1 2.2 collective-permute-done.5
  285.3 1.2 pad_maximum_fusion.1
  286.6 0.2 reduce-scatter.5.cloned.1.call-start
  286.8 1.6 copy.65
  288.4 1.0 copy.66
  289.4 40.4 %all-gather.5.cloned.1.call-done.wide = bf16[6144,512]{1,0:T(8,128)(2,1)} async-done(((bf16[1536,512]{1,0:T(8,128)(2,1)}), bf16[6144,512]{1,0:T(8,128)(2,1)}) %all-gather.5.cloned.1.call-update) | async-done | bytes 6291472 | tf_op jit(solution)/shard_map/all_gather | solution.py:60
  329.8 68.4 %edge_backward.1 = (f32[4608,512]{1,0:T(8,128)}, bf16[6144,512]{1,0:T(8,128)(2,1)}, f32[1536,512]{1,0:T(8,128)}, f32[512,512]{1,0:T(8,128)}, f32[8,512]{1,0:T(8,128)}, /*index=5*/f32[512,512]{1,0:T(8,128)}) custom-call(s32[1]{0:T(128)S(6)} %copy.85.count, s32[4608]{0:T(1024)} %fusion.26.recv, s32[9,1,512]{2,1,0:T(1,128)} %reshape.88.send, ...), custom_call_target="tpu_custom_call" | custom-call | tf_op jit(solution)/shard_map/edge_backward/pallas_call | solution.py:370
  398.3 0.9 copy-done.5
  399.4 3.2 fusion.8
  402.7 1.5 fusion.36
  404.2 52.6 %reduce-scatter.5.cloned.1.call-done = bf16[1536,512]{1,0:T(8,128)(2,1)} async-done(((bf16[6144,512]{1,0:T(8,128)(2,1)}), bf16[1536,512]{1,0:T(8,128)(2,1)}) %reduce-scatter.5.cloned.1.call-update) | async-done | bytes 1572880 | tf_op jit(solution)/shard_map/reduce_scatter | solution.py:64
  456.8 2.1 fusion.37
  458.8 4.2 collective-permute-start.6
  463.1 5.2 all-to-all-start.1
  468.3 26.2 %collective-permute-done.6 = bf16[512,512]{1,0:T(8,128)(2,1)S(1)} collective-permute-done((bf16[512,512]{1,0:T(8,128)(2,1)}, bf16[512,512]{1,0:T(8,128)(2,1)S(1)}, u32[]{:S(2)}, u32[]{:S(2)}) %collective-permute-start.6) | collective-permute-done | bytes 524320 | tf_op jit(solution)/shard_map/ppermute | solution.py:14
  494.6 0.8 copy-done.13
  495.4 3.5 collective-permute-done.7
  498.8 1.9 fusion.16
  500.8 2.9 fusion.13
  503.7 2.0 copy.69
  505.8 5.0 all-to-all-start.3
  511.0 1.3 convert_bitcast_fusion.2
  512.4 1.1 add.154
  513.5 41.6 %all-reduce = (f32[512]{0:T(512)}, f32[512]{0:T(512)}, f32[512]{0:T(512)}, f32[512]{0:T(512)}, f32[512]{0:T(512)}, /*index=5*/f32[512]{0:T(512)}, f32[512]{0:T(512)}, f32[512]{0:T(512)}) all-reduce(f32[512]{0:T(512)S(1)} %bitcast.89, f32[512]{0:T(512)S(1)} %bitcast.88, ...), channel_id=1, replica_groups=mesh['blk'=8,'sub'=4] {'blk','sub'}, use_global_device_ids=true, to_apply=%region_7.8 | all-reduce | flops 4096 | bytes 32768 | tf_op jit(solution)/shard_map/psum | solution.py:474
  555.3 1.1 add.161
  556.4 102.6 %all-reduce.4.cloned.1.call-done = (f32[1536,512]{1,0:T(8,128)}, f32[512,512]{1,0:T(8,128)}, f32[1024,512]{1,0:T(8,128)}, f32[512,512]{1,0:T(8,128)}) async-done(((f32[1536,512]{1,0:T(8,128)}, f32[512,512]{1,0:T(8,128)}, f32[1024,512]{1,0:T(8,128)}, f32[512,512]{1,0:T(8,128)}), (f32[1536,512]{1,0:T(8,128)}, f32[512,512]{1,0:T(8,128)}, f32[1024,512]{1,0:T(8,128)}, ...) | async-done | bytes 7340048 | tf_op jit(solution)/shard_map/psum | solution.py:474
  659.0 3.9 copy.86
  663.0 1.0 copy.87
  663.9 1.0 copy-done.12
  664.9 1.3 copy.88
  666.3 0.6 copy-done.15
  666.9 1.0 copy.89
  (89 shorter events, 1.5 us)
Async XLA Ops:
  7.2 243.3 %copy-start = (bf16[1024,512]{1,0:T(8,128)(2,1)S(1)}, bf16[1024,512]{1,0:T(8,128)(2,1)}, u32[]{:S(2)}) copy-start(bf16[1024,512]{1,0:T(8,128)(2,1)} %param.30) | copy-start | bytes 3145732
  7.2 95.6 %all-gather.3.cloned.1.call-start = ((), (), s32[]{:S(2)}) async-start(), calls=%async_computation.6 | async-start | bytes 7864320 | tf_op jit(solution)/shard_map/all_gather | solution.py:60
  31.5 26.9 %copy-start.3 = (bf16[512,512]{0,1:T(8,128)(2,1)}, bf16[512,512]{0,1:T(8,128)(2,1)S(1)}, u32[]{:S(2)}) copy-start(bf16[512,512]{0,1:T(8,128)(2,1)S(1)} %copy.62) | copy-start | bytes 1572868
  31.5 27.0 %copy-start.22 = (s32[4608]{0:T(1024)S(1)}, s32[4608]{0:T(1024)}, u32[]{:S(2)}) copy-start(s32[4608]{0:T(1024)} %param.21) | copy-start | bytes 55300
  31.6 28.3 %copy-start.23 = (s32[4608]{0:T(1024)S(1)}, s32[4608]{0:T(1024)}, u32[]{:S(2)}) copy-start(s32[4608]{0:T(1024)} %param.22) | copy-start | bytes 55300
  31.6 23.4 %collective-permute-start = (bf16[512,512]{1,0:T(8,128)(2,1)S(1)}, bf16[512,512]{1,0:T(8,128)(2,1)S(1)}, u32[]{:S(2)}, u32[]{:S(2)}) collective-permute-start(bf16[512,512]{1,0:T(8,128)(2,1)S(1)} %bitcast.69), channel_id=1, source_target_pairs={{28,0},{0,4},{4,8},{8,12},{12,16},{16,20},{20,24},{24,28},{29,1},{... | collective-permute-start | bytes 1572872 | tf_op jit(solution)/shard_map/ppermute | solution.py:14
  32.9 24.3 %collective-permute-start.1 = (bf16[512,512]{1,0:T(8,128)(2,1)S(1)}, bf16[512,512]{1,0:T(8,128)(2,1)S(1)}, u32[]{:S(2)}, u32[]{:S(2)}) collective-permute-start(bf16[512,512]{1,0:T(8,128)(2,1)S(1)} %bitcast.70), channel_id=1, source_target_pairs={{4,0},{8,4},{12,8},{16,12},{20,16},{24,20},{28,24},{0,28},{5,1},{9... | collective-permute-start | bytes 1572872 | tf_op jit(solution)/shard_map/ppermute | solution.py:14
  58.5 158.6 %reduce-scatter.3.cloned.1.call-start = ((), (), s32[]{:S(2)}) async-start(), calls=%async_computation.7 | async-start | bytes 7864320 | tf_op jit(solution)/shard_map/reduce_scatter | solution.py:64
  158.5 64.8 %copy-start.9 = (f32[16,16384]{1,0:T(8,128)S(1)}, f32[16,16384]{1,0:T(8,128)}, u32[]{:S(2)}) copy-start(f32[16,16384]{1,0:T(8,128)} %param.36) | copy-start | bytes 3145732
  219.1 29.8 %collective-permute-start.2 = (bf16[512,512]{1,0:T(8,128)(2,1)}, bf16[512,512]{1,0:T(8,128)(2,1)S(1)}, u32[]{:S(2)}, u32[]{:S(2)}) collective-permute-start(bf16[512,512]{1,0:T(8,128)(2,1)} %get-tuple-element.58), channel_id=1, source_target_pairs={{4,0},{8,4},{12,8},{16,12},{20,16},{24,20},{28,24},{0,28},{5,1},{9... | collective-permute-start | bytes 1572872 | tf_op jit(solution)/shard_map/ppermute | solution.py:14
  223.3 25.8 %collective-permute-start.3 = (bf16[512,512]{1,0:T(8,128)(2,1)S(1)}, bf16[512,512]{1,0:T(8,128)(2,1)}, u32[]{:S(2)}, u32[]{:S(2)}) collective-permute-start(bf16[512,512]{1,0:T(8,128)(2,1)S(1)} %get-tuple-element.59), channel_id=1, source_target_pairs={{28,0},{0,4},{4,8},{8,12},{12,16},{16,20},{20,24},{24,28},{29,1},{... | collective-permute-start | bytes 1572872 | tf_op jit(solution)/shard_map/ppermute | solution.py:14
  223.4 27.1 %copy-start.4 = (bf16[512,512]{0,1:T(8,128)(2,1)S(1)}, bf16[512,512]{0,1:T(8,128)(2,1)}, u32[]{:S(2)}) copy-start(bf16[512,512]{0,1:T(8,128)(2,1)} %copy-done.3) | copy-start | bytes 1572868
  223.4 27.1 %copy-start.29 = (f32[512]{0:T(512)S(1)}, f32[512]{0:T(512)}, u32[]{:S(2)}) copy-start(f32[512]{0:T(512)} %param.31) | copy-start | bytes 6148
  224.3 28.5 %all-to-all-start.2 = ((bf16[16,32,512]{2,0,1:T(8,128)(2,1)}), bf16[16,32,512]{2,0,1:T(8,128)(2,1)S(1)}, u32[]{:S(2)}, u32[]{:S(2)}) async-start(bf16[16,32,512]{2,0,1:T(8,128)(2,1)} %bitcast.67), calls=%async_computation.3 | async-start | bytes 1048576 | tf_op jit(solution)/shard_map/all_to_all | solution.py:46
  229.4 100.5 %all-gather.5.cloned.1.call-start = ((), (), s32[]{:S(2)}) async-start(), calls=%async_computation.8 | async-start | bytes 7864320 | tf_op jit(solution)/shard_map/all_gather | solution.py:60
  250.5 0.8 copy-start.19
  250.5 1.2 copy-start.27
  250.6 1.2 copy-start.30
  251.8 1.0 copy-start.31
  251.8 1.0 copy-start.24
  252.7 0.9 copy-start.26
  253.1 2.0 copy-start.28
  253.1 1.9 copy-start.32
  255.0 0.8 copy-start.20
  255.8 2.1 copy-start.17
  256.5 1.3 copy-start.6
  257.9 28.9 %copy-start.2 = (bf16[1536,512]{1,0:T(8,128)(2,1)S(1)}, bf16[1536,512]{1,0:T(8,128)(2,1)}, u32[]{:S(2)}) copy-start(bf16[1536,512]{1,0:T(8,128)(2,1)} %w_one.1) | copy-start | bytes 4718596
  257.9 25.1 %collective-permute-start.4 = (bf16[512,512]{1,0:T(8,128)(2,1)S(1)}, bf16[512,512]{1,0:T(8,128)(2,1)S(1)}, u32[]{:S(2)}, u32[]{:S(2)}) collective-permute-start(bf16[512,512]{1,0:T(8,128)(2,1)S(1)} %slice.82), channel_id=1, source_target_pairs={{28,0},{0,4},{4,8},{8,12},{12,16},{16,20},{20,24},{24,28},{29,1},{... | collective-permute-start | bytes 1572872 | tf_op jit(solution)/shard_map/ppermute | solution.py:14
  260.6 24.7 %collective-permute-start.5 = (bf16[512,512]{1,0:T(8,128)(2,1)S(1)}, bf16[512,512]{1,0:T(8,128)(2,1)S(1)}, u32[]{:S(2)}, u32[]{:S(2)}) collective-permute-start(bf16[512,512]{1,0:T(8,128)(2,1)S(1)} %slice.82), channel_id=1, source_target_pairs={{4,0},{8,4},{12,8},{16,12},{20,16},{24,20},{28,24},{0,28},{5,1},{9... | collective-permute-start | bytes 1572872 | tf_op jit(solution)/shard_map/ppermute | solution.py:14
  286.5 1.9 copy-start.11
  286.6 170.2 %reduce-scatter.5.cloned.1.call-start = ((), (), s32[]{:S(2)}) async-start(), calls=%async_computation.9 | async-start | bytes 7864320 | tf_op jit(solution)/shard_map/reduce_scatter | solution.py:64
  398.2 1.0 copy-start.5
  398.2 1.2 copy-start.18
  398.3 260.7 %all-reduce.4.cloned.1.call-start = ((), (), s32[]{:S(2)}) async-start(), calls=%async_computation.10 | async-start | bytes 14680064 | tf_op jit(solution)/shard_map/psum | solution.py:474
  399.4 3.2 copy-start.21
  399.4 3.2 copy-start.33
  458.8 35.7 %collective-permute-start.6 = (bf16[512,512]{1,0:T(8,128)(2,1)}, bf16[512,512]{1,0:T(8,128)(2,1)S(1)}, u32[]{:S(2)}, u32[]{:S(2)}) collective-permute-start(bf16[512,512]{1,0:T(8,128)(2,1)} %get-tuple-element.56), channel_id=1, source_target_pairs={{4,0},{8,4},{12,8},{16,12},{20,16},{24,20},{28,24},{0,28},{5,1},{9... | collective-permute-start | bytes 1572872 | tf_op jit(solution)/shard_map/ppermute | solution.py:14
  463.1 35.7 %collective-permute-start.7 = (bf16[512,512]{1,0:T(8,128)(2,1)S(1)}, bf16[512,512]{1,0:T(8,128)(2,1)}, u32[]{:S(2)}, u32[]{:S(2)}) collective-permute-start(bf16[512,512]{1,0:T(8,128)(2,1)S(1)} %get-tuple-element.57), channel_id=1, source_target_pairs={{28,0},{0,4},{4,8},{8,12},{12,16},{16,20},{20,24},{24,28},{29,1},{... | collective-permute-start | bytes 1572872 | tf_op jit(solution)/shard_map/ppermute | solution.py:14
  463.1 42.7 %all-to-all-start.1 = ((bf16[32,16,512]{2,1,0:T(8,128)(2,1)}), bf16[32,16,512]{2,1,0:T(8,128)(2,1)}, u32[]{:S(2)}, u32[]{:S(2)}) async-start(bf16[32,16,512]{2,1,0:T(8,128)(2,1)} %bitcast.8), calls=%async_computation.2 | async-start | bytes 1048576 | tf_op jit(solution)/shard_map/all_to_all | solution.py:52
  468.3 32.5 %copy-start.7 = (f32[512,1024]{1,0:T(8,128)S(1)}, f32[512,1024]{1,0:T(8,128)}, u32[]{:S(2)}) copy-start(f32[512,1024]{1,0:T(8,128)} %copy-done.6) | copy-start | bytes 6291460
  494.6 0.8 copy-start.13
  498.8 1.9 copy-start.14
  505.8 49.3 %all-to-all-start.3 = ((bf16[32,16,512]{2,1,0:T(8,128)(2,1)}), bf16[32,16,512]{2,1,0:T(8,128)(2,1)S(1)}, u32[]{:S(2)}, u32[]{:S(2)}) async-start(bf16[32,16,512]{2,1,0:T(8,128)(2,1)} %bitcast.16), calls=%async_computation.5 | async-start | bytes 1048576 | tf_op jit(solution)/shard_map/all_to_all | solution.py:52
  510.8 1.6 copy-start.8
  512.4 1.1 copy-start.25
  513.5 41.8 %copy-start.10 = (f32[16,16384]{1,0:T(8,128)S(1)}, f32[16,16384]{1,0:T(8,128)}, u32[]{:S(2)}) copy-start(f32[16,16384]{1,0:T(8,128)} %param.36) | copy-start | bytes 3145732
  659.0 4.0 copy-start.16
  663.0 2.0 copy-start.12
  664.9 2.0 copy-start.15
  664.9 2.9 copy-start.1
Sparse Core Ops, SparseCore 0:
  58.6 44.1 all-gather.2
  158.6 58.3 reduce-scatter.2
  286.7 43.1 all-gather.4
  398.4 58.3 reduce-scatter.4
  463.9 195.0 all-reduce.3

commit v3 on v2

--- a/solution.py
+++ b/solution.py
@@ -8,12 +8,6 @@
 EPSILON = 1e-05
 
 
-def shifted(block, axis, distance):
-    devices = range(lax.axis_size(axis))
-    route = [((i - distance) % len(devices), i) for i in devices]
-    return lax.ppermute(block, axis, route)
-
-
 def norm_apply(values, gain, shift):
     average = jnp.mean(values, -1, keepdims=True)
     centred = values - average
@@ -52,25 +46,6 @@
     return lax.all_to_all(
         values.astype(jnp.bfloat16), ("blk", "sub"), split_axis=0, concat_axis=1, tiled=True
     ).astype(jnp.float32)
-
-
-def widened(rows):
-    below = shifted(rows, "blk", 1)
-    above = shifted(rows, "blk", -1)
-    return lax.all_gather(jnp.concatenate([below, rows, above], 0), "sub", axis=0, tiled=True)
-
-
-def combine_sums(wide_sums, per_device):
-    mine = lax.psum_scatter(
-        wide_sums.astype(jnp.bfloat16), "sub", scatter_dimension=0, tiled=True
-    )
-    from_above = shifted(mine[:per_device], "blk", -1)
-    from_below = shifted(mine[2 * per_device :], "blk", 1)
-    return (
-        mine[per_device : 2 * per_device].astype(jnp.float32)
-        + from_above.astype(jnp.float32)
-        + from_below.astype(jnp.float32)
-    )
 
 
 TILE = 512
@@ -397,6 +372,233 @@
         compiler_params=pltpu.CompilerParams(vmem_limit_bytes=VMEM_BYTES),
         name="edge_backward",
     )(count, recv, send.reshape(steps, 1, TILE), cotangent, edge, received, first, second, wide, nodes, w_one_t, w_two_t, gain)
+
+
+MESH = pl.DeviceIdType.MESH
+PIECES = 4
+
+
+def places():
+    groups = lax.axis_size("blk")
+    group, sub = lax.axis_index("blk"), lax.axis_index("sub")
+    odd = lax.rem(group, 2)
+    return dict(
+        group=group,
+        sub=sub,
+        sibling=sub + 1 - 2 * lax.rem(sub, 2),
+        partner=lax.rem(sub + 2, 4),
+        beside=group + 1 - 2 * odd,
+        onward=lax.rem(group + 2 - 4 * odd + groups, groups),
+        source=lax.rem(group - 2 + 4 * odd + groups, groups),
+        near=2 - 2 * odd,
+        far=2 * odd,
+    )
+
+
+def meet(senders, count):
+    barrier = pltpu.get_barrier_semaphore()
+    for device in senders:
+        pl.semaphore_signal(barrier, inc=1, device_id=device, device_id_type=MESH)
+    pl.semaphore_wait(barrier, count)
+
+
+def spread_kernel(own, table, send_sems, recv_sems, keep_sem):
+    at = places()
+    group, sub, partner, near, far = at["group"], at["sub"], at["partner"], at["near"], at["far"]
+    to_sibling = (group, at["sibling"])
+    to_partner = (group, partner)
+    to_beside = (at["beside"], sub)
+    to_onward = (at["onward"], sub)
+    size = own.shape[0] // PIECES
+    meet((to_sibling, to_partner, to_beside, (at["source"], sub)), 4)
+
+    def copy(kind, piece, source, slot, device):
+        return pltpu.make_async_remote_copy(
+            src_ref=source.at[pl.ds(piece * size, size)],
+            dst_ref=table.at[slot[0], slot[1], pl.ds(piece * size, size)],
+            send_sem=send_sems.at[kind, piece],
+            recv_sem=recv_sems.at[kind, piece],
+            device_id=device,
+            device_id_type=MESH,
+        )
+
+    def move(kind, piece):
+        if kind == 0:
+            return copy(0, piece, own, (1, sub), to_partner)
+        if kind == 1:
+            return copy(1, piece, own, (far, sub), to_beside)
+        if kind == 2:
+            return copy(2, piece, own, (1, sub), to_sibling)
+        slot, target, device = {
+            3: ((1, partner), (far, partner), to_beside),
+            4: ((1, partner), (1, partner), to_sibling),
+            5: ((near, sub), (far, sub), to_onward),
+            6: ((near, sub), (near, sub), to_sibling),
+            7: ((near, partner), (far, partner), to_onward),
+            8: ((near, partner), (near, partner), to_sibling),
+            9: ((far, sub), (far, sub), to_sibling),
+            10: ((far, partner), (far, partner), to_sibling),
+        }[kind]
+        return copy(kind, piece, table.at[slot[0], slot[1]], target, device)
+
+    keep = pltpu.make_async_copy(own, table.at[1, sub], keep_sem)
+    for piece in range(PIECES):
+        for kind in (0, 1, 2):
+            move(kind, piece).start()
+    keep.start()
+
+    def relay(arrived, kinds, piece):
+        move(arrived, piece).wait_recv()
+        for kind in kinds:
+            move(kind, piece).start()
+
+    for piece in range(PIECES):
+        relay(0, (3, 4), piece)
+        relay(1, (5, 6), piece)
+    for piece in range(PIECES):
+        relay(3, (7, 8), piece)
+        relay(5, (9,), piece)
+    for piece in range(PIECES):
+        relay(7, (10,), piece)
+    for kind in range(11):
+        for piece in range(PIECES):
+            if kind in (2, 4, 6, 8, 9, 10):
+                move(kind, piece).wait_recv()
+            move(kind, piece).wait_send()
+    keep.wait()
+
+
+def spread(own, collective):
+    rows, width = own.shape
+    return pl.pallas_call(
+        spread_kernel,
+        in_specs=[pl.BlockSpec(memory_space=pl.ANY)],
+        out_specs=pl.BlockSpec(memory_space=pl.ANY),
+        out_shape=jax.ShapeDtypeStruct((3, 4, rows, width), own.dtype),
+        scratch_shapes=[
+            pltpu.SemaphoreType.DMA((11, PIECES)),
+            pltpu.SemaphoreType.DMA((11, PIECES)),
+            pltpu.SemaphoreType.DMA,
+        ],
+        compiler_params=pltpu.CompilerParams(collective_id=collective, has_side_effects=True),
+        name="spread_rows",
+    )(own).reshape(12 * rows, width)
+
+
+def collect_kernel(
+    sums, out, mine, landed, far_out, far_in, near_out, near_in, pair_out, pair_in,
+    keep_sems, give_sems, take_sems, send_sems, recv_sems,
+):
+    at = places()
+    group, sub, partner, near, far = at["group"], at["sub"], at["partner"], at["near"], at["far"]
+    sibling = at["sibling"]
+    size = out.shape[0] // PIECES
+    meet(((group, sibling), (group, partner), (at["beside"], sub), (at["onward"], sub)), 4)
+    relations = (far, near, 1)
+
+    def part(ref, piece):
+        return ref.at[pl.ds(piece * size, size)]
+
+    def keep(role, side, piece):
+        return pltpu.make_async_copy(
+            part(sums.at[relations[role], (sub, partner)[side]], piece),
+            part(mine.at[role, side], piece),
+            keep_sems.at[role, side, piece],
+        )
+
+    def give(role, side, piece):
+        return pltpu.make_async_remote_copy(
+            src_ref=part(sums.at[relations[role], (sibling, lax.rem(sibling + 2, 4))[side]], piece),
+            dst_ref=part(landed.at[role, side], piece),
+            send_sem=give_sems.at[role, side, piece],
+            recv_sem=take_sems.at[role, side, piece],
+            device_id=(group, sibling),
+            device_id_type=MESH,
+        )
+
+    def hop(kind, piece):
+        source, target, device = {
+            0: (far_out.at[0], far_in.at[0], (at["source"], sub)),
+            1: (far_out.at[1], far_in.at[1], (at["source"], sub)),
+            2: (near_out.at[0], near_in.at[0], (at["beside"], sub)),
+            3: (near_out.at[1], near_in.at[1], (at["beside"], sub)),
+            4: (pair_out, pair_in, (group, partner)),
+        }[kind]
+        return pltpu.make_async_remote_copy(
+            src_ref=part(source, piece),
+            dst_ref=part(target, piece),
+            send_sem=send_sems.at[kind, piece],
+            recv_sem=recv_sems.at[kind, piece],
+            device_id=device,
+            device_id_type=MESH,
+        )
+
+    order = [(role, side, piece) for role in range(3) for side in (1, 0) for piece in range(PIECES)]
+    for item in order:
+        give(*item).start()
+        keep(*item).start()
+
+    def local(role, side, piece):
+        keep(role, side, piece).wait()
+        give(role, side, piece).wait_recv()
+        rows = pl.ds(piece * size, size)
+        return mine[role, side, rows, :].astype(jnp.float32) + landed[role, side, rows, :].astype(jnp.float32)
+
+    def arrived(kind, ref, piece):
+        hop(kind, piece).wait_recv()
+        return ref[pl.ds(piece * size, size), :].astype(jnp.float32)
+
+    for side in (1, 0):
+        for piece in range(PIECES):
+            far_out[side, pl.ds(piece * size, size), :] = local(0, side, piece).astype(jnp.bfloat16)
+            hop(side, piece).start()
+    for side in (1, 0):
+        for piece in range(PIECES):
+            value = local(1, side, piece) + arrived(side, far_in.at[side], piece)
+            near_out[side, pl.ds(piece * size, size), :] = value.astype(jnp.bfloat16)
+            hop(2 + side, piece).start()
+    for piece in range(PIECES):
+        value = local(2, 1, piece) + arrived(3, near_in.at[1], piece)
+        pair_out[pl.ds(piece * size, size), :] = value.astype(jnp.bfloat16)
+        hop(4, piece).start()
+    for piece in range(PIECES):
+        value = local(2, 0, piece) + arrived(2, near_in.at[0], piece) + arrived(4, pair_in, piece)
+        out[pl.ds(piece * size, size), :] = value
+    for item in order:
+        give(*item).wait_send()
+    for kind in range(5):
+        for piece in range(PIECES):
+            hop(kind, piece).wait_send()
+
+
+def collect(sums, rows, collective):
+    width = sums.shape[1]
+    low = jnp.bfloat16
+    return pl.pallas_call(
+        collect_kernel,
+        in_specs=[pl.BlockSpec(memory_space=pl.ANY)],
+        out_specs=pl.BlockSpec(memory_space=pltpu.VMEM),
+        out_shape=jax.ShapeDtypeStruct((rows, width), jnp.float32),
+        scratch_shapes=[
+            pltpu.VMEM((3, 2, rows, width), low),
+            pltpu.VMEM((3, 2, rows, width), low),
+            pltpu.VMEM((2, rows, width), low),
+            pltpu.VMEM((2, rows, width), low),
+            pltpu.VMEM((2, rows, width), low),
+            pltpu.VMEM((2, rows, width), low),
+            pltpu.VMEM((rows, width), low),
+            pltpu.VMEM((rows, width), low),
+            pltpu.SemaphoreType.DMA((3, 2, PIECES)),
+            pltpu.SemaphoreType.DMA((3, 2, PIECES)),
+            pltpu.SemaphoreType.DMA((3, 2, PIECES)),
+            pltpu.SemaphoreType.DMA((5, PIECES)),
+            pltpu.SemaphoreType.DMA((5, PIECES)),
+        ],
+        compiler_params=pltpu.CompilerParams(
+            collective_id=collective, has_side_effects=True, vmem_limit_bytes=VMEM_BYTES
+        ),
+        name="collect_sums",
+    )(sums.reshape(3, 4, rows, width))
 
 
 def shards(
@@ -432,14 +634,13 @@
     my_start = (block_index * sub_count + sub_index) * per_device
     send_local = senders - my_start
     relative = (receivers // per_group - block_index + 1 + groups) % groups
-    recv_sub = receivers % per_group // per_device
-    recv_wide = (recv_sub * 3 + relative) * per_device + receivers % per_device
-    wide_low = widened(node_low)
+    recv_wide = relative * per_group + receivers % per_group
+    wide_low = spread(node_low, 0)
     edge_result, first_pre, second_pre, received, wide_sums = edge_forward(
         edge_count, recv_wide, send_local, edge_input, wide_low, node_low,
         edge_w_one, edge_b_one[None], edge_w_two, edge_b_two[None], edge_gain[None], edge_shift[None],
     )
-    gathered = combine_sums(wide_sums, per_device)
+    gathered = collect(wide_sums, per_device, 1)
     joined = jnp.concatenate([node_low, gathered.astype(jnp.bfloat16)], axis=1)
     third_pre = matmul(joined, node_w_one) + node_b_one
     third_act = jax.nn.silu(third_pre).astype(jnp.bfloat16)
@@ -456,32 +657,27 @@
     grad_joined = right_matmul(third_low, node_w_one)
     grad_nodes = grad_joined[:, :width]
     grad_gathered = grad_joined[:, width:]
-    wide_grad = widened(grad_gathered.astype(jnp.bfloat16))
-    node_summed = lax.psum(
-        (grad_node_w_one, grad_node_b_one, grad_node_w_two, grad_node_b_two, grad_node_gain, grad_node_shift),
-        ("blk", "sub"),
-    )
+    wide_grad = spread(grad_gathered.astype(jnp.bfloat16), 2)
+    node_grads = (
+        grad_node_w_one, grad_node_b_one, grad_node_w_two, grad_node_b_two, grad_node_gain, grad_node_shift
+    )
+    wide_grad, node_grads = lax.optimization_barrier((wide_grad, node_grads))
+    node_summed = lax.psum(node_grads, ("blk", "sub"))
     node_out = node_input + to_channels(node_branch.T)
     edge_grad, receiver_wide, grad_edge_w_one, grad_edge_w_two, vectors, sender_grad = edge_backward(
         edge_count, recv_wide, send_local, edge_cotangent, edge_input, received, first_pre, second_pre,
         wide_grad, node_low, edge_w_one.T, edge_w_two.T, edge_gain[None],
     )
     grad_edge_b_one, grad_edge_b_two, grad_edge_gain, grad_edge_shift = (vectors[i] for i in range(4))
-    high, rest = split_low(combine_sums(receiver_wide, per_device))
+    high, rest = split_low(collect(receiver_wide, per_device, 3))
     receiver_weight = edge_w_one[2 * width :]
     receiver_grad = right_matmul(high, receiver_weight) + right_matmul(rest, receiver_weight)
     node_total = grad_nodes + sender_grad + receiver_grad
-    summed = lax.psum(
-        (
-            grad_edge_w_one,
-            grad_edge_b_one,
-            grad_edge_w_two,
-            grad_edge_b_two,
-            grad_edge_gain,
-            grad_edge_shift,
-        ),
-        ("blk", "sub"),
-    )
+    edge_grads = (
+        grad_edge_w_one, grad_edge_b_one, grad_edge_w_two, grad_edge_b_two, grad_edge_gain, grad_edge_shift
+    )
+    edge_grads, node_summed = lax.optimization_barrier((edge_grads, node_summed))
+    summed = lax.psum(edge_grads, ("blk", "sub"))
     node_grad = node_cotangent + to_channels(node_total.T)
     return (
         node_out,

time: 675 us -> 558 us (0.83)
  waiting for transfers between devices: 389 us -> 116 us
  Pallas kernels: 124 us -> 285 us
  blocking collectives: 64.2 us -> 82.9 us
  starting transfers between devices: 33.9 us -> 17.8 us
    pallas_call x0 -> x4, Pallas kernels: none -> 161 us  [the longest x2 87.5 us: collect(): pl.pallas_call(collect_kernel, in_specs=[pl.BlockSpec(memory_space=pl.ANY...]
    reduce_scatter x2 -> x0, waiting for transfers between devices: 111 us -> none  [combine_sums(): lax.psum_scatter(wide_sums.astype(jnp.bfloat16), 'sub', scatter_dimension...]
    ppermute x8 -> x0, waiting for transfers between devices: 92.7 us -> none  [shifted(): return lax.ppermute(block, axis, route)]
    all_gather x2 -> x0, waiting for transfers between devices: 82.8 us -> none  [widened(): lax.all_gather(jnp.concatenate([below, rows, above], 0), 'sub', axis=0, t...]
    psum x1 -> x2, blocking collectives: 41.6 us -> 82.9 us  [the longest x1 42.4 us: shards(): node_summed = lax.psum(node_grads, ('blk', 'sub'))]
    all_to_all x1 -> x0, blocking collectives: 22.7 us -> none  [to_nodes(): lax.all_to_all(channels.astype(jnp.bfloat16), ('blk', 'sub'), split_axis=...]
    ppermute x8 -> x0, starting transfers between devices: 18.1 us -> none  [shifted(): return lax.ppermute(block, axis, route)]
    psum x1 -> x2, waiting for transfers between devices: 103 us -> 84.8 us  [the longest x1 84.8 us: shards(): summed = lax.psum(edge_grads, ('blk', 'sub'))]
  transfers between devices with their start and end apart: 16 -> 6, of which waited for: 13 -> 3; matrix products, arithmetic and copies ran while one was open for 4% -> 3% of each run, Pallas kernels for 0% -> 45%
where the time goes in v3:
time: 558 us; the launch traced here: 557 us
  Pallas kernels  285 us (51%)
  waiting for transfers between devices  116 us (21%)
  blocking collectives  82.9 us (15%)
  local copies, waits for them, and re-layouts  21.7 us (4%)
  starting transfers between devices  17.8 us (3%)
  between operations  15.1 us (3%)
  matrix products  9.93 us (2%)
  other arithmetic  8.13 us (1%)
    pallas_call x2, Pallas kernels, collect(): pl.pallas_call(collect_kernel, in_specs=[pl.BlockSpec(memory_space=pl.ANY...  87.5 us
    psum x1, waiting for transfers between devices, shards(): summed = lax.psum(edge_grads, ('blk', 'sub'))  84.8 us
    pallas_call x2, Pallas kernels, spread(): pl.pallas_call(spread_kernel, in_specs=[pl.BlockSpec(memory_space=pl.ANY)...  73.6 us
    pallas_call x1, Pallas kernels, edge_backward(): pl.pallas_call(backward_kernel, grid=(steps,), in_specs=[scalar, scalar,...  68.7 us
    pallas_call x1, Pallas kernels, edge_forward(): pl.pallas_call(forward_kernel, grid=(steps,), in_specs=[scalar, scalar, p...  55.8 us
    psum x1, blocking collectives, shards(): node_summed = lax.psum(node_grads, ('blk', 'sub'))  42.4 us
    psum x1, blocking collectives, shards(): summed = lax.psum(edge_grads, ('blk', 'sub'))  40.5 us
    all_to_all x2, waiting for transfers between devices, to_channels(): lax.all_to_all(values.astype(jnp.bfloat16), ('blk', 'sub'), split_axis=0,...  17.6 us
  transfers between devices with their start and end apart: 6, of which 3 were waited for; matrix products, arithmetic and copies ran while one was open for 3% of the time, Pallas kernels for 45%

profile of v3, /device:TPU:0, one launch (start us, length us, event | category | flops | bytes accessed | tf_op | source)
XLA Modules:
  0.0 556.8 jit_solution(6642314594386827833)
XLA Ops:
  7.2 1.4 convert_element_type.73
  8.6 0.9 copy.80
  9.5 7.3 %all-to-all-start = ((bf16[16,32,512]{2,0,1:T(8,128)(2,1)}), bf16[16,32,512]{2,0,1:T(8,128)(2,1)S(1)}, u32[]{:S(2)}, u32[]{:S(2)}) async-start(bf16[16,32,512]{2,0,1:T(8,128)(2,1)} %bitcast.72), calls=%async_computation | async-start | bytes 1048576 | tf_op jit(solution)/shard_map/all_to_all | solution.py:40
  16.9 0.6 reshape.100.send
  18.1 0.1 convert_element_type.80
  18.2 0.9 copy.79
  19.1 13.3 %all-to-all-done = bf16[16,32,512]{2,0,1:T(8,128)(2,1)S(1)} async-done(((bf16[16,32,512]{2,0,1:T(8,128)(2,1)}), bf16[16,32,512]{2,0,1:T(8,128)(2,1)S(1)}, u32[]{:S(2)}, u32[]{:S(2)}) %all-to-all-start) | async-done | bytes 524320 | tf_op jit(solution)/shard_map/all_to_all | solution.py:40
  32.4 3.1 all-to-all-start.2
  35.4 0.0 all-reduce.9.cloned.1.call-start
  35.5 0.6 fusion.20.recv
  36.1 1.0 copy.62
  37.1 39.2 %spread_rows.2 = bf16[3,4,512,512]{3,2,1,0:T(8,128)(2,1)} custom-call(bf16[512,512]{1,0:T(8,128)(2,1)} %bitcast.75), custom_call_target="tpu_custom_call" | custom-call | tf_op jit(solution)/shard_map/spread_rows/pallas_call | solution.py:473
  76.3 55.8 %edge_forward.1 = (f32[4608,512]{1,0:T(8,128)}, f32[4608,512]{1,0:T(8,128)}, f32[4608,512]{1,0:T(8,128)}, bf16[4608,512]{1,0:T(8,128)(2,1)}, bf16[6144,512]{1,0:T(8,128)(2,1)}) custom-call(s32[1]{0:T(128)S(6)} %copy.85.count, s32[4608]{0:T(1024)} %fusion.20.recv, s32[9,1,512]{2,1,0:T(1,128)} %reshape.100.send, bf16[4608,512]{1,0:T(8,128)(2,1)} %edge.3, ...), custom_call_target="tpu_custom_call" | custom-call | tf_op jit(solution)/shard_map/edge_forward/pallas_call | solution.py:249
  132.1 42.1 %collect_sums.2 = f32[512,512]{1,0:T(8,128)} custom-call(bf16[3,4,512,512]{3,2,1,0:T(8,128)(2,1)} %bitcast.81), custom_call_target="tpu_custom_call" | custom-call | tf_op jit(solution)/shard_map/collect_sums/pallas_call | solution.py:577
  174.2 1.3 convert_element_type.74
  175.6 0.7 convolution_add_fusion.2
  176.3 0.0 copy-done.14
  176.4 0.4 copy-done.21
  176.8 0.6 fusion.27
  177.4 0.4 copy-done.25
  177.8 0.3 fusion.6
  178.1 0.6 fusion.8
  178.7 1.3 convert_reduce_fusion
  180.0 1.5 fusion.25
  181.5 0.7 convert_reduce_fusion.1
  182.2 0.3 copy-done.15
  182.5 2.1 fusion.9
  184.6 0.7 fusion.28
  185.4 1.3 copy-done.5
  186.7 0.9 slice.39.own
  187.5 34.4 %spread_rows.3 = bf16[3,4,512,512]{3,2,1,0:T(8,128)(2,1)} custom-call(bf16[512,512]{1,0:T(8,128)(2,1)} %slice.39.own), custom_call_target="tpu_custom_call" | custom-call | tf_op jit(solution)/shard_map/spread_rows/pallas_call | solution.py:473
  221.9 0.1 fusion.7
  222.1 0.1 reduce_sum.98
  222.2 0.0 all-reduce.9.cloned.1.call-update
  222.2 1.1 copy-done.2
  223.3 1.6 copy.65
  225.0 1.0 copy.66
  226.0 68.7 %edge_backward.1 = (f32[4608,512]{1,0:T(8,128)}, bf16[6144,512]{1,0:T(8,128)(2,1)}, f32[1536,512]{1,0:T(8,128)}, f32[512,512]{1,0:T(8,128)}, f32[8,512]{1,0:T(8,128)}, /*index=5*/f32[512,512]{1,0:T(8,128)}) custom-call(s32[1]{0:T(128)S(6)} %copy.85.count, s32[4608]{0:T(1024)} %fusion.20.recv, s32[9,1,512]{2,1,0:T(1,128)} %reshape.100.send, ...), custom_call_target="tpu_custom_call" | custom-call | tf_op jit(solution)/shard_map/edge_backward/pallas_call | solution.py:345
  294.7 45.3 %collect_sums.3 = f32[512,512]{1,0:T(8,128)} custom-call(bf16[3,4,512,512]{3,2,1,0:T(8,128)(2,1)} %bitcast.80), custom_call_target="tpu_custom_call" | custom-call | tf_op jit(solution)/shard_map/collect_sums/pallas_call | solution.py:577
  340.0 1.8 fusion.11
  341.9 1.8 fusion.3
  343.7 1.0 copy.69
  344.7 3.5 all-to-all-start.3
  348.2 0.0 all-reduce.7.cloned.1.call-start
  348.2 42.4 %all-reduce.1 = (f32[512]{0:T(512)}, f32[512]{0:T(512)}, f32[512]{0:T(512)}, f32[512]{0:T(512)}) all-reduce(f32[512]{0:T(512)S(1)} %get-tuple-element.59, f32[512]{0:T(512)S(1)} %get-tuple-element.61, f32[512]{0:T(512)S(1)} %get-tuple-element.62, f32[512]{0:T(512)S(1)} %reduce_sum.98), channel_id=1, replica_groups=mesh['blk'=8,'sub'=4] {'blk','sub'}, use_global_device_ids=true, to_apply=%region_9.10 | all-reduce | flops 2048 | bytes 16384 | tf_op jit(solution)/shard_map/psum | solution.py:665
  390.6 0.0 all-reduce.9.cloned.1.call-done
  390.6 0.0 all-reduce.7.cloned.1.call-update
  390.7 3.9 all-to-all-start.1
  394.6 0.1 convert_bitcast_fusion.1
  394.7 0.1 copy.76
  394.8 1.0 copy-done.7
  395.8 1.1 add.134
  396.9 17.6 %all-to-all-done.1 = bf16[32,16,512]{2,1,0:T(8,128)(2,1)S(1)} async-done(((bf16[32,16,512]{2,1,0:T(8,128)(2,1)}), bf16[32,16,512]{2,1,0:T(8,128)(2,1)S(1)}, u32[]{:S(2)}, u32[]{:S(2)}) %all-to-all-start.1) | async-done | bytes 524320 | tf_op jit(solution)/shard_map/all_to_all | solution.py:46
  414.5 0.1 convert_bitcast_fusion.2
  414.6 0.1 copy.75
  414.7 1.1 add.129
  415.8 40.5 %all-reduce = (f32[512]{0:T(512)}, f32[512]{0:T(512)}, f32[512]{0:T(512)}, f32[512]{0:T(512)}) all-reduce(f32[512]{0:T(512)S(1)} %bitcast.94, f32[512]{0:T(512)S(1)} %bitcast.93, f32[512]{0:T(512)S(1)} %bitcast.92, f32[512]{0:T(512)S(1)} %bitcast.91), channel_id=1, replica_groups=mesh['blk'=8,'sub'=4] {'blk','sub'}, use_global_device_ids=true, to_apply=%region_15.16 | all-reduce | flops 2048 | bytes 16384 | tf_op jit(solution)/shard_map/psum | solution.py:680
  456.3 84.8 %all-reduce.7.cloned.1.call-done = (f32[1536,512]{1,0:T(8,128)}, f32[512,512]{1,0:T(8,128)}) async-done(((f32[1536,512]{1,0:T(8,128)}, f32[512,512]{1,0:T(8,128)}), (f32[1536,512]{1,0:T(8,128)}, f32[512,512]{1,0:T(8,128)})) %all-reduce.7.cloned.1.call-update) | async-done | bytes 4194320 | tf_op jit(solution)/shard_map/psum | solution.py:680
  541.1 3.9 copy.86
  545.1 1.0 copy.87
  546.0 1.0 copy-done.10
  547.0 1.3 copy.88
  548.3 0.6 copy-done.12
  549.0 1.0 copy.89
  (52 shorter events, 0.2 us)
Async XLA Ops:
  7.2 168.4 %copy-start = (bf16[1024,512]{1,0:T(8,128)(2,1)S(1)}, bf16[1024,512]{1,0:T(8,128)(2,1)}, u32[]{:S(2)}) copy-start(bf16[1024,512]{1,0:T(8,128)(2,1)} %param.30) | copy-start | bytes 3145732
  7.2 9.6 %copy-start.16 = (s32[4608]{0:T(1024)S(1)}, s32[4608]{0:T(1024)}, u32[]{:S(2)}) copy-start(s32[4608]{0:T(1024)} %param.21) | copy-start | bytes 55300
  7.2 10.9 %copy-start.6 = (f32[16,16384]{1,0:T(8,128)S(1)}, f32[16,16384]{1,0:T(8,128)}, u32[]{:S(2)}) copy-start(f32[16,16384]{1,0:T(8,128)} %param.36) | copy-start | bytes 3145732
  9.5 22.9 %all-to-all-start = ((bf16[16,32,512]{2,0,1:T(8,128)(2,1)}), bf16[16,32,512]{2,0,1:T(8,128)(2,1)S(1)}, u32[]{:S(2)}, u32[]{:S(2)}) async-start(bf16[16,32,512]{2,0,1:T(8,128)(2,1)} %bitcast.72), calls=%async_computation | async-start | bytes 1048576 | tf_op jit(solution)/shard_map/all_to_all | solution.py:40
  16.8 18.7 %copy-start.17 = (s32[4608]{0:T(1024)S(1)}, s32[4608]{0:T(1024)}, u32[]{:S(2)}) copy-start(s32[4608]{0:T(1024)} %param.22) | copy-start | bytes 55300
  32.4 145.4 %all-to-all-start.2 = ((bf16[16,32,512]{2,0,1:T(8,128)(2,1)}), bf16[16,32,512]{2,0,1:T(8,128)(2,1)S(1)}, u32[]{:S(2)}, u32[]{:S(2)}) async-start(bf16[16,32,512]{2,0,1:T(8,128)(2,1)} %bitcast.71), calls=%async_computation.2 | async-start | bytes 1048576 | tf_op jit(solution)/shard_map/all_to_all | solution.py:40
  35.4 355.2 %all-reduce.9.cloned.1.call-start = ((), (), s32[]{:S(2)}) async-start(), calls=%async_computation.5 | async-start | bytes 6291456 | tf_op jit(solution)/shard_map/psum | solution.py:665
  132.1 43.5 %copy-start.4 = (bf16[512,512]{0,1:T(8,128)(2,1)S(1)}, bf16[512,512]{0,1:T(8,128)(2,1)}, u32[]{:S(2)}) copy-start(bf16[512,512]{0,1:T(8,128)(2,1)} %copy.62) | copy-start | bytes 1572868
  132.1 43.5 %copy-start.23 = (f32[512]{0:T(512)S(1)}, f32[512]{0:T(512)}, u32[]{:S(2)}) copy-start(f32[512]{0:T(512)} %param.31) | copy-start | bytes 6148
  175.6 0.8 copy-start.14
  175.6 1.2 copy-start.21
  175.6 1.2 copy-start.24
  176.8 1.0 copy-start.25
  176.8 1.0 copy-start.18
  177.8 0.9 copy-start.20
  178.1 1.9 copy-start.26
  180.0 1.5 copy-start.22
  181.5 1.0 copy-start.15
  185.3 1.3 copy-start.5
  221.9 1.4 copy-start.2
  223.3 1.6 copy-start.9
  340.0 1.9 copy-start.3
  340.0 1.9 copy-start.11
  343.7 46.9 %copy-start.19 = (f32[8,512]{1,0:T(8,128)S(1)}, f32[8,512]{1,0:T(8,128)}, u32[]{:S(2)}) copy-start(f32[8,512]{1,0:T(8,128)} %get-tuple-element.56) | copy-start | bytes 49156
  344.7 46.0 %all-to-all-start.3 = ((bf16[32,16,512]{2,1,0:T(8,128)(2,1)}), bf16[32,16,512]{2,1,0:T(8,128)(2,1)S(1)}, u32[]{:S(2)}, u32[]{:S(2)}) async-start(bf16[32,16,512]{2,1,0:T(8,128)(2,1)} %bitcast.22), calls=%async_computation.3 | async-start | bytes 1048576 | tf_op jit(solution)/shard_map/all_to_all | solution.py:46
  348.2 192.9 %all-reduce.7.cloned.1.call-start = ((), (), s32[]{:S(2)}) async-start(), calls=%async_computation.4 | async-start | bytes 8388608 | tf_op jit(solution)/shard_map/psum | solution.py:680
  390.7 23.8 %all-to-all-start.1 = ((bf16[32,16,512]{2,1,0:T(8,128)(2,1)}), bf16[32,16,512]{2,1,0:T(8,128)(2,1)S(1)}, u32[]{:S(2)}, u32[]{:S(2)}) async-start(bf16[32,16,512]{2,1,0:T(8,128)(2,1)} %bitcast.10), calls=%async_computation.1 | async-start | bytes 1048576 | tf_op jit(solution)/shard_map/all_to_all | solution.py:46
  394.6 1.2 copy-start.7
  396.9 17.9 %copy-start.8 = (f32[16,16384]{1,0:T(8,128)S(1)}, f32[16,16384]{1,0:T(8,128)}, u32[]{:S(2)}) copy-start(f32[16,16384]{1,0:T(8,128)} %param.19) | copy-start | bytes 3145732
  541.1 4.0 copy-start.13
  545.1 2.0 copy-start.10
  547.0 2.0 copy-start.12
  547.0 2.9 copy-start.1
Sparse Core Ops, SparseCore 0:
  222.3 160.5 all-reduce.8
  390.8 150.2 all-reduce.6

commit v4 on v3

--- a/solution.py
+++ b/solution.py
@@ -269,13 +269,16 @@
             pltpu.SemaphoreType.DMA((2,)),
         ],
         compiler_params=pltpu.CompilerParams(vmem_limit_bytes=VMEM_BYTES),
+        cost_estimate=pl.CostEstimate(
+            flops=20 * edges * width * width, bytes_accessed=40 * edges * width, transcendentals=2 * edges * width
+        ),
         name="edge_forward",
     )(count, recv, send.reshape(steps, 1, TILE), edge, wide, nodes, w_one, b_one, w_two, b_two, gain, shift)
 
 
 def backward_kernel(
     count, recv, send, cotangent, edge, received, first, second, wide, nodes, w_one_t, w_two_t, gain,
-    grad, sums, grad_one, grad_two, vectors, sender_grad,
+    grad, sums, grads, vectors, sender_grad,
     table, total, rows, stage, sems, by_sender,
 ):
     step = pl.program_id(0)
@@ -287,8 +290,7 @@
     def _():
         load_table(wide, table, stage, sems)
         clear(total)
-        grad_one[...] = jnp.zeros_like(grad_one)
-        grad_two[...] = jnp.zeros_like(grad_two)
+        grads[...] = jnp.zeros_like(grads)
         vectors[...] = jnp.zeros_like(vectors)
         by_sender[...] = jnp.zeros_like(by_sender)
 
@@ -307,13 +309,13 @@
     pre = first[...]
     logistic = jax.nn.sigmoid(pre)
     act = (pre * logistic).astype(jnp.bfloat16)
-    grad_two[...] += dot_left(act, second_low)
+    grads[3 * width :] += dot_left(act, second_low)
     grad_first = dot(second_low, w_two_t[...]) * (logistic * (1.0 + pre * (1.0 - logistic)))
     first_low = grad_first.astype(jnp.bfloat16)
     first_wide = first_low.astype(jnp.float32)
     vectors[0:1, :] += jnp.sum(first_wide, 0, keepdims=True)
-    grad_one[:width] += dot_left(edge[...], first_low)
-    grad_one[2 * width :] += dot_left(received[...], first_low)
+    grads[:width] += dot_left(edge[...], first_low)
+    grads[2 * width : 3 * width] += dot_left(received[...], first_low)
     node = lax.broadcasted_iota(jnp.int32, (nodes.shape[0], TILE), 0)
     chosen = jnp.where(node == send[0], 1.0, 0.0).astype(jnp.bfloat16)
     by_sender[...] += dot(chosen, first_low)
@@ -324,7 +326,7 @@
     @pl.when(step == pl.num_programs(0) - 1)
     def _():
         high, rest = split_low(by_sender[...])
-        grad_one[width : 2 * width] = dot_left(nodes[...], high) + dot_left(nodes[...], rest)
+        grads[width : 2 * width] = dot_left(nodes[...], high) + dot_left(nodes[...], rest)
         middle = w_one_t[:, width : 2 * width]
         sender_grad[...] = dot(high, middle) + dot(rest, middle)
         store_table(total, sums, stage, sems)
@@ -351,13 +353,12 @@
         ],
         out_specs=[
             tile, pl.BlockSpec(memory_space=pl.ANY),
-            whole(3 * width), whole(width), whole(8), whole(per_device),
+            whole(4 * width), whole(8), whole(per_device),
         ],
         out_shape=[
             jax.ShapeDtypeStruct((edges, width), jnp.float32),
             jax.ShapeDtypeStruct(wide.shape, jnp.bfloat16),
-            jax.ShapeDtypeStruct((3 * width, width), jnp.float32),
-            jax.ShapeDtypeStruct((width, width), jnp.float32),
+            jax.ShapeDtypeStruct((4 * width, width), jnp.float32),
             jax.ShapeDtypeStruct((8, width), jnp.float32),
             jax.ShapeDtypeStruct((per_device, width), jnp.float32),
         ],
@@ -370,6 +371,9 @@
             pltpu.VMEM((per_device, width), jnp.float32),
         ],
         compiler_params=pltpu.CompilerParams(vmem_limit_bytes=VMEM_BYTES),
+        cost_estimate=pl.CostEstimate(
+            flops=24 * edges * width * width, bytes_accessed=40 * edges * width, transcendentals=2 * edges * width
+        ),
         name="edge_backward",
     )(count, recv, send.reshape(steps, 1, TILE), cotangent, edge, received, first, second, wide, nodes, w_one_t, w_two_t, gain)
 
@@ -599,6 +603,322 @@
         ),
         name="collect_sums",
     )(sums.reshape(3, 4, rows, width))
+
+
+def finish_kernel(
+    sums, grads, vectors, out, reduced, reduced_vectors,
+    mine, landed, far_out, far_in, near_out, near_in, pair_out, pair_in,
+    half, half_in, cross_out, cross_in, side_out, side_in, ring_out, ring_in, held, held_in,
+    keep_sems, give_sems, take_sems, send_sems, recv_sems,
+    load_sem, load_vector_sem, step_send, step_recv, ring_send, ring_recv, vector_send, vector_recv,
+):
+    at = places()
+    group, sub, partner, near, far = at["group"], at["sub"], at["partner"], at["near"], at["far"]
+    sibling = at["sibling"]
+    groups = lax.axis_size("blk")
+    along = groups // 2
+    odd, spot = lax.rem(group, 2), group // 2
+    core, chip = lax.rem(sub, 2), sub // 2
+    size = out.shape[0] // PIECES
+    low = jnp.bfloat16
+    wide = jnp.float32
+    to_sibling, to_partner, to_beside = (group, sibling), (group, partner), (at["beside"], sub)
+    peers = [(2 * lax.rem(spot + k, along) + odd, sub) for k in range(1, along)]
+    meet((to_sibling, to_partner, to_beside, *peers), 3 + len(peers))
+    relations = (far, near, 1)
+
+    rows = grads.shape[0]
+    n_half, n_cross, n_side, n_ring = rows // 2, rows // 4, rows // 8, rows // 8 // along
+    at_half = pl.multiple_of(core * n_half, n_half)
+    at_cross = pl.multiple_of(at_half + chip * n_cross, n_cross)
+    at_side = pl.multiple_of(at_cross + odd * n_side, n_side)
+    at_ring = pl.multiple_of(at_side + spot * n_ring, n_ring)
+
+    def remote(source, target, send, recv, device):
+        return pltpu.make_async_remote_copy(
+            src_ref=source, dst_ref=target, send_sem=send, recv_sem=recv,
+            device_id=device, device_id_type=MESH,
+        )
+
+    def step(kind):
+        if kind == 0:
+            other = pl.ds(pl.multiple_of((1 - core) * n_half, n_half), n_half)
+            source, target, device = grads.at[other], half_in, to_sibling
+        elif kind == 1:
+            source, target, device = cross_out, cross_in, to_partner
+        elif kind == 2:
+            source, target, device = side_out, side_in, to_beside
+        else:
+            start, count, device = {
+                3: (at_side, n_side, to_beside),
+                4: (at_cross, n_cross, to_partner),
+                5: (at_half, n_half, to_sibling),
+            }[kind]
+            source = target = reduced.at[pl.ds(start, count)]
+        return remote(source, target, step_send.at[kind], step_recv.at[kind], device)
+
+    def ring(kind, k):
+        if kind == 0:
+            spot_to = lax.rem(spot + k, along)
+            source = ring_out.at[pl.ds(pl.multiple_of(spot_to * n_ring, n_ring), n_ring)]
+            target = ring_in.at[k - 1]
+        else:
+            source = target = reduced.at[pl.ds(at_ring, n_ring)]
+        return remote(source, target, ring_send.at[kind, k - 1], ring_recv.at[kind, k - 1], peers[k - 1])
+
+    def vector(kind):
+        device = (to_sibling, to_partner, to_beside, *peers)[kind]
+        return remote(
+            held.at[min(kind, 3)], held_in.at[kind], vector_send.at[kind], vector_recv.at[kind], device
+        )
+
+    def pieces(count, body):
+        block = min(count, 128)
+
+        def run(i, carry):
+            body(pl.multiple_of(i * block, block), block)
+            return carry
+
+        lax.fori_loop(0, count // block, run, 0)
+
+    load = pltpu.make_async_copy(grads.at[pl.ds(at_half, n_half)], half, load_sem)
+    load_vector = pltpu.make_async_copy(vectors, held.at[0], load_vector_sem)
+
+    def part(ref, piece):
+        return ref.at[pl.ds(piece * size, size)]
+
+    def keep(role, side, piece):
+        return pltpu.make_async_copy(
+            part(sums.at[relations[role], (sub, partner)[side]], piece),
+            part(mine.at[role, side], piece),
+            keep_sems.at[role, side, piece],
+        )
+
+    def give(role, side, piece):
+        return remote(
+            part(sums.at[relations[role], (sibling, lax.rem(sibling + 2, 4))[side]], piece),
+            part(landed.at[role, side], piece),
+            give_sems.at[role, side, piece], take_sems.at[role, side, piece], to_sibling,
+        )
+
+    def hop(kind, piece):
+        source, target, device = {
+            0: (far_out.at[0], far_in.at[0], (at["source"], sub)),
+            1: (far_out.at[1], far_in.at[1], (at["source"], sub)),
+            2: (near_out.at[0], near_in.at[0], to_beside),
+            3: (near_out.at[1], near_in.at[1], to_beside),
+            4: (pair_out, pair_in, to_partner),
+        }[kind]
+        return remote(
+            part(source, piece), part(target, piece), send_sems.at[kind, piece], recv_sems.at[kind, piece], device
+        )
+
+    order = [(role, side, piece) for role in range(3) for side in (1, 0) for piece in range(PIECES)]
+
+    def local(role, side, piece):
+        keep(role, side, piece).wait()
+        give(role, side, piece).wait_recv()
+        span = pl.ds(piece * size, size)
+        return mine[role, side, span, :].astype(wide) + landed[role, side, span, :].astype(wide)
+
+    def arrived(kind, ref, piece):
+        hop(kind, piece).wait_recv()
+        return ref[pl.ds(piece * size, size), :].astype(wide)
+
+    def far_step(side, piece):
+        far_out[side, pl.ds(piece * size, size), :] = local(0, side, piece).astype(low)
+        hop(side, piece).start()
+
+    def near_step(side, piece):
+        value = local(1, side, piece) + arrived(side, far_in.at[side], piece)
+        near_out[side, pl.ds(piece * size, size), :] = value.astype(low)
+        hop(2 + side, piece).start()
+
+    def pair_step(piece):
+        value = local(2, 1, piece) + arrived(3, near_in.at[1], piece)
+        pair_out[pl.ds(piece * size, size), :] = value.astype(low)
+        hop(4, piece).start()
+
+    def last_step(piece):
+        value = local(2, 0, piece) + arrived(2, near_in.at[0], piece) + arrived(4, pair_in, piece)
+        out[pl.ds(piece * size, size), :] = value
+
+    def add_half():
+        load.wait()
+        step(0).wait_recv()
+        other = (1 - chip) * n_cross
+
+        def send_part(i, block):
+            span = pl.ds(pl.multiple_of(other + i, block), block)
+            cross_out[pl.ds(i, block), :] = (half[span, :] + half_in[span, :]).astype(low)
+
+        pieces(n_cross, send_part)
+        step(1).start()
+        load_vector.wait()
+        vector(0).start()
+
+    def add_cross():
+        mine_at, other = chip * n_cross, (1 - odd) * n_side
+        step(1).wait_recv()
+
+        def send_part(i, block):
+            span = pl.ds(pl.multiple_of(other + i, block), block)
+            here = pl.ds(pl.multiple_of(mine_at + other + i, block), block)
+            side_out[pl.ds(i, block), :] = (half[here, :] + half_in[here, :] + cross_in[span, :].astype(wide)).astype(low)
+
+        pieces(n_side, send_part)
+        step(2).start()
+        vector(0).wait_recv()
+        held[1] = held[0] + held_in[0]
+        vector(1).start()
+
+    def add_side():
+        from_side = odd * n_side
+        step(2).wait_recv()
+
+        def keep_part(i, block):
+            span = pl.ds(pl.multiple_of(from_side + i, block), block)
+            here = pl.ds(pl.multiple_of(chip * n_cross + from_side + i, block), block)
+            value = half[here, :] + half_in[here, :] + cross_in[span, :].astype(wide) + side_in[pl.ds(i, block), :].astype(wide)
+            half[here, :] = value
+            ring_out[pl.ds(i, block), :] = value.astype(low)
+
+        pieces(n_side, keep_part)
+        for k in range(1, along):
+            ring(0, k).start()
+        vector(1).wait_recv()
+        held[2] = held[1] + held_in[1]
+        vector(2).start()
+
+    def add_ring():
+        here = pl.ds(pl.multiple_of(chip * n_cross + odd * n_side + spot * n_ring, n_ring), n_ring)
+        value = half[here, :]
+        for k in range(1, along):
+            ring(0, k).wait_recv()
+            value = value + ring_in[k - 1].astype(wide)
+        reduced[pl.ds(at_ring, n_ring), :] = value.astype(low)
+        for k in range(1, along):
+            ring(1, k).start()
+        vector(2).wait_recv()
+        held[3] = held[2] + held_in[2]
+        for k in range(1, along):
+            vector(2 + k).start()
+
+    def share_side():
+        for k in range(1, along):
+            ring(1, k).wait_recv()
+        step(3).start()
+
+    def share_cross():
+        step(3).wait_recv()
+        step(4).start()
+        value = held[3]
+        for k in range(1, along):
+            vector(2 + k).wait_recv()
+            value = value + held_in[2 + k]
+        reduced_vectors[...] = value
+
+    def share_half():
+        step(4).wait_recv()
+        step(5).start()
+
+    for item in order[: 2 * PIECES]:
+        give(*item).start()
+        keep(*item).start()
+    step(0).start()
+    load.start()
+    load_vector.start()
+    for item in order[2 * PIECES :]:
+        give(*item).start()
+        keep(*item).start()
+    for side in (1, 0):
+        for piece in range(PIECES):
+            far_step(side, piece)
+    add_half()
+    for piece in range(PIECES):
+        near_step(1, piece)
+    for piece in range(PIECES // 2):
+        near_step(0, piece)
+    add_cross()
+    for piece in range(PIECES // 2, PIECES):
+        near_step(0, piece)
+    for piece in range(PIECES):
+        pair_step(piece)
+    add_side()
+    for piece in range(PIECES):
+        last_step(piece)
+    add_ring()
+    share_side()
+    share_cross()
+    share_half()
+    step(5).wait_recv()
+    for item in order:
+        give(*item).wait_send()
+    for kind in range(5):
+        for piece in range(PIECES):
+            hop(kind, piece).wait_send()
+    for kind in range(6):
+        step(kind).wait_send()
+    for k in range(1, along):
+        ring(0, k).wait_send()
+        ring(1, k).wait_send()
+    for kind in range(2 + along):
+        vector(kind).wait_send()
+
+
+def finish(sums, grads, vectors, rows, collective):
+    width = sums.shape[1]
+    low, wide = jnp.bfloat16, jnp.float32
+    count = grads.shape[0]
+    along = lax.axis_size("blk") // 2
+    half = pltpu.VMEM((count // 2, width), wide)
+    return pl.pallas_call(
+        finish_kernel,
+        in_specs=[pl.BlockSpec(memory_space=pl.ANY)] * 3,
+        out_specs=[pl.BlockSpec(memory_space=pltpu.VMEM)] * 3,
+        out_shape=[
+            jax.ShapeDtypeStruct((rows, width), wide),
+            jax.ShapeDtypeStruct(grads.shape, low),
+            jax.ShapeDtypeStruct(vectors.shape, wide),
+        ],
+        scratch_shapes=[
+            pltpu.VMEM((3, 2, rows, width), low),
+            pltpu.VMEM((3, 2, rows, width), low),
+            pltpu.VMEM((2, rows, width), low),
+            pltpu.VMEM((2, rows, width), low),
+            pltpu.VMEM((2, rows, width), low),
+            pltpu.VMEM((2, rows, width), low),
+            pltpu.VMEM((rows, width), low),
+            pltpu.VMEM((rows, width), low),
+            half,
+            half,
+            pltpu.VMEM((count // 4, width), low),
+            pltpu.VMEM((count // 4, width), low),
+            pltpu.VMEM((count // 8, width), low),
+            pltpu.VMEM((count // 8, width), low),
+            pltpu.VMEM((count // 8, width), low),
+            pltpu.VMEM((along - 1, count // 8 // along, width), low),
+            pltpu.VMEM((4, *vectors.shape), wide),
+            pltpu.VMEM((2 + along, *vectors.shape), wide),
+            pltpu.SemaphoreType.DMA((3, 2, PIECES)),
+            pltpu.SemaphoreType.DMA((3, 2, PIECES)),
+            pltpu.SemaphoreType.DMA((3, 2, PIECES)),
+            pltpu.SemaphoreType.DMA((5, PIECES)),
+            pltpu.SemaphoreType.DMA((5, PIECES)),
+            pltpu.SemaphoreType.DMA,
+            pltpu.SemaphoreType.DMA,
+            pltpu.SemaphoreType.DMA((6,)),
+            pltpu.SemaphoreType.DMA((6,)),
+            pltpu.SemaphoreType.DMA((2, along - 1)),
+            pltpu.SemaphoreType.DMA((2, along - 1)),
+            pltpu.SemaphoreType.DMA((2 + along,)),
+            pltpu.SemaphoreType.DMA((2 + along,)),
+        ],
+        compiler_params=pltpu.CompilerParams(
+            collective_id=collective, has_side_effects=True, vmem_limit_bytes=VMEM_BYTES
+        ),
+        name="finish_sums",
+    )(sums.reshape(3, 4, rows, width), grads, vectors)
 
 
 def shards(
@@ -658,44 +978,41 @@
     grad_nodes = grad_joined[:, :width]
     grad_gathered = grad_joined[:, width:]
     wide_grad = spread(grad_gathered.astype(jnp.bfloat16), 2)
-    node_grads = (
-        grad_node_w_one, grad_node_b_one, grad_node_w_two, grad_node_b_two, grad_node_gain, grad_node_shift
-    )
+    node_grads = (grad_node_w_one, grad_node_w_two)
     wide_grad, node_grads = lax.optimization_barrier((wide_grad, node_grads))
     node_summed = lax.psum(node_grads, ("blk", "sub"))
     node_out = node_input + to_channels(node_branch.T)
-    edge_grad, receiver_wide, grad_edge_w_one, grad_edge_w_two, vectors, sender_grad = edge_backward(
+    edge_grad, receiver_wide, edge_grads, vectors, sender_grad = edge_backward(
         edge_count, recv_wide, send_local, edge_cotangent, edge_input, received, first_pre, second_pre,
         wide_grad, node_low, edge_w_one.T, edge_w_two.T, edge_gain[None],
     )
-    grad_edge_b_one, grad_edge_b_two, grad_edge_gain, grad_edge_shift = (vectors[i] for i in range(4))
-    high, rest = split_low(collect(receiver_wide, per_device, 3))
+    node_vectors = jnp.stack([grad_node_b_one, grad_node_b_two, grad_node_gain, grad_node_shift])
+    receiver_sums, summed, vectors = finish(
+        receiver_wide, edge_grads, jnp.concatenate([vectors[:4], node_vectors]), per_device, 3
+    )
+    summed = summed.astype(jnp.float32)
+    high, rest = split_low(receiver_sums)
     receiver_weight = edge_w_one[2 * width :]
     receiver_grad = right_matmul(high, receiver_weight) + right_matmul(rest, receiver_weight)
     node_total = grad_nodes + sender_grad + receiver_grad
-    edge_grads = (
-        grad_edge_w_one, grad_edge_b_one, grad_edge_w_two, grad_edge_b_two, grad_edge_gain, grad_edge_shift
-    )
-    edge_grads, node_summed = lax.optimization_barrier((edge_grads, node_summed))
-    summed = lax.psum(edge_grads, ("blk", "sub"))
     node_grad = node_cotangent + to_channels(node_total.T)
     return (
         node_out,
         edge_result,
         node_grad,
         edge_grad,
-        summed[0],
-        summed[1],
-        summed[2],
-        summed[3],
-        summed[4],
-        summed[5],
+        summed[: 3 * width],
+        vectors[0],
+        summed[3 * width :],
+        vectors[1],
+        vectors[2],
+        vectors[3],
         node_summed[0],
+        vectors[4],
         node_summed[1],
-        node_summed[2],
-        node_summed[3],
-        node_summed[4],
-        node_summed[5],
+        vectors[5],
+        vectors[6],
+        vectors[7],
     )
 
 

time: 558 us -> 539 us (0.966)
  blocking collectives: 82.9 us -> 0 us
  waiting for transfers between devices: 116 us -> 150 us
  Pallas kernels: 285 us -> 311 us
    psum x1, waiting for transfers between devices: 0.02 us -> 112 us  [shards(): node_summed = lax.psum(node_grads, ('blk', 'sub'))]
    psum x1 -> x0, waiting for transfers between devices: 84.8 us -> none  [shards(): summed = lax.psum(edge_grads, ('blk', 'sub'))]
    psum x2 -> x0, blocking collectives: 82.9 us -> none  [the longest x1 42.4 us: shards(): node_summed = lax.psum(node_grads, ('blk', 'sub'))]
    pallas_call x0 -> x1, Pallas kernels: none -> 70.4 us  [finish(): pl.pallas_call(finish_kernel, in_specs=[pl.BlockSpec(memory_space=pl.ANY)...]
    pallas_call x2 -> x1, Pallas kernels: 87.5 us -> 42.3 us  [collect(): pl.pallas_call(collect_kernel, in_specs=[pl.BlockSpec(memory_space=pl.ANY...]
    all_to_all x2, waiting for transfers between devices: 17.6 us -> 29.1 us  [to_channels(): lax.all_to_all(values.astype(jnp.bfloat16), ('blk', 'sub'), split_axis=0,...]
    unnamed x60 -> x54, local copies, waits for them, and re-layouts: 16.2 us -> 11.1 us
  transfers between devices with their start and end apart: 6 -> 5, of which waited for: 3 -> 4; matrix products, arithmetic and copies ran while one was open for 3% -> 4% of each run, Pallas kernels for 45% -> 26%
where the time goes in v4:
time: 539 us; the launch traced here: 538 us
  Pallas kernels  311 us (58%)
  waiting for transfers between devices  150 us (28%)
  local copies, waits for them, and re-layouts  21.7 us (4%)
  starting transfers between devices  19 us (4%)
  between operations  15 us (3%)
  other arithmetic  11.4 us (2%)
  matrix products  10.6 us (2%)
    psum x1, waiting for transfers between devices, shards(): node_summed = lax.psum(node_grads, ('blk', 'sub'))  112 us
    pallas_call x2, Pallas kernels, spread(): pl.pallas_call(spread_kernel, in_specs=[pl.BlockSpec(memory_space=pl.ANY)...  74.1 us
    pallas_call x1, Pallas kernels, finish(): pl.pallas_call(finish_kernel, in_specs=[pl.BlockSpec(memory_space=pl.ANY)...  70.4 us
    pallas_call x1, Pallas kernels, edge_backward(): pl.pallas_call(backward_kernel, grid=(steps,), in_specs=[scalar, scalar,...  68.6 us
    pallas_call x1, Pallas kernels, edge_forward(): pl.pallas_call(forward_kernel, grid=(steps,), in_specs=[scalar, scalar, p...  55.8 us
    pallas_call x1, Pallas kernels, collect(): pl.pallas_call(collect_kernel, in_specs=[pl.BlockSpec(memory_space=pl.ANY...  42.3 us
    all_to_all x2, waiting for transfers between devices, to_channels(): lax.all_to_all(values.astype(jnp.bfloat16), ('blk', 'sub'), split_axis=0,...  29.1 us
    unnamed x54, local copies, waits for them, and re-layouts  11.1 us
  transfers between devices with their start and end apart: 5, of which 4 were waited for; matrix products, arithmetic and copies ran while one was open for 4% of the time, Pallas kernels for 26%

profile of v4, /device:TPU:0, one launch (start us, length us, event | category | flops | bytes accessed | tf_op | source)
XLA Modules:
  0.0 538.4 jit_solution(5017672211427690392)
XLA Ops:
  7.2 0.0 copy-start
  7.2 1.4 convert_element_type.76
  8.6 0.9 copy.80
  9.4 7.3 %all-to-all-start = ((bf16[16,32,512]{2,0,1:T(8,128)(2,1)}), bf16[16,32,512]{2,0,1:T(8,128)(2,1)S(1)}, u32[]{:S(2)}, u32[]{:S(2)}) async-start(bf16[16,32,512]{2,0,1:T(8,128)(2,1)} %bitcast.89), calls=%async_computation | async-start | bytes 1048576 | tf_op jit(solution)/shard_map/all_to_all | solution.py:40
  16.8 0.6 reshape.105.send
  18.1 1.3 convert_element_type.83
  19.3 0.9 copy.79
  20.2 1.6 copy.65
  21.8 2.1 copy.66
  23.8 0.6 fusion.20.recv
  24.5 7.8 %all-to-all-done = bf16[16,32,512]{2,0,1:T(8,128)(2,1)S(1)} async-done(((bf16[16,32,512]{2,0,1:T(8,128)(2,1)}), bf16[16,32,512]{2,0,1:T(8,128)(2,1)S(1)}, u32[]{:S(2)}, u32[]{:S(2)}) %all-to-all-start) | async-done | bytes 524320 | tf_op jit(solution)/shard_map/all_to_all | solution.py:40
  32.3 3.1 all-to-all-start.2
  35.4 1.0 copy.62
  36.4 39.7 %spread_rows.2 = bf16[3,4,512,512]{3,2,1,0:T(8,128)(2,1)} custom-call(bf16[512,512]{1,0:T(8,128)(2,1)} %bitcast.91), custom_call_target="tpu_custom_call" | custom-call | tf_op jit(solution)/shard_map/spread_rows/pallas_call | solution.py:477
  76.1 55.8 %edge_forward.1 = (f32[4608,512]{1,0:T(8,128)}, f32[4608,512]{1,0:T(8,128)}, f32[4608,512]{1,0:T(8,128)}, bf16[4608,512]{1,0:T(8,128)(2,1)}, bf16[6144,512]{1,0:T(8,128)(2,1)}) custom-call(s32[1]{0:T(128)S(6)} %copy.83.count, s32[4608]{0:T(1024)} %fusion.20.recv, s32[9,1,512]{2,1,0:T(1,128)} %reshape.105.send, bf16[4608,512]{1,0:T(8,128)(2,1)} %edge.3, ...), custom_call_target="tpu_custom_call" | custom-call | flops 24159191040 | bytes 94371840 | tf_op jit(solution)/shard_map/edge_forward/pallas_call | solution.py:249
  131.8 0.0 copy-start.10
  131.8 0.0 copy-start.21
  131.9 42.3 %collect_sums.1 = f32[512,512]{1,0:T(8,128)} custom-call(bf16[3,4,512,512]{3,2,1,0:T(8,128)(2,1)} %bitcast.81), custom_call_target="tpu_custom_call" | custom-call | tf_op jit(solution)/shard_map/collect_sums/pallas_call | solution.py:581
  174.2 1.3 convert_element_type.77
  175.5 0.8 copy-done.12
  176.3 0.7 convolution_add_fusion.2
  177.0 0.3 copy-done.19
  177.3 0.6 fusion.27
  177.9 0.4 copy-done.23
  178.3 0.3 fusion.6
  178.6 0.0 copy-start.24
  178.6 0.6 fusion.8
  179.2 1.3 convert_reduce_fusion
  180.5 1.5 fusion.25
  182.0 0.7 convert_reduce_fusion.1
  182.7 0.3 copy-done.13
  183.1 2.1 fusion.9
  185.2 0.7 fusion.28
  185.9 1.3 copy-done.3
  187.2 0.9 slice.69.own
  188.1 34.4 %spread_rows.3 = bf16[3,4,512,512]{3,2,1,0:T(8,128)(2,1)} custom-call(bf16[512,512]{1,0:T(8,128)(2,1)} %slice.69.own), custom_call_target="tpu_custom_call" | custom-call | tf_op jit(solution)/shard_map/spread_rows/pallas_call | solution.py:477
  222.5 68.6 %edge_backward.1 = (f32[4608,512]{1,0:T(8,128)}, bf16[6144,512]{1,0:T(8,128)(2,1)}, f32[2048,512]{1,0:T(8,128)}, f32[8,512]{1,0:T(8,128)}, f32[512,512]{1,0:T(8,128)}) custom-call(s32[1]{0:T(128)S(6)} %copy.83.count, s32[4608]{0:T(1024)} %fusion.20.recv, s32[9,1,512]{2,1,0:T(1,128)} %reshape.105.send, bf16[4608,512]{1,0:T(8,128)(2,1)} %cotangent.1, ...), custom_call_target="tpu_custom_call" | custom-call | flops 28991029248 | bytes 94371840 | tf_op jit(solution)/shard_map/edge_backward/pallas_call | solution.py:347
  291.1 0.7 slice.45
  291.8 0.1 fusion.7
  292.0 0.1 reshape.111
  292.1 0.6 concatenate.7.vectors
  292.7 70.4 %finish_sums.1 = (f32[512,512]{1,0:T(8,128)}, bf16[2048,512]{1,0:T(8,128)(2,1)}, f32[8,512]{1,0:T(8,128)}) custom-call(bf16[3,4,512,512]{3,2,1,0:T(8,128)(2,1)} %bitcast.80, f32[2048,512]{1,0:T(8,128)} %get-tuple-element.40.grads, f32[8,512]{1,0:T(8,128)} %concatenate.7.vectors), custom_call_target="tpu_custom_call" | custom-call | tf_op jit(solution)/shard_map/finish_sums/pallas_call | solution.py:875
  363.1 1.8 fusion.11
  365.0 0.0 copy-done.4
  365.0 2.4 fusion.3
  367.4 1.0 copy.69
  368.4 5.3 all-to-all-start.3
  373.7 0.0 all-reduce.3.cloned.1.call-start
  373.8 0.7 all-reduce.3.cloned.1.call-update
  374.5 14.8 %all-to-all-done.3 = bf16[32,16,512]{2,1,0:T(8,128)(2,1)S(1)} async-done(((bf16[32,16,512]{2,1,0:T(8,128)(2,1)}), bf16[32,16,512]{2,1,0:T(8,128)(2,1)S(1)}, u32[]{:S(2)}, u32[]{:S(2)}) %all-to-all-start.3) | async-done | bytes 524320 | tf_op jit(solution)/shard_map/all_to_all | solution.py:46
  389.3 3.3 all-to-all-start.1
  392.6 2.1 slice.59
  394.7 1.1 slice.60
  395.8 0.6 fusion.26
  396.4 1.2 convert_bitcast_fusion.1
  397.6 0.1 copy.76
  397.7 1.1 add.114
  398.8 14.3 %all-to-all-done.1 = bf16[32,16,512]{2,1,0:T(8,128)(2,1)} async-done(((bf16[32,16,512]{2,1,0:T(8,128)(2,1)}), bf16[32,16,512]{2,1,0:T(8,128)(2,1)}, u32[]{:S(2)}, u32[]{:S(2)}) %all-to-all-start.1) | async-done | bytes 524320 | tf_op jit(solution)/shard_map/all_to_all | solution.py:46
  413.1 1.2 convert_bitcast_fusion.2
  414.2 0.1 copy.75
  414.3 1.1 add.109
  415.4 112.0 %all-reduce.3.cloned.1.call-done = (f32[1024,512]{1,0:T(8,128)}, f32[512,512]{1,0:T(8,128)}) async-done(((f32[1024,512]{1,0:T(8,128)}, f32[512,512]{1,0:T(8,128)}), (f32[1024,512]{1,0:T(8,128)}, f32[512,512]{1,0:T(8,128)})) %all-reduce.3.cloned.1.call-update) | async-done | bytes 3145744 | tf_op jit(solution)/shard_map/psum | solution.py:983
  527.4 3.2 copy.84
  530.6 1.0 copy.85
  (45 shorter events, 0.1 us)
Async XLA Ops:
  7.2 169.1 %copy-start = (bf16[1024,512]{1,0:T(8,128)(2,1)S(1)}, bf16[1024,512]{1,0:T(8,128)(2,1)}, u32[]{:S(2)}) copy-start(bf16[1024,512]{1,0:T(8,128)(2,1)} %param.30) | copy-start | bytes 3145732
  7.2 9.6 %copy-start.14 = (s32[4608]{0:T(1024)S(1)}, s32[4608]{0:T(1024)}, u32[]{:S(2)}) copy-start(s32[4608]{0:T(1024)} %param.21) | copy-start | bytes 55300
  9.4 10.8 %copy-start.5 = (bf16[1536,512]{1,0:T(8,128)(2,1)S(1)}, bf16[1536,512]{1,0:T(8,128)(2,1)}, u32[]{:S(2)}) copy-start(bf16[1536,512]{1,0:T(8,128)(2,1)} %w_one.1) | copy-start | bytes 4718596
  9.4 22.9 %all-to-all-start = ((bf16[16,32,512]{2,0,1:T(8,128)(2,1)}), bf16[16,32,512]{2,0,1:T(8,128)(2,1)S(1)}, u32[]{:S(2)}, u32[]{:S(2)}) async-start(bf16[16,32,512]{2,0,1:T(8,128)(2,1)} %bitcast.89), calls=%async_computation | async-start | bytes 1048576 | tf_op jit(solution)/shard_map/all_to_all | solution.py:40
  20.2 3.6 copy-start.15
  32.3 146.0 %all-to-all-start.2 = ((bf16[16,32,512]{2,0,1:T(8,128)(2,1)}), bf16[16,32,512]{2,0,1:T(8,128)(2,1)S(1)}, u32[]{:S(2)}, u32[]{:S(2)}) async-start(bf16[16,32,512]{2,0,1:T(8,128)(2,1)} %bitcast.90), calls=%async_computation.2 | async-start | bytes 1048576 | tf_op jit(solution)/shard_map/all_to_all | solution.py:40
  131.8 44.4 %copy-start.10 = (bf16[512,512]{0,1:T(8,128)(2,1)S(1)}, bf16[512,512]{0,1:T(8,128)(2,1)}, u32[]{:S(2)}) copy-start(bf16[512,512]{0,1:T(8,128)(2,1)} %copy.62) | copy-start | bytes 1572868
  131.8 44.4 %copy-start.21 = (f32[512]{0:T(512)S(1)}, f32[512]{0:T(512)}, u32[]{:S(2)}) copy-start(f32[512]{0:T(512)} %param.31) | copy-start | bytes 6148
  175.5 0.8 copy-start.12
  176.3 1.0 copy-start.19
  176.3 1.0 copy-start.22
  177.3 1.0 copy-start.23
  177.3 1.0 copy-start.16
  178.3 0.9 copy-start.18
  178.6 1.9 copy-start.24
  180.5 1.5 copy-start.20
  182.0 1.0 copy-start.13
  185.9 1.3 copy-start.3
  292.7 70.4 %copy-start.6 = (bf16[1536,512]{1,0:T(8,128)(2,1)S(1)}, bf16[1536,512]{1,0:T(8,128)(2,1)}, u32[]{:S(2)}) copy-start(bf16[1536,512]{1,0:T(8,128)(2,1)} %w_one.1) | copy-start | bytes 4718596
  363.1 1.9 copy-start.4
  368.4 20.8 %all-to-all-start.3 = ((bf16[32,16,512]{2,1,0:T(8,128)(2,1)}), bf16[32,16,512]{2,1,0:T(8,128)(2,1)S(1)}, u32[]{:S(2)}, u32[]{:S(2)}) async-start(bf16[32,16,512]{2,1,0:T(8,128)(2,1)} %bitcast.25), calls=%async_computation.3 | async-start | bytes 1048576 | tf_op jit(solution)/shard_map/all_to_all | solution.py:46
  373.7 18.9 %copy-start.2 = (bf16[2048,512]{1,0:T(8,128)(2,1)S(1)}, bf16[2048,512]{1,0:T(8,128)(2,1)}, u32[]{:S(2)}) copy-start(bf16[2048,512]{1,0:T(8,128)(2,1)} %get-tuple-element.44) | copy-start | bytes 6291460
  373.7 153.7 %all-reduce.3.cloned.1.call-start = ((), (), s32[]{:S(2)}) async-start(), calls=%async_computation.4 | async-start | bytes 6291456 | tf_op jit(solution)/shard_map/psum | solution.py:983
  389.3 5.5 %copy-start.9 = (bf16[32,16,512]{2,1,0:T(8,128)(2,1)}, bf16[32,16,512]{2,1,0:T(8,128)(2,1)S(1)}, u32[]{:S(2)}) copy-start(bf16[32,16,512]{2,1,0:T(8,128)(2,1)S(1)} %all-to-all-done.3) | copy-start | bytes 1572868
  389.3 23.8 %all-to-all-start.1 = ((bf16[32,16,512]{2,1,0:T(8,128)(2,1)}), bf16[32,16,512]{2,1,0:T(8,128)(2,1)}, u32[]{:S(2)}, u32[]{:S(2)}) async-start(bf16[32,16,512]{2,1,0:T(8,128)(2,1)} %bitcast.10), calls=%async_computation.1 | async-start | bytes 1048576 | tf_op jit(solution)/shard_map/all_to_all | solution.py:46
  394.7 1.1 copy-start.17
  395.8 1.9 copy-start.7
  398.8 15.5 %copy-start.8 = (f32[16,16384]{1,0:T(8,128)S(1)}, f32[16,16384]{1,0:T(8,128)}, u32[]{:S(2)}) copy-start(f32[16,16384]{1,0:T(8,128)} %param.19) | copy-start | bytes 3145732
  527.4 3.2 copy-start.11
  527.4 4.2 copy-start.1
Sparse Core Ops, SparseCore 0:
  380.1 147.2 all-reduce.2

commit v5 on v4

--- a/solution.py
+++ b/solution.py
@@ -1,3 +1,4 @@
+import math
 import jax
 import jax.numpy as jnp
 from jax import lax
@@ -37,9 +38,7 @@
 
 
 def to_nodes(channels):
-    return lax.all_to_all(
-        channels.astype(jnp.bfloat16), ("blk", "sub"), split_axis=1, concat_axis=0, tiled=True
-    )
+    return lax.all_to_all(channels, ("blk", "sub"), split_axis=1, concat_axis=0, tiled=True)
 
 
 def to_channels(values):
@@ -277,17 +276,28 @@
 
 
 def backward_kernel(
-    count, recv, send, cotangent, edge, received, first, second, wide, nodes, w_one_t, w_two_t, gain,
-    grad, sums, grads, vectors, sender_grad,
-    table, total, rows, stage, sems, by_sender,
+    count, recv, send, cotangent, edge, received, first, second, wide, node_one, node_two, nodes, w_one_t, w_two_t, gain,
+    grad, sums, all_grads, vectors, sender_grad,
+    table, total, rows, stage, sems, by_sender, grads, pass_sems,
 ):
     step = pl.program_id(0)
     base = step * TILE
     width = nodes.shape[1]
     parts = width // LANES
 
+    first_node = node_one.shape[0]
+    passed = (
+        pltpu.make_async_copy(node_one, all_grads.at[pl.ds(4 * width, first_node)], pass_sems.at[0]),
+        pltpu.make_async_copy(
+            node_two, all_grads.at[pl.ds(4 * width + first_node, node_two.shape[0])], pass_sems.at[1]
+        ),
+        pltpu.make_async_copy(grads, all_grads.at[pl.ds(0, 4 * width)], pass_sems.at[2]),
+    )
+
     @pl.when(step == 0)
     def _():
+        passed[0].start()
+        passed[1].start()
         load_table(wide, table, stage, sems)
         clear(total)
         grads[...] = jnp.zeros_like(grads)
@@ -327,12 +337,17 @@
     def _():
         high, rest = split_low(by_sender[...])
         grads[width : 2 * width] = dot_left(nodes[...], high) + dot_left(nodes[...], rest)
+        passed[2].start()
         middle = w_one_t[:, width : 2 * width]
         sender_grad[...] = dot(high, middle) + dot(rest, middle)
         store_table(total, sums, stage, sems)
-
-
-def edge_backward(count, recv, send, cotangent, edge, received, first, second, wide, nodes, w_one_t, w_two_t, gain):
+        for copy in passed:
+            copy.wait()
+
+
+def edge_backward(
+    count, recv, send, cotangent, edge, received, first, second, wide, node_one, node_two, nodes, w_one_t, w_two_t, gain
+):
     edges, width = edge.shape
     steps = edges // TILE
     parts = width // LANES
@@ -341,6 +356,11 @@
     scalar = pl.BlockSpec(memory_space=pltpu.SMEM)
     tile = pl.BlockSpec((TILE, width), lambda i: (i, 0))
 
+    across = pl.BlockSpec(memory_space=pl.ANY)
+    unit = 64 * lax.axis_size("blk")
+    held = 4 * width + node_one.shape[0] + node_two.shape[0]
+    padded = -(-held // unit) * unit
+
     def whole(rows):
         return pl.BlockSpec((rows, width), lambda i: (0, 0))
 
@@ -349,16 +369,15 @@
         grid=(steps,),
         in_specs=[
             scalar, scalar, pl.BlockSpec((1, 1, TILE), lambda i: (i, 0, 0)), tile, tile, tile, tile, tile,
-            pl.BlockSpec(memory_space=pl.ANY), hold, hold, hold, hold,
+            across, across, across, hold, hold, hold, hold,
         ],
         out_specs=[
-            tile, pl.BlockSpec(memory_space=pl.ANY),
-            whole(4 * width), whole(8), whole(per_device),
+            tile, across, across, whole(8), whole(per_device),
         ],
         out_shape=[
             jax.ShapeDtypeStruct((edges, width), jnp.float32),
             jax.ShapeDtypeStruct(wide.shape, jnp.bfloat16),
-            jax.ShapeDtypeStruct((4 * width, width), jnp.float32),
+            jax.ShapeDtypeStruct((padded, width), jnp.float32),
             jax.ShapeDtypeStruct((8, width), jnp.float32),
             jax.ShapeDtypeStruct((per_device, width), jnp.float32),
         ],
@@ -369,13 +388,15 @@
             pltpu.VMEM((2, CHUNK, width), jnp.bfloat16),
             pltpu.SemaphoreType.DMA((2,)),
             pltpu.VMEM((per_device, width), jnp.float32),
+            pltpu.VMEM((4 * width, width), jnp.float32),
+            pltpu.SemaphoreType.DMA((3,)),
         ],
         compiler_params=pltpu.CompilerParams(vmem_limit_bytes=VMEM_BYTES),
         cost_estimate=pl.CostEstimate(
             flops=24 * edges * width * width, bytes_accessed=40 * edges * width, transcendentals=2 * edges * width
         ),
         name="edge_backward",
-    )(count, recv, send.reshape(steps, 1, TILE), cotangent, edge, received, first, second, wide, nodes, w_one_t, w_two_t, gain)
+    )(count, recv, send.reshape(steps, 1, TILE), cotangent, edge, received, first, second, wide, node_one, node_two, nodes, w_one_t, w_two_t, gain)
 
 
 MESH = pl.DeviceIdType.MESH
@@ -673,7 +694,7 @@
         )
 
     def pieces(count, body):
-        block = min(count, 128)
+        block = math.gcd(count, 128)
 
         def run(i, carry):
             body(pl.multiple_of(i * block, block), block)
@@ -947,8 +968,8 @@
     block_index = lax.axis_index("blk")
     sub_index = lax.axis_index("sub")
     width = edge_input.shape[1]
-    node_low = to_nodes(node_input).T
-    node_upstream = to_nodes(node_cotangent).T.astype(jnp.float32)
+    node_low = to_nodes(node_input.astype(jnp.bfloat16)).T
+    node_upstream = to_nodes(node_cotangent).T
     per_device = node_low.shape[0]
     per_group = per_device * sub_count
     my_start = (block_index * sub_count + sub_index) * per_device
@@ -978,17 +999,14 @@
     grad_nodes = grad_joined[:, :width]
     grad_gathered = grad_joined[:, width:]
     wide_grad = spread(grad_gathered.astype(jnp.bfloat16), 2)
-    node_grads = (grad_node_w_one, grad_node_w_two)
-    wide_grad, node_grads = lax.optimization_barrier((wide_grad, node_grads))
-    node_summed = lax.psum(node_grads, ("blk", "sub"))
     node_out = node_input + to_channels(node_branch.T)
-    edge_grad, receiver_wide, edge_grads, vectors, sender_grad = edge_backward(
+    edge_grad, receiver_wide, grads, vectors, sender_grad = edge_backward(
         edge_count, recv_wide, send_local, edge_cotangent, edge_input, received, first_pre, second_pre,
-        wide_grad, node_low, edge_w_one.T, edge_w_two.T, edge_gain[None],
+        wide_grad, grad_node_w_one, grad_node_w_two, node_low, edge_w_one.T, edge_w_two.T, edge_gain[None],
     )
     node_vectors = jnp.stack([grad_node_b_one, grad_node_b_two, grad_node_gain, grad_node_shift])
     receiver_sums, summed, vectors = finish(
-        receiver_wide, edge_grads, jnp.concatenate([vectors[:4], node_vectors]), per_device, 3
+        receiver_wide, grads, jnp.concatenate([vectors[:4], node_vectors]), per_device, 3
     )
     summed = summed.astype(jnp.float32)
     high, rest = split_low(receiver_sums)
@@ -1003,13 +1021,13 @@
         edge_grad,
         summed[: 3 * width],
         vectors[0],
-        summed[3 * width :],
+        summed[3 * width : 4 * width],
         vectors[1],
         vectors[2],
         vectors[3],
-        node_summed[0],
+        summed[4 * width : 6 * width],
         vectors[4],
-        node_summed[1],
+        summed[6 * width : 7 * width],
         vectors[5],
         vectors[6],
         vectors[7],

time: 539 us -> 470 us (0.87)
  waiting for transfers between devices: 150 us -> 13.6 us
  Pallas kernels: 311 us -> 382 us
  between operations: 15 us -> 1.68 us
  starting transfers between devices: 19 us -> 29.3 us
    psum x1 -> x0, waiting for transfers between devices: 112 us -> none  [shards(): node_summed = lax.psum(node_grads, ('blk', 'sub'))]
    pallas_call x1, Pallas kernels: 68.6 us -> 101 us  [edge_backward(): pl.pallas_call(backward_kernel, grid=(steps,), in_specs=[scalar, scalar,...]
    pallas_call x1, Pallas kernels: 70.4 us -> 93.8 us  [finish(): pl.pallas_call(finish_kernel, in_specs=[pl.BlockSpec(memory_space=pl.ANY)...]
    all_to_all x2, waiting for transfers between devices: 29.1 us -> 5.92 us  [to_channels(): lax.all_to_all(values.astype(jnp.bfloat16), ('blk', 'sub'), split_axis=0,...]
    all_to_all x2, starting transfers between devices: 8.59 us -> 18.9 us  [to_channels(): lax.all_to_all(values.astype(jnp.bfloat16), ('blk', 'sub'), split_axis=0,...]
    pallas_call x2, Pallas kernels: 74.1 us -> 84 us  [spread(): pl.pallas_call(spread_kernel, in_specs=[pl.BlockSpec(memory_space=pl.ANY)...]
    unnamed x54 -> x48, local copies, waits for them, and re-layouts: 11.1 us -> 6.01 us
  transfers between devices with their start and end apart: 5 -> 4, of which waited for: 4 -> 2; matrix products, arithmetic and copies ran while one was open for 4% -> 6% of each run, Pallas kernels for 26% -> 81%
where the time goes in v5:
time: 470 us; the launch traced here: 469 us
  Pallas kernels  382 us (81%)
  starting transfers between devices  29.3 us (6%)
  local copies, waits for them, and re-layouts  22.8 us (5%)
  waiting for transfers between devices  13.6 us (3%)
  matrix products  11.9 us (3%)
  other arithmetic  7.81 us (2%)
    pallas_call x1, Pallas kernels, edge_backward(): pl.pallas_call(backward_kernel, grid=(steps,), in_specs=[scalar, scalar,...  101 us
    pallas_call x1, Pallas kernels, finish(): pl.pallas_call(finish_kernel, in_specs=[pl.BlockSpec(memory_space=pl.ANY)...  93.8 us
    pallas_call x2, Pallas kernels, spread(): pl.pallas_call(spread_kernel, in_specs=[pl.BlockSpec(memory_space=pl.ANY)...  84 us
    pallas_call x1, Pallas kernels, edge_forward(): pl.pallas_call(forward_kernel, grid=(steps,), in_specs=[scalar, scalar, p...  55.8 us
    pallas_call x1, Pallas kernels, collect(): pl.pallas_call(collect_kernel, in_specs=[pl.BlockSpec(memory_space=pl.ANY...  47.2 us
    all_to_all x2, starting transfers between devices, to_channels(): lax.all_to_all(values.astype(jnp.bfloat16), ('blk', 'sub'), split_axis=0,...  18.9 us
    all_to_all x2, starting transfers between devices, to_nodes(): lax.all_to_all(channels, ('blk', 'sub'), split_axis=1, concat_axis=0, til...  10.4 us
  transfers between devices with their start and end apart: 4, of which 2 were waited for; matrix products, arithmetic and copies ran while one was open for 6% of the time, Pallas kernels for 81%

profile of v5, /device:TPU:0, one launch (start us, length us, event | category | flops | bytes accessed | tf_op | source)
XLA Modules:
  0.0 468.7 jit_solution(7109582761530053446)
XLA Ops:
  0.6 0.0 copy-start
  0.7 1.4 convert_element_type.61
  2.0 0.9 copy.80
  2.9 7.3 %all-to-all-start = ((bf16[16,32,512]{2,0,1:T(8,128)(2,1)}), bf16[16,32,512]{2,0,1:T(8,128)(2,1)S(1)}, u32[]{:S(2)}, u32[]{:S(2)}) async-start(bf16[16,32,512]{2,0,1:T(8,128)(2,1)} %bitcast.84), calls=%async_computation | async-start | bytes 1048576 | tf_op jit(solution)/shard_map/all_to_all | solution.py:41
  10.9 0.6 reshape.104.send
  11.5 2.1 copy.66
  13.6 2.3 copy.79
  15.9 1.6 copy.65
  17.4 0.6 fusion.15.recv
  18.1 7.7 %all-to-all-done = bf16[16,32,512]{2,0,1:T(8,128)(2,1)S(1)} async-done(((bf16[16,32,512]{2,0,1:T(8,128)(2,1)}), bf16[16,32,512]{2,0,1:T(8,128)(2,1)S(1)}, u32[]{:S(2)}, u32[]{:S(2)}) %all-to-all-start) | async-done | bytes 524320 | tf_op jit(solution)/shard_map/all_to_all | solution.py:41
  25.8 3.1 all-to-all-start.2
  28.8 1.0 copy.62
  29.9 45.3 %spread_rows.2 = bf16[3,4,512,512]{3,2,1,0:T(8,128)(2,1)} custom-call(bf16[512,512]{1,0:T(8,128)(2,1)} %bitcast.85), custom_call_target="tpu_custom_call" | custom-call | tf_op jit(solution)/shard_map/spread_rows/pallas_call | solution.py:498
  75.1 55.8 %edge_forward.1 = (f32[4608,512]{1,0:T(8,128)}, f32[4608,512]{1,0:T(8,128)}, f32[4608,512]{1,0:T(8,128)}, bf16[4608,512]{1,0:T(8,128)(2,1)}, bf16[6144,512]{1,0:T(8,128)(2,1)}) custom-call(s32[1]{0:T(128)S(6)} %copy.81.count, s32[4608]{0:T(1024)} %fusion.15.recv, s32[9,1,512]{2,1,0:T(1,128)} %reshape.104.send, bf16[4608,512]{1,0:T(8,128)(2,1)} %edge.3, ...), custom_call_target="tpu_custom_call" | custom-call | flops 24159191040 | bytes 94371840 | tf_op jit(solution)/shard_map/edge_forward/pallas_call | solution.py:248
  130.9 0.0 copy-start.8
  130.9 0.0 copy-start.19
  130.9 47.2 %collect_sums.1 = f32[512,512]{1,0:T(8,128)} custom-call(bf16[3,4,512,512]{3,2,1,0:T(8,128)(2,1)} %bitcast.74), custom_call_target="tpu_custom_call" | custom-call | tf_op jit(solution)/shard_map/collect_sums/pallas_call | solution.py:602
  178.2 1.3 convert_element_type.62
  179.5 0.0 copy-start.10
  179.5 0.0 copy-start.17
  179.5 0.0 copy-start.20
  179.5 0.7 convolution_add_fusion.2
  180.3 0.0 copy-done.10
  180.3 0.4 copy-done.17
  180.8 0.6 fusion.24
  181.3 0.4 copy-done.21
  181.7 0.2 multiply_reduce_fusion
  182.0 0.5 fusion.4
  182.5 0.0 copy-start.22
  182.5 1.3 convert_reduce_fusion
  183.8 0.1 copy-done.22
  183.8 0.7 convert_reduce_fusion.1
  184.6 0.0 copy-start.11
  184.6 1.5 fusion.21.node_two
  186.1 2.1 fusion.5.node_one
  188.1 2.1 fusion.25
  190.2 2.9 all-to-all-start.1
  193.1 2.1 slice.79.own
  195.2 38.7 %spread_rows.3 = bf16[3,4,512,512]{3,2,1,0:T(8,128)(2,1)} custom-call(bf16[512,512]{1,0:T(8,128)(2,1)} %slice.79.own), custom_call_target="tpu_custom_call" | custom-call | tf_op jit(solution)/shard_map/spread_rows/pallas_call | solution.py:498
  233.9 100.9 %edge_backward.1 = (f32[4608,512]{1,0:T(8,128)}, bf16[6144,512]{1,0:T(8,128)(2,1)}, f32[3584,512]{1,0:T(8,128)}, f32[8,512]{1,0:T(8,128)}, f32[512,512]{1,0:T(8,128)}) custom-call(s32[1]{0:T(128)S(6)} %copy.81.count, s32[4608]{0:T(1024)} %fusion.15.recv, s32[9,1,512]{2,1,0:T(1,128)} %reshape.104.send, bf16[4608,512]{1,0:T(8,128)(2,1)} %cotangent.1, ...), custom_call_target="tpu_custom_call" | custom-call | flops 28991029248 | bytes 94371840 | tf_op jit(solution)/shard_map/edge_backward/pallas_call | solution.py:367
  334.8 0.1 bitcast_reduce_fusion
  335.0 0.1 reshape.110
  335.1 0.7 slice.51
  335.8 0.6 concatenate.7.vectors
  336.4 93.8 %finish_sums.1 = (f32[512,512]{1,0:T(8,128)}, bf16[3584,512]{1,0:T(8,128)(2,1)}, f32[8,512]{1,0:T(8,128)}) custom-call(bf16[3,4,512,512]{3,2,1,0:T(8,128)(2,1)} %bitcast.77, f32[3584,512]{1,0:T(8,128)} %get-tuple-element.36.grads, f32[8,512]{1,0:T(8,128)} %concatenate.7.vectors), custom_call_target="tpu_custom_call" | custom-call | tf_op jit(solution)/shard_map/finish_sums/pallas_call | solution.py:896
  430.2 1.8 fusion.7
  432.1 0.0 copy-done.3
  432.1 2.5 fusion.3
  434.6 1.0 copy.69
  435.6 16.0 %all-to-all-start.3 = ((bf16[32,16,512]{2,1,0:T(8,128)(2,1)}), bf16[32,16,512]{2,1,0:T(8,128)(2,1)S(1)}, u32[]{:S(2)}, u32[]{:S(2)}) async-start(bf16[32,16,512]{2,1,0:T(8,128)(2,1)} %bitcast.25), calls=%async_computation.3 | async-start | bytes 1048576 | tf_op jit(solution)/shard_map/all_to_all | solution.py:45
  451.6 3.0 slice.69
  454.6 2.1 slice.67
  456.7 0.6 fusion.23
  457.3 1.6 fusion.22
  458.9 0.1 convert_bitcast_fusion.1
  459.0 0.1 copy.75
  459.1 1.0 copy-done.6
  460.1 1.1 add.105
  461.2 5.9 %all-to-all-done.3 = bf16[32,16,512]{2,1,0:T(8,128)(2,1)S(1)} async-done(((bf16[32,16,512]{2,1,0:T(8,128)(2,1)}), bf16[32,16,512]{2,1,0:T(8,128)(2,1)S(1)}, u32[]{:S(2)}, u32[]{:S(2)}) %all-to-all-start.3) | async-done | bytes 524320 | tf_op jit(solution)/shard_map/all_to_all | solution.py:45
  467.1 0.1 convert_bitcast_fusion
  467.2 0.0 copy-start.1
  467.3 0.1 copy.76
  467.3 1.1 add.110
  468.4 0.3 copy-done.1
  (36 shorter events, 0.1 us)
Async XLA Ops:
  0.6 178.8 %copy-start = (bf16[1024,512]{1,0:T(8,128)(2,1)S(1)}, bf16[1024,512]{1,0:T(8,128)(2,1)}, u32[]{:S(2)}) copy-start(bf16[1024,512]{1,0:T(8,128)(2,1)} %param.30) | copy-start | bytes 3145732
  0.7 10.2 %copy-start.12 = (s32[4608]{0:T(1024)S(1)}, s32[4608]{0:T(1024)}, u32[]{:S(2)}) copy-start(s32[4608]{0:T(1024)} %param.21) | copy-start | bytes 55300
  2.9 13.0 %copy-start.4 = (bf16[1536,512]{1,0:T(8,128)(2,1)S(1)}, bf16[1536,512]{1,0:T(8,128)(2,1)}, u32[]{:S(2)}) copy-start(bf16[1536,512]{1,0:T(8,128)(2,1)} %w_one.1) | copy-start | bytes 4718596
  2.9 22.9 %all-to-all-start = ((bf16[16,32,512]{2,0,1:T(8,128)(2,1)}), bf16[16,32,512]{2,0,1:T(8,128)(2,1)S(1)}, u32[]{:S(2)}, u32[]{:S(2)}) async-start(bf16[16,32,512]{2,0,1:T(8,128)(2,1)} %bitcast.84), calls=%async_computation | async-start | bytes 1048576 | tf_op jit(solution)/shard_map/all_to_all | solution.py:41
  13.6 3.9 copy-start.13
  25.8 156.0 %all-to-all-start.2 = ((f32[16,32,512]{2,0,1:T(8,128)}), f32[16,32,512]{2,0,1:T(8,128)S(1)}, u32[]{:S(2)}, u32[]{:S(2)}) async-start(f32[16,32,512]{2,0,1:T(8,128)} %bitcast.81), calls=%async_computation.2 | async-start | bytes 2097152 | tf_op jit(solution)/shard_map/all_to_all | solution.py:41
  130.9 48.6 %copy-start.8 = (bf16[512,512]{0,1:T(8,128)(2,1)S(1)}, bf16[512,512]{0,1:T(8,128)(2,1)}, u32[]{:S(2)}) copy-start(bf16[512,512]{0,1:T(8,128)(2,1)} %copy.62) | copy-start | bytes 1572868
  130.9 48.6 %copy-start.19 = (f32[512]{0:T(512)S(1)}, f32[512]{0:T(512)}, u32[]{:S(2)}) copy-start(f32[512]{0:T(512)} %param.31) | copy-start | bytes 6148
  179.5 0.8 copy-start.10
  179.5 1.2 copy-start.17
  179.5 1.2 copy-start.20
  180.8 1.0 copy-start.21
  180.8 1.0 copy-start.14
  181.7 0.8 copy-start.16
  182.5 1.3 copy-start.18
  182.5 1.4 copy-start.22
  184.6 1.5 copy-start.9
  184.6 1.5 copy-start.11
  190.2 245.4 %all-to-all-start.1 = ((bf16[32,16,512]{2,1,0:T(8,128)(2,1)}), bf16[32,16,512]{2,1,0:T(8,128)(2,1)S(1)}, u32[]{:S(2)}, u32[]{:S(2)}) async-start(bf16[32,16,512]{2,1,0:T(8,128)(2,1)} %bitcast.10), calls=%async_computation.1 | async-start | bytes 1048576 | tf_op jit(solution)/shard_map/all_to_all | solution.py:45
  336.4 93.8 %copy-start.5 = (bf16[1536,512]{1,0:T(8,128)(2,1)S(1)}, bf16[1536,512]{1,0:T(8,128)(2,1)}, u32[]{:S(2)}) copy-start(bf16[1536,512]{1,0:T(8,128)(2,1)} %w_one.1) | copy-start | bytes 4718596
  430.2 1.9 copy-start.3
  435.6 31.5 %all-to-all-start.3 = ((bf16[32,16,512]{2,1,0:T(8,128)(2,1)}), bf16[32,16,512]{2,1,0:T(8,128)(2,1)S(1)}, u32[]{:S(2)}, u32[]{:S(2)}) async-start(bf16[32,16,512]{2,1,0:T(8,128)(2,1)} %bitcast.25), calls=%async_computation.3 | async-start | bytes 1048576 | tf_op jit(solution)/shard_map/all_to_all | solution.py:45
  451.6 3.0 copy-start.2
  454.6 2.1 copy-start.15
  458.9 1.2 copy-start.6
  461.2 6.2 %copy-start.7 = (f32[16,16384]{1,0:T(8,128)S(1)}, f32[16,16384]{1,0:T(8,128)}, u32[]{:S(2)}) copy-start(f32[16,16384]{1,0:T(8,128)} %param.36) | copy-start | bytes 3145732
  467.2 1.5 copy-start.1

commit v6 on v3

--- a/solution.py
+++ b/solution.py
@@ -1,3 +1,6 @@
+import functools
+import math
+
 import jax
 import jax.numpy as jnp
 from jax import lax
@@ -37,9 +40,7 @@
 
 
 def to_nodes(channels):
-    return lax.all_to_all(
-        channels.astype(jnp.bfloat16), ("blk", "sub"), split_axis=1, concat_axis=0, tiled=True
-    )
+    return lax.all_to_all(channels, ("blk", "sub"), split_axis=1, concat_axis=0, tiled=True)
 
 
 def to_channels(values):
@@ -269,26 +270,37 @@
             pltpu.SemaphoreType.DMA((2,)),
         ],
         compiler_params=pltpu.CompilerParams(vmem_limit_bytes=VMEM_BYTES),
+        cost_estimate=pl.CostEstimate(
+            flops=20 * edges * width * width, bytes_accessed=40 * edges * width, transcendentals=2 * edges * width
+        ),
         name="edge_forward",
     )(count, recv, send.reshape(steps, 1, TILE), edge, wide, nodes, w_one, b_one, w_two, b_two, gain, shift)
 
 
 def backward_kernel(
-    count, recv, send, cotangent, edge, received, first, second, wide, nodes, w_one_t, w_two_t, gain,
-    grad, sums, grad_one, grad_two, vectors, sender_grad,
-    table, total, rows, stage, sems, by_sender,
+    count, recv, send, cotangent, edge, received, first, second, wide, node_one, node_two, node_part, nodes, w_one_t, w_two_t, gain,
+    grad, sums, all_grads, vectors, sender_grad,
+    table, total, rows, stage, sems, by_sender, grads, pass_sems,
 ):
     step = pl.program_id(0)
     base = step * TILE
     width = nodes.shape[1]
     parts = width // LANES
 
+    first_node = node_one.shape[0]
+    passed = (
+        pltpu.make_async_copy(node_one, grads.at[pl.ds(4 * width, first_node)], pass_sems.at[0]),
+        pltpu.make_async_copy(node_two, grads.at[pl.ds(4 * width + first_node, node_two.shape[0])], pass_sems.at[1]),
+        pltpu.make_async_copy(grads, all_grads, pass_sems.at[2]),
+    )
+
     @pl.when(step == 0)
     def _():
+        passed[0].start()
+        passed[1].start()
         load_table(wide, table, stage, sems)
         clear(total)
-        grad_one[...] = jnp.zeros_like(grad_one)
-        grad_two[...] = jnp.zeros_like(grad_two)
+        grads[: 4 * width] = jnp.zeros((4 * width, width), grads.dtype)
         vectors[...] = jnp.zeros_like(vectors)
         by_sender[...] = jnp.zeros_like(by_sender)
 
@@ -307,13 +319,13 @@
     pre = first[...]
     logistic = jax.nn.sigmoid(pre)
     act = (pre * logistic).astype(jnp.bfloat16)
-    grad_two[...] += dot_left(act, second_low)
+    grads[3 * width : 4 * width] += dot_left(act, second_low)
     grad_first = dot(second_low, w_two_t[...]) * (logistic * (1.0 + pre * (1.0 - logistic)))
     first_low = grad_first.astype(jnp.bfloat16)
     first_wide = first_low.astype(jnp.float32)
     vectors[0:1, :] += jnp.sum(first_wide, 0, keepdims=True)
-    grad_one[:width] += dot_left(edge[...], first_low)
-    grad_one[2 * width :] += dot_left(received[...], first_low)
+    grads[:width] += dot_left(edge[...], first_low)
+    grads[2 * width : 3 * width] += dot_left(received[...], first_low)
     node = lax.broadcasted_iota(jnp.int32, (nodes.shape[0], TILE), 0)
     chosen = jnp.where(node == send[0], 1.0, 0.0).astype(jnp.bfloat16)
     by_sender[...] += dot(chosen, first_low)
@@ -324,13 +336,20 @@
     @pl.when(step == pl.num_programs(0) - 1)
     def _():
         high, rest = split_low(by_sender[...])
-        grad_one[width : 2 * width] = dot_left(nodes[...], high) + dot_left(nodes[...], rest)
+        grads[width : 2 * width] = dot_left(nodes[...], high) + dot_left(nodes[...], rest)
+        passed[0].wait()
+        passed[1].wait()
+        passed[2].start()
         middle = w_one_t[:, width : 2 * width]
-        sender_grad[...] = dot(high, middle) + dot(rest, middle)
+        sender_grad[...] = node_part[...] + dot(high, middle) + dot(rest, middle)
         store_table(total, sums, stage, sems)
-
-
-def edge_backward(count, recv, send, cotangent, edge, received, first, second, wide, nodes, w_one_t, w_two_t, gain):
+        passed[2].wait()
+
+
+def edge_backward(
+    count, recv, send, cotangent, edge, received, first, second, wide, node_one, node_two, node_part, nodes,
+    w_one_t, w_two_t, gain,
+):
     edges, width = edge.shape
     steps = edges // TILE
     parts = width // LANES
@@ -339,6 +358,11 @@
     scalar = pl.BlockSpec(memory_space=pltpu.SMEM)
     tile = pl.BlockSpec((TILE, width), lambda i: (i, 0))
 
+    across = pl.BlockSpec(memory_space=pl.ANY)
+    unit = 64 * lax.axis_size("blk")
+    held = 4 * width + node_one.shape[0] + node_two.shape[0]
+    padded = -(-held // unit) * unit
+
     def whole(rows):
         return pl.BlockSpec((rows, width), lambda i: (0, 0))
 
@@ -347,17 +371,15 @@
         grid=(steps,),
         in_specs=[
             scalar, scalar, pl.BlockSpec((1, 1, TILE), lambda i: (i, 0, 0)), tile, tile, tile, tile, tile,
-            pl.BlockSpec(memory_space=pl.ANY), hold, hold, hold, hold,
+            across, across, across, hold, hold, hold, hold, hold,
         ],
         out_specs=[
-            tile, pl.BlockSpec(memory_space=pl.ANY),
-            whole(3 * width), whole(width), whole(8), whole(per_device),
+            tile, across, across, whole(8), whole(per_device),
         ],
         out_shape=[
             jax.ShapeDtypeStruct((edges, width), jnp.float32),
             jax.ShapeDtypeStruct(wide.shape, jnp.bfloat16),
-            jax.ShapeDtypeStruct((3 * width, width), jnp.float32),
-            jax.ShapeDtypeStruct((width, width), jnp.float32),
+            jax.ShapeDtypeStruct((padded, width), jnp.float32),
             jax.ShapeDtypeStruct((8, width), jnp.float32),
             jax.ShapeDtypeStruct((per_device, width), jnp.float32),
         ],
@@ -368,68 +390,291 @@
             pltpu.VMEM((2, CHUNK, width), jnp.bfloat16),
             pltpu.SemaphoreType.DMA((2,)),
             pltpu.VMEM((per_device, width), jnp.float32),
+            pltpu.VMEM((padded, width), jnp.float32),
+            pltpu.SemaphoreType.DMA((3,)),
         ],
         compiler_params=pltpu.CompilerParams(vmem_limit_bytes=VMEM_BYTES),
+        cost_estimate=pl.CostEstimate(
+            flops=24 * edges * width * width, bytes_accessed=40 * edges * width, transcendentals=2 * edges * width
+        ),
         name="edge_backward",
-    )(count, recv, send.reshape(steps, 1, TILE), cotangent, edge, received, first, second, wide, nodes, w_one_t, w_two_t, gain)
+    )(
+        count, recv, send.reshape(steps, 1, TILE), cotangent, edge, received, first, second, wide, node_one, node_two,
+        node_part, nodes, w_one_t, w_two_t, gain,
+    )
 
 
 MESH = pl.DeviceIdType.MESH
 PIECES = 4
+LOW = jnp.bfloat16
+WIDE = jnp.float32
 
 
 def places():
     groups = lax.axis_size("blk")
     group, sub = lax.axis_index("blk"), lax.axis_index("sub")
     odd = lax.rem(group, 2)
+    along = groups // 2
+    spot = group // 2
+    beside = group + 1 - 2 * odd
     return dict(
         group=group,
         sub=sub,
+        core=lax.rem(sub, 2),
+        chip=sub // 2,
+        odd=odd,
+        spot=spot,
+        along=along,
         sibling=sub + 1 - 2 * lax.rem(sub, 2),
         partner=lax.rem(sub + 2, 4),
-        beside=group + 1 - 2 * odd,
-        onward=lax.rem(group + 2 - 4 * odd + groups, groups),
-        source=lax.rem(group - 2 + 4 * odd + groups, groups),
+        to_sibling=(group, sub + 1 - 2 * lax.rem(sub, 2)),
+        to_partner=(group, lax.rem(sub + 2, 4)),
+        to_beside=(beside, sub),
+        to_onward=(lax.rem(group + 2 - 4 * odd + groups, groups), sub),
+        to_source=(lax.rem(group - 2 + 4 * odd + groups, groups), sub),
+        peers=[(2 * lax.rem(spot + k, along) + odd, sub) for k in range(1, along)],
         near=2 - 2 * odd,
         far=2 * odd,
     )
 
 
-def meet(senders, count):
+def meet(senders):
     barrier = pltpu.get_barrier_semaphore()
     for device in senders:
         pl.semaphore_signal(barrier, inc=1, device_id=device, device_id_type=MESH)
-    pl.semaphore_wait(barrier, count)
-
-
-def spread_kernel(own, table, send_sems, recv_sems, keep_sem):
-    at = places()
-    group, sub, partner, near, far = at["group"], at["sub"], at["partner"], at["near"], at["far"]
-    to_sibling = (group, at["sibling"])
-    to_partner = (group, partner)
-    to_beside = (at["beside"], sub)
-    to_onward = (at["onward"], sub)
+    pl.semaphore_wait(barrier, len(senders))
+
+
+def meet_all():
+    barrier = pltpu.get_barrier_semaphore()
+    subs = lax.axis_size("sub")
+    devices = lax.axis_size("blk") * subs
+    here = lax.axis_index("blk") * subs + lax.axis_index("sub")
+
+    def greet(k, carry):
+        there = lax.rem(here + k, devices)
+        pl.semaphore_signal(barrier, inc=1, device_id=(there // subs, lax.rem(there, subs)), device_id_type=MESH)
+        return carry
+
+    lax.fori_loop(1, devices, greet, 0)
+    pl.semaphore_wait(barrier, devices - 1)
+
+
+def remote(source, target, send, recv, device):
+    return pltpu.make_async_remote_copy(
+        src_ref=source, dst_ref=target, send_sem=send, recv_sem=recv, device_id=device, device_id_type=MESH
+    )
+
+
+def in_pieces(count, body):
+    block = math.gcd(count, 128)
+
+    def run(i, carry):
+        body(pl.multiple_of(i * block, block), block)
+        return carry
+
+    lax.fori_loop(0, count // block, run, 0)
+
+
+def reducer_scratch(rows, width, along):
+    return [
+        pltpu.VMEM((rows // 2, width), WIDE),
+        pltpu.VMEM((rows // 2, width), WIDE),
+        pltpu.VMEM((rows // 4, width), LOW),
+        pltpu.VMEM((rows // 4, width), LOW),
+        pltpu.VMEM((rows // 8, width), LOW),
+        pltpu.VMEM((rows // 8, width), LOW),
+        pltpu.VMEM((rows // 8, width), LOW),
+        pltpu.VMEM((along - 1, rows // 8 // along, width), LOW),
+        pltpu.SemaphoreType.DMA,
+        pltpu.SemaphoreType.DMA((6,)),
+        pltpu.SemaphoreType.DMA((6,)),
+        pltpu.SemaphoreType.DMA((2, along - 1)),
+        pltpu.SemaphoreType.DMA((2, along - 1)),
+    ]
+
+
+def reducer(at, grads, reduced, first, rows, swap, refs):
+    (
+        half, half_in, cross_out, cross_in, side_out, side_in, ring_out, ring_in,
+        load_sem, step_send, step_recv, ring_send, ring_recv,
+    ) = refs
+    along, peers = at["along"], at["peers"]
+    turns = [(at["chip"], at["to_partner"]), (at["odd"], at["to_beside"])]
+    (bit_one, device_one), (bit_two, device_two) = turns[::-1] if swap else turns
+    core, spot = at["core"], at["spot"]
+    n_half, n_cross, n_side, n_ring = rows // 2, rows // 4, rows // 8, rows // 8 // along
+    at_half = first + core * n_half
+    at_cross = at_half + bit_one * n_cross
+    at_side = at_cross + bit_two * n_side
+    at_ring = at_side + spot * n_ring
+
+    def span(start, count):
+        return pl.ds(pl.multiple_of(start, 16), count)
+
+    def step(kind):
+        if kind == 0:
+            source, target, device = grads.at[span(first + (1 - core) * n_half, n_half)], half_in, at["to_sibling"]
+        elif kind == 1:
+            source, target, device = cross_out, cross_in, device_one
+        elif kind == 2:
+            source, target, device = side_out, side_in, device_two
+        else:
+            start, count, device = {
+                3: (at_side, n_side, device_two),
+                4: (at_cross, n_cross, device_one),
+                5: (at_half, n_half, at["to_sibling"]),
+            }[kind]
+            source = target = reduced.at[span(start, count)]
+        return remote(source, target, step_send.at[kind], step_recv.at[kind], device)
+
+    def ring(kind, k):
+        if kind == 0:
+            source = ring_out.at[span(lax.rem(spot + k, along) * n_ring, n_ring)]
+            target = ring_in.at[k - 1]
+        else:
+            source = target = reduced.at[span(at_ring, n_ring)]
+        return remote(source, target, ring_send.at[kind, k - 1], ring_recv.at[kind, k - 1], peers[k - 1])
+
+    load = pltpu.make_async_copy(grads.at[span(at_half, n_half)], half, load_sem)
+
+    def start():
+        step(0).start()
+        load.start()
+
+    def add_half():
+        load.wait()
+        step(0).wait_recv()
+        other = (1 - bit_one) * n_cross
+
+        def part(i, block):
+            here = pl.ds(pl.multiple_of(other + i, block), block)
+            cross_out[pl.ds(i, block), :] = (half[here, :] + half_in[here, :]).astype(LOW)
+
+        in_pieces(n_cross, part)
+        step(1).start()
+
+    def add_cross():
+        mine, other = bit_one * n_cross, (1 - bit_two) * n_side
+        step(1).wait_recv()
+
+        def part(i, block):
+            there = pl.ds(pl.multiple_of(other + i, block), block)
+            here = pl.ds(pl.multiple_of(mine + other + i, block), block)
+            side_out[pl.ds(i, block), :] = (half[here, :] + half_in[here, :] + cross_in[there, :].astype(WIDE)).astype(LOW)
+
+        in_pieces(n_side, part)
+        step(2).start()
+
+    def add_side():
+        mine, kept = bit_one * n_cross, bit_two * n_side
+        step(2).wait_recv()
+
+        def part(i, block):
+            there = pl.ds(pl.multiple_of(kept + i, block), block)
+            here = pl.ds(pl.multiple_of(mine + kept + i, block), block)
+            flat = pl.ds(i, block)
+            value = half[here, :] + half_in[here, :] + cross_in[there, :].astype(WIDE) + side_in[flat, :].astype(WIDE)
+            half[here, :] = value
+            ring_out[flat, :] = value.astype(LOW)
+
+        in_pieces(n_side, part)
+        for k in range(1, along):
+            ring(0, k).start()
+
+    def add_ring():
+        value = half[span(bit_one * n_cross + bit_two * n_side + spot * n_ring, n_ring), :]
+        for k in range(1, along):
+            ring(0, k).wait_recv()
+            value = value + ring_in[k - 1].astype(WIDE)
+        reduced[span(at_ring, n_ring), :] = value.astype(LOW)
+        for k in range(1, along):
+            ring(1, k).start()
+
+    def share_side():
+        for k in range(1, along):
+            ring(1, k).wait_recv()
+        step(3).start()
+
+    def share_cross():
+        step(3).wait_recv()
+        step(4).start()
+
+    def share_half():
+        step(4).wait_recv()
+        step(5).start()
+
+    def last():
+        step(5).wait_recv()
+
+    def drain():
+        for kind in range(6):
+            step(kind).wait_send()
+        for k in range(1, along):
+            ring(0, k).wait_send()
+            ring(1, k).wait_send()
+
+    return [start, add_half, add_cross, add_side, add_ring, share_side, share_cross, share_half, last, drain]
+
+
+def vector_scratch(shape, along):
+    return [
+        pltpu.VMEM((4, *shape), WIDE),
+        pltpu.VMEM((2 + along, *shape), WIDE),
+        pltpu.SemaphoreType.DMA((2 + along,)),
+        pltpu.SemaphoreType.DMA((2 + along,)),
+    ]
+
+
+def vector_reducer(at, vectors, reduced, refs):
+    held, held_in, send_sems, recv_sems = refs
+    along = at["along"]
+    devices = (at["to_sibling"], at["to_partner"], at["to_beside"], *at["peers"])
+
+    def move(kind):
+        return remote(held.at[min(kind, 3)], held_in.at[kind], send_sems.at[kind], recv_sems.at[kind], devices[kind])
+
+    def start():
+        held[0] = vectors[...]
+        move(0).start()
+
+    def turn(kind):
+        def run():
+            move(kind).wait_recv()
+            held[kind + 1] = held[kind] + held_in[kind]
+            for k in range(kind + 1, kind + 2 if kind < 2 else 2 + along):
+                move(k).start()
+
+        return run
+
+    def last():
+        value = held[3]
+        for k in range(3, 2 + along):
+            move(k).wait_recv()
+            value = value + held_in[k]
+        reduced[...] = value
+        for k in range(2 + along):
+            move(k).wait_send()
+
+    return [start, turn(0), turn(1), turn(2), last]
+
+
+def both(streams):
+    return [lambda steps=steps: [step() for step in steps] for steps in zip(*streams)]
+
+
+def spread_moves(at, own, table, keep_sem, send_sems, recv_sems):
+    sub, partner, near, far = at["sub"], at["partner"], at["near"], at["far"]
+    to_sibling, to_partner, to_beside, to_onward = (
+        at["to_sibling"], at["to_partner"], at["to_beside"], at["to_onward"]
+    )
     size = own.shape[0] // PIECES
-    meet((to_sibling, to_partner, to_beside, (at["source"], sub)), 4)
-
-    def copy(kind, piece, source, slot, device):
-        return pltpu.make_async_remote_copy(
-            src_ref=source.at[pl.ds(piece * size, size)],
-            dst_ref=table.at[slot[0], slot[1], pl.ds(piece * size, size)],
-            send_sem=send_sems.at[kind, piece],
-            recv_sem=recv_sems.at[kind, piece],
-            device_id=device,
-            device_id_type=MESH,
-        )
 
     def move(kind, piece):
-        if kind == 0:
-            return copy(0, piece, own, (1, sub), to_partner)
-        if kind == 1:
-            return copy(1, piece, own, (far, sub), to_beside)
-        if kind == 2:
-            return copy(2, piece, own, (1, sub), to_sibling)
-        slot, target, device = {
+        source, slot, device = {
+            0: (None, (1, sub), to_partner),
+            1: (None, (far, sub), to_beside),
+            2: (None, (1, sub), to_sibling),
             3: ((1, partner), (far, partner), to_beside),
             4: ((1, partner), (1, partner), to_sibling),
             5: ((near, sub), (far, sub), to_onward),
@@ -439,62 +684,106 @@
             9: ((far, sub), (far, sub), to_sibling),
             10: ((far, partner), (far, partner), to_sibling),
         }[kind]
-        return copy(kind, piece, table.at[slot[0], slot[1]], target, device)
+        source = own if source is None else table.at[source[0], source[1]]
+        rows = pl.ds(piece * size, size)
+        return remote(
+            source.at[rows], table.at[slot[0], slot[1], rows],
+            send_sems.at[kind, piece], recv_sems.at[kind, piece], device,
+        )
 
     keep = pltpu.make_async_copy(own, table.at[1, sub], keep_sem)
-    for piece in range(PIECES):
-        for kind in (0, 1, 2):
-            move(kind, piece).start()
-    keep.start()
+
+    def start():
+        for piece in range(PIECES):
+            for kind in (0, 1, 2):
+                move(kind, piece).start()
+        keep.start()
 
     def relay(arrived, kinds, piece):
         move(arrived, piece).wait_recv()
         for kind in kinds:
             move(kind, piece).start()
 
-    for piece in range(PIECES):
+    def one(piece):
         relay(0, (3, 4), piece)
         relay(1, (5, 6), piece)
-    for piece in range(PIECES):
+
+    def two(piece):
         relay(3, (7, 8), piece)
         relay(5, (9,), piece)
-    for piece in range(PIECES):
+
+    def three(piece):
         relay(7, (10,), piece)
-    for kind in range(11):
+
+    def drain():
+        for kind in range(11):
+            for piece in range(PIECES):
+                if kind in (2, 4, 6, 8, 9, 10):
+                    move(kind, piece).wait_recv()
+                move(kind, piece).wait_send()
+        keep.wait()
+
+    return start, one, two, three, drain
+
+
+def spread_scratch():
+    return [
+        pltpu.SemaphoreType.DMA,
+        pltpu.SemaphoreType.DMA((11, PIECES)),
+        pltpu.SemaphoreType.DMA((11, PIECES)),
+    ]
+
+
+def spread_kernel(own, table, *refs):
+    at = places()
+    meet((at["to_sibling"], at["to_partner"], at["to_beside"], at["to_source"]))
+    start, one, two, three, drain = spread_moves(at, own, table, *refs)
+    start()
+    for stage in (one, two, three):
         for piece in range(PIECES):
-            if kind in (2, 4, 6, 8, 9, 10):
-                move(kind, piece).wait_recv()
-            move(kind, piece).wait_send()
-    keep.wait()
+            stage(piece)
+    drain()
 
 
 def spread(own, collective):
     rows, width = own.shape
     return pl.pallas_call(
         spread_kernel,
-        in_specs=[pl.BlockSpec(memory_space=pl.ANY)],
+        in_specs=[pl.BlockSpec(memory_space=pltpu.VMEM)],
         out_specs=pl.BlockSpec(memory_space=pl.ANY),
         out_shape=jax.ShapeDtypeStruct((3, 4, rows, width), own.dtype),
-        scratch_shapes=[
-            pltpu.SemaphoreType.DMA((11, PIECES)),
-            pltpu.SemaphoreType.DMA((11, PIECES)),
-            pltpu.SemaphoreType.DMA,
-        ],
+        scratch_shapes=spread_scratch(),
         compiler_params=pltpu.CompilerParams(collective_id=collective, has_side_effects=True),
         name="spread_rows",
     )(own).reshape(12 * rows, width)
 
 
-def collect_kernel(
-    sums, out, mine, landed, far_out, far_in, near_out, near_in, pair_out, pair_in,
-    keep_sems, give_sems, take_sems, send_sems, recv_sems,
-):
-    at = places()
-    group, sub, partner, near, far = at["group"], at["sub"], at["partner"], at["near"], at["far"]
-    sibling = at["sibling"]
+def collect_scratch(rows, width):
+    return [
+        pltpu.VMEM((3, 2, rows, width), LOW),
+        pltpu.VMEM((3, 2, rows, width), LOW),
+        pltpu.VMEM((2, rows, width), LOW),
+        pltpu.VMEM((2, rows, width), LOW),
+        pltpu.VMEM((2, rows, width), LOW),
+        pltpu.VMEM((2, rows, width), LOW),
+        pltpu.VMEM((rows, width), LOW),
+        pltpu.VMEM((rows, width), LOW),
+        pltpu.SemaphoreType.DMA((3, 2, PIECES)),
+        pltpu.SemaphoreType.DMA((3, 2, PIECES)),
+        pltpu.SemaphoreType.DMA((3, 2, PIECES)),
+        pltpu.SemaphoreType.DMA((5, PIECES)),
+        pltpu.SemaphoreType.DMA((5, PIECES)),
+    ]
+
+
+def collect_moves(at, sums, out, refs):
+    (
+        mine, landed, far_out, far_in, near_out, near_in, pair_out, pair_in,
+        keep_sems, give_sems, take_sems, send_sems, recv_sems,
+    ) = refs
+    sub, partner, sibling = at["sub"], at["partner"], at["sibling"]
+    relations = (at["far"], at["near"], 1)
     size = out.shape[0] // PIECES
-    meet(((group, sibling), (group, partner), (at["beside"], sub), (at["onward"], sub)), 4)
-    relations = (far, near, 1)
 
     def part(ref, piece):
         return ref.at[pl.ds(piece * size, size)]
@@ -507,98 +796,249 @@
         )
 
     def give(role, side, piece):
-        return pltpu.make_async_remote_copy(
-            src_ref=part(sums.at[relations[role], (sibling, lax.rem(sibling + 2, 4))[side]], piece),
-            dst_ref=part(landed.at[role, side], piece),
-            send_sem=give_sems.at[role, side, piece],
-            recv_sem=take_sems.at[role, side, piece],
-            device_id=(group, sibling),
-            device_id_type=MESH,
+        return remote(
+            part(sums.at[relations[role], (sibling, lax.rem(sibling + 2, 4))[side]], piece),
+            part(landed.at[role, side], piece),
+            give_sems.at[role, side, piece], take_sems.at[role, side, piece], at["to_sibling"],
         )
 
     def hop(kind, piece):
         source, target, device = {
-            0: (far_out.at[0], far_in.at[0], (at["source"], sub)),
-            1: (far_out.at[1], far_in.at[1], (at["source"], sub)),
-            2: (near_out.at[0], near_in.at[0], (at["beside"], sub)),
-            3: (near_out.at[1], near_in.at[1], (at["beside"], sub)),
-            4: (pair_out, pair_in, (group, partner)),
+            0: (far_out.at[0], far_in.at[0], at["to_source"]),
+            1: (far_out.at[1], far_in.at[1], at["to_source"]),
+            2: (near_out.at[0], near_in.at[0], at["to_beside"]),
+            3: (near_out.at[1], near_in.at[1], at["to_beside"]),
+            4: (pair_out, pair_in, at["to_partner"]),
         }[kind]
-        return pltpu.make_async_remote_copy(
-            src_ref=part(source, piece),
-            dst_ref=part(target, piece),
-            send_sem=send_sems.at[kind, piece],
-            recv_sem=recv_sems.at[kind, piece],
-            device_id=device,
-            device_id_type=MESH,
+        return remote(
+            part(source, piece), part(target, piece), send_sems.at[kind, piece], recv_sems.at[kind, piece], device
         )
 
     order = [(role, side, piece) for role in range(3) for side in (1, 0) for piece in range(PIECES)]
-    for item in order:
-        give(*item).start()
-        keep(*item).start()
 
     def local(role, side, piece):
         keep(role, side, piece).wait()
         give(role, side, piece).wait_recv()
         rows = pl.ds(piece * size, size)
-        return mine[role, side, rows, :].astype(jnp.float32) + landed[role, side, rows, :].astype(jnp.float32)
+        return mine[role, side, rows, :].astype(WIDE) + landed[role, side, rows, :].astype(WIDE)
 
     def arrived(kind, ref, piece):
         hop(kind, piece).wait_recv()
-        return ref[pl.ds(piece * size, size), :].astype(jnp.float32)
-
-    for side in (1, 0):
-        for piece in range(PIECES):
-            far_out[side, pl.ds(piece * size, size), :] = local(0, side, piece).astype(jnp.bfloat16)
-            hop(side, piece).start()
-    for side in (1, 0):
-        for piece in range(PIECES):
-            value = local(1, side, piece) + arrived(side, far_in.at[side], piece)
-            near_out[side, pl.ds(piece * size, size), :] = value.astype(jnp.bfloat16)
-            hop(2 + side, piece).start()
-    for piece in range(PIECES):
+        return ref[pl.ds(piece * size, size), :].astype(WIDE)
+
+    def start(role):
+        for item in order:
+            if item[0] == role:
+                give(*item).start()
+                keep(*item).start()
+
+    def far_step(side, piece):
+        far_out[side, pl.ds(piece * size, size), :] = local(0, side, piece).astype(LOW)
+        hop(side, piece).start()
+
+    def near_step(side, piece):
+        value = local(1, side, piece) + arrived(side, far_in.at[side], piece)
+        near_out[side, pl.ds(piece * size, size), :] = value.astype(LOW)
+        hop(2 + side, piece).start()
+
+    def pair_step(piece):
         value = local(2, 1, piece) + arrived(3, near_in.at[1], piece)
-        pair_out[pl.ds(piece * size, size), :] = value.astype(jnp.bfloat16)
+        pair_out[pl.ds(piece * size, size), :] = value.astype(LOW)
         hop(4, piece).start()
-    for piece in range(PIECES):
+
+    def last_step(piece):
         value = local(2, 0, piece) + arrived(2, near_in.at[0], piece) + arrived(4, pair_in, piece)
         out[pl.ds(piece * size, size), :] = value
-    for item in order:
-        give(*item).wait_send()
-    for kind in range(5):
-        for piece in range(PIECES):
-            hop(kind, piece).wait_send()
+
+    def drain():
+        for item in order:
+            give(*item).wait_send()
+        for kind in range(5):
+            for piece in range(PIECES):
+                hop(kind, piece).wait_send()
+
+    return start, far_step, near_step, pair_step, last_step, drain
+
+
+def collect_kernel(sums, out, *refs):
+    at = places()
+    meet((at["to_sibling"], at["to_partner"], at["to_beside"], at["to_onward"]))
+    start, far_step, near_step, pair_step, last_step, drain = collect_moves(at, sums, out, refs)
+    for role in range(3):
+        start(role)
+    for step in (far_step, near_step):
+        for side in (1, 0):
+            for piece in range(PIECES):
+                step(side, piece)
+    for piece in range(PIECES):
+        pair_step(piece)
+    for piece in range(PIECES):
+        last_step(piece)
+    drain()
 
 
 def collect(sums, rows, collective):
     width = sums.shape[1]
-    low = jnp.bfloat16
     return pl.pallas_call(
         collect_kernel,
         in_specs=[pl.BlockSpec(memory_space=pl.ANY)],
         out_specs=pl.BlockSpec(memory_space=pltpu.VMEM),
-        out_shape=jax.ShapeDtypeStruct((rows, width), jnp.float32),
-        scratch_shapes=[
-            pltpu.VMEM((3, 2, rows, width), low),
-            pltpu.VMEM((3, 2, rows, width), low),
-            pltpu.VMEM((2, rows, width), low),
-            pltpu.VMEM((2, rows, width), low),
-            pltpu.VMEM((2, rows, width), low),
-            pltpu.VMEM((2, rows, width), low),
-            pltpu.VMEM((rows, width), low),
-            pltpu.VMEM((rows, width), low),
-            pltpu.SemaphoreType.DMA((3, 2, PIECES)),
-            pltpu.SemaphoreType.DMA((3, 2, PIECES)),
-            pltpu.SemaphoreType.DMA((3, 2, PIECES)),
-            pltpu.SemaphoreType.DMA((5, PIECES)),
-            pltpu.SemaphoreType.DMA((5, PIECES)),
-        ],
+        out_shape=jax.ShapeDtypeStruct((rows, width), WIDE),
+        scratch_shapes=collect_scratch(rows, width),
         compiler_params=pltpu.CompilerParams(
             collective_id=collective, has_side_effects=True, vmem_limit_bytes=VMEM_BYTES
         ),
         name="collect_sums",
     )(sums.reshape(3, 4, rows, width))
+
+
+def exchange_scratch(rows, width, devices):
+    slab = width // devices * (rows // LANES)
+    return [
+        pltpu.VMEM((devices * slab, LANES), WIDE),
+        pltpu.VMEM((devices * slab, LANES), LOW),
+        pltpu.VMEM((devices, slab, LANES), LOW),
+        pltpu.VMEM((slab, LANES), WIDE),
+        pltpu.SemaphoreType.DMA((devices - 1,)),
+        pltpu.SemaphoreType.DMA((devices - 1,)),
+    ]
+
+
+def exchange_moves(residual, out, refs):
+    flat, packed, landed, opened, send_sems, recv_sems = refs
+    subs = lax.axis_size("sub")
+    devices = lax.axis_size("blk") * subs
+    here = lax.axis_index("blk") * subs + lax.axis_index("sub")
+    slab = landed.shape[1]
+    channels = out.shape[0]
+    parts = slab // channels
+    nodes = parts * LANES
+
+    def move(k):
+        there = lax.rem(here + k, devices)
+        return remote(
+            packed.at[pl.ds(pl.multiple_of(there * slab, slab), slab)], landed.at[here],
+            send_sems.at[k - 1], recv_sems.at[k - 1], (there // subs, lax.rem(there, subs)),
+        )
+
+    def start(values):
+        lay_rows(flat, 0, values.T)
+
+        def cast(i, block):
+            packed[pl.ds(i, block), :] = flat[pl.ds(i, block), :].astype(LOW)
+
+        in_pieces(flat.shape[0], cast)
+
+        def send(k, carry):
+            move(k).start()
+            return carry
+
+        lax.fori_loop(1, devices, send, 0)
+
+    def open_slab(source, device):
+        opened[...] = source.astype(WIDE)
+        for j in range(parts):
+            columns = pl.ds(pl.multiple_of(device * nodes + j * LANES, LANES), LANES)
+            out[:, columns] = residual[:, columns] + opened[pl.ds(j, channels, stride=parts), :]
+
+    def last():
+        open_slab(packed[pl.ds(pl.multiple_of(here * slab, slab), slab), :], here)
+
+        def take(k, carry):
+            move(k).wait_recv()
+            device = lax.rem(here - k + devices, devices)
+            open_slab(landed[device], device)
+            return carry
+
+        lax.fori_loop(1, devices, take, 0)
+
+        def sent(k, carry):
+            move(k).wait_send()
+            return carry
+
+        lax.fori_loop(1, devices, sent, 0)
+
+    return start, last
+
+
+def finish_kernel(
+    cut, sums, grads, vectors, node_part, weight, residual, node_grad, reduced, reduced_vectors, total, *refs
+):
+    at = places()
+    meet_all()
+    sizes = len(reducer_scratch(64, 128, 2))
+    count = len(collect_scratch(64, 128))
+    start, far_step, near_step, pair_step, last_step, drain = collect_moves(at, sums, total, refs[:count])
+    refs = refs[count:]
+    steps = both([
+        reducer(at, grads, reduced, 0, cut, False, refs[:sizes]),
+        reducer(at, grads, reduced, cut, grads.shape[0] - cut, True, refs[sizes : 2 * sizes]),
+    ])
+    refs = refs[2 * sizes :]
+    vector_steps = vector_reducer(at, vectors, reduced_vectors, refs[:4])
+    exchange, receive = exchange_moves(residual, node_grad, refs[4:])
+    start(0)
+    steps[0]()
+    vector_steps[0]()
+    start(1)
+    start(2)
+    for side in (1, 0):
+        for piece in range(PIECES):
+            far_step(side, piece)
+    steps[1]()
+    vector_steps[1]()
+    for piece in range(PIECES):
+        near_step(1, piece)
+    steps[2]()
+    vector_steps[2]()
+    for piece in range(PIECES):
+        near_step(0, piece)
+    for piece in range(PIECES):
+        pair_step(piece)
+    steps[3]()
+    vector_steps[3]()
+    for piece in range(PIECES):
+        last_step(piece)
+    steps[4]()
+    high, rest = split_low(total[...])
+    exchange(node_part[...] + dot(high, weight[...]) + dot(rest, weight[...]))
+    for step in steps[5:8]:
+        step()
+    receive()
+    steps[8]()
+    vector_steps[4]()
+    drain()
+    steps[9]()
+
+
+def finish(sums, grads, vectors, node_part, weight, residual, cut, collective):
+    rows, width = node_part.shape
+    along = lax.axis_size("blk") // 2
+    devices = lax.axis_size("blk") * lax.axis_size("sub")
+    hold = pl.BlockSpec(memory_space=pltpu.VMEM)
+    across = pl.BlockSpec(memory_space=pl.ANY)
+    return pl.pallas_call(
+        functools.partial(finish_kernel, cut),
+        in_specs=[across, across, hold, hold, hold, hold],
+        out_specs=[hold] * 3,
+        out_shape=[
+            jax.ShapeDtypeStruct(residual.shape, WIDE),
+            jax.ShapeDtypeStruct(grads.shape, LOW),
+            jax.ShapeDtypeStruct(vectors.shape, WIDE),
+        ],
+        scratch_shapes=[
+            pltpu.VMEM((rows, width), WIDE),
+            *collect_scratch(rows, width),
+            *reducer_scratch(cut, width, along),
+            *reducer_scratch(grads.shape[0] - cut, width, along),
+            *vector_scratch(vectors.shape, along),
+            *exchange_scratch(rows, width, devices),
+        ],
+        compiler_params=pltpu.CompilerParams(
+            collective_id=collective, has_side_effects=True, vmem_limit_bytes=VMEM_BYTES
+        ),
+        name="finish_sums",
+    )(sums.reshape(3, 4, rows, width), grads, vectors, node_part, weight, residual)
 
 
 def shards(
@@ -627,8 +1067,8 @@
     block_index = lax.axis_index("blk")
     sub_index = lax.axis_index("sub")
     width = edge_input.shape[1]
-    node_low = to_nodes(node_input).T
-    node_upstream = to_nodes(node_cotangent).T.astype(jnp.float32)
+    node_low = to_nodes(node_input.astype(jnp.bfloat16)).T
+    node_upstream = to_nodes(node_cotangent).T
     per_device = node_low.shape[0]
     per_group = per_device * sub_count
     my_start = (block_index * sub_count + sub_index) * per_device
@@ -655,47 +1095,38 @@
     grad_node_w_one = left_matmul(joined, third_low)
     grad_node_b_one = jnp.sum(third_low.astype(jnp.float32), 0)
     grad_joined = right_matmul(third_low, node_w_one)
-    grad_nodes = grad_joined[:, :width]
     grad_gathered = grad_joined[:, width:]
     wide_grad = spread(grad_gathered.astype(jnp.bfloat16), 2)
-    node_grads = (
-        grad_node_w_one, grad_node_b_one, grad_node_w_two, grad_node_b_two, grad_node_gain, grad_node_shift
-    )
-    wide_grad, node_grads = lax.optimization_barrier((wide_grad, node_grads))
-    node_summed = lax.psum(node_grads, ("blk", "sub"))
     node_out = node_input + to_channels(node_branch.T)
-    edge_grad, receiver_wide, grad_edge_w_one, grad_edge_w_two, vectors, sender_grad = edge_backward(
+    w_one_t = edge_w_one.T
+    edge_grad, receiver_wide, grads, vectors, node_part = edge_backward(
         edge_count, recv_wide, send_local, edge_cotangent, edge_input, received, first_pre, second_pre,
-        wide_grad, node_low, edge_w_one.T, edge_w_two.T, edge_gain[None],
-    )
-    grad_edge_b_one, grad_edge_b_two, grad_edge_gain, grad_edge_shift = (vectors[i] for i in range(4))
-    high, rest = split_low(collect(receiver_wide, per_device, 3))
-    receiver_weight = edge_w_one[2 * width :]
-    receiver_grad = right_matmul(high, receiver_weight) + right_matmul(rest, receiver_weight)
-    node_total = grad_nodes + sender_grad + receiver_grad
-    edge_grads = (
-        grad_edge_w_one, grad_edge_b_one, grad_edge_w_two, grad_edge_b_two, grad_edge_gain, grad_edge_shift
-    )
-    edge_grads, node_summed = lax.optimization_barrier((edge_grads, node_summed))
-    summed = lax.psum(edge_grads, ("blk", "sub"))
-    node_grad = node_cotangent + to_channels(node_total.T)
+        wide_grad, grad_node_w_one, grad_node_w_two, grad_joined[:, :width], node_low, w_one_t, edge_w_two.T,
+        edge_gain[None],
+    )
+    node_vectors = jnp.stack([grad_node_b_one, grad_node_b_two, grad_node_gain, grad_node_shift])
+    node_grad, summed, vectors = finish(
+        receiver_wide, grads, jnp.concatenate([vectors[:4], node_vectors]), node_part, w_one_t[:, 2 * width :],
+        node_cotangent, 4 * width, 3,
+    )
+    summed = summed.astype(jnp.float32)
     return (
         node_out,
         edge_result,
         node_grad,
         edge_grad,
-        summed[0],
-        summed[1],
-        summed[2],
-        summed[3],
-        summed[4],
-        summed[5],
-        node_summed[0],
-        node_summed[1],
-        node_summed[2],
-        node_summed[3],
-        node_summed[4],
-        node_summed[5],
+        summed[: 3 * width],
+        vectors[0],
+        summed[3 * width : 4 * width],
+        vectors[1],
+        vectors[2],
+        vectors[3],
+        summed[4 * width : 6 * width],
+        vectors[4],
+        summed[6 * width : 7 * width],
+        vectors[5],
+        vectors[6],
+        vectors[7],
     )
 
 

time: 558 us -> 405 us (0.73)
  waiting for transfers between devices: 116 us -> 7.51 us
  blocking collectives: 82.9 us -> 0 us
  Pallas kernels: 285 us -> 347 us
  between operations: 15.1 us -> 1.68 us
    pallas_call x2 -> x3, Pallas kernels: 73.6 us -> 174 us  [the longest x1 94.5 us: finish(): pl.pallas_call(functools.partial(finish_kernel, cut), in_specs=[across, a...]
    psum x2 -> x0, waiting for transfers between devices: 84.8 us -> none  [the longest x1 84.8 us: shards(): summed = lax.psum(edge_grads, ('blk', 'sub'))]
    psum x2 -> x0, blocking collectives: 82.9 us -> none  [the longest x1 42.4 us: shards(): node_summed = lax.psum(node_grads, ('blk', 'sub'))]
    pallas_call x2 -> x1, Pallas kernels: 87.5 us -> 47.2 us  [collect(): pl.pallas_call(collect_kernel, in_specs=[pl.BlockSpec(memory_space=pl.ANY...]
    all_to_all x2 -> x1, waiting for transfers between devices: 17.6 us -> 0.01 us  [to_channels(): lax.all_to_all(values.astype(jnp.bfloat16), ('blk', 'sub'), split_axis=0,...]
    unnamed x60 -> x47, local copies, waits for them, and re-layouts: 16.2 us -> 6.02 us
    slice x1 -> x7, local copies, waits for them, and re-layouts: 0.01 us -> 10.1 us  [the longest x1 3.67 us: shards(): summed[:3 * width]]
    all_to_all x2, waiting for transfers between devices: 13.3 us -> 7.51 us  [to_nodes(): lax.all_to_all(channels, ('blk', 'sub'), split_axis=1, concat_axis=0, til...]
  transfers between devices with their start and end apart: 6 -> 3, of which waited for: 3 -> 1; matrix products, arithmetic and copies ran while one was open for 3% -> 5% of each run, Pallas kernels for 45% -> 77%
where the time goes in v6:
time: 405 us; the launch traced here: 404 us
  Pallas kernels  347 us (86%)
  local copies, waits for them, and re-layouts  21.4 us (5%)
  starting transfers between devices  13.6 us (3%)
  waiting for transfers between devices  7.51 us (2%)
  other arithmetic  6.72 us (2%)
  matrix products  6.29 us (2%)
    pallas_call x1, Pallas kernels, finish(): pl.pallas_call(functools.partial(finish_kernel, cut), in_specs=[across, a...  94.5 us
    pallas_call x2, Pallas kernels, spread(): pl.pallas_call(spread_kernel, in_specs=[pl.BlockSpec(memory_space=pltpu.V...  79 us
    pallas_call x1, Pallas kernels, edge_backward(): pl.pallas_call(backward_kernel, grid=(steps,), in_specs=[scalar, scalar,...  70.1 us
    pallas_call x1, Pallas kernels, edge_forward(): pl.pallas_call(forward_kernel, grid=(steps,), in_specs=[scalar, scalar, p...  55.8 us
    pallas_call x1, Pallas kernels, collect(): pl.pallas_call(collect_kernel, in_specs=[pl.BlockSpec(memory_space=pl.ANY...  47.2 us
    all_to_all x2, starting transfers between devices, to_nodes(): lax.all_to_all(channels, ('blk', 'sub'), split_axis=1, concat_axis=0, til...  10.4 us
  transfers between devices with their start and end apart: 3, of which 1 were waited for; matrix products, arithmetic and copies ran while one was open for 5% of the time, Pallas kernels for 77%

profile of v6, /device:TPU:0, one launch (start us, length us, event | category | flops | bytes accessed | tf_op | source)
XLA Modules:
  0.0 403.8 jit_solution(18386967566072502974)
XLA Ops:
  0.6 0.0 copy-start
  0.7 0.0 copy-start.3
  0.7 1.4 convert_element_type.37
  2.1 0.9 copy.63
  3.0 7.3 %all-to-all-start = ((bf16[16,32,512]{2,0,1:T(8,128)(2,1)}), bf16[16,32,512]{2,0,1:T(8,128)(2,1)S(1)}, u32[]{:S(2)}, u32[]{:S(2)}) async-start(bf16[16,32,512]{2,0,1:T(8,128)(2,1)} %bitcast.66), calls=%async_computation | async-start | bytes 1048576 | tf_op jit(solution)/shard_map/all_to_all | solution.py:43
  10.3 0.6 reshape.99.send
  11.6 0.0 copy-start.12
  11.6 1.1 copy.62
  12.7 1.7 copy.55
  14.4 0.0 copy-start.5
  14.4 2.4 copy.56
  16.8 0.9 slice.67.weight
  17.7 0.6 fusion.7.recv
  18.3 7.5 %all-to-all-done = bf16[16,32,512]{2,0,1:T(8,128)(2,1)S(1)} async-done(((bf16[16,32,512]{2,0,1:T(8,128)(2,1)}), bf16[16,32,512]{2,0,1:T(8,128)(2,1)S(1)}, u32[]{:S(2)}, u32[]{:S(2)}) %all-to-all-start) | async-done | bytes 524320 | tf_op jit(solution)/shard_map/all_to_all | solution.py:43
  25.8 3.1 all-to-all-start.2
  28.9 1.0 copy.52
  29.9 45.3 %spread_rows.2 = bf16[3,4,512,512]{3,2,1,0:T(8,128)(2,1)} custom-call(bf16[512,512]{1,0:T(8,128)(2,1)} %bitcast.77), custom_call_target="tpu_custom_call" | custom-call | tf_op jit(solution)/shard_map/spread_rows/pallas_call | solution.py:750
  75.2 55.8 %edge_forward.1 = (f32[4608,512]{1,0:T(8,128)}, f32[4608,512]{1,0:T(8,128)}, f32[4608,512]{1,0:T(8,128)}, bf16[4608,512]{1,0:T(8,128)(2,1)}, bf16[6144,512]{1,0:T(8,128)(2,1)}) custom-call(s32[1]{0:T(128)S(6)} %copy.65.count, s32[4608]{0:T(1024)} %fusion.7.recv, s32[9,1,512]{2,1,0:T(1,128)} %reshape.99.send, bf16[4608,512]{1,0:T(8,128)(2,1)} %edge.3, ...), custom_call_target="tpu_custom_call" | custom-call | flops 24159191040 | bytes 94371840 | tf_op jit(solution)/shard_map/edge_forward/pallas_call | solution.py:250
  131.0 0.0 copy-start.6
  131.0 0.0 copy-start.18
  131.0 47.2 %collect_sums.1 = f32[512,512]{1,0:T(8,128)} custom-call(bf16[3,4,512,512]{3,2,1,0:T(8,128)(2,1)} %bitcast.68), custom_call_target="tpu_custom_call" | custom-call | tf_op jit(solution)/shard_map/collect_sums/pallas_call | solution.py:882
  178.2 0.0 copy-start.16
  178.2 0.0 copy-start.19
  178.3 1.3 convert_element_type.38
  179.6 0.0 copy-start.9
  179.7 0.7 convolution_add_fusion.1
  180.4 0.0 copy-start.20
  180.4 0.0 copy-start.13
  180.4 0.0 copy-start.15
  180.4 0.6 fusion.16
  181.0 0.3 copy-done.20
  181.4 0.0 all-to-all-done.2
  181.4 0.0 copy-start.21
  181.4 0.2 multiply_reduce_fusion
  181.6 0.5 fusion.1
  182.1 0.0 copy-done.15
  182.1 0.0 copy-start.17
  182.1 1.3 convert_reduce_fusion
  183.4 1.5 fusion.13.node_two
  184.9 0.7 convert_reduce_fusion.1
  185.6 0.3 copy-done.7
  185.9 0.2 copy-done.10
  186.1 2.1 fusion.2.node_one
  188.1 0.7 fusion.17
  188.9 0.9 slice.73.own
  189.7 1.1 slice.66.node_part
  190.8 33.8 %spread_rows.3 = bf16[3,4,512,512]{3,2,1,0:T(8,128)(2,1)} custom-call(bf16[512,512]{1,0:T(8,128)(2,1)} %slice.73.own), custom_call_target="tpu_custom_call" | custom-call | tf_op jit(solution)/shard_map/spread_rows/pallas_call | solution.py:750
  224.6 3.2 all-to-all-start.1
  227.8 70.1 %edge_backward.1 = (f32[4608,512]{1,0:T(8,128)}, bf16[6144,512]{1,0:T(8,128)(2,1)}, f32[3584,512]{1,0:T(8,128)}, f32[8,512]{1,0:T(8,128)}, f32[512,512]{1,0:T(8,128)}) custom-call(s32[1]{0:T(128)S(6)} %copy.65.count, s32[4608]{0:T(1024)} %fusion.7.recv, s32[9,1,512]{2,1,0:T(1,128)} %reshape.99.send, bf16[4608,512]{1,0:T(8,128)(2,1)} %cotangent.1, ...), custom_call_target="tpu_custom_call" | custom-call | flops 28991029248 | bytes 94371840 | tf_op jit(solution)/shard_map/edge_backward/pallas_call | solution.py:369
  297.9 0.7 slice.51
  298.7 0.1 bitcast_reduce_fusion
  298.8 0.1 reshape.105
  298.9 0.6 concatenate.7.vectors
  299.5 94.5 %finish_sums.1 = (f32[16,16384]{1,0:T(8,128)}, bf16[3584,512]{1,0:T(8,128)(2,1)}, f32[8,512]{1,0:T(8,128)}) custom-call(bf16[3,4,512,512]{3,2,1,0:T(8,128)(2,1)} %bitcast.67, f32[3584,512]{1,0:T(8,128)} %get-tuple-element.35.grads, f32[8,512]{1,0:T(8,128)} %concatenate.7.vectors, f32[512,512]{1,0:T(8,128)} %get-tuple-element.37.node_part, ...), custom_call_target="tpu_custom_call" | custom-call | tf_op jit(solution)/shard_map/finish_sums/pallas_call | solution.py:1020
  394.1 3.7 slice.68
  397.7 0.0 copy-done.2
  397.7 1.6 slice.70
  399.3 0.6 fusion.15
  399.9 1.6 fusion.14
  401.5 0.0 all-to-all-done.1
  401.6 0.1 convert_bitcast_fusion
  401.7 0.1 copy.59
  401.8 1.1 add.93
  402.9 1.0 copy.66
  (29 shorter events, 0.1 us)
Async XLA Ops:
  0.6 179.0 %copy-start = (bf16[1024,512]{1,0:T(8,128)(2,1)S(1)}, bf16[1024,512]{1,0:T(8,128)(2,1)}, u32[]{:S(2)}) copy-start(bf16[1024,512]{1,0:T(8,128)(2,1)} %param.30) | copy-start | bytes 3145732
  0.7 9.6 %copy-start.11 = (s32[4608]{0:T(1024)S(1)}, s32[4608]{0:T(1024)}, u32[]{:S(2)}) copy-start(s32[4608]{0:T(1024)} %param.21) | copy-start | bytes 55300
  0.7 10.9 %copy-start.3 = (f32[16,16384]{1,0:T(8,128)S(1)}, f32[16,16384]{1,0:T(8,128)}, u32[]{:S(2)}) copy-start(f32[16,16384]{1,0:T(8,128)} %residual.1) | copy-start | bytes 3145732
  3.0 22.9 %all-to-all-start = ((bf16[16,32,512]{2,0,1:T(8,128)(2,1)}), bf16[16,32,512]{2,0,1:T(8,128)(2,1)S(1)}, u32[]{:S(2)}, u32[]{:S(2)}) async-start(bf16[16,32,512]{2,0,1:T(8,128)(2,1)} %bitcast.66), calls=%async_computation | async-start | bytes 1048576 | tf_op jit(solution)/shard_map/all_to_all | solution.py:43
  11.6 6.1 %copy-start.12 = (s32[4608]{0:T(1024)S(1)}, s32[4608]{0:T(1024)}, u32[]{:S(2)}) copy-start(s32[4608]{0:T(1024)} %param.22) | copy-start | bytes 55300
  14.4 11.4 %copy-start.5 = (bf16[1536,512]{0,1:T(8,128)(2,1)}, bf16[1536,512]{0,1:T(8,128)(2,1)S(1)}, u32[]{:S(2)}) copy-start(bf16[1536,512]{0,1:T(8,128)(2,1)S(1)} %copy.55) | copy-start | bytes 4718596
  25.8 155.5 %all-to-all-start.2 = ((f32[16,32,512]{2,0,1:T(8,128)}), f32[16,32,512]{2,0,1:T(8,128)S(1)}, u32[]{:S(2)}, u32[]{:S(2)}) async-start(f32[16,32,512]{2,0,1:T(8,128)} %bitcast.65), calls=%async_computation.2 | async-start | bytes 2097152 | tf_op jit(solution)/shard_map/all_to_all | solution.py:43
  131.0 48.6 %copy-start.6 = (bf16[512,512]{0,1:T(8,128)(2,1)S(1)}, bf16[512,512]{0,1:T(8,128)(2,1)}, u32[]{:S(2)}) copy-start(bf16[512,512]{0,1:T(8,128)(2,1)} %copy.52) | copy-start | bytes 1572868
  131.0 48.6 %copy-start.18 = (f32[512]{0:T(512)S(1)}, f32[512]{0:T(512)}, u32[]{:S(2)}) copy-start(f32[512]{0:T(512)} %param.31) | copy-start | bytes 6148
  178.2 2.1 copy-start.16
  178.2 2.1 copy-start.19
  179.6 1.4 copy-start.9
  180.4 1.0 copy-start.20
  180.4 1.0 copy-start.13
  180.4 1.7 copy-start.15
  181.4 2.0 copy-start.21
  182.1 2.8 copy-start.17
  184.9 1.0 copy-start.7
  184.9 1.2 copy-start.10
  224.6 177.0 %all-to-all-start.1 = ((bf16[32,16,512]{2,1,0:T(8,128)(2,1)}), bf16[32,16,512]{2,1,0:T(8,128)(2,1)S(1)}, u32[]{:S(2)}, u32[]{:S(2)}) async-start(bf16[32,16,512]{2,1,0:T(8,128)(2,1)} %bitcast.10), calls=%async_computation.1 | async-start | bytes 1048576 | tf_op jit(solution)/shard_map/all_to_all | solution.py:47
  394.0 3.7 copy-start.2
  397.7 1.6 copy-start.14
  399.9 1.8 copy-start.4
  401.6 1.3 copy-start.8
  401.6 2.3 copy-start.1

commit v7 on v6

--- a/solution.py
+++ b/solution.py
@@ -1041,6 +1041,134 @@
     )(sums.reshape(3, 4, rows, width), grads, vectors, node_part, weight, residual)
 
 
+def scatter_scratch(channels, nodes, devices):
+    slab = channels * (nodes // LANES)
+    return [
+        pltpu.VMEM((devices * slab, LANES), WIDE),
+        pltpu.VMEM((devices * slab, LANES), LOW),
+        pltpu.VMEM((devices, slab, LANES), LOW),
+        pltpu.VMEM((slab, LANES), WIDE),
+        pltpu.VMEM((nodes // LANES * devices * channels, LANES), WIDE),
+        pltpu.SemaphoreType.DMA((devices - 1,)),
+        pltpu.SemaphoreType.DMA((devices - 1,)),
+    ]
+
+
+def scatter_moves(shard, refs):
+    flat, packed, landed, opened, square, send_sems, recv_sems = refs
+    subs = lax.axis_size("sub")
+    devices = lax.axis_size("blk") * subs
+    here = lax.axis_index("blk") * subs + lax.axis_index("sub")
+    slab = landed.shape[1]
+    channels = shard.shape[0]
+    parts = slab // channels
+    nodes = parts * LANES
+
+    def move(k):
+        there = lax.rem(here + k, devices)
+        return remote(
+            packed.at[pl.ds(pl.multiple_of(there * slab, slab), slab)], landed.at[here],
+            send_sems.at[k - 1], recv_sems.at[k - 1], (there // subs, lax.rem(there, subs)),
+        )
+
+    def start():
+        def pack(k, carry):
+            device = lax.rem(here + k, devices)
+            rows = pl.ds(pl.multiple_of(device * slab, slab), slab)
+            for j in range(parts):
+                columns = pl.ds(pl.multiple_of(device * nodes + j * LANES, LANES), LANES)
+                flat[pl.ds(device * slab + j, channels, stride=parts), :] = shard[:, columns]
+            packed[rows, :] = flat[rows, :].astype(LOW)
+            return carry
+
+        def send(k, carry):
+            pack(k, carry)
+            move(k).start()
+            return carry
+
+        lax.fori_loop(1, devices, send, 0)
+        pack(0, 0)
+
+    def open_slab(source, device):
+        opened[...] = source.astype(WIDE)
+        for j in range(parts):
+            rows = pl.ds(pl.multiple_of((j * devices + device) * channels, channels), channels)
+            square[rows, :] = opened[pl.ds(j, channels, stride=parts), :]
+
+    def last(rows):
+        open_slab(packed[pl.ds(pl.multiple_of(here * slab, slab), slab), :], here)
+
+        def take(k, carry):
+            move(k).wait_recv()
+            device = lax.rem(here - k + devices, devices)
+            open_slab(landed[device], device)
+            return carry
+
+        lax.fori_loop(1, devices, take, 0)
+        width = devices * channels
+        for j in range(parts):
+            rows[j * LANES : (j + 1) * LANES, :] = square[j * width : (j + 1) * width, :].T.astype(LOW)
+
+    def drain():
+        def sent(k, carry):
+            move(k).wait_send()
+            return carry
+
+        lax.fori_loop(1, devices, sent, 0)
+
+    return start, last, drain
+
+
+def begin_kernel(shard, later, own, table, later_out, held, held_sem, *refs):
+    at = places()
+    fetch = pltpu.make_async_copy(later, held, held_sem)
+    fetch.start()
+    meet_all()
+    start, last, drain = scatter_moves(shard, refs[3:])
+    start()
+    last(own)
+    begin, one, two, three, end = spread_moves(at, own, table, *refs[:3])
+    begin()
+    fetch.wait()
+    give = pltpu.make_async_copy(held, later_out, held_sem)
+    give.start()
+    drain()
+    for stage in (one, two, three):
+        for piece in range(PIECES):
+            stage(piece)
+    give.wait()
+    end()
+
+
+def begin(shard, later, rows, collective):
+    channels, nodes = shard.shape
+    devices = lax.axis_size("blk") * lax.axis_size("sub")
+    width = channels * devices
+    hold = pl.BlockSpec(memory_space=pltpu.VMEM)
+    across = pl.BlockSpec(memory_space=pl.ANY)
+    own, table, later = pl.pallas_call(
+        begin_kernel,
+        in_specs=[hold, across],
+        out_specs=[hold, across, across],
+        out_shape=[
+            jax.ShapeDtypeStruct((rows, width), LOW),
+            jax.ShapeDtypeStruct((3, 4, rows, width), LOW),
+            jax.ShapeDtypeStruct(later.shape, later.dtype),
+        ],
+        scratch_shapes=[
+            pltpu.VMEM(later.shape, later.dtype),
+            pltpu.SemaphoreType.DMA,
+            *spread_scratch(),
+            *scatter_scratch(channels, rows, devices),
+        ],
+        compiler_params=pltpu.CompilerParams(
+            collective_id=collective, has_side_effects=True, vmem_limit_bytes=VMEM_BYTES
+        ),
+        name="begin_rows",
+    )(shard, later)
+    return own, table.reshape(12 * rows, width), later
+
+
 def shards(
     node_input,
     edge_input,
@@ -1067,15 +1195,14 @@
     block_index = lax.axis_index("blk")
     sub_index = lax.axis_index("sub")
     width = edge_input.shape[1]
-    node_low = to_nodes(node_input.astype(jnp.bfloat16)).T
-    node_upstream = to_nodes(node_cotangent).T
-    per_device = node_low.shape[0]
+    per_device = node_input.shape[1] // (groups * sub_count)
+    node_low, wide_low, cotangent_later = begin(node_input, node_cotangent, per_device, 0)
+    node_upstream = to_nodes(cotangent_later).T
     per_group = per_device * sub_count
     my_start = (block_index * sub_count + sub_index) * per_device
     send_local = senders - my_start
     relative = (receivers // per_group - block_index + 1 + groups) % groups
     recv_wide = relative * per_group + receivers % per_group
-    wide_low = spread(node_low, 0)
     edge_result, first_pre, second_pre, received, wide_sums = edge_forward(
         edge_count, recv_wide, send_local, edge_input, wide_low, node_low,
         edge_w_one, edge_b_one[None], edge_w_two, edge_b_two[None], edge_gain[None], edge_shift[None],

time: 405 us -> 397 us (0.980)
  Pallas kernels: 347 us -> 356 us
  starting transfers between devices: 13.6 us -> 5.61 us
  waiting for transfers between devices: 7.51 us -> 0.01 us
    pallas_call x0 -> x1, Pallas kernels: none -> 55.6 us  [begin(): pl.pallas_call(begin_kernel, in_specs=[hold, across], out_specs=[hold, ac...]
    pallas_call x2 -> x1, Pallas kernels: 79 us -> 36.2 us  [spread(): pl.pallas_call(spread_kernel, in_specs=[pl.BlockSpec(memory_space=pltpu.V...]
    all_to_all x2 -> x1, starting transfers between devices: 10.4 us -> 2.65 us  [to_nodes(): lax.all_to_all(channels, ('blk', 'sub'), split_axis=1, concat_axis=0, til...]
    all_to_all x2 -> x1, waiting for transfers between devices: 7.51 us -> 0.01 us  [to_nodes(): lax.all_to_all(channels, ('blk', 'sub'), split_axis=1, concat_axis=0, til...]
  transfers between devices with their start and end apart: 3 -> 2, of which waited for: 1 -> 0; matrix products, arithmetic and copies ran while one was open for 5% -> 5% of each run, Pallas kernels for 77% -> 67%
where the time goes in v7:
time: 397 us; the launch traced here: 396 us
  Pallas kernels  356 us (90%)
  local copies, waits for them, and re-layouts  21.4 us (5%)
  matrix products  6.3 us (2%)
  starting transfers between devices  5.61 us (1%)
  other arithmetic  5.3 us (1%)
    pallas_call x1, Pallas kernels, finish(): pl.pallas_call(functools.partial(finish_kernel, cut), in_specs=[across, a...  94.5 us
    pallas_call x1, Pallas kernels, edge_backward(): pl.pallas_call(backward_kernel, grid=(steps,), in_specs=[scalar, scalar,...  70.1 us
    pallas_call x1, Pallas kernels, edge_forward(): pl.pallas_call(forward_kernel, grid=(steps,), in_specs=[scalar, scalar, p...  55.8 us
    pallas_call x1, Pallas kernels, begin(): pl.pallas_call(begin_kernel, in_specs=[hold, across], out_specs=[hold, ac...  55.6 us
    pallas_call x1, Pallas kernels, collect(): pl.pallas_call(collect_kernel, in_specs=[pl.BlockSpec(memory_space=pl.ANY...  43.9 us
    pallas_call x1, Pallas kernels, spread(): pl.pallas_call(spread_kernel, in_specs=[pl.BlockSpec(memory_space=pltpu.V...  36.2 us
  transfers between devices with their start and end apart: 2, of which 0 were waited for; matrix products, arithmetic and copies ran while one was open for 5% of the time, Pallas kernels for 67%

profile of v7, /device:TPU:0, one launch (start us, length us, event | category | flops | bytes accessed | tf_op | source)
XLA Modules:
  0.0 396.3 jit_solution(13792903227449661080)
XLA Ops:
  0.6 0.0 copy-start
  0.7 0.0 copy-start.8
  0.7 0.0 copy-start.9
  0.7 55.6 %begin_rows.1 = (bf16[512,512]{1,0:T(8,128)(2,1)}, bf16[3,4,512,512]{3,2,1,0:T(8,128)(2,1)}, f32[16,16384]{1,0:T(8,128)}) custom-call(f32[16,16384]{1,0:T(8,128)} %shard.1, f32[16,16384]{1,0:T(8,128)} %residual.1), custom_call_target="tpu_custom_call" | custom-call | tf_op jit(solution)/shard_map/begin_rows/pallas_call | solution.py:1149
  56.3 0.0 copy-start.7
  56.4 2.3 copy.53
  58.7 2.6 all-to-all-start.1
  61.4 0.0 copy-done.8
  61.4 0.6 reshape.96.send
  62.0 0.0 copy-done.9
  62.0 0.6 fusion.7.recv
  63.3 2.6 copy.45
  65.9 0.0 copy-done.7
  65.9 1.0 copy.46
  66.9 55.8 %edge_forward.1 = (f32[4608,512]{1,0:T(8,128)}, f32[4608,512]{1,0:T(8,128)}, f32[4608,512]{1,0:T(8,128)}, bf16[4608,512]{1,0:T(8,128)(2,1)}, bf16[6144,512]{1,0:T(8,128)(2,1)}) custom-call(s32[1]{0:T(128)S(6)} %copy.55.count, s32[4608]{0:T(1024)} %fusion.7.recv, s32[9,1,512]{2,1,0:T(1,128)} %reshape.96.send, bf16[4608,512]{1,0:T(8,128)(2,1)} %edge.3, ...), custom_call_target="tpu_custom_call" | custom-call | flops 24159191040 | bytes 94371840 | tf_op jit(solution)/shard_map/edge_forward/pallas_call | solution.py:250
  122.7 0.0 copy-start.17
  122.7 43.9 %collect_sums.1 = f32[512,512]{1,0:T(8,128)} custom-call(bf16[3,4,512,512]{3,2,1,0:T(8,128)(2,1)} %bitcast.60), custom_call_target="tpu_custom_call" | custom-call | tf_op jit(solution)/shard_map/collect_sums/pallas_call | solution.py:882
  166.6 0.0 copy-start.13
  166.6 0.0 copy-start.18
  166.6 1.3 convert_element_type.34
  167.9 0.0 copy-start.5
  167.9 2.1 slice.67.weight
  170.0 0.0 copy-done.15
  170.0 0.7 convolution_add_fusion.1
  170.8 0.0 copy-done.13
  170.8 0.0 copy-done.18
  170.8 0.0 copy-start.19
  170.8 0.0 copy-start.10
  170.8 0.0 copy-start.12
  170.8 0.6 fusion.16
  171.4 0.3 copy-done.19
  171.8 0.0 all-to-all-done.1
  171.8 0.0 copy-start.20
  171.8 0.2 multiply_reduce_fusion
  172.0 0.5 fusion.1
  172.5 0.0 copy-start.14
  172.5 1.3 convert_reduce_fusion
  173.8 1.5 fusion.13.node_two
  175.3 0.7 convert_reduce_fusion.1
  176.0 0.3 copy-done.6
  176.3 0.2 copy-done.16
  176.5 2.1 fusion.2.node_one
  178.5 0.7 fusion.17
  179.3 0.9 slice.73.own
  180.1 1.1 slice.66.node_part
  181.2 36.2 %spread_rows.1 = bf16[3,4,512,512]{3,2,1,0:T(8,128)(2,1)} custom-call(bf16[512,512]{1,0:T(8,128)(2,1)} %slice.73.own), custom_call_target="tpu_custom_call" | custom-call | tf_op jit(solution)/shard_map/spread_rows/pallas_call | solution.py:750
  217.4 3.0 all-to-all-start
  220.4 70.1 %edge_backward.1 = (f32[4608,512]{1,0:T(8,128)}, bf16[6144,512]{1,0:T(8,128)(2,1)}, f32[3584,512]{1,0:T(8,128)}, f32[8,512]{1,0:T(8,128)}, f32[512,512]{1,0:T(8,128)}) custom-call(s32[1]{0:T(128)S(6)} %copy.55.count, s32[4608]{0:T(1024)} %fusion.7.recv, s32[9,1,512]{2,1,0:T(1,128)} %reshape.96.send, bf16[4608,512]{1,0:T(8,128)(2,1)} %cotangent.1, ...), custom_call_target="tpu_custom_call" | custom-call | flops 28991029248 | bytes 94371840 | tf_op jit(solution)/shard_map/edge_backward/pallas_call | solution.py:369
  290.5 0.7 slice.51
  291.2 0.1 bitcast_reduce_fusion
  291.3 0.1 reshape.102
  291.4 0.6 concatenate.7.vectors
  292.1 94.5 %finish_sums.1 = (f32[16,16384]{1,0:T(8,128)}, bf16[3584,512]{1,0:T(8,128)(2,1)}, f32[8,512]{1,0:T(8,128)}) custom-call(bf16[3,4,512,512]{3,2,1,0:T(8,128)(2,1)} %bitcast.59, f32[3584,512]{1,0:T(8,128)} %get-tuple-element.41.grads, f32[8,512]{1,0:T(8,128)} %concatenate.7.vectors, f32[512,512]{1,0:T(8,128)} %get-tuple-element.43.node_part, ...), custom_call_target="tpu_custom_call" | custom-call | tf_op jit(solution)/shard_map/finish_sums/pallas_call | solution.py:1020
  386.5 3.7 slice.68
  390.2 1.6 slice.70
  391.8 0.6 fusion.15
  392.4 1.6 fusion.14
  394.0 0.0 all-to-all-done
  394.0 0.1 convert_bitcast_fusion
  394.2 0.1 copy.51
  394.3 0.0 copy-done.3
  394.3 1.1 add.93
  395.3 1.0 copy.56
  396.3 0.0 copy-done.1
  (22 shorter events, 0.1 us)
Async XLA Ops:
  0.6 169.4 %copy-start = (bf16[1024,512]{1,0:T(8,128)(2,1)S(1)}, bf16[1024,512]{1,0:T(8,128)(2,1)}, u32[]{:S(2)}) copy-start(bf16[1024,512]{1,0:T(8,128)(2,1)} %param.30) | copy-start | bytes 3145732
  0.7 60.7 %copy-start.8 = (s32[4608]{0:T(1024)S(1)}, s32[4608]{0:T(1024)}, u32[]{:S(2)}) copy-start(s32[4608]{0:T(1024)} %param.21) | copy-start | bytes 55300
  0.7 61.3 %copy-start.9 = (s32[4608]{0:T(1024)S(1)}, s32[4608]{0:T(1024)}, u32[]{:S(2)}) copy-start(s32[4608]{0:T(1024)} %param.22) | copy-start | bytes 55300
  56.3 9.5 %copy-start.7 = (bf16[512,512]{1,0:T(8,128)(2,1)S(1)}, bf16[512,512]{1,0:T(8,128)(2,1)}, u32[]{:S(2)}) copy-start(bf16[512,512]{1,0:T(8,128)(2,1)} %w_two.1) | copy-start | bytes 1572868
  58.7 113.1 %all-to-all-start.1 = ((f32[16,32,512]{2,0,1:T(8,128)}), f32[16,32,512]{2,0,1:T(8,128)S(1)}, u32[]{:S(2)}, u32[]{:S(2)}) async-start(f32[16,32,512]{2,0,1:T(8,128)} %bitcast.58), calls=%async_computation.1 | async-start | bytes 2097152 | tf_op jit(solution)/shard_map/all_to_all | solution.py:43
  122.6 47.4 %copy-start.15 = (bf16[512,512]{1,0:T(8,128)(2,1)S(1)}, bf16[512,512]{1,0:T(8,128)(2,1)}, u32[]{:S(2)}) copy-start(bf16[512,512]{1,0:T(8,128)(2,1)} %get-tuple-element.32.nodes) | copy-start | bytes 1572868
  122.7 47.4 %copy-start.17 = (f32[512]{0:T(512)S(1)}, f32[512]{0:T(512)}, u32[]{:S(2)}) copy-start(f32[512]{0:T(512)} %param.31) | copy-start | bytes 6148
  166.6 4.2 %copy-start.13 = (bf16[512,512]{1,0:T(8,128)(2,1)S(1)}, bf16[512,512]{1,0:T(8,128)(2,1)}, u32[]{:S(2)}) copy-start(bf16[512,512]{1,0:T(8,128)(2,1)} %param.32) | copy-start | bytes 1572868
  166.6 4.2 %copy-start.18 = (f32[512]{0:T(512)S(1)}, f32[512]{0:T(512)}, u32[]{:S(2)}) copy-start(f32[512]{0:T(512)} %param.33) | copy-start | bytes 6148
  167.9 3.5 copy-start.5
  170.8 1.0 copy-start.19
  170.8 1.0 copy-start.10
  170.8 1.7 copy-start.12
  171.8 2.0 copy-start.20
  172.5 2.8 copy-start.14
  175.3 1.0 copy-start.6
  175.3 1.2 copy-start.16
  217.4 176.6 %all-to-all-start = ((bf16[32,16,512]{2,1,0:T(8,128)(2,1)}), bf16[32,16,512]{2,1,0:T(8,128)(2,1)S(1)}, u32[]{:S(2)}, u32[]{:S(2)}) async-start(bf16[32,16,512]{2,1,0:T(8,128)(2,1)} %bitcast.7), calls=%async_computation | async-start | bytes 1048576 | tf_op jit(solution)/shard_map/all_to_all | solution.py:47
  386.5 3.7 copy-start.2
  390.2 1.6 copy-start.11
  392.4 1.8 copy-start.3
  394.0 1.3 copy-start.4
  394.0 2.3 copy-start.1

commit v8 on v7

--- a/solution.py
+++ b/solution.py
@@ -65,6 +65,12 @@
     )
 
 
+def dot_right(left, right):
+    return lax.dot_general(
+        left, right, (((1,), (1,)), ((), ())), preferred_element_type=jnp.float32
+    )
+
+
 def split_low(values):
     high = values.astype(jnp.bfloat16)
     return high, (values - high.astype(jnp.float32)).astype(jnp.bfloat16)
@@ -108,42 +114,6 @@
         return lax.fori_loop(0, CHUNK // 64, piece, carry)
 
     lax.fori_loop(0, steps, body, 0)
-
-
-def store_table(table, wide, stage, sems):
-    steps = wide.shape[0] // CHUNK
-    parts = wide.shape[1] // LANES
-
-    def send(i, slot):
-        return pltpu.make_async_copy(stage.at[slot], wide.at[pl.ds(i * CHUNK, CHUNK)], sems.at[slot])
-
-    def body(i, carry):
-        slot = lax.rem(i, 2)
-
-        @pl.when(i >= 2)
-        def _():
-            send(i - 2, slot).wait()
-
-        def piece(k, carry):
-            values = read_rows(table, i * CHUNK + k * 64, 64, parts)
-            stage[slot, pl.ds(k * 64, 64), :] = values.astype(jnp.bfloat16)
-            return carry
-
-        lax.fori_loop(0, CHUNK // 64, piece, 0)
-        send(i, slot).start()
-        return carry
-
-    lax.fori_loop(0, steps, body, 0)
-    for i in (steps - 2, steps - 1):
-        send(i, i % 2).wait()
-
-
-def clear(table):
-    def body(i, carry):
-        table[pl.ds(i * 512, 512), :] = jnp.zeros((512, LANES), table.dtype)
-        return carry
-
-    lax.fori_loop(0, table.shape[0] // 512, body, 0)
 
 
 def gather_rows(index, base, table, rows, parts):
@@ -161,26 +131,6 @@
     lax.fori_loop(0, count // 16, body, 0)
 
 
-def add_rows(index, base, rows, table, parts):
-    count = rows.shape[0] // parts
-
-    def body(i, carry):
-        for u in range(0, 16, 2):
-            slot = i * 16 + u
-            one, two = index[base + slot], index[base + slot + 1]
-            at_one = pl.ds(pl.multiple_of(one * parts, parts), parts)
-            at_two = pl.ds(pl.multiple_of(two * parts, parts), parts)
-            held_one, held_two = table[at_one, :], table[at_two, :]
-            sum_one = held_one + rows[pl.ds(pl.multiple_of(slot * parts, parts), parts), :]
-            held_two = jnp.where(one == two, sum_one, held_two)
-            sum_two = held_two + rows[pl.ds(pl.multiple_of((slot + 1) * parts, parts), parts), :]
-            table[at_one, :] = sum_one
-            table[at_two, :] = sum_two
-        return carry
-
-    lax.fori_loop(0, count // 16, body, 0)
-
-
 def row_normal(values):
     average = jnp.mean(values, -1, keepdims=True)
     centred = values - average
@@ -191,8 +141,8 @@
 
 def forward_kernel(
     count, recv, send, edge, wide, nodes, w_one, b_one, w_two, b_two, gain, shift,
-    result, first, second, received, sums,
-    table, total, rows, stage, sems,
+    result, first, second, received, message,
+    table, rows, stage, sems,
 ):
     step = pl.program_id(0)
     base = step * TILE
@@ -202,20 +152,24 @@
     @pl.when(step == 0)
     def _():
         load_table(wide, table, stage, sems)
-        clear(total)
 
     gather_rows(recv, base, table, rows, parts)
     from_recv = read_rows(rows, 0, TILE, parts).astype(jnp.bfloat16)
     received[...] = from_recv
-    column = jnp.broadcast_to(send[0], (LANES, TILE)).T
-    lane = lax.broadcasted_iota(jnp.int32, (TILE, LANES), 1)
-    chosen = jnp.concatenate(
-        [
-            jnp.where(column == lane + j * LANES, 1.0, 0.0).astype(jnp.bfloat16)
-            for j in range(nodes.shape[0] // LANES)
-        ],
-        axis=1,
-    )
+    lane = lax.broadcasted_iota(jnp.int32, (LANES, LANES), 1)
+    chosen = []
+    for i in range(TILE // LANES):
+        column = jnp.broadcast_to(send[pl.ds(step * (TILE // LANES) + i, 1), :], (LANES, LANES)).T
+        chosen.append(
+            jnp.concatenate(
+                [
+                    jnp.where(column == lane + j * LANES, 1.0, 0.0).astype(jnp.bfloat16)
+                    for j in range(nodes.shape[0] // LANES)
+                ],
+                axis=1,
+            )
+        )
+    chosen = jnp.concatenate(chosen, axis=0)
     from_send = dot(chosen, nodes[...]).astype(jnp.bfloat16)
     pre = (
         dot(edge[...], w_one[:width])
@@ -232,12 +186,7 @@
     live = base + lax.broadcasted_iota(jnp.int32, (TILE, 1), 0) < count[0]
     outcome = edge[...].astype(jnp.float32) + jnp.where(live, branch, 0.0)
     result[...] = outcome
-    lay_rows(rows, 0, jnp.where(live, outcome, 0.0))
-    add_rows(recv, base, rows, total, parts)
-
-    @pl.when(step == pl.num_programs(0) - 1)
-    def _():
-        store_table(total, sums, stage, sems)
+    message[...] = jnp.where(live, outcome, 0.0).astype(jnp.bfloat16)
 
 
 def edge_forward(count, recv, send, edge, wide, nodes, w_one, b_one, w_two, b_two, gain, shift):
@@ -251,19 +200,18 @@
         forward_kernel,
         grid=(steps,),
         in_specs=[
-            scalar, scalar, pl.BlockSpec((1, 1, TILE), lambda i: (i, 0, 0)), tile,
+            scalar, scalar, hold, tile,
             pl.BlockSpec(memory_space=pl.ANY), hold, hold, hold, hold, hold, hold, hold,
         ],
-        out_specs=[tile, tile, tile, tile, pl.BlockSpec(memory_space=pl.ANY)],
+        out_specs=[tile] * 5,
         out_shape=[
             jax.ShapeDtypeStruct((edges, width), jnp.float32),
             jax.ShapeDtypeStruct((edges, width), jnp.float32),
             jax.ShapeDtypeStruct((edges, width), jnp.float32),
             jax.ShapeDtypeStruct((edges, width), jnp.bfloat16),
-            jax.ShapeDtypeStruct(wide.shape, jnp.bfloat16),
+            jax.ShapeDtypeStruct((edges, width), jnp.bfloat16),
         ],
         scratch_shapes=[
-            pltpu.VMEM((wide.shape[0] * parts, LANES), jnp.float32),
             pltpu.VMEM((wide.shape[0] * parts, LANES), jnp.float32),
             pltpu.VMEM((TILE * parts, LANES), jnp.float32),
             pltpu.VMEM((2, CHUNK, width), jnp.bfloat16),
@@ -274,13 +222,13 @@
             flops=20 * edges * width * width, bytes_accessed=40 * edges * width, transcendentals=2 * edges * width
         ),
         name="edge_forward",
-    )(count, recv, send.reshape(steps, 1, TILE), edge, wide, nodes, w_one, b_one, w_two, b_two, gain, shift)
+    )(count, recv, send, edge, wide, nodes, w_one, b_one, w_two, b_two, gain, shift)
 
 
 def backward_kernel(
-    count, recv, send, cotangent, edge, received, first, second, wide, node_one, node_two, node_part, nodes, w_one_t, w_two_t, gain,
-    grad, sums, all_grads, vectors, sender_grad,
-    table, total, rows, stage, sems, by_sender, grads, pass_sems,
+    count, recv, send, cotangent, edge, received, first, second, wide, node_one, node_two, node_part, nodes, w_one, w_two, gain,
+    grad, message, all_grads, vectors, sender_grad,
+    table, rows, stage, sems, by_sender, grads, pass_sems,
 ):
     step = pl.program_id(0)
     base = step * TILE
@@ -299,7 +247,6 @@
         passed[0].start()
         passed[1].start()
         load_table(wide, table, stage, sems)
-        clear(total)
         grads[: 4 * width] = jnp.zeros((4 * width, width), grads.dtype)
         vectors[...] = jnp.zeros_like(vectors)
         by_sender[...] = jnp.zeros_like(by_sender)
@@ -320,18 +267,22 @@
     logistic = jax.nn.sigmoid(pre)
     act = (pre * logistic).astype(jnp.bfloat16)
     grads[3 * width : 4 * width] += dot_left(act, second_low)
-    grad_first = dot(second_low, w_two_t[...]) * (logistic * (1.0 + pre * (1.0 - logistic)))
+    grad_first = dot_right(second_low, w_two[...]) * (logistic * (1.0 + pre * (1.0 - logistic)))
     first_low = grad_first.astype(jnp.bfloat16)
-    first_wide = first_low.astype(jnp.float32)
-    vectors[0:1, :] += jnp.sum(first_wide, 0, keepdims=True)
+    message[...] = first_low
+    vectors[0:1, :] += jnp.sum(first_low.astype(jnp.float32), 0, keepdims=True)
     grads[:width] += dot_left(edge[...], first_low)
     grads[2 * width : 3 * width] += dot_left(received[...], first_low)
-    node = lax.broadcasted_iota(jnp.int32, (nodes.shape[0], TILE), 0)
-    chosen = jnp.where(node == send[0], 1.0, 0.0).astype(jnp.bfloat16)
+    node = lax.broadcasted_iota(jnp.int32, (nodes.shape[0], LANES), 0)
+    chosen = jnp.concatenate(
+        [
+            jnp.where(node == send[pl.ds(step * (TILE // LANES) + i, 1), :], 1.0, 0.0).astype(jnp.bfloat16)
+            for i in range(TILE // LANES)
+        ],
+        axis=1,
+    )
     by_sender[...] += dot(chosen, first_low)
-    grad[...] = upstream + dot(first_low, w_one_t[:, :width])
-    lay_rows(rows, 0, first_wide)
-    add_rows(recv, base, rows, total, parts)
+    grad[...] = upstream + dot_right(first_low, w_one[:width])
 
     @pl.when(step == pl.num_programs(0) - 1)
     def _():
@@ -340,15 +291,14 @@
         passed[0].wait()
         passed[1].wait()
         passed[2].start()
-        middle = w_one_t[:, width : 2 * width]
-        sender_grad[...] = node_part[...] + dot(high, middle) + dot(rest, middle)
-        store_table(total, sums, stage, sems)
+        middle = w_one[width : 2 * width]
+        sender_grad[...] = node_part[...] + dot_right(high, middle) + dot_right(rest, middle)
         passed[2].wait()
 
 
 def edge_backward(
     count, recv, send, cotangent, edge, received, first, second, wide, node_one, node_two, node_part, nodes,
-    w_one_t, w_two_t, gain,
+    w_one, w_two, gain,
 ):
     edges, width = edge.shape
     steps = edges // TILE
@@ -370,21 +320,20 @@
         backward_kernel,
         grid=(steps,),
         in_specs=[
-            scalar, scalar, pl.BlockSpec((1, 1, TILE), lambda i: (i, 0, 0)), tile, tile, tile, tile, tile,
+            scalar, scalar, hold, tile, tile, tile, tile, tile,
             across, across, across, hold, hold, hold, hold, hold,
         ],
         out_specs=[
-            tile, across, across, whole(8), whole(per_device),
+            tile, tile, across, whole(8), whole(per_device),
         ],
         out_shape=[
             jax.ShapeDtypeStruct((edges, width), jnp.float32),
-            jax.ShapeDtypeStruct(wide.shape, jnp.bfloat16),
+            jax.ShapeDtypeStruct((edges, width), jnp.bfloat16),
             jax.ShapeDtypeStruct((padded, width), jnp.float32),
             jax.ShapeDtypeStruct((8, width), jnp.float32),
             jax.ShapeDtypeStruct((per_device, width), jnp.float32),
         ],
         scratch_shapes=[
-            pltpu.VMEM((wide.shape[0] * parts, LANES), jnp.float32),
             pltpu.VMEM((wide.shape[0] * parts, LANES), jnp.float32),
             pltpu.VMEM((TILE * parts, LANES), jnp.float32),
             pltpu.VMEM((2, CHUNK, width), jnp.bfloat16),
@@ -399,8 +348,8 @@
         ),
         name="edge_backward",
     )(
-        count, recv, send.reshape(steps, 1, TILE), cotangent, edge, received, first, second, wide, node_one, node_two,
-        node_part, nodes, w_one_t, w_two_t, gain,
+        count, recv, send, cotangent, edge, received, first, second, wide, node_one, node_two,
+        node_part, nodes, w_one, w_two, gain,
     )
 
 
@@ -758,48 +707,51 @@
     )(own).reshape(12 * rows, width)
 
 
-def collect_scratch(rows, width):
+HALVES = 2
+ORDER = (
+    (0, 1, 0), (0, 1, 1), (1, 1, 0), (0, 0, 0), (1, 1, 1), (0, 0, 1),
+    (1, 0, 0), (2, 1, 0), (1, 0, 1), (2, 1, 1), (2, 0, 0), (2, 0, 1),
+)
+
+
+def collect_scratch(rows, width, edges):
     return [
-        pltpu.VMEM((3, 2, rows, width), LOW),
-        pltpu.VMEM((3, 2, rows, width), LOW),
+        pltpu.VMEM((edges, width), LOW),
+        pltpu.VMEM((2, 3, 2, rows, width), WIDE),
+        pltpu.VMEM((3, 2, rows, width), WIDE),
         pltpu.VMEM((2, rows, width), LOW),
         pltpu.VMEM((2, rows, width), LOW),
         pltpu.VMEM((2, rows, width), LOW),
         pltpu.VMEM((2, rows, width), LOW),
         pltpu.VMEM((rows, width), LOW),
         pltpu.VMEM((rows, width), LOW),
-        pltpu.SemaphoreType.DMA((3, 2, PIECES)),
-        pltpu.SemaphoreType.DMA((3, 2, PIECES)),
-        pltpu.SemaphoreType.DMA((3, 2, PIECES)),
+        pltpu.SemaphoreType.DMA,
+        pltpu.SemaphoreType.DMA((3, 2, HALVES)),
+        pltpu.SemaphoreType.DMA((3, 2, HALVES)),
         pltpu.SemaphoreType.DMA((5, PIECES)),
         pltpu.SemaphoreType.DMA((5, PIECES)),
     ]
 
 
-def collect_moves(at, sums, out, refs):
+def collect_moves(at, index, messages, out, refs):
     (
-        mine, landed, far_out, far_in, near_out, near_in, pair_out, pair_in,
-        keep_sems, give_sems, take_sems, send_sems, recv_sems,
+        held, parts, landed, far_out, far_in, near_out, near_in, pair_out, pair_in,
+        load_sem, give_sems, take_sems, send_sems, recv_sems,
     ) = refs
     sub, partner, sibling = at["sub"], at["partner"], at["sibling"]
-    relations = (at["far"], at["near"], 1)
-    size = out.shape[0] // PIECES
-
-    def part(ref, piece):
+    rows = out.shape[0]
+    size = rows // PIECES
+    part_rows = rows // HALVES
+    load = pltpu.make_async_copy(messages, held, load_sem)
+
+    def piece_of(ref, piece):
         return ref.at[pl.ds(piece * size, size)]
 
-    def keep(role, side, piece):
-        return pltpu.make_async_copy(
-            part(sums.at[relations[role], (sub, partner)[side]], piece),
-            part(mine.at[role, side], piece),
-            keep_sems.at[role, side, piece],
-        )
-
-    def give(role, side, piece):
+    def give(role, side, half):
+        span = pl.ds(pl.multiple_of(half * part_rows, part_rows), part_rows)
         return remote(
-            part(sums.at[relations[role], (sibling, lax.rem(sibling + 2, 4))[side]], piece),
-            part(landed.at[role, side], piece),
-            give_sems.at[role, side, piece], take_sems.at[role, side, piece], at["to_sibling"],
+            parts.at[0, role, side, span], landed.at[role, side, span],
+            give_sems.at[role, side, half], take_sems.at[role, side, half], at["to_sibling"],
         )
 
     def hop(kind, piece):
@@ -811,85 +763,127 @@
             4: (pair_out, pair_in, at["to_partner"]),
         }[kind]
         return remote(
-            part(source, piece), part(target, piece), send_sems.at[kind, piece], recv_sems.at[kind, piece], device
+            piece_of(source, piece), piece_of(target, piece),
+            send_sems.at[kind, piece], recv_sems.at[kind, piece], device,
         )
 
-    order = [(role, side, piece) for role in range(3) for side in (1, 0) for piece in range(PIECES)]
+    def add_messages(step):
+        def pick(column):
+            return lax.rem(sum(int(item[column]) << (2 * i) for i, item in enumerate(ORDER)) >> (2 * step), 4)
+
+        role, side, half = pick(0), pick(1), pick(2)
+        relation = jnp.where(role == 0, at["far"], jnp.where(role == 1, at["near"], 1))
+        span = pl.ds(pl.multiple_of(half * part_rows, part_rows), part_rows)
+
+        def whose(w, carry):
+            first = jnp.where(w == 0, sibling, sub)
+            target = lax.rem(first + 2 * side, 4)
+            base = (relation * 4 + target) * rows + half * part_rows
+            node = lax.broadcasted_iota(jnp.int32, (part_rows, LANES), 0) + base
+            chosen = jnp.concatenate(
+                [jnp.where(node == index[j : j + 1, :], 1.0, 0.0).astype(LOW) for j in range(index.shape[0])], axis=1
+            )
+            parts[w, role, side, span, :] = dot(chosen, held[...])
+            return carry
+
+        lax.fori_loop(0, 2, whose, 0)
+        give(role, side, half).start()
 
     def local(role, side, piece):
-        keep(role, side, piece).wait()
-        give(role, side, piece).wait_recv()
-        rows = pl.ds(piece * size, size)
-        return mine[role, side, rows, :].astype(WIDE) + landed[role, side, rows, :].astype(WIDE)
+        span = pl.ds(piece * size, size)
+        return parts[1, role, side, span, :] + landed[role, side, span, :]
 
     def arrived(kind, ref, piece):
         hop(kind, piece).wait_recv()
         return ref[pl.ds(piece * size, size), :].astype(WIDE)
 
-    def start(role):
-        for item in order:
-            if item[0] == role:
-                give(*item).start()
-                keep(*item).start()
-
-    def far_step(side, piece):
-        far_out[side, pl.ds(piece * size, size), :] = local(0, side, piece).astype(LOW)
-        hop(side, piece).start()
-
-    def near_step(side, piece):
-        value = local(1, side, piece) + arrived(side, far_in.at[side], piece)
-        near_out[side, pl.ds(piece * size, size), :] = value.astype(LOW)
-        hop(2 + side, piece).start()
-
-    def pair_step(piece):
-        value = local(2, 1, piece) + arrived(3, near_in.at[1], piece)
-        pair_out[pl.ds(piece * size, size), :] = value.astype(LOW)
-        hop(4, piece).start()
-
-    def last_step(piece):
-        value = local(2, 0, piece) + arrived(2, near_in.at[0], piece) + arrived(4, pair_in, piece)
-        out[pl.ds(piece * size, size), :] = value
+    def pieces(half):
+        return range(half * PIECES // HALVES, (half + 1) * PIECES // HALVES)
+
+    def far_step(side, half):
+        give(0, side, half).wait_recv()
+        for piece in pieces(half):
+            far_out[side, pl.ds(piece * size, size), :] = local(0, side, piece).astype(LOW)
+            hop(side, piece).start()
+
+    def near_step(side, half):
+        give(1, side, half).wait_recv()
+        for piece in pieces(half):
+            value = local(1, side, piece) + arrived(side, far_in.at[side], piece)
+            near_out[side, pl.ds(piece * size, size), :] = value.astype(LOW)
+            hop(2 + side, piece).start()
+
+    def pair_step(half):
+        give(2, 1, half).wait_recv()
+        for piece in pieces(half):
+            value = local(2, 1, piece) + arrived(3, near_in.at[1], piece)
+            pair_out[pl.ds(piece * size, size), :] = value.astype(LOW)
+            hop(4, piece).start()
+
+    def last_step(half):
+        give(2, 0, half).wait_recv()
+        for piece in pieces(half):
+            value = local(2, 0, piece) + arrived(2, near_in.at[0], piece) + arrived(4, pair_in, piece)
+            out[pl.ds(piece * size, size), :] = value
 
     def drain():
-        for item in order:
+        for item in ORDER:
             give(*item).wait_send()
         for kind in range(5):
             for piece in range(PIECES):
                 hop(kind, piece).wait_send()
 
-    return start, far_step, near_step, pair_step, last_step, drain
-
-
-def collect_kernel(sums, out, *refs):
+    events = {
+        1: [lambda: far_step(1, 0)],
+        2: [lambda: far_step(1, 1)],
+        3: [lambda: near_step(1, 0)],
+        4: [lambda: far_step(0, 0)],
+        5: [lambda: near_step(1, 1), lambda: far_step(0, 1)],
+        7: [lambda: near_step(0, 0), lambda: pair_step(0)],
+        9: [lambda: near_step(0, 1), lambda: pair_step(1)],
+    }
+
+    def run(more):
+        def step(i, carry):
+            add_messages(i)
+            for k in sorted(set(events) | set(more)):
+                @pl.when(i == k)
+                def _():
+                    for event in events.get(k, []) + more.get(k, []):
+                        event()
+
+            return carry
+
+        lax.fori_loop(0, len(ORDER), step, 0)
+        for half in range(HALVES):
+            last_step(half)
+
+    return load, run, drain
+
+
+def collect_kernel(index, messages, out, *refs):
     at = places()
+    load, run, drain = collect_moves(at, index, messages, out, refs)
+    load.start()
     meet((at["to_sibling"], at["to_partner"], at["to_beside"], at["to_onward"]))
-    start, far_step, near_step, pair_step, last_step, drain = collect_moves(at, sums, out, refs)
-    for role in range(3):
-        start(role)
-    for step in (far_step, near_step):
-        for side in (1, 0):
-            for piece in range(PIECES):
-                step(side, piece)
-    for piece in range(PIECES):
-        pair_step(piece)
-    for piece in range(PIECES):
-        last_step(piece)
+    load.wait()
+    run({})
     drain()
 
 
-def collect(sums, rows, collective):
-    width = sums.shape[1]
+def collect(index, messages, rows, collective):
+    edges, width = messages.shape
     return pl.pallas_call(
         collect_kernel,
-        in_specs=[pl.BlockSpec(memory_space=pl.ANY)],
+        in_specs=[pl.BlockSpec(memory_space=pltpu.VMEM), pl.BlockSpec(memory_space=pl.ANY)],
         out_specs=pl.BlockSpec(memory_space=pltpu.VMEM),
         out_shape=jax.ShapeDtypeStruct((rows, width), WIDE),
-        scratch_shapes=collect_scratch(rows, width),
+        scratch_shapes=collect_scratch(rows, width, edges),
         compiler_params=pltpu.CompilerParams(
             collective_id=collective, has_side_effects=True, vmem_limit_bytes=VMEM_BYTES
         ),
         name="collect_sums",
-    )(sums.reshape(3, 4, rows, width))
+    )(index.reshape(edges // LANES, LANES), messages)
 
 
 def exchange_scratch(rows, width, devices):
@@ -962,13 +956,14 @@
 
 
 def finish_kernel(
-    cut, sums, grads, vectors, node_part, weight, residual, node_grad, reduced, reduced_vectors, total, *refs
+    cut, index, messages, grads, vectors, node_part, weight, residual, node_grad, reduced, reduced_vectors, total, *refs
 ):
     at = places()
+    sizes = len(reducer_scratch(64, 128, 2))
+    count = len(collect_scratch(64, 128, 64))
+    load, run, drain = collect_moves(at, index, messages, total, refs[:count])
+    load.start()
     meet_all()
-    sizes = len(reducer_scratch(64, 128, 2))
-    count = len(collect_scratch(64, 128))
-    start, far_step, near_step, pair_step, last_step, drain = collect_moves(at, sums, total, refs[:count])
     refs = refs[count:]
     steps = both([
         reducer(at, grads, reduced, 0, cut, False, refs[:sizes]),
@@ -977,32 +972,19 @@
     refs = refs[2 * sizes :]
     vector_steps = vector_reducer(at, vectors, reduced_vectors, refs[:4])
     exchange, receive = exchange_moves(residual, node_grad, refs[4:])
-    start(0)
     steps[0]()
     vector_steps[0]()
-    start(1)
-    start(2)
-    for side in (1, 0):
-        for piece in range(PIECES):
-            far_step(side, piece)
-    steps[1]()
-    vector_steps[1]()
-    for piece in range(PIECES):
-        near_step(1, piece)
-    steps[2]()
-    vector_steps[2]()
-    for piece in range(PIECES):
-        near_step(0, piece)
-    for piece in range(PIECES):
-        pair_step(piece)
-    steps[3]()
-    vector_steps[3]()
-    for piece in range(PIECES):
-        last_step(piece)
-    steps[4]()
+    load.wait()
+    run({
+        1: [steps[1], vector_steps[1]],
+        4: [steps[2], vector_steps[2]],
+        6: [steps[3], vector_steps[3]],
+        8: [steps[4]],
+        10: [steps[5]],
+    })
     high, rest = split_low(total[...])
-    exchange(node_part[...] + dot(high, weight[...]) + dot(rest, weight[...]))
-    for step in steps[5:8]:
+    exchange(node_part[...] + dot_right(high, weight[...]) + dot_right(rest, weight[...]))
+    for step in steps[6:8]:
         step()
     receive()
     steps[8]()
@@ -1011,15 +993,19 @@
     steps[9]()
 
 
-def finish(sums, grads, vectors, node_part, weight, residual, cut, collective):
+def finish(index, messages, grads, vectors, node_part, weight, residual, cut, collective):
     rows, width = node_part.shape
+    edges = messages.shape[0]
     along = lax.axis_size("blk") // 2
     devices = lax.axis_size("blk") * lax.axis_size("sub")
     hold = pl.BlockSpec(memory_space=pltpu.VMEM)
     across = pl.BlockSpec(memory_space=pl.ANY)
     return pl.pallas_call(
         functools.partial(finish_kernel, cut),
-        in_specs=[across, across, hold, hold, hold, hold],
+        grid=(1,),
+        in_specs=[
+            hold, across, across, hold, hold, pl.BlockSpec((width, width), lambda i: (2, 0)), hold,
+        ],
         out_specs=[hold] * 3,
         out_shape=[
             jax.ShapeDtypeStruct(residual.shape, WIDE),
@@ -1028,7 +1014,7 @@
         ],
         scratch_shapes=[
             pltpu.VMEM((rows, width), WIDE),
-            *collect_scratch(rows, width),
+            *collect_scratch(rows, width, edges),
             *reducer_scratch(cut, width, along),
             *reducer_scratch(grads.shape[0] - cut, width, along),
             *vector_scratch(vectors.shape, along),
@@ -1038,7 +1024,7 @@
             collective_id=collective, has_side_effects=True, vmem_limit_bytes=VMEM_BYTES
         ),
         name="finish_sums",
-    )(sums.reshape(3, 4, rows, width), grads, vectors, node_part, weight, residual)
+    )(index.reshape(edges // LANES, LANES), messages, grads, vectors, node_part, weight, residual)
 
 
 def scatter_scratch(channels, nodes, devices):
@@ -1119,7 +1105,9 @@
     return start, last, drain
 
 
-def begin_kernel(shard, later, own, table, later_out, held, held_sem, *refs):
+def begin_kernel(
+    shard, later, senders, receivers, own, table, later_out, send_local, recv_wide, held, held_sem, *refs
+):
     at = places()
     fetch = pltpu.make_async_copy(later, held, held_sem)
     fetch.start()
@@ -1129,6 +1117,11 @@
     last(own)
     begin, one, two, three, end = spread_moves(at, own, table, *refs[:3])
     begin()
+    rows = own.shape[0]
+    groups, subs = lax.axis_size("blk"), lax.axis_size("sub")
+    send_local[...] = senders[...] - (at["group"] * subs + at["sub"]) * rows
+    relative = lax.rem(receivers[...] // (rows * subs) - at["group"] + 1 + groups, groups)
+    recv_wide[...] = relative * (rows * subs) + lax.rem(receivers[...], rows * subs)
     fetch.wait()
     give = pltpu.make_async_copy(held, later_out, held_sem)
     give.start()
@@ -1140,20 +1133,23 @@
     end()
 
 
-def begin(shard, later, rows, collective):
+def begin(shard, later, senders, receivers, rows, collective):
     channels, nodes = shard.shape
     devices = lax.axis_size("blk") * lax.axis_size("sub")
     width = channels * devices
     hold = pl.BlockSpec(memory_space=pltpu.VMEM)
     across = pl.BlockSpec(memory_space=pl.ANY)
-    own, table, later = pl.pallas_call(
+    lines = (senders.shape[0] // LANES, LANES)
+    own, table, later, send_local, recv_wide = pl.pallas_call(
         begin_kernel,
-        in_specs=[hold, across],
-        out_specs=[hold, across, across],
+        in_specs=[hold, across, hold, hold],
+        out_specs=[hold, across, across, hold, hold],
         out_shape=[
             jax.ShapeDtypeStruct((rows, width), LOW),
             jax.ShapeDtypeStruct((3, 4, rows, width), LOW),
             jax.ShapeDtypeStruct(later.shape, later.dtype),
+            jax.ShapeDtypeStruct(lines, jnp.int32),
+            jax.ShapeDtypeStruct(lines, jnp.int32),
         ],
         scratch_shapes=[
             pltpu.VMEM(later.shape, later.dtype),
@@ -1165,8 +1161,8 @@
             collective_id=collective, has_side_effects=True, vmem_limit_bytes=VMEM_BYTES
         ),
         name="begin_rows",
-    )(shard, later)
-    return own, table.reshape(12 * rows, width), later
+    )(shard, later, senders.reshape(lines), receivers.reshape(lines))
+    return own, table.reshape(12 * rows, width), later, send_local, recv_wide
 
 
 def shards(
@@ -1192,22 +1188,18 @@
 ):
     groups = lax.axis_size("blk")
     sub_count = lax.axis_size("sub")
-    block_index = lax.axis_index("blk")
-    sub_index = lax.axis_index("sub")
     width = edge_input.shape[1]
     per_device = node_input.shape[1] // (groups * sub_count)
-    node_low, wide_low, cotangent_later = begin(node_input, node_cotangent, per_device, 0)
+    node_low, wide_low, cotangent_later, send_local, recv_wide = begin(
+        node_input, node_cotangent, senders, receivers, per_device, 0
+    )
     node_upstream = to_nodes(cotangent_later).T
-    per_group = per_device * sub_count
-    my_start = (block_index * sub_count + sub_index) * per_device
-    send_local = senders - my_start
-    relative = (receivers // per_group - block_index + 1 + groups) % groups
-    recv_wide = relative * per_group + receivers % per_group
-    edge_result, first_pre, second_pre, received, wide_sums = edge_forward(
-        edge_count, recv_wide, send_local, edge_input, wide_low, node_low,
+    recv_list = recv_wide.reshape(-1)
+    edge_result, first_pre, second_pre, received, messages = edge_forward(
+        edge_count, recv_list, send_local, edge_input, wide_low, node_low,
         edge_w_one, edge_b_one[None], edge_w_two, edge_b_two[None], edge_gain[None], edge_shift[None],
     )
-    gathered = collect(wide_sums, per_device, 1)
+    gathered = collect(recv_list, messages, per_device, 1)
     joined = jnp.concatenate([node_low, gathered.astype(jnp.bfloat16)], axis=1)
     third_pre = matmul(joined, node_w_one) + node_b_one
     third_act = jax.nn.silu(third_pre).astype(jnp.bfloat16)
@@ -1225,15 +1217,14 @@
     grad_gathered = grad_joined[:, width:]
     wide_grad = spread(grad_gathered.astype(jnp.bfloat16), 2)
     node_out = node_input + to_channels(node_branch.T)
-    w_one_t = edge_w_one.T
-    edge_grad, receiver_wide, grads, vectors, node_part = edge_backward(
-        edge_count, recv_wide, send_local, edge_cotangent, edge_input, received, first_pre, second_pre,
-        wide_grad, grad_node_w_one, grad_node_w_two, grad_joined[:, :width], node_low, w_one_t, edge_w_two.T,
+    edge_grad, messages, grads, vectors, node_part = edge_backward(
+        edge_count, recv_list, send_local, edge_cotangent, edge_input, received, first_pre, second_pre,
+        wide_grad, grad_node_w_one, grad_node_w_two, grad_joined[:, :width], node_low, edge_w_one, edge_w_two,
         edge_gain[None],
     )
     node_vectors = jnp.stack([grad_node_b_one, grad_node_b_two, grad_node_gain, grad_node_shift])
     node_grad, summed, vectors = finish(
-        receiver_wide, grads, jnp.concatenate([vectors[:4], node_vectors]), node_part, w_one_t[:, 2 * width :],
+        recv_list, messages, grads, jnp.concatenate([vectors[:4], node_vectors]), node_part, edge_w_one,
         node_cotangent, 4 * width, 3,
     )
     summed = summed.astype(jnp.float32)

time: 397 us -> 359 us (0.904)
  Pallas kernels: 356 us -> 321 us
  local copies, waits for them, and re-layouts: 21.4 us -> 14.4 us
    pallas_call x4, Pallas kernels: 250 us -> 229 us  [the longest x1 87.9 us: finish(): pl.pallas_call(functools.partial(finish_kernel, cut), grid=(1,), in_specs...]
    pallas_call x1, Pallas kernels: 70.1 us -> 51.4 us  [edge_backward(): pl.pallas_call(backward_kernel, grid=(steps,), in_specs=[scalar, scalar,...]
    pallas_call x1, Pallas kernels: 36.2 us -> 40.5 us  [spread(): pl.pallas_call(spread_kernel, in_specs=[pl.BlockSpec(memory_space=pltpu.V...]
    unnamed x45 -> x37, local copies, waits for them, and re-layouts: 5.45 us -> 1.4 us
  transfers between devices with their start and end apart: 2 -> 2, of which waited for: 0 -> 0; matrix products, arithmetic and copies ran while one was open for 5% -> 3% of each run, Pallas kernels for 67% -> 75%
where the time goes in v8:
time: 359 us; the launch traced here: 355 us
  Pallas kernels  321 us (89%)
  local copies, waits for them, and re-layouts  14.4 us (4%)
  starting transfers between devices  7.52 us (2%)
  matrix products  6.31 us (2%)
  other arithmetic  4.65 us (1%)
    pallas_call x1, Pallas kernels, finish(): pl.pallas_call(functools.partial(finish_kernel, cut), grid=(1,), in_specs...  87.9 us
    pallas_call x1, Pallas kernels, begin(): pl.pallas_call(begin_kernel, in_specs=[hold, across, hold, hold], out_spe...  55.7 us
    pallas_call x1, Pallas kernels, edge_backward(): pl.pallas_call(backward_kernel, grid=(steps,), in_specs=[scalar, scalar,...  51.4 us
    pallas_call x1, Pallas kernels, collect(): pl.pallas_call(collect_kernel, in_specs=[pl.BlockSpec(memory_space=pltpu....  48.5 us
    pallas_call x1, Pallas kernels, spread(): pl.pallas_call(spread_kernel, in_specs=[pl.BlockSpec(memory_space=pltpu.V...  40.5 us
    pallas_call x1, Pallas kernels, edge_forward(): pl.pallas_call(forward_kernel, grid=(steps,), in_specs=[scalar, scalar, h...  36.8 us
  transfers between devices with their start and end apart: 2, of which 0 were waited for; matrix products, arithmetic and copies ran while one was open for 3% of the time, Pallas kernels for 75%

profile of v8, /device:TPU:0, one launch (start us, length us, event | category | flops | bytes accessed | tf_op | source)
XLA Modules:
  0.0 355.4 jit_solution(18285932785194660841)
XLA Ops:
  0.6 0.0 copy-start
  0.7 55.7 %begin_rows.1 = (bf16[512,512]{1,0:T(8,128)(2,1)}, bf16[3,4,512,512]{3,2,1,0:T(8,128)(2,1)}, f32[16,16384]{1,0:T(8,128)}, s32[36,128]{1,0:T(8,128)}, s32[36,128]{1,0:T(8,128)}) custom-call(f32[16,16384]{1,0:T(8,128)} %shard.1, f32[16,16384]{1,0:T(8,128)} %residual.1, s32[36,128]{1,0:T(8,128)} %bitcast.63, s32[36,128]{1,0:T(8,128)} %bitcast.64), custom_call_target="tpu_custom_call" | custom-call | tf_op jit(solution)/shard_map/begin_rows/pallas_call | solution.py:1143
  56.4 2.3 copy.47
  58.7 2.6 all-to-all-start.1
  62.0 36.8 %edge_forward.1 = (f32[4608,512]{1,0:T(8,128)}, f32[4608,512]{1,0:T(8,128)}, f32[4608,512]{1,0:T(8,128)}, bf16[4608,512]{1,0:T(8,128)(2,1)}, bf16[4608,512]{1,0:T(8,128)(2,1)}) custom-call(s32[1]{0:T(128)S(6)} %copy.49.count, s32[4608]{0:T(1024)} %bitcast.61, s32[36,128]{1,0:T(8,128)} %get-tuple-element.36.send, bf16[4608,512]{1,0:T(8,128)(2,1)} %edge.3, ...), custom_call_target="tpu_custom_call" | custom-call | flops 24159191040 | bytes 94371840 | tf_op jit(solution)/shard_map/edge_forward/pallas_call | solution.py:199
  98.8 0.0 copy-start.12
  98.8 0.0 copy-start.14
  98.8 48.5 %collect_sums.1 = f32[512,512]{1,0:T(8,128)} custom-call(s32[36,128]{1,0:T(8,128)} %get-tuple-element.35.index, bf16[4608,512]{1,0:T(8,128)(2,1)} %get-tuple-element.38.messages), custom_call_target="tpu_custom_call" | custom-call | tf_op jit(solution)/shard_map/collect_sums/pallas_call | solution.py:876
  147.4 0.0 copy-start.10
  147.4 0.0 copy-start.15
  147.4 1.3 convert_element_type.34
  148.7 0.0 copy-done
  148.7 0.0 copy-done.12
  148.8 0.0 copy-done.14
  148.8 0.0 copy-start.5
  148.8 0.7 convolution_add_fusion.1
  149.5 0.0 copy-done.10
  149.5 0.0 copy-done.15
  149.5 0.0 copy-start.16
  149.5 0.0 copy-start.7
  149.5 0.0 copy-start.9
  149.5 0.6 fusion.10
  150.1 0.0 copy-done.5
  150.2 0.3 copy-done.16
  150.5 0.0 all-to-all-done.1
  150.5 0.0 copy-done.7
  150.5 0.0 copy-start.11
  150.5 0.0 copy-start.17
  150.5 0.2 multiply_reduce_fusion
  150.8 0.5 fusion.1
  151.2 0.0 copy-done.9
  151.2 1.3 convert_reduce_fusion
  152.5 0.0 copy-done.11
  152.5 0.0 copy-done.17
  152.5 0.7 convert_reduce_fusion.1
  153.2 0.0 copy-start.6
  153.3 0.0 copy-start.13
  153.3 1.5 fusion.7.node_two
  154.7 0.0 copy-done.6
  154.7 0.0 copy-done.13
  154.7 2.1 fusion.2.node_one
  156.8 0.7 fusion.11
  157.6 0.9 slice.68.own
  158.4 1.1 slice.62.node_part
  159.5 4.9 %all-to-all-start = ((bf16[32,16,512]{2,1,0:T(8,128)(2,1)}), bf16[32,16,512]{2,1,0:T(8,128)(2,1)S(1)}, u32[]{:S(2)}, u32[]{:S(2)}) async-start(bf16[32,16,512]{2,1,0:T(8,128)(2,1)} %bitcast.9), calls=%async_computation | async-start | bytes 1048576 | tf_op jit(solution)/shard_map/all_to_all | solution.py:47
  164.4 40.5 %spread_rows.1 = bf16[3,4,512,512]{3,2,1,0:T(8,128)(2,1)} custom-call(bf16[512,512]{1,0:T(8,128)(2,1)} %slice.68.own), custom_call_target="tpu_custom_call" | custom-call | tf_op jit(solution)/shard_map/spread_rows/pallas_call | solution.py:699
  204.9 51.4 %edge_backward.1 = (f32[4608,512]{1,0:T(8,128)}, bf16[4608,512]{1,0:T(8,128)(2,1)}, f32[3584,512]{1,0:T(8,128)}, f32[8,512]{1,0:T(8,128)}, f32[512,512]{1,0:T(8,128)}) custom-call(s32[1]{0:T(128)S(6)} %copy.49.count, s32[4608]{0:T(1024)} %bitcast.62, s32[36,128]{1,0:T(8,128)} %get-tuple-element.36.send, bf16[4608,512]{1,0:T(8,128)(2,1)} %cotangent.1, ...), custom_call_target="tpu_custom_call" | custom-call | flops 28991029248 | bytes 94371840 | tf_op jit(solution)/shard_map/edge_backward/pallas_call | solution.py:319
  256.3 0.1 bitcast_reduce_fusion
  256.5 0.1 reshape.101
  256.6 0.7 slice.48
  257.3 0.6 concatenate.7.vectors
  257.9 87.9 %finish_sums.1 = (f32[16,16384]{1,0:T(8,128)}, bf16[3584,512]{1,0:T(8,128)(2,1)}, f32[8,512]{1,0:T(8,128)}) custom-call(s32[36,128]{1,0:T(8,128)} %get-tuple-element.35.index, bf16[4608,512]{1,0:T(8,128)(2,1)} %get-tuple-element.44.messages, f32[3584,512]{1,0:T(8,128)} %get-tuple-element.45.grads, f32[8,512]{1,0:T(8,128)} %concatenate.7.vectors, ...), custom_call_target="tpu_custom_call" | custom-call | tf_op jit(solution)/shard_map/finish_sums/pallas_call | solution.py:1003
  345.8 0.0 copy-start.2
  345.8 3.0 slice.65
  348.8 0.0 copy-done.2
  348.8 2.1 slice.63
  350.9 0.0 copy-done.8
  350.9 0.6 fusion.9
  351.5 1.6 fusion.8
  353.1 0.0 all-to-all-done
  353.2 0.1 convert_bitcast_fusion
  353.3 0.1 copy.45
  353.4 1.1 add.60
  354.5 1.0 copy.50
  (10 shorter events, 0.0 us)
Async XLA Ops:
  0.6 148.1 %copy-start = (bf16[1024,512]{1,0:T(8,128)(2,1)S(1)}, bf16[1024,512]{1,0:T(8,128)(2,1)}, u32[]{:S(2)}) copy-start(bf16[1024,512]{1,0:T(8,128)(2,1)} %param.30) | copy-start | bytes 3145732
  58.7 91.8 %all-to-all-start.1 = ((f32[16,32,512]{2,0,1:T(8,128)}), f32[16,32,512]{2,0,1:T(8,128)S(1)}, u32[]{:S(2)}, u32[]{:S(2)}) async-start(f32[16,32,512]{2,0,1:T(8,128)} %bitcast.57), calls=%async_computation.1 | async-start | bytes 2097152 | tf_op jit(solution)/shard_map/all_to_all | solution.py:43
  98.8 50.0 %copy-start.12 = (bf16[512,512]{1,0:T(8,128)(2,1)S(1)}, bf16[512,512]{1,0:T(8,128)(2,1)}, u32[]{:S(2)}) copy-start(bf16[512,512]{1,0:T(8,128)(2,1)} %get-tuple-element.34.nodes) | copy-start | bytes 1572868
  98.8 50.0 %copy-start.14 = (f32[512]{0:T(512)S(1)}, f32[512]{0:T(512)}, u32[]{:S(2)}) copy-start(f32[512]{0:T(512)} %param.31) | copy-start | bytes 6148
  147.4 2.1 copy-start.10
  147.4 2.1 copy-start.15
  148.8 1.4 copy-start.5
  149.5 1.0 copy-start.16
  149.5 1.0 copy-start.7
  149.5 1.7 copy-start.9
  150.5 2.0 copy-start.11
  150.5 2.0 copy-start.17
  153.2 1.5 copy-start.6
  153.3 1.5 copy-start.13
  159.5 193.6 %all-to-all-start = ((bf16[32,16,512]{2,1,0:T(8,128)(2,1)}), bf16[32,16,512]{2,1,0:T(8,128)(2,1)S(1)}, u32[]{:S(2)}, u32[]{:S(2)}) async-start(bf16[32,16,512]{2,1,0:T(8,128)(2,1)} %bitcast.9), calls=%async_computation | async-start | bytes 1048576 | tf_op jit(solution)/shard_map/all_to_all | solution.py:47
  345.8 3.0 copy-start.2
  348.8 2.1 copy-start.8
  351.5 1.8 copy-start.3
  353.1 1.3 copy-start.4
  353.2 2.3 copy-start.1

commit v9 on v8

--- a/solution.py
+++ b/solution.py
@@ -1,4 +1,3 @@
-import functools
 import math
 
 import jax
@@ -11,42 +10,8 @@
 EPSILON = 1e-05
 
 
-def norm_apply(values, gain, shift):
-    average = jnp.mean(values, -1, keepdims=True)
-    centred = values - average
-    variance = jnp.mean(centred * centred, -1, keepdims=True)
-    return centred * lax.rsqrt(variance + EPSILON) * gain + shift
-
-
-def silu_slope(values):
-    logistic = jax.nn.sigmoid(values)
-    return logistic * (1.0 + values * (1.0 - logistic))
-
-
-def matmul(left, right):
-    return jnp.dot(left, right, preferred_element_type=jnp.float32)
-
-
-def left_matmul(left, right):
-    return lax.dot_general(
-        left, right, (((0,), (0,)), ((), ())), preferred_element_type=jnp.float32
-    )
-
-
-def right_matmul(left, right):
-    return lax.dot_general(
-        left, right, (((1,), (1,)), ((), ())), preferred_element_type=jnp.float32
-    )
-
-
 def to_nodes(channels):
     return lax.all_to_all(channels, ("blk", "sub"), split_axis=1, concat_axis=0, tiled=True)
-
-
-def to_channels(values):
-    return lax.all_to_all(
-        values.astype(jnp.bfloat16), ("blk", "sub"), split_axis=0, concat_axis=1, tiled=True
-    ).astype(jnp.float32)
 
 
 TILE = 512
@@ -226,28 +191,19 @@
 
 
 def backward_kernel(
-    count, recv, send, cotangent, edge, received, first, second, wide, node_one, node_two, node_part, nodes, w_one, w_two, gain,
+    count, recv, send, cotangent, edge, received, first, second, wide, node_part, nodes, w_one, w_two, gain,
     grad, message, all_grads, vectors, sender_grad,
-    table, rows, stage, sems, by_sender, grads, pass_sems,
+    table, rows, stage, sems, by_sender, grads, give_sem,
 ):
     step = pl.program_id(0)
     base = step * TILE
     width = nodes.shape[1]
     parts = width // LANES
 
-    first_node = node_one.shape[0]
-    passed = (
-        pltpu.make_async_copy(node_one, grads.at[pl.ds(4 * width, first_node)], pass_sems.at[0]),
-        pltpu.make_async_copy(node_two, grads.at[pl.ds(4 * width + first_node, node_two.shape[0])], pass_sems.at[1]),
-        pltpu.make_async_copy(grads, all_grads, pass_sems.at[2]),
-    )
-
     @pl.when(step == 0)
     def _():
-        passed[0].start()
-        passed[1].start()
         load_table(wide, table, stage, sems)
-        grads[: 4 * width] = jnp.zeros((4 * width, width), grads.dtype)
+        grads[...] = jnp.zeros_like(grads)
         vectors[...] = jnp.zeros_like(vectors)
         by_sender[...] = jnp.zeros_like(by_sender)
 
@@ -288,17 +244,15 @@
     def _():
         high, rest = split_low(by_sender[...])
         grads[width : 2 * width] = dot_left(nodes[...], high) + dot_left(nodes[...], rest)
-        passed[0].wait()
-        passed[1].wait()
-        passed[2].start()
+        give = pltpu.make_async_copy(grads, all_grads, give_sem)
+        give.start()
         middle = w_one[width : 2 * width]
         sender_grad[...] = node_part[...] + dot_right(high, middle) + dot_right(rest, middle)
-        passed[2].wait()
+        give.wait()
 
 
 def edge_backward(
-    count, recv, send, cotangent, edge, received, first, second, wide, node_one, node_two, node_part, nodes,
-    w_one, w_two, gain,
+    count, recv, send, cotangent, edge, received, first, second, wide, node_part, nodes, w_one, w_two, gain
 ):
     edges, width = edge.shape
     steps = edges // TILE
@@ -309,9 +263,6 @@
     tile = pl.BlockSpec((TILE, width), lambda i: (i, 0))
 
     across = pl.BlockSpec(memory_space=pl.ANY)
-    unit = 64 * lax.axis_size("blk")
-    held = 4 * width + node_one.shape[0] + node_two.shape[0]
-    padded = -(-held // unit) * unit
 
     def whole(rows):
         return pl.BlockSpec((rows, width), lambda i: (0, 0))
@@ -321,7 +272,7 @@
         grid=(steps,),
         in_specs=[
             scalar, scalar, hold, tile, tile, tile, tile, tile,
-            across, across, across, hold, hold, hold, hold, hold,
+            across, hold, hold, hold, hold, hold,
         ],
         out_specs=[
             tile, tile, across, whole(8), whole(per_device),
@@ -329,7 +280,7 @@
         out_shape=[
             jax.ShapeDtypeStruct((edges, width), jnp.float32),
             jax.ShapeDtypeStruct((edges, width), jnp.bfloat16),
-            jax.ShapeDtypeStruct((padded, width), jnp.float32),
+            jax.ShapeDtypeStruct((4 * width, width), jnp.float32),
             jax.ShapeDtypeStruct((8, width), jnp.float32),
             jax.ShapeDtypeStruct((per_device, width), jnp.float32),
         ],
@@ -339,8 +290,8 @@
             pltpu.VMEM((2, CHUNK, width), jnp.bfloat16),
             pltpu.SemaphoreType.DMA((2,)),
             pltpu.VMEM((per_device, width), jnp.float32),
-            pltpu.VMEM((padded, width), jnp.float32),
-            pltpu.SemaphoreType.DMA((3,)),
+            pltpu.VMEM((4 * width, width), jnp.float32),
+            pltpu.SemaphoreType.DMA,
         ],
         compiler_params=pltpu.CompilerParams(vmem_limit_bytes=VMEM_BYTES),
         cost_estimate=pl.CostEstimate(
@@ -348,7 +299,7 @@
         ),
         name="edge_backward",
     )(
-        count, recv, send, cotangent, edge, received, first, second, wide, node_one, node_two,
+        count, recv, send, cotangent, edge, received, first, second, wide,
         node_part, nodes, w_one, w_two, gain,
     )
 
@@ -425,9 +376,35 @@
     lax.fori_loop(0, count // block, run, 0)
 
 
-def reducer_scratch(rows, width, along):
+def streams_of(rows):
+    unit = 64 * lax.axis_size("blk")
+    first = -(-(rows // unit) // 2) * unit
+    return [first, rows - first] if first < rows else [first]
+
+
+def padded_rows(rows):
+    unit = 64 * lax.axis_size("blk")
+    return -(-rows // unit) * unit
+
+
+def reducers_scratch(rows, width, along, loaded):
     return [
-        pltpu.VMEM((rows // 2, width), WIDE),
+        ref for part in streams_of(rows) for ref in reducer_scratch(part, width, along, loaded)
+    ]
+
+
+def reducers(at, grads, reduced, refs, loaded):
+    rows = grads.shape[0]
+    count = 13 if loaded else 11
+    made, first = [], 0
+    for i, part in enumerate(streams_of(rows)):
+        made.append(reducer(at, grads, reduced, first, part, i > 0, refs[i * count : (i + 1) * count]))
+        first += part
+    return both(made), refs[len(made) * count :]
+
+
+def reducer_scratch(rows, width, along, loaded):
+    return ([pltpu.VMEM((rows // 2, width), WIDE)] if loaded else []) + [
         pltpu.VMEM((rows // 2, width), WIDE),
         pltpu.VMEM((rows // 4, width), LOW),
         pltpu.VMEM((rows // 4, width), LOW),
@@ -435,7 +412,7 @@
         pltpu.VMEM((rows // 8, width), LOW),
         pltpu.VMEM((rows // 8, width), LOW),
         pltpu.VMEM((along - 1, rows // 8 // along, width), LOW),
-        pltpu.SemaphoreType.DMA,
+    ] + ([pltpu.SemaphoreType.DMA] if loaded else []) + [
         pltpu.SemaphoreType.DMA((6,)),
         pltpu.SemaphoreType.DMA((6,)),
         pltpu.SemaphoreType.DMA((2, along - 1)),
@@ -447,7 +424,7 @@
     (
         half, half_in, cross_out, cross_in, side_out, side_in, ring_out, ring_in,
         load_sem, step_send, step_recv, ring_send, ring_recv,
-    ) = refs
+    ) = refs if len(refs) == 13 else (None, *refs[:7], None, *refs[7:])
     along, peers = at["along"], at["peers"]
     turns = [(at["chip"], at["to_partner"]), (at["odd"], at["to_beside"])]
     (bit_one, device_one), (bit_two, device_two) = turns[::-1] if swap else turns
@@ -485,14 +462,19 @@
             source = target = reduced.at[span(at_ring, n_ring)]
         return remote(source, target, ring_send.at[kind, k - 1], ring_recv.at[kind, k - 1], peers[k - 1])
 
-    load = pltpu.make_async_copy(grads.at[span(at_half, n_half)], half, load_sem)
+    if half is None:
+        half, load = grads.at[span(at_half, n_half)], None
+    else:
+        load = pltpu.make_async_copy(grads.at[span(at_half, n_half)], half, load_sem)
 
     def start():
         step(0).start()
-        load.start()
+        if load is not None:
+            load.start()
 
     def add_half():
-        load.wait()
+        if load is not None:
+            load.wait()
         step(0).wait_recv()
         other = (1 - bit_one) * n_cross
 
@@ -683,30 +665,6 @@
     ]
 
 
-def spread_kernel(own, table, *refs):
-    at = places()
-    meet((at["to_sibling"], at["to_partner"], at["to_beside"], at["to_source"]))
-    start, one, two, three, drain = spread_moves(at, own, table, *refs)
-    start()
-    for stage in (one, two, three):
-        for piece in range(PIECES):
-            stage(piece)
-    drain()
-
-
-def spread(own, collective):
-    rows, width = own.shape
-    return pl.pallas_call(
-        spread_kernel,
-        in_specs=[pl.BlockSpec(memory_space=pltpu.VMEM)],
-        out_specs=pl.BlockSpec(memory_space=pl.ANY),
-        out_shape=jax.ShapeDtypeStruct((3, 4, rows, width), own.dtype),
-        scratch_shapes=spread_scratch(),
-        compiler_params=pltpu.CompilerParams(collective_id=collective, has_side_effects=True),
-        name="spread_rows",
-    )(own).reshape(12 * rows, width)
-
-
 HALVES = 2
 ORDER = (
     (0, 1, 0), (0, 1, 1), (1, 1, 0), (0, 0, 0), (1, 1, 1), (0, 0, 1),
@@ -861,31 +819,6 @@
     return load, run, drain
 
 
-def collect_kernel(index, messages, out, *refs):
-    at = places()
-    load, run, drain = collect_moves(at, index, messages, out, refs)
-    load.start()
-    meet((at["to_sibling"], at["to_partner"], at["to_beside"], at["to_onward"]))
-    load.wait()
-    run({})
-    drain()
-
-
-def collect(index, messages, rows, collective):
-    edges, width = messages.shape
-    return pl.pallas_call(
-        collect_kernel,
-        in_specs=[pl.BlockSpec(memory_space=pltpu.VMEM), pl.BlockSpec(memory_space=pl.ANY)],
-        out_specs=pl.BlockSpec(memory_space=pltpu.VMEM),
-        out_shape=jax.ShapeDtypeStruct((rows, width), WIDE),
-        scratch_shapes=collect_scratch(rows, width, edges),
-        compiler_params=pltpu.CompilerParams(
-            collective_id=collective, has_side_effects=True, vmem_limit_bytes=VMEM_BYTES
-        ),
-        name="collect_sums",
-    )(index.reshape(edges // LANES, LANES), messages)
-
-
 def exchange_scratch(rows, width, devices):
     slab = width // devices * (rows // LANES)
     return [
@@ -956,20 +889,14 @@
 
 
 def finish_kernel(
-    cut, index, messages, grads, vectors, node_part, weight, residual, node_grad, reduced, reduced_vectors, total, *refs
+    index, messages, grads, vectors, node_part, weight, residual, node_grad, reduced, reduced_vectors, total, *refs
 ):
     at = places()
-    sizes = len(reducer_scratch(64, 128, 2))
     count = len(collect_scratch(64, 128, 64))
     load, run, drain = collect_moves(at, index, messages, total, refs[:count])
     load.start()
     meet_all()
-    refs = refs[count:]
-    steps = both([
-        reducer(at, grads, reduced, 0, cut, False, refs[:sizes]),
-        reducer(at, grads, reduced, cut, grads.shape[0] - cut, True, refs[sizes : 2 * sizes]),
-    ])
-    refs = refs[2 * sizes :]
+    steps, refs = reducers(at, grads, reduced, refs[count:], True)
     vector_steps = vector_reducer(at, vectors, reduced_vectors, refs[:4])
     exchange, receive = exchange_moves(residual, node_grad, refs[4:])
     steps[0]()
@@ -993,7 +920,7 @@
     steps[9]()
 
 
-def finish(index, messages, grads, vectors, node_part, weight, residual, cut, collective):
+def finish(index, messages, grads, vectors, node_part, weight, residual, collective):
     rows, width = node_part.shape
     edges = messages.shape[0]
     along = lax.axis_size("blk") // 2
@@ -1001,7 +928,7 @@
     hold = pl.BlockSpec(memory_space=pltpu.VMEM)
     across = pl.BlockSpec(memory_space=pl.ANY)
     return pl.pallas_call(
-        functools.partial(finish_kernel, cut),
+        finish_kernel,
         grid=(1,),
         in_specs=[
             hold, across, across, hold, hold, pl.BlockSpec((width, width), lambda i: (2, 0)), hold,
@@ -1015,8 +942,7 @@
         scratch_shapes=[
             pltpu.VMEM((rows, width), WIDE),
             *collect_scratch(rows, width, edges),
-            *reducer_scratch(cut, width, along),
-            *reducer_scratch(grads.shape[0] - cut, width, along),
+            *reducers_scratch(grads.shape[0], width, along, True),
             *vector_scratch(vectors.shape, along),
             *exchange_scratch(rows, width, devices),
         ],
@@ -1025,6 +951,122 @@
         ),
         name="finish_sums",
     )(index.reshape(edges // LANES, LANES), messages, grads, vectors, node_part, weight, residual)
+
+
+def middle_kernel(
+    index, messages, node_low, upstream, w_one, b_one, w_two, b_two, gain, shift, residual,
+    table, node_part, node_out, reduced, reduced_vectors, total, sent, grads, vectors, *refs
+):
+    at = places()
+    count = len(collect_scratch(64, 128, 64))
+    load, run, drain = collect_moves(at, index, messages, total, refs[:count])
+    load.start()
+    meet_all()
+    refs = refs[count:]
+    start, one, two, three, end = spread_moves(at, sent, table, *refs[:3])
+    steps, refs = reducers(at, grads, reduced, refs[3:], False)
+    vector_steps = vector_reducer(at, vectors, reduced_vectors, refs[:4])
+    exchange, receive = exchange_moves(residual, node_out, refs[4:])
+    load.wait()
+    run({})
+
+    width = total.shape[1]
+    low = total[...].astype(LOW)
+    pre = dot(node_low[...], w_one[:width]) + dot(low, w_one[width:]) + b_one[...]
+    logistic = jax.nn.sigmoid(pre)
+    act = (pre * logistic).astype(LOW)
+    normal, scale = row_normal(dot(act, w_two[...]) + b_two[...])
+    given = upstream[...].T
+    scaled = given * gain[...]
+    slope = jnp.mean(scaled * normal, -1, keepdims=True)
+    fourth = scale * (scaled - jnp.mean(scaled, -1, keepdims=True) - normal * slope)
+    fourth_low = fourth.astype(LOW)
+    third = dot_right(fourth_low, w_two[...]) * (logistic * (1.0 + pre * (1.0 - logistic)))
+    third_low = third.astype(LOW)
+    sent[...] = dot_right(third_low, w_one[width:]).astype(LOW)
+    start()
+    grads[:width] = dot_left(node_low[...], third_low)
+    grads[width : 2 * width] = dot_left(low, third_low)
+    grads[2 * width : 3 * width] = dot_left(act, fourth_low)
+    steps[0]()
+    vectors[...] = jnp.zeros_like(vectors)
+    vectors[0:1] = jnp.sum(third_low.astype(WIDE), 0, keepdims=True)
+    vectors[1:2] = jnp.sum(fourth_low.astype(WIDE), 0, keepdims=True)
+    vectors[2:3] = jnp.sum(given * normal, 0, keepdims=True)
+    vectors[3:4] = jnp.sum(given, 0, keepdims=True)
+    vector_steps[0]()
+    node_part[...] = dot_right(third_low, w_one[:width])
+    exchange(normal * gain[...] + shift[...])
+
+    one(0)
+    steps[1]()
+    vector_steps[1]()
+    one(1)
+    one(2)
+    steps[2]()
+    vector_steps[2]()
+    one(3)
+    two(0)
+    steps[3]()
+    vector_steps[3]()
+    two(1)
+    two(2)
+    steps[4]()
+    two(3)
+    steps[5]()
+    three(0)
+    three(1)
+    steps[6]()
+    three(2)
+    three(3)
+    steps[7]()
+    receive()
+    vector_steps[4]()
+    end()
+    steps[8]()
+    steps[9]()
+    drain()
+
+
+def middle(index, messages, node_low, upstream, w_one, b_one, w_two, b_two, gain, shift, residual, collective):
+    rows, width = node_low.shape
+    edges = messages.shape[0]
+    along = lax.axis_size("blk") // 2
+    devices = lax.axis_size("blk") * lax.axis_size("sub")
+    grad_rows = padded_rows(3 * width)
+    hold = pl.BlockSpec(memory_space=pltpu.VMEM)
+    across = pl.BlockSpec(memory_space=pl.ANY)
+    table, node_part, node_out, reduced, reduced_vectors = pl.pallas_call(
+        middle_kernel,
+        in_specs=[hold, across] + [hold] * 9,
+        out_specs=[across] + [hold] * 4,
+        out_shape=[
+            jax.ShapeDtypeStruct((3, 4, rows, width), LOW),
+            jax.ShapeDtypeStruct((rows, width), WIDE),
+            jax.ShapeDtypeStruct(residual.shape, WIDE),
+            jax.ShapeDtypeStruct((grad_rows, width), LOW),
+            jax.ShapeDtypeStruct((8, width), WIDE),
+        ],
+        scratch_shapes=[
+            pltpu.VMEM((rows, width), WIDE),
+            pltpu.VMEM((rows, width), LOW),
+            pltpu.VMEM((grad_rows, width), WIDE),
+            pltpu.VMEM((8, width), WIDE),
+            *collect_scratch(rows, width, edges),
+            *spread_scratch(),
+            *reducers_scratch(grad_rows, width, along, False),
+            *vector_scratch((8, width), along),
+            *exchange_scratch(rows, width, devices),
+        ],
+        compiler_params=pltpu.CompilerParams(
+            collective_id=collective, has_side_effects=True, vmem_limit_bytes=VMEM_BYTES
+        ),
+        name="middle_nodes",
+    )(
+        index.reshape(edges // LANES, LANES), messages, node_low, upstream,
+        w_one, b_one, w_two, b_two, gain, shift, residual,
+    )
+    return table.reshape(12 * rows, width), node_part, node_out, reduced, reduced_vectors
 
 
 def scatter_scratch(channels, nodes, devices):
@@ -1193,41 +1235,26 @@
     node_low, wide_low, cotangent_later, send_local, recv_wide = begin(
         node_input, node_cotangent, senders, receivers, per_device, 0
     )
-    node_upstream = to_nodes(cotangent_later).T
+    node_upstream = to_nodes(cotangent_later)
     recv_list = recv_wide.reshape(-1)
     edge_result, first_pre, second_pre, received, messages = edge_forward(
         edge_count, recv_list, send_local, edge_input, wide_low, node_low,
         edge_w_one, edge_b_one[None], edge_w_two, edge_b_two[None], edge_gain[None], edge_shift[None],
     )
-    gathered = collect(recv_list, messages, per_device, 1)
-    joined = jnp.concatenate([node_low, gathered.astype(jnp.bfloat16)], axis=1)
-    third_pre = matmul(joined, node_w_one) + node_b_one
-    third_act = jax.nn.silu(third_pre).astype(jnp.bfloat16)
-    fourth_pre = matmul(third_act, node_w_two) + node_b_two
-    node_branch, node_norm_back = jax.vjp(norm_apply, fourth_pre, node_gain, node_shift)
-    grad_fourth, grad_node_gain, grad_node_shift = node_norm_back(node_upstream)
-    fourth_low = grad_fourth.astype(jnp.bfloat16)
-    grad_node_w_two = left_matmul(third_act, fourth_low)
-    grad_node_b_two = jnp.sum(fourth_low.astype(jnp.float32), 0)
-    grad_third = right_matmul(fourth_low, node_w_two) * silu_slope(third_pre)
-    third_low = grad_third.astype(jnp.bfloat16)
-    grad_node_w_one = left_matmul(joined, third_low)
-    grad_node_b_one = jnp.sum(third_low.astype(jnp.float32), 0)
-    grad_joined = right_matmul(third_low, node_w_one)
-    grad_gathered = grad_joined[:, width:]
-    wide_grad = spread(grad_gathered.astype(jnp.bfloat16), 2)
-    node_out = node_input + to_channels(node_branch.T)
+    wide_grad, node_part, node_out, node_summed, node_vectors = middle(
+        recv_list, messages, node_low, node_upstream, node_w_one, node_b_one[None], node_w_two, node_b_two[None],
+        node_gain[None], node_shift[None], node_input, 1,
+    )
     edge_grad, messages, grads, vectors, node_part = edge_backward(
         edge_count, recv_list, send_local, edge_cotangent, edge_input, received, first_pre, second_pre,
-        wide_grad, grad_node_w_one, grad_node_w_two, grad_joined[:, :width], node_low, edge_w_one, edge_w_two,
+        wide_grad, node_part, node_low, edge_w_one, edge_w_two,
         edge_gain[None],
     )
-    node_vectors = jnp.stack([grad_node_b_one, grad_node_b_two, grad_node_gain, grad_node_shift])
     node_grad, summed, vectors = finish(
-        recv_list, messages, grads, jnp.concatenate([vectors[:4], node_vectors]), node_part, edge_w_one,
-        node_cotangent, 4 * width, 3,
+        recv_list, messages, grads, vectors, node_part, edge_w_one, node_cotangent, 3
     )
     summed = summed.astype(jnp.float32)
+    node_summed = node_summed.astype(jnp.float32)
     return (
         node_out,
         edge_result,
@@ -1235,16 +1262,16 @@
         edge_grad,
         summed[: 3 * width],
         vectors[0],
-        summed[3 * width : 4 * width],
+        summed[3 * width :],
         vectors[1],
         vectors[2],
         vectors[3],
-        summed[4 * width : 6 * width],
-        vectors[4],
-        summed[6 * width : 7 * width],
-        vectors[5],
-        vectors[6],
-        vectors[7],
+        node_summed[: 2 * width],
+        node_vectors[0],
+        node_summed[2 * width : 3 * width],
+        node_vectors[1],
+        node_vectors[2],
+        node_vectors[3],
     )
 
 

time: 359 us -> 355 us (0.989)
  Pallas kernels: 321 us -> 336 us
  matrix products: 6.31 us -> 0 us
  starting transfers between devices: 7.52 us -> 2.65 us
  other arithmetic: 4.65 us -> 0 us
    pallas_call x3 -> x2, Pallas kernels: 177 us -> 194 us  [the longest x1 118 us: middle(): pl.pallas_call(middle_kernel, in_specs=[hold, across] + [hold] * 9, out_s...]
    dot_general x6 -> x0, matrix products: 6.31 us -> none  [the longest x2 3.55 us: left_matmul(): lax.dot_general(left, right, (((0,), (0,)), ((), ())), preferred_element_...]
    all_to_all x1 -> x0, starting transfers between devices: 4.88 us -> none  [to_channels(): lax.all_to_all(values.astype(jnp.bfloat16), ('blk', 'sub'), split_axis=0,...]
    slice x6 -> x5, local copies, waits for them, and re-layouts: 7.86 us -> 6.16 us  [the longest x1 2.26 us: shards(): summed[3 * width:]]
  transfers between devices with their start and end apart: 2 -> 1, of which waited for: 0 -> 0; matrix products, arithmetic and copies ran while one was open for 3% -> 0% of each run, Pallas kernels for 75% -> 10%
where the time goes in v9:
time: 355 us
  Pallas kernels  336 us (95%)
  local copies, waits for them, and re-layouts  14.9 us (4%)
    pallas_call x1, Pallas kernels, middle(): pl.pallas_call(middle_kernel, in_specs=[hold, across] + [hold] * 9, out_s...  118 us
    pallas_call x1, Pallas kernels, finish(): pl.pallas_call(finish_kernel, grid=(1,), in_specs=[hold, across, across,...  75.4 us
    pallas_call x1, Pallas kernels, begin(): pl.pallas_call(begin_kernel, in_specs=[hold, across, hold, hold], out_spe...  55.6 us
    pallas_call x1, Pallas kernels, edge_backward(): pl.pallas_call(backward_kernel, grid=(steps,), in_specs=[scalar, scalar,...  49.7 us
    pallas_call x1, Pallas kernels, edge_forward(): pl.pallas_call(forward_kernel, grid=(steps,), in_specs=[scalar, scalar, h...  36.8 us
  transfers between devices with their start and end apart: 1, of which 0 were waited for; matrix products, arithmetic and copies ran while one was open for 0% of the time, Pallas kernels for 10%

profile of v9, /device:TPU:0, one launch (start us, length us, event | category | flops | bytes accessed | tf_op | source)
XLA Modules:
  0.0 354.7 jit_solution(8339422859997668648)
XLA Ops:
  0.6 55.6 %begin_rows.1 = (bf16[512,512]{1,0:T(8,128)(2,1)}, bf16[3,4,512,512]{3,2,1,0:T(8,128)(2,1)}, f32[16,16384]{1,0:T(8,128)}, s32[36,128]{1,0:T(8,128)}, s32[36,128]{1,0:T(8,128)}) custom-call(f32[16,16384]{1,0:T(8,128)} %residual.2, f32[16,16384]{1,0:T(8,128)} %residual.3, s32[36,128]{1,0:T(8,128)} %bitcast.32, s32[36,128]{1,0:T(8,128)} %bitcast.33), custom_call_target="tpu_custom_call" | custom-call | tf_op jit(solution)/shard_map/begin_rows/pallas_call | solution.py:1185
  56.3 2.3 copy.38
  58.6 2.6 all-to-all-start
  61.9 36.8 %edge_forward.1 = (f32[4608,512]{1,0:T(8,128)}, f32[4608,512]{1,0:T(8,128)}, f32[4608,512]{1,0:T(8,128)}, bf16[4608,512]{1,0:T(8,128)(2,1)}, bf16[4608,512]{1,0:T(8,128)(2,1)}) custom-call(s32[1]{0:T(128)S(6)} %copy.41.count, s32[4608]{0:T(1024)} %bitcast.30, s32[36,128]{1,0:T(8,128)} %get-tuple-element.40.send, bf16[4608,512]{1,0:T(8,128)(2,1)} %edge.3, ...), custom_call_target="tpu_custom_call" | custom-call | flops 24159191040 | bytes 94371840 | tf_op jit(solution)/shard_map/edge_forward/pallas_call | solution.py:164
  98.7 0.0 all-to-all-done
  98.7 0.0 copy-start.1
  98.7 1.0 copy-done.1
  99.7 118.2 %middle_nodes.1 = (bf16[3,4,512,512]{3,2,1,0:T(8,128)(2,1)}, f32[512,512]{1,0:T(8,128)}, f32[16,16384]{1,0:T(8,128)}, bf16[1536,512]{1,0:T(8,128)(2,1)}, f32[8,512]{1,0:T(8,128)}) custom-call(s32[36,128]{1,0:T(8,128)} %get-tuple-element.39.index, bf16[4608,512]{1,0:T(8,128)(2,1)} %get-tuple-element.43.messages, ...), custom_call_target="tpu_custom_call" | custom-call | tf_op jit(solution)/shard_map/middle_nodes/pallas_call | solution.py:1039
  217.9 49.7 %edge_backward.1 = (f32[4608,512]{1,0:T(8,128)}, bf16[4608,512]{1,0:T(8,128)(2,1)}, f32[2048,512]{1,0:T(8,128)}, f32[8,512]{1,0:T(8,128)}, f32[512,512]{1,0:T(8,128)}) custom-call(s32[1]{0:T(128)S(6)} %copy.41.count, s32[4608]{0:T(1024)} %bitcast.31, s32[36,128]{1,0:T(8,128)} %get-tuple-element.40.send, bf16[4608,512]{1,0:T(8,128)(2,1)} %cotangent.1, ...), custom_call_target="tpu_custom_call" | custom-call | flops 28991029248 | bytes 94371840 | tf_op jit(solution)/shard_map/edge_backward/pallas_call | solution.py:270
  267.7 75.4 %finish_sums.1 = (f32[16,16384]{1,0:T(8,128)}, bf16[2048,512]{1,0:T(8,128)(2,1)}, f32[8,512]{1,0:T(8,128)}) custom-call(s32[36,128]{1,0:T(8,128)} %get-tuple-element.39.index, bf16[4608,512]{1,0:T(8,128)(2,1)} %get-tuple-element.52.messages, f32[2048,512]{1,0:T(8,128)} %get-tuple-element.53.grads, f32[8,512]{1,0:T(8,128)} %get-tuple-element.54.vectors, ...), custom_call_target="tpu_custom_call" | custom-call | tf_op jit(solution)/shard_map/finish_sums/pallas_call | solution.py:930
  343.0 0.0 copy-start
  343.0 2.3 slice.49
  345.3 3.5 slice.48
  348.8 0.0 copy-start.5
  348.8 0.0 copy-start.4
  348.8 0.0 copy-start.2
  348.8 0.0 copy-start.3
  348.8 0.0 copy-done
  348.8 1.1 slice.51
  349.9 1.6 slice.50
  351.5 0.0 copy-done.5
  351.5 0.6 fusion.1
  352.1 0.0 copy-done.4
  352.1 0.6 fusion
  352.7 0.0 copy-done.2
  352.7 1.0 copy.42
  353.7 0.0 copy-done.3
  353.7 1.0 copy.43
Async XLA Ops:
  58.6 40.1 %all-to-all-start = ((f32[16,32,512]{2,0,1:T(8,128)}), f32[16,32,512]{2,0,1:T(8,128)S(1)}, u32[]{:S(2)}, u32[]{:S(2)}) async-start(f32[16,32,512]{2,0,1:T(8,128)} %bitcast.27), calls=%async_computation | async-start | bytes 2097152 | tf_op jit(solution)/shard_map/all_to_all | solution.py:14
  98.7 1.0 copy-start.1
  343.0 5.8 %copy-start = (bf16[1536,512]{1,0:T(8,128)(2,1)S(1)}, bf16[1536,512]{1,0:T(8,128)(2,1)}, u32[]{:S(2)}) copy-start(bf16[1536,512]{1,0:T(8,128)(2,1)} %get-tuple-element.60) | copy-start | bytes 4718596
  348.8 2.7 copy-start.5
  348.8 3.3 copy-start.4
  348.8 3.9 %copy-start.2 = (f32[16,16384]{1,0:T(8,128)S(1)}, f32[16,16384]{1,0:T(8,128)}, u32[]{:S(2)}) copy-start(f32[16,16384]{1,0:T(8,128)} %get-tuple-element.86) | copy-start | bytes 3145732
  348.8 4.9 %copy-start.3 = (f32[16,16384]{1,0:T(8,128)S(1)}, f32[16,16384]{1,0:T(8,128)}, u32[]{:S(2)}) copy-start(f32[16,16384]{1,0:T(8,128)} %get-tuple-element.88) | copy-start | bytes 3145732

commit v10 on v9

--- a/solution.py
+++ b/solution.py
@@ -55,6 +55,7 @@
 
 
 def load_table(wide, table, stage, sems):
+    parts = table.shape[1]
     steps = wide.shape[0] // CHUNK
 
     def fetch(i, slot):
@@ -73,7 +74,8 @@
 
         def piece(k, carry):
             values = stage[slot, pl.ds(k * 64, 64), :].astype(jnp.float32)
-            lay_rows(table, i * CHUNK + k * 64, values)
+            for j in range(parts):
+                table[pl.ds(i * CHUNK + k * 64, 64), j, :] = values[:, j * LANES : (j + 1) * LANES]
             return carry
 
         return lax.fori_loop(0, CHUNK // 64, piece, carry)
@@ -87,10 +89,7 @@
     def body(i, carry):
         for u in range(16):
             slot = i * 16 + u
-            place = index[base + slot]
-            rows[pl.ds(pl.multiple_of(slot * parts, parts), parts), :] = table[
-                pl.ds(pl.multiple_of(place * parts, parts), parts), :
-            ]
+            rows[pl.ds(pl.multiple_of(slot * parts, parts), parts), :] = table[index[base + slot]]
         return carry
 
     lax.fori_loop(0, count // 16, body, 0)
@@ -177,7 +176,7 @@
             jax.ShapeDtypeStruct((edges, width), jnp.bfloat16),
         ],
         scratch_shapes=[
-            pltpu.VMEM((wide.shape[0] * parts, LANES), jnp.float32),
+            pltpu.VMEM((wide.shape[0], parts, LANES), jnp.float32),
             pltpu.VMEM((TILE * parts, LANES), jnp.float32),
             pltpu.VMEM((2, CHUNK, width), jnp.bfloat16),
             pltpu.SemaphoreType.DMA((2,)),
@@ -192,10 +191,36 @@
 
 def backward_kernel(
     count, recv, send, cotangent, edge, received, first, second, wide, node_part, nodes, w_one, w_two, gain,
-    grad, message, all_grads, vectors, sender_grad,
-    table, rows, stage, sems, by_sender, grads, give_sem,
+    node_grads, node_vectors,
+    grad, message, all_grads, vectors, sender_grad, node_reduced, vectors_reduced,
+    table, rows, stage, sems, by_sender, grads, give_sem, reduced, reduced_sem, *refs,
 ):
     step = pl.program_id(0)
+    at = places()
+    moves, refs = reducers(at, node_grads, reduced, refs, True)
+    vector_moves = vector_reducer(at, node_vectors, vectors_reduced, refs)
+
+    @pl.when(step == 0)
+    def _():
+        meet((at["to_sibling"], at["to_partner"], at["to_beside"], *at["peers"]))
+        moves[0]()
+        vector_moves[0]()
+
+    for when, events in (
+        (1, [moves[1], vector_moves[1]]),
+        (2, [moves[2], vector_moves[2]]),
+        (4, [moves[3], vector_moves[3]]),
+        (5, [moves[4]]),
+        (6, [moves[5]]),
+        (7, [moves[6]]),
+        (8, [moves[7], vector_moves[4]]),
+    ):
+
+        @pl.when(step == when)
+        def _():
+            for event in events:
+                event()
+
     base = step * TILE
     width = nodes.shape[1]
     parts = width // LANES
@@ -248,16 +273,24 @@
         give.start()
         middle = w_one[width : 2 * width]
         sender_grad[...] = node_part[...] + dot_right(high, middle) + dot_right(rest, middle)
+        moves[8]()
+        give_reduced = pltpu.make_async_copy(reduced, node_reduced, reduced_sem)
+        give_reduced.start()
+        moves[9]()
         give.wait()
+        give_reduced.wait()
 
 
 def edge_backward(
-    count, recv, send, cotangent, edge, received, first, second, wide, node_part, nodes, w_one, w_two, gain
+    count, recv, send, cotangent, edge, received, first, second, wide, node_part, nodes, w_one, w_two, gain,
+    node_grads, node_vectors, collective,
 ):
     edges, width = edge.shape
     steps = edges // TILE
     parts = width // LANES
     per_device = nodes.shape[0]
+    along = lax.axis_size("blk") // 2
+    node_rows = node_grads.shape[0]
     hold = pl.BlockSpec(memory_space=pltpu.VMEM)
     scalar = pl.BlockSpec(memory_space=pltpu.SMEM)
     tile = pl.BlockSpec((TILE, width), lambda i: (i, 0))
@@ -272,10 +305,10 @@
         grid=(steps,),
         in_specs=[
             scalar, scalar, hold, tile, tile, tile, tile, tile,
-            across, hold, hold, hold, hold, hold,
+            across, hold, hold, hold, hold, hold, across, hold,
         ],
         out_specs=[
-            tile, tile, across, whole(8), whole(per_device),
+            tile, tile, across, whole(8), whole(per_device), across, whole(8),
         ],
         out_shape=[
             jax.ShapeDtypeStruct((edges, width), jnp.float32),
@@ -283,24 +316,32 @@
             jax.ShapeDtypeStruct((4 * width, width), jnp.float32),
             jax.ShapeDtypeStruct((8, width), jnp.float32),
             jax.ShapeDtypeStruct((per_device, width), jnp.float32),
+            jax.ShapeDtypeStruct((node_rows, width), jnp.bfloat16),
+            jax.ShapeDtypeStruct((8, width), jnp.float32),
         ],
         scratch_shapes=[
-            pltpu.VMEM((wide.shape[0] * parts, LANES), jnp.float32),
+            pltpu.VMEM((wide.shape[0], parts, LANES), jnp.float32),
             pltpu.VMEM((TILE * parts, LANES), jnp.float32),
             pltpu.VMEM((2, CHUNK, width), jnp.bfloat16),
             pltpu.SemaphoreType.DMA((2,)),
             pltpu.VMEM((per_device, width), jnp.float32),
             pltpu.VMEM((4 * width, width), jnp.float32),
             pltpu.SemaphoreType.DMA,
-        ],
-        compiler_params=pltpu.CompilerParams(vmem_limit_bytes=VMEM_BYTES),
+            pltpu.VMEM((node_rows, width), jnp.bfloat16),
+            pltpu.SemaphoreType.DMA,
+            *reducers_scratch(node_rows, width, along, True),
+            *vector_scratch((8, width), along),
+        ],
+        compiler_params=pltpu.CompilerParams(
+            collective_id=collective, has_side_effects=True, vmem_limit_bytes=VMEM_BYTES
+        ),
         cost_estimate=pl.CostEstimate(
             flops=24 * edges * width * width, bytes_accessed=40 * edges * width, transcendentals=2 * edges * width
         ),
         name="edge_backward",
     )(
         count, recv, send, cotangent, edge, received, first, second, wide,
-        node_part, nodes, w_one, w_two, gain,
+        node_part, nodes, w_one, w_two, gain, node_grads, node_vectors,
     )
 
 
@@ -955,7 +996,7 @@
 
 def middle_kernel(
     index, messages, node_low, upstream, w_one, b_one, w_two, b_two, gain, shift, residual,
-    table, node_part, node_out, reduced, reduced_vectors, total, sent, grads, vectors, *refs
+    table, node_part, node_out, grads, vectors, total, sent, *refs
 ):
     at = places()
     count = len(collect_scratch(64, 128, 64))
@@ -964,9 +1005,7 @@
     meet_all()
     refs = refs[count:]
     start, one, two, three, end = spread_moves(at, sent, table, *refs[:3])
-    steps, refs = reducers(at, grads, reduced, refs[3:], False)
-    vector_steps = vector_reducer(at, vectors, reduced_vectors, refs[:4])
-    exchange, receive = exchange_moves(residual, node_out, refs[4:])
+    exchange, receive = exchange_moves(residual, node_out, refs[3:])
     load.wait()
     run({})
 
@@ -988,55 +1027,30 @@
     grads[:width] = dot_left(node_low[...], third_low)
     grads[width : 2 * width] = dot_left(low, third_low)
     grads[2 * width : 3 * width] = dot_left(act, fourth_low)
-    steps[0]()
     vectors[...] = jnp.zeros_like(vectors)
     vectors[0:1] = jnp.sum(third_low.astype(WIDE), 0, keepdims=True)
     vectors[1:2] = jnp.sum(fourth_low.astype(WIDE), 0, keepdims=True)
     vectors[2:3] = jnp.sum(given * normal, 0, keepdims=True)
     vectors[3:4] = jnp.sum(given, 0, keepdims=True)
-    vector_steps[0]()
     node_part[...] = dot_right(third_low, w_one[:width])
     exchange(normal * gain[...] + shift[...])
 
-    one(0)
-    steps[1]()
-    vector_steps[1]()
-    one(1)
-    one(2)
-    steps[2]()
-    vector_steps[2]()
-    one(3)
-    two(0)
-    steps[3]()
-    vector_steps[3]()
-    two(1)
-    two(2)
-    steps[4]()
-    two(3)
-    steps[5]()
-    three(0)
-    three(1)
-    steps[6]()
-    three(2)
-    three(3)
-    steps[7]()
+    for stage in (one, two, three):
+        for piece in range(PIECES):
+            stage(piece)
     receive()
-    vector_steps[4]()
     end()
-    steps[8]()
-    steps[9]()
     drain()
 
 
 def middle(index, messages, node_low, upstream, w_one, b_one, w_two, b_two, gain, shift, residual, collective):
     rows, width = node_low.shape
     edges = messages.shape[0]
-    along = lax.axis_size("blk") // 2
     devices = lax.axis_size("blk") * lax.axis_size("sub")
     grad_rows = padded_rows(3 * width)
     hold = pl.BlockSpec(memory_space=pltpu.VMEM)
     across = pl.BlockSpec(memory_space=pl.ANY)
-    table, node_part, node_out, reduced, reduced_vectors = pl.pallas_call(
+    table, node_part, node_out, grads, vectors = pl.pallas_call(
         middle_kernel,
         in_specs=[hold, across] + [hold] * 9,
         out_specs=[across] + [hold] * 4,
@@ -1044,18 +1058,14 @@
             jax.ShapeDtypeStruct((3, 4, rows, width), LOW),
             jax.ShapeDtypeStruct((rows, width), WIDE),
             jax.ShapeDtypeStruct(residual.shape, WIDE),
-            jax.ShapeDtypeStruct((grad_rows, width), LOW),
+            jax.ShapeDtypeStruct((grad_rows, width), WIDE),
             jax.ShapeDtypeStruct((8, width), WIDE),
         ],
         scratch_shapes=[
             pltpu.VMEM((rows, width), WIDE),
             pltpu.VMEM((rows, width), LOW),
-            pltpu.VMEM((grad_rows, width), WIDE),
-            pltpu.VMEM((8, width), WIDE),
             *collect_scratch(rows, width, edges),
             *spread_scratch(),
-            *reducers_scratch(grad_rows, width, along, False),
-            *vector_scratch((8, width), along),
             *exchange_scratch(rows, width, devices),
         ],
         compiler_params=pltpu.CompilerParams(
@@ -1066,7 +1076,7 @@
         index.reshape(edges // LANES, LANES), messages, node_low, upstream,
         w_one, b_one, w_two, b_two, gain, shift, residual,
     )
-    return table.reshape(12 * rows, width), node_part, node_out, reduced, reduced_vectors
+    return table.reshape(12 * rows, width), node_part, node_out, grads, vectors
 
 
 def scatter_scratch(channels, nodes, devices):
@@ -1241,14 +1251,14 @@
         edge_count, recv_list, send_local, edge_input, wide_low, node_low,
         edge_w_one, edge_b_one[None], edge_w_two, edge_b_two[None], edge_gain[None], edge_shift[None],
     )
-    wide_grad, node_part, node_out, node_summed, node_vectors = middle(
+    wide_grad, node_part, node_out, node_grads, node_vectors = middle(
         recv_list, messages, node_low, node_upstream, node_w_one, node_b_one[None], node_w_two, node_b_two[None],
         node_gain[None], node_shift[None], node_input, 1,
     )
-    edge_grad, messages, grads, vectors, node_part = edge_backward(
+    edge_grad, messages, grads, vectors, node_part, node_summed, node_vectors = edge_backward(
         edge_count, recv_list, send_local, edge_cotangent, edge_input, received, first_pre, second_pre,
         wide_grad, node_part, node_low, edge_w_one, edge_w_two,
-        edge_gain[None],
+        edge_gain[None], node_grads, node_vectors, 2,
     )
     node_grad, summed, vectors = finish(
         recv_list, messages, grads, vectors, node_part, edge_w_one, node_cotangent, 3

time: 355 us -> 356 us (level)
  Pallas kernels: 336 us -> 332 us
  local copies, waits for them, and re-layouts: 14.9 us -> 18.8 us
    pallas_call x1, Pallas kernels: 118 us -> 94.1 us  [middle(): pl.pallas_call(middle_kernel, in_specs=[hold, across] + [hold] * 9, out_s...]
    pallas_call x1, Pallas kernels: 49.7 us -> 67.6 us  [edge_backward(): pl.pallas_call(backward_kernel, grid=(steps,), in_specs=[scalar, scalar,...]
    pallas_call x1, Pallas kernels: 36.8 us -> 40.6 us  [edge_forward(): pl.pallas_call(forward_kernel, grid=(steps,), in_specs=[scalar, scalar, h...]
    unnamed x14 -> x21, local copies, waits for them, and re-layouts: 2.92 us -> 6.68 us
  transfers between devices with their start and end apart: 1 -> 1, of which waited for: 0 -> 0; matrix products, arithmetic and copies ran while one was open for 0% -> 0% of each run, Pallas kernels for 10% -> 11%
where the time goes in v10:
time: 356 us; the launch traced here: 355 us
  Pallas kernels  332 us (93%)
  local copies, waits for them, and re-layouts  18.8 us (5%)
    pallas_call x1, Pallas kernels, middle(): pl.pallas_call(middle_kernel, in_specs=[hold, across] + [hold] * 9, out_s...  94.1 us
    pallas_call x1, Pallas kernels, finish(): pl.pallas_call(finish_kernel, grid=(1,), in_specs=[hold, across, across,...  74.4 us
    pallas_call x1, Pallas kernels, edge_backward(): pl.pallas_call(backward_kernel, grid=(steps,), in_specs=[scalar, scalar,...  67.6 us
    pallas_call x1, Pallas kernels, begin(): pl.pallas_call(begin_kernel, in_specs=[hold, across, hold, hold], out_spe...  55.6 us
    pallas_call x1, Pallas kernels, edge_forward(): pl.pallas_call(forward_kernel, grid=(steps,), in_specs=[scalar, scalar, h...  40.6 us
  transfers between devices with their start and end apart: 1, of which 0 were waited for; matrix products, arithmetic and copies ran while one was open for 0% of the time, Pallas kernels for 11%

profile of v10, /device:TPU:0, one launch (start us, length us, event | category | flops | bytes accessed | tf_op | source)
XLA Modules:
  0.0 355.1 jit_solution(8458247761805687244)
XLA Ops:
  0.6 55.6 %begin_rows.1 = (bf16[512,512]{1,0:T(8,128)(2,1)}, bf16[3,4,512,512]{3,2,1,0:T(8,128)(2,1)}, f32[16,16384]{1,0:T(8,128)}, s32[36,128]{1,0:T(8,128)}, s32[36,128]{1,0:T(8,128)}) custom-call(f32[16,16384]{1,0:T(8,128)} %residual.2, f32[16,16384]{1,0:T(8,128)} %residual.3, s32[36,128]{1,0:T(8,128)} %bitcast.34, s32[36,128]{1,0:T(8,128)} %bitcast.35), custom_call_target="tpu_custom_call" | custom-call | tf_op jit(solution)/shard_map/begin_rows/pallas_call | solution.py:1195
  56.3 2.3 copy.38
  58.6 2.6 all-to-all-start
  61.9 40.6 %edge_forward.1 = (f32[4608,512]{1,0:T(8,128)}, f32[4608,512]{1,0:T(8,128)}, f32[4608,512]{1,0:T(8,128)}, bf16[4608,512]{1,0:T(8,128)(2,1)}, bf16[4608,512]{1,0:T(8,128)(2,1)}) custom-call(s32[1]{0:T(128)S(6)} %copy.42.count, s32[4608]{0:T(1024)} %bitcast.32, s32[36,128]{1,0:T(8,128)} %get-tuple-element.42.send, bf16[4608,512]{1,0:T(8,128)(2,1)} %edge.3, ...), custom_call_target="tpu_custom_call" | custom-call | flops 24159191040 | bytes 94371840 | tf_op jit(solution)/shard_map/edge_forward/pallas_call | solution.py:163
  102.5 0.0 all-to-all-done
  102.5 0.0 copy-start.1
  102.5 1.0 copy-done.1
  103.5 94.1 %middle_nodes.1 = (bf16[3,4,512,512]{3,2,1,0:T(8,128)(2,1)}, f32[512,512]{1,0:T(8,128)}, f32[16,16384]{1,0:T(8,128)}, f32[1536,512]{1,0:T(8,128)}, f32[8,512]{1,0:T(8,128)}) custom-call(s32[36,128]{1,0:T(8,128)} %get-tuple-element.41.index, bf16[4608,512]{1,0:T(8,128)(2,1)} %get-tuple-element.45.messages, bf16[512,512]{1,0:T(8,128)(2,1)} %get-tuple-element.44.nodes.node_low, ...), custom_call_target="tpu_custom_call" | custom-call | tf_op jit(solution)/shard_map/middle_nodes/pallas_call | solution.py:1053
  197.6 67.6 %edge_backward.1 = (f32[4608,512]{1,0:T(8,128)}, bf16[4608,512]{1,0:T(8,128)(2,1)}, f32[2048,512]{1,0:T(8,128)}, f32[8,512]{1,0:T(8,128)}, f32[512,512]{1,0:T(8,...) custom-call(s32[1]{0:T(128)S(6)} %copy.42.count, s32[4608]{0:T(1024)} %bitcast.33, s32[36,128]{1,0:T(8,128)} %get-tuple-element.42.send, ...), custom_call_target="tpu_custom_call" | custom-call | flops 28991029248 | bytes 94371840 | tf_op jit(solution)/shard_map/edge_backward/pallas_call | solution.py:303
  265.2 74.4 %finish_sums.1 = (f32[16,16384]{1,0:T(8,128)}, bf16[2048,512]{1,0:T(8,128)(2,1)}, f32[8,512]{1,0:T(8,128)}) custom-call(s32[36,128]{1,0:T(8,128)} %get-tuple-element.41.index, bf16[4608,512]{1,0:T(8,128)(2,1)} %get-tuple-element.56.messages, f32[2048,512]{1,0:T(8,128)} %get-tuple-element.57.grads, f32[8,512]{1,0:T(8,128)} %get-tuple-element.58.vectors, ...), custom_call_target="tpu_custom_call" | custom-call | tf_op jit(solution)/shard_map/finish_sums/pallas_call | solution.py:971
  339.5 0.0 copy-start
  339.5 0.0 slice-start
  339.5 2.3 slice.49
  341.8 0.0 slice-start.1
  341.8 3.7 %slice.48 = f32[1536,512]{1,0:T(8,128)} slice(bf16[2048,512]{1,0:T(8,128)(2,1)} %get-tuple-element.62), slice={[0:1536], [0:512]} | slice | bytes 6291456 | tf_op jit(solution)/shard_map/slice | solution.py:1273
  345.5 0.0 copy-start.5
  345.5 0.0 copy-start.4
  345.5 0.0 copy-start.2
  345.5 0.0 copy-start.3
  345.5 0.0 copy-done
  345.5 1.1 slice.51
  346.6 0.0 slice-start.2
  346.6 1.6 slice.50
  348.2 0.0 copy-done.5
  348.2 0.6 fusion.1
  348.8 0.0 copy-done.4
  348.8 0.6 fusion
  349.4 0.0 copy-done.2
  349.4 1.0 copy.43
  350.4 0.0 copy-done.3
  350.4 1.0 copy.44
  351.4 0.0 slice-done
  351.4 0.0 slice-done.1
  351.4 0.0 slice-done.2
  351.4 3.7 %copy.45 = f32[4608,512]{1,0:T(8,128)} copy(f32[4608,512]{1,0:T(8,128)S(1)} %bitcast.29) | data formatting | bytes 18874368
  (1 shorter events, 0.0 us)
Async XLA Ops:
  58.6 43.9 %all-to-all-start = ((f32[16,32,512]{2,0,1:T(8,128)}), f32[16,32,512]{2,0,1:T(8,128)S(1)}, u32[]{:S(2)}, u32[]{:S(2)}) async-start(f32[16,32,512]{2,0,1:T(8,128)} %bitcast.27), calls=%async_computation | async-start | bytes 2097152 | tf_op jit(solution)/shard_map/all_to_all | solution.py:14
  102.5 1.0 copy-start.1
  339.5 6.0 %copy-start = (bf16[1536,512]{1,0:T(8,128)(2,1)S(1)}, bf16[1536,512]{1,0:T(8,128)(2,1)}, u32[]{:S(2)}) copy-start(bf16[1536,512]{1,0:T(8,128)(2,1)} %get-tuple-element.64) | copy-start | bytes 4718596
  339.5 11.8 %slice-start = ((s8[9437184]{0:T(1024)(128)(4,1)}), s8[4194304]{0:T(1024)(128)(4,1)S(1)}, s32[]{:S(2)}) async-start(s8[9437184]{0:T(1024)(128)(4,1)} %bitcast.28), calls=%async_computation.1 | async-start | bytes 8388608
  341.8 9.5 %slice-start.1 = ((s8[9437184]{0:T(1024)(128)(4,1)}), s8[4194304]{0:T(1024)(128)(4,1)S(1)}, s32[]{:S(2)}) async-start(s8[9437184]{0:T(1024)(128)(4,1)} %bitcast.28), calls=%async_computation.2 | async-start | bytes 8388608
  345.5 2.7 copy-start.5
  345.5 3.3 copy-start.4
  345.5 3.9 %copy-start.2 = (f32[16,16384]{1,0:T(8,128)S(1)}, f32[16,16384]{1,0:T(8,128)}, u32[]{:S(2)}) copy-start(f32[16,16384]{1,0:T(8,128)} %get-tuple-element.90) | copy-start | bytes 3145732
  345.5 4.9 %copy-start.3 = (f32[16,16384]{1,0:T(8,128)S(1)}, f32[16,16384]{1,0:T(8,128)}, u32[]{:S(2)}) copy-start(f32[16,16384]{1,0:T(8,128)} %get-tuple-element.92) | copy-start | bytes 3145732
  346.6 4.8 %slice-start.2 = ((s8[9437184]{0:T(1024)(128)(4,1)}), s8[1048576]{0:T(1024)(128)(4,1)S(1)}, s32[]{:S(2)}) async-start(s8[9437184]{0:T(1024)(128)(4,1)} %bitcast.28), calls=%async_computation.3 | async-start | bytes 2097152

commit v11 on v9

--- a/solution.py
+++ b/solution.py
@@ -8,10 +8,6 @@
 from jax.sharding import PartitionSpec as P
 
 EPSILON = 1e-05
-
-
-def to_nodes(channels):
-    return lax.all_to_all(channels, ("blk", "sub"), split_axis=1, concat_axis=0, tiled=True)
 
 
 TILE = 512
@@ -306,6 +302,7 @@
 
 MESH = pl.DeviceIdType.MESH
 PIECES = 4
+SPLIT = False
 LOW = jnp.bfloat16
 WIDE = jnp.float32
 
@@ -376,35 +373,37 @@
     lax.fori_loop(0, count // block, run, 0)
 
 
-def streams_of(rows):
-    unit = 64 * lax.axis_size("blk")
-    first = -(-(rows // unit) // 2) * unit
-    return [first, rows - first] if first < rows else [first]
-
-
 def padded_rows(rows):
     unit = 64 * lax.axis_size("blk")
     return -(-rows // unit) * unit
 
 
-def reducers_scratch(rows, width, along, loaded):
+def streams_of(sources):
+    unit = 64 * lax.axis_size("blk")
+    streams = []
+    for i, rows in enumerate(sources):
+        first = -(-(rows // unit) // 2) * unit if SPLIT else rows
+        streams.append((i, 0, first))
+        if first < rows:
+            streams.append((i, first, rows - first))
+    return streams
+
+
+def reducers_scratch(sources, width, along):
+    return [ref for _, _, rows in streams_of(sources) for ref in reducer_scratch(rows, width, along)]
+
+
+def reducers(at, sources, reduced, refs):
+    made = []
+    for i, (which, start, rows) in enumerate(streams_of([source.shape[0] for source in sources])):
+        first = start + sum(source.shape[0] for source in sources[:which])
+        made.append(reducer(at, sources[which], start, reduced, first, rows, i % 2 > 0, refs[i * 13 : i * 13 + 13]))
+    return both(made), refs[len(made) * 13 :]
+
+
+def reducer_scratch(rows, width, along):
     return [
-        ref for part in streams_of(rows) for ref in reducer_scratch(part, width, along, loaded)
-    ]
-
-
-def reducers(at, grads, reduced, refs, loaded):
-    rows = grads.shape[0]
-    count = 13 if loaded else 11
-    made, first = [], 0
-    for i, part in enumerate(streams_of(rows)):
-        made.append(reducer(at, grads, reduced, first, part, i > 0, refs[i * count : (i + 1) * count]))
-        first += part
-    return both(made), refs[len(made) * count :]
-
-
-def reducer_scratch(rows, width, along, loaded):
-    return ([pltpu.VMEM((rows // 2, width), WIDE)] if loaded else []) + [
+        pltpu.VMEM((rows // 2, width), WIDE),
         pltpu.VMEM((rows // 2, width), WIDE),
         pltpu.VMEM((rows // 4, width), LOW),
         pltpu.VMEM((rows // 4, width), LOW),
@@ -412,7 +411,7 @@
         pltpu.VMEM((rows // 8, width), LOW),
         pltpu.VMEM((rows // 8, width), LOW),
         pltpu.VMEM((along - 1, rows // 8 // along, width), LOW),
-    ] + ([pltpu.SemaphoreType.DMA] if loaded else []) + [
+        pltpu.SemaphoreType.DMA,
         pltpu.SemaphoreType.DMA((6,)),
         pltpu.SemaphoreType.DMA((6,)),
         pltpu.SemaphoreType.DMA((2, along - 1)),
@@ -420,11 +419,11 @@
     ]
 
 
-def reducer(at, grads, reduced, first, rows, swap, refs):
+def reducer(at, grads, source_first, reduced, first, rows, swap, refs):
     (
         half, half_in, cross_out, cross_in, side_out, side_in, ring_out, ring_in,
         load_sem, step_send, step_recv, ring_send, ring_recv,
-    ) = refs if len(refs) == 13 else (None, *refs[:7], None, *refs[7:])
+    ) = refs
     along, peers = at["along"], at["peers"]
     turns = [(at["chip"], at["to_partner"]), (at["odd"], at["to_beside"])]
     (bit_one, device_one), (bit_two, device_two) = turns[::-1] if swap else turns
@@ -440,7 +439,8 @@
 
     def step(kind):
         if kind == 0:
-            source, target, device = grads.at[span(first + (1 - core) * n_half, n_half)], half_in, at["to_sibling"]
+            other = span(source_first + (1 - core) * n_half, n_half)
+            source, target, device = grads.at[other], half_in, at["to_sibling"]
         elif kind == 1:
             source, target, device = cross_out, cross_in, device_one
         elif kind == 2:
@@ -462,19 +462,14 @@
             source = target = reduced.at[span(at_ring, n_ring)]
         return remote(source, target, ring_send.at[kind, k - 1], ring_recv.at[kind, k - 1], peers[k - 1])
 
-    if half is None:
-        half, load = grads.at[span(at_half, n_half)], None
-    else:
-        load = pltpu.make_async_copy(grads.at[span(at_half, n_half)], half, load_sem)
+    load = pltpu.make_async_copy(grads.at[span(source_first + core * n_half, n_half)], half, load_sem)
 
     def start():
         step(0).start()
-        if load is not None:
-            load.start()
+        load.start()
 
     def add_half():
-        if load is not None:
-            load.wait()
+        load.wait()
         step(0).wait_recv()
         other = (1 - bit_one) * n_cross
 
@@ -889,14 +884,15 @@
 
 
 def finish_kernel(
-    index, messages, grads, vectors, node_part, weight, residual, node_grad, reduced, reduced_vectors, total, *refs
+    index, messages, edge_grads, node_grads, vectors, node_part, weight, residual,
+    node_grad, reduced, reduced_vectors, total, *refs,
 ):
     at = places()
     count = len(collect_scratch(64, 128, 64))
     load, run, drain = collect_moves(at, index, messages, total, refs[:count])
     load.start()
     meet_all()
-    steps, refs = reducers(at, grads, reduced, refs[count:], True)
+    steps, refs = reducers(at, (edge_grads, node_grads), reduced, refs[count:])
     vector_steps = vector_reducer(at, vectors, reduced_vectors, refs[:4])
     exchange, receive = exchange_moves(residual, node_grad, refs[4:])
     steps[0]()
@@ -920,9 +916,10 @@
     steps[9]()
 
 
-def finish(index, messages, grads, vectors, node_part, weight, residual, collective):
+def finish(index, messages, edge_grads, node_grads, vectors, node_part, weight, residual, collective):
     rows, width = node_part.shape
     edges = messages.shape[0]
+    sources = [edge_grads.shape[0], node_grads.shape[0]]
     along = lax.axis_size("blk") // 2
     devices = lax.axis_size("blk") * lax.axis_size("sub")
     hold = pl.BlockSpec(memory_space=pltpu.VMEM)
@@ -931,18 +928,18 @@
         finish_kernel,
         grid=(1,),
         in_specs=[
-            hold, across, across, hold, hold, pl.BlockSpec((width, width), lambda i: (2, 0)), hold,
+            hold, across, across, across, hold, hold, pl.BlockSpec((width, width), lambda i: (2, 0)), hold,
         ],
         out_specs=[hold] * 3,
         out_shape=[
             jax.ShapeDtypeStruct(residual.shape, WIDE),
-            jax.ShapeDtypeStruct(grads.shape, LOW),
+            jax.ShapeDtypeStruct((sum(sources), width), LOW),
             jax.ShapeDtypeStruct(vectors.shape, WIDE),
         ],
         scratch_shapes=[
             pltpu.VMEM((rows, width), WIDE),
             *collect_scratch(rows, width, edges),
-            *reducers_scratch(grads.shape[0], width, along, True),
+            *reducers_scratch(sources, width, along),
             *vector_scratch(vectors.shape, along),
             *exchange_scratch(rows, width, devices),
         ],
@@ -950,12 +947,12 @@
             collective_id=collective, has_side_effects=True, vmem_limit_bytes=VMEM_BYTES
         ),
         name="finish_sums",
-    )(index.reshape(edges // LANES, LANES), messages, grads, vectors, node_part, weight, residual)
+    )(index.reshape(edges // LANES, LANES), messages, edge_grads, node_grads, vectors, node_part, weight, residual)
 
 
 def middle_kernel(
     index, messages, node_low, upstream, w_one, b_one, w_two, b_two, gain, shift, residual,
-    table, node_part, node_out, reduced, reduced_vectors, total, sent, grads, vectors, *refs
+    table, node_part, node_out, grads, vectors, total, sent, *refs
 ):
     at = places()
     count = len(collect_scratch(64, 128, 64))
@@ -964,9 +961,7 @@
     meet_all()
     refs = refs[count:]
     start, one, two, three, end = spread_moves(at, sent, table, *refs[:3])
-    steps, refs = reducers(at, grads, reduced, refs[3:], False)
-    vector_steps = vector_reducer(at, vectors, reduced_vectors, refs[:4])
-    exchange, receive = exchange_moves(residual, node_out, refs[4:])
+    exchange, receive = exchange_moves(residual, node_out, refs[3:])
     load.wait()
     run({})
 
@@ -988,55 +983,30 @@
     grads[:width] = dot_left(node_low[...], third_low)
     grads[width : 2 * width] = dot_left(low, third_low)
     grads[2 * width : 3 * width] = dot_left(act, fourth_low)
-    steps[0]()
     vectors[...] = jnp.zeros_like(vectors)
     vectors[0:1] = jnp.sum(third_low.astype(WIDE), 0, keepdims=True)
     vectors[1:2] = jnp.sum(fourth_low.astype(WIDE), 0, keepdims=True)
     vectors[2:3] = jnp.sum(given * normal, 0, keepdims=True)
     vectors[3:4] = jnp.sum(given, 0, keepdims=True)
-    vector_steps[0]()
     node_part[...] = dot_right(third_low, w_one[:width])
     exchange(normal * gain[...] + shift[...])
 
-    one(0)
-    steps[1]()
-    vector_steps[1]()
-    one(1)
-    one(2)
-    steps[2]()
-    vector_steps[2]()
-    one(3)
-    two(0)
-    steps[3]()
-    vector_steps[3]()
-    two(1)
-    two(2)
-    steps[4]()
-    two(3)
-    steps[5]()
-    three(0)
-    three(1)
-    steps[6]()
-    three(2)
-    three(3)
-    steps[7]()
+    for stage in (one, two, three):
+        for piece in range(PIECES):
+            stage(piece)
     receive()
-    vector_steps[4]()
     end()
-    steps[8]()
-    steps[9]()
     drain()
 
 
 def middle(index, messages, node_low, upstream, w_one, b_one, w_two, b_two, gain, shift, residual, collective):
     rows, width = node_low.shape
     edges = messages.shape[0]
-    along = lax.axis_size("blk") // 2
     devices = lax.axis_size("blk") * lax.axis_size("sub")
     grad_rows = padded_rows(3 * width)
     hold = pl.BlockSpec(memory_space=pltpu.VMEM)
     across = pl.BlockSpec(memory_space=pl.ANY)
-    table, node_part, node_out, reduced, reduced_vectors = pl.pallas_call(
+    table, node_part, node_out, grads, vectors = pl.pallas_call(
         middle_kernel,
         in_specs=[hold, across] + [hold] * 9,
         out_specs=[across] + [hold] * 4,
@@ -1044,18 +1014,14 @@
             jax.ShapeDtypeStruct((3, 4, rows, width), LOW),
             jax.ShapeDtypeStruct((rows, width), WIDE),
             jax.ShapeDtypeStruct(residual.shape, WIDE),
-            jax.ShapeDtypeStruct((grad_rows, width), LOW),
+            jax.ShapeDtypeStruct((grad_rows, width), WIDE),
             jax.ShapeDtypeStruct((8, width), WIDE),
         ],
         scratch_shapes=[
             pltpu.VMEM((rows, width), WIDE),
             pltpu.VMEM((rows, width), LOW),
-            pltpu.VMEM((grad_rows, width), WIDE),
-            pltpu.VMEM((8, width), WIDE),
             *collect_scratch(rows, width, edges),
             *spread_scratch(),
-            *reducers_scratch(grad_rows, width, along, False),
-            *vector_scratch((8, width), along),
             *exchange_scratch(rows, width, devices),
         ],
         compiler_params=pltpu.CompilerParams(
@@ -1066,7 +1032,7 @@
         index.reshape(edges // LANES, LANES), messages, node_low, upstream,
         w_one, b_one, w_two, b_two, gain, shift, residual,
     )
-    return table.reshape(12 * rows, width), node_part, node_out, reduced, reduced_vectors
+    return table.reshape(12 * rows, width), node_part, node_out, grads, vectors
 
 
 def scatter_scratch(channels, nodes, devices):
@@ -1148,7 +1114,7 @@
 
 
 def begin_kernel(
-    shard, later, senders, receivers, own, table, later_out, send_local, recv_wide, held, held_sem, *refs
+    shard, later, senders, receivers, own, table, later_out, send_local, recv_wide, held, held_sem, slab_sems, *refs
 ):
     at = places()
     fetch = pltpu.make_async_copy(later, held, held_sem)
@@ -1165,13 +1131,26 @@
     relative = lax.rem(receivers[...] // (rows * subs) - at["group"] + 1 + groups, groups)
     recv_wide[...] = relative * (rows * subs) + lax.rem(receivers[...], rows * subs)
     fetch.wait()
-    give = pltpu.make_async_copy(held, later_out, held_sem)
-    give.start()
+    devices, _, nodes = later_out.shape
+
+    def slab(k):
+        columns = pl.ds(pl.multiple_of(k * nodes, LANES), nodes)
+        return pltpu.make_async_copy(held.at[:, columns], later_out.at[k], slab_sems.at[k])
+
+    def give(k, carry):
+        slab(k).start()
+        return carry
+
+    def given(k, carry):
+        slab(k).wait()
+        return carry
+
+    lax.fori_loop(0, devices, give, 0)
     drain()
     for stage in (one, two, three):
         for piece in range(PIECES):
             stage(piece)
-    give.wait()
+    lax.fori_loop(0, devices, given, 0)
     end()
 
 
@@ -1189,13 +1168,14 @@
         out_shape=[
             jax.ShapeDtypeStruct((rows, width), LOW),
             jax.ShapeDtypeStruct((3, 4, rows, width), LOW),
-            jax.ShapeDtypeStruct(later.shape, later.dtype),
+            jax.ShapeDtypeStruct((devices, channels, rows), later.dtype),
             jax.ShapeDtypeStruct(lines, jnp.int32),
             jax.ShapeDtypeStruct(lines, jnp.int32),
         ],
         scratch_shapes=[
             pltpu.VMEM(later.shape, later.dtype),
             pltpu.SemaphoreType.DMA,
+            pltpu.SemaphoreType.DMA((devices,)),
             *spread_scratch(),
             *scatter_scratch(channels, rows, devices),
         ],
@@ -1235,26 +1215,27 @@
     node_low, wide_low, cotangent_later, send_local, recv_wide = begin(
         node_input, node_cotangent, senders, receivers, per_device, 0
     )
-    node_upstream = to_nodes(cotangent_later)
+    node_upstream = lax.all_to_all(
+        cotangent_later, ("blk", "sub"), split_axis=0, concat_axis=0, tiled=True
+    ).reshape(width, per_device)
     recv_list = recv_wide.reshape(-1)
     edge_result, first_pre, second_pre, received, messages = edge_forward(
         edge_count, recv_list, send_local, edge_input, wide_low, node_low,
         edge_w_one, edge_b_one[None], edge_w_two, edge_b_two[None], edge_gain[None], edge_shift[None],
     )
-    wide_grad, node_part, node_out, node_summed, node_vectors = middle(
+    wide_grad, node_part, node_out, node_grads, node_vectors = middle(
         recv_list, messages, node_low, node_upstream, node_w_one, node_b_one[None], node_w_two, node_b_two[None],
         node_gain[None], node_shift[None], node_input, 1,
     )
-    edge_grad, messages, grads, vectors, node_part = edge_backward(
+    edge_grad, messages, edge_grads, vectors, node_part = edge_backward(
         edge_count, recv_list, send_local, edge_cotangent, edge_input, received, first_pre, second_pre,
-        wide_grad, node_part, node_low, edge_w_one, edge_w_two,
-        edge_gain[None],
+        wide_grad, node_part, node_low, edge_w_one, edge_w_two, edge_gain[None],
     )
     node_grad, summed, vectors = finish(
-        recv_list, messages, grads, vectors, node_part, edge_w_one, node_cotangent, 3
+        recv_list, messages, edge_grads, node_grads, jnp.concatenate([vectors[:4], node_vectors[:4]]), node_part,
+        edge_w_one, node_cotangent, 3,
     )
     summed = summed.astype(jnp.float32)
-    node_summed = node_summed.astype(jnp.float32)
     return (
         node_out,
         edge_result,
@@ -1262,16 +1243,16 @@
         edge_grad,
         summed[: 3 * width],
         vectors[0],
-        summed[3 * width :],
+        summed[3 * width : 4 * width],
         vectors[1],
         vectors[2],
         vectors[3],
-        node_summed[: 2 * width],
-        node_vectors[0],
-        node_summed[2 * width : 3 * width],
-        node_vectors[1],
-        node_vectors[2],
-        node_vectors[3],
+        summed[4 * width : 6 * width],
+        vectors[4],
+        summed[6 * width : 7 * width],
+        vectors[5],
+        vectors[6],
+        vectors[7],
     )
 
 

time: 355 us -> 343 us (0.966)
  Pallas kernels: 336 us -> 324 us
  local copies, waits for them, and re-layouts: 14.9 us -> 10.9 us
    pallas_call x1, Pallas kernels: 118 us -> 94 us  [middle(): pl.pallas_call(middle_kernel, in_specs=[hold, across] + [hold] * 9, out_s...]
    pallas_call x1, Pallas kernels: 75.4 us -> 88 us  [finish(): pl.pallas_call(finish_kernel, grid=(1,), in_specs=[hold, across, across,...]
  transfers between devices with their start and end apart: 1 -> 1, of which waited for: 0 -> 0; matrix products, arithmetic and copies ran while one was open for 0% -> 0% of each run, Pallas kernels for 10% -> 11%
where the time goes in v11:
time: 343 us; the launch traced here: 340 us
  Pallas kernels  324 us (94%)
  local copies, waits for them, and re-layouts  10.9 us (3%)
    pallas_call x1, Pallas kernels, middle(): pl.pallas_call(middle_kernel, in_specs=[hold, across] + [hold] * 9, out_s...  94 us
    pallas_call x1, Pallas kernels, finish(): pl.pallas_call(finish_kernel, grid=(1,), in_specs=[hold, across, across,...  88 us
    pallas_call x1, Pallas kernels, begin(): pl.pallas_call(begin_kernel, in_specs=[hold, across, hold, hold], out_spe...  55.9 us
    pallas_call x1, Pallas kernels, edge_backward(): pl.pallas_call(backward_kernel, grid=(steps,), in_specs=[scalar, scalar,...  49.5 us
    pallas_call x1, Pallas kernels, edge_forward(): pl.pallas_call(forward_kernel, grid=(steps,), in_specs=[scalar, scalar, h...  36.8 us
  transfers between devices with their start and end apart: 1, of which 0 were waited for; matrix products, arithmetic and copies ran while one was open for 0% of the time, Pallas kernels for 11%

profile of v11, /device:TPU:0, one launch (start us, length us, event | category | flops | bytes accessed | tf_op | source)
XLA Modules:
  0.0 339.8 jit_solution(15346087219288312078)
XLA Ops:
  0.6 55.9 %begin_rows.1 = (bf16[512,512]{1,0:T(8,128)(2,1)}, bf16[3,4,512,512]{3,2,1,0:T(8,128)(2,1)}, f32[32,16,512]{2,1,0:T(8,128)}, s32[36,128]{1,0:T(8,128)}, s32[36,128]{1,0:T(8,128)}) custom-call(f32[16,16384]{1,0:T(8,128)} %residual.2, f32[16,16384]{1,0:T(8,128)} %residual.3, s32[36,128]{1,0:T(8,128)} %bitcast.25, s32[36,128]{1,0:T(8,128)} %bitcast.26), custom_call_target="tpu_custom_call" | custom-call | tf_op jit(solution)/shard_map/begin_rows/pallas_call | solution.py:1164
  56.5 2.7 all-to-all-start
  59.9 36.8 %edge_forward.1 = (f32[4608,512]{1,0:T(8,128)}, f32[4608,512]{1,0:T(8,128)}, f32[4608,512]{1,0:T(8,128)}, bf16[4608,512]{1,0:T(8,128)(2,1)}, bf16[4608,512]{1,0:T(8,128)(2,1)}) custom-call(s32[1]{0:T(128)S(6)} %copy.37.count, s32[4608]{0:T(1024)} %bitcast.23, s32[36,128]{1,0:T(8,128)} %get-tuple-element.40.send, bf16[4608,512]{1,0:T(8,128)(2,1)} %edge.3, ...), custom_call_target="tpu_custom_call" | custom-call | flops 24159191040 | bytes 94371840 | tf_op jit(solution)/shard_map/edge_forward/pallas_call | solution.py:160
  96.7 0.0 all-to-all-done
  96.7 0.0 copy-start.1
  96.7 1.0 copy-done.1
  97.7 94.0 %middle_nodes.1 = (bf16[3,4,512,512]{3,2,1,0:T(8,128)(2,1)}, f32[512,512]{1,0:T(8,128)}, f32[16,16384]{1,0:T(8,128)}, f32[1536,512]{1,0:T(8,128)}, f32[8,512]{1,0:T(8,128)}) custom-call(s32[36,128]{1,0:T(8,128)} %get-tuple-element.39.index, bf16[4608,512]{1,0:T(8,128)(2,1)} %get-tuple-element.43.messages, bf16[512,512]{1,0:T(8,128)(2,1)} %get-tuple-element.42.nodes.node_low, ...), custom_call_target="tpu_custom_call" | custom-call | tf_op jit(solution)/shard_map/middle_nodes/pallas_call | solution.py:1009
  191.7 0.0 copy-start.5
  191.7 49.5 %edge_backward.1 = (f32[4608,512]{1,0:T(8,128)}, bf16[4608,512]{1,0:T(8,128)(2,1)}, f32[2048,512]{1,0:T(8,128)}, f32[8,512]{1,0:T(8,128)}, f32[512,512]{1,0:T(8,128)}) custom-call(s32[1]{0:T(128)S(6)} %copy.37.count, s32[4608]{0:T(1024)} %bitcast.24, s32[36,128]{1,0:T(8,128)} %get-tuple-element.40.send, bf16[4608,512]{1,0:T(8,128)(2,1)} %cotangent.1, ...), custom_call_target="tpu_custom_call" | custom-call | flops 28991029248 | bytes 94371840 | tf_op jit(solution)/shard_map/edge_backward/pallas_call | solution.py:266
  241.3 0.7 slice.42
  242.0 0.0 copy-done.5
  242.0 0.6 pad_maximum_fusion.vectors
  242.6 88.0 %finish_sums.1 = (f32[16,16384]{1,0:T(8,128)}, bf16[3584,512]{1,0:T(8,128)(2,1)}, f32[8,512]{1,0:T(8,128)}) custom-call(s32[36,128]{1,0:T(8,128)} %get-tuple-element.39.index, bf16[4608,512]{1,0:T(8,128)(2,1)} %get-tuple-element.52.messages, f32[2048,512]{1,0:T(8,128)} %get-tuple-element.53.edge_grads, f32[1536,512]{1,0:T(8,128)} %get-tuple-element.54.node_grads, ...), custom_call_target="tpu_custom_call" | custom-call | tf_op jit(solution)/shard_map/finish_sums/pallas_call | solution.py:927
  330.6 0.0 copy-start
  330.6 3.0 slice.58
  333.6 0.0 copy-done
  333.6 0.0 copy-start.4
  333.6 0.0 copy-start.2
  333.6 1.6 fusion
  335.2 0.0 copy-start.3
  335.2 2.1 slice.56
  337.3 0.0 copy-done.4
  337.3 0.6 fusion.1
  337.9 0.0 copy-done.2
  337.9 1.0 copy.38
  338.9 0.0 copy-done.3
  338.9 1.0 copy.39
  (1 shorter events, 0.0 us)
Async XLA Ops:
  56.5 40.1 %all-to-all-start = ((f32[32,16,512]{2,1,0:T(8,128)}), f32[32,16,512]{2,1,0:T(8,128)S(1)}, u32[]{:S(2)}, u32[]{:S(2)}) async-start(f32[32,16,512]{2,1,0:T(8,128)} %get-tuple-element.44), calls=%async_computation | async-start | bytes 2097152 | tf_op jit(solution)/shard_map/all_to_all | solution.py:1218
  96.7 1.0 copy-start.1
  191.7 50.3 %copy-start.5 = (f32[8,512]{1,0:T(8,128)S(1)}, f32[8,512]{1,0:T(8,128)}, u32[]{:S(2)}) copy-start(f32[8,512]{1,0:T(8,128)} %get-tuple-element.56) | copy-start | bytes 49156
  330.6 3.0 copy-start
  333.6 3.7 %copy-start.4 = (f32[8,512]{1,0:T(8,128)S(1)}, f32[8,512]{1,0:T(8,128)}, u32[]{:S(2)}) copy-start(f32[8,512]{1,0:T(8,128)} %get-tuple-element.61) | copy-start | bytes 49156
  333.6 4.3 %copy-start.2 = (f32[16,16384]{1,0:T(8,128)S(1)}, f32[16,16384]{1,0:T(8,128)}, u32[]{:S(2)}) copy-start(f32[16,16384]{1,0:T(8,128)} %get-tuple-element.88) | copy-start | bytes 3145732
  335.2 3.7 %copy-start.3 = (f32[16,16384]{1,0:T(8,128)S(1)}, f32[16,16384]{1,0:T(8,128)}, u32[]{:S(2)}) copy-start(f32[16,16384]{1,0:T(8,128)} %get-tuple-element.90) | copy-start | bytes 3145732

commit v12 on v11

--- a/solution.py
+++ b/solution.py
@@ -56,14 +56,15 @@
     def fetch(i, slot):
         return pltpu.make_async_copy(wide.at[pl.ds(i * CHUNK, CHUNK)], stage.at[slot], sems.at[slot])
 
-    fetch(0, 0).start()
+    for i in range(3):
+        fetch(i, i).start()
 
     def body(i, carry):
-        slot = lax.rem(i, 2)
-
-        @pl.when(i + 1 < steps)
+        slot = lax.rem(i, 4)
+
+        @pl.when(i + 3 < steps)
         def _():
-            fetch(i + 1, 1 - slot).start()
+            fetch(i + 3, lax.rem(i + 3, 4)).start()
 
         fetch(i, slot).wait()
 
@@ -90,6 +91,12 @@
         return carry
 
     lax.fori_loop(0, count // 16, body, 0)
+
+
+def gather_inline(index, base, table, rows, parts):
+    for slot in range(rows.shape[0] // parts):
+        place = index[base + slot]
+        rows[slot * parts : (slot + 1) * parts, :] = table[pl.ds(pl.multiple_of(place * parts, parts), parts), :]
 
 
 def row_normal(values):
@@ -113,10 +120,12 @@
     @pl.when(step == 0)
     def _():
         load_table(wide, table, stage, sems)
-
-    gather_rows(recv, base, table, rows, parts)
-    from_recv = read_rows(rows, 0, TILE, parts).astype(jnp.bfloat16)
-    received[...] = from_recv
+        gather_rows(recv, base, table, rows, parts)
+
+    later = jnp.where(step + 1 < pl.num_programs(0), base + TILE, 0)
+    received[...] = read_rows(rows, 0, TILE, parts).astype(jnp.bfloat16)
+    gather_inline(recv, later, table, rows, parts)
+    from_recv = received[...]
     lane = lax.broadcasted_iota(jnp.int32, (LANES, LANES), 1)
     chosen = []
     for i in range(TILE // LANES):
@@ -175,8 +184,8 @@
         scratch_shapes=[
             pltpu.VMEM((wide.shape[0] * parts, LANES), jnp.float32),
             pltpu.VMEM((TILE * parts, LANES), jnp.float32),
-            pltpu.VMEM((2, CHUNK, width), jnp.bfloat16),
-            pltpu.SemaphoreType.DMA((2,)),
+            pltpu.VMEM((4, CHUNK, width), jnp.bfloat16),
+            pltpu.SemaphoreType.DMA((4,)),
         ],
         compiler_params=pltpu.CompilerParams(vmem_limit_bytes=VMEM_BYTES),
         cost_estimate=pl.CostEstimate(
@@ -202,10 +211,13 @@
         grads[...] = jnp.zeros_like(grads)
         vectors[...] = jnp.zeros_like(vectors)
         by_sender[...] = jnp.zeros_like(by_sender)
-
-    gather_rows(recv, base, table, rows, parts)
+        gather_rows(recv, base, table, rows, parts)
+
     live = base + lax.broadcasted_iota(jnp.int32, (TILE, 1), 0) < count[0]
     upstream = cotangent[...].astype(jnp.float32) + jnp.where(live, read_rows(rows, 0, TILE, parts), 0.0)
+    grad[...] = upstream
+    later = jnp.where(step + 1 < pl.num_programs(0), base + TILE, 0)
+    gather_inline(recv, later, table, rows, parts)
     masked = jnp.where(live, upstream, 0.0)
     normal, scale = row_normal(second[...])
     vectors[2:3, :] += jnp.sum(masked * normal, 0, keepdims=True)
@@ -234,7 +246,7 @@
         axis=1,
     )
     by_sender[...] += dot(chosen, first_low)
-    grad[...] = upstream + dot_right(first_low, w_one[:width])
+    grad[...] += dot_right(first_low, w_one[:width])
 
     @pl.when(step == pl.num_programs(0) - 1)
     def _():
@@ -283,8 +295,8 @@
         scratch_shapes=[
             pltpu.VMEM((wide.shape[0] * parts, LANES), jnp.float32),
             pltpu.VMEM((TILE * parts, LANES), jnp.float32),
-            pltpu.VMEM((2, CHUNK, width), jnp.bfloat16),
-            pltpu.SemaphoreType.DMA((2,)),
+            pltpu.VMEM((4, CHUNK, width), jnp.bfloat16),
+            pltpu.SemaphoreType.DMA((4,)),
             pltpu.VMEM((per_device, width), jnp.float32),
             pltpu.VMEM((4 * width, width), jnp.float32),
             pltpu.SemaphoreType.DMA,
@@ -302,7 +314,7 @@
 
 MESH = pl.DeviceIdType.MESH
 PIECES = 4
-SPLIT = False
+SPLIT = True
 LOW = jnp.bfloat16
 WIDE = jnp.float32
 
@@ -885,7 +897,7 @@
 
 def finish_kernel(
     index, messages, edge_grads, node_grads, vectors, node_part, weight, residual,
-    node_grad, reduced, reduced_vectors, total, *refs,
+    node_grad, one_out, two_out, three_out, four_out, reduced_vectors, total, reduced, out_sems, *refs,
 ):
     at = places()
     count = len(collect_scratch(64, 128, 64))
@@ -901,19 +913,31 @@
     run({
         1: [steps[1], vector_steps[1]],
         4: [steps[2], vector_steps[2]],
-        6: [steps[3], vector_steps[3]],
-        8: [steps[4]],
-        10: [steps[5]],
+        7: [steps[3], vector_steps[3]],
+        10: [steps[4]],
     })
+    steps[5]()
     high, rest = split_low(total[...])
     exchange(node_part[...] + dot_right(high, weight[...]) + dot_right(rest, weight[...]))
-    for step in steps[6:8]:
-        step()
+    steps[6]()
+    steps[7]()
     receive()
     steps[8]()
+    width = total.shape[1]
+    nodes_at = edge_grads.shape[0]
+    copies = [
+        pltpu.make_async_copy(reduced.at[pl.ds(first, target.shape[0])], target, out_sems.at[i])
+        for i, (first, target) in enumerate((
+            (0, one_out), (3 * width, two_out), (nodes_at, three_out), (nodes_at + 2 * width, four_out)
+        ))
+    ]
+    for copy in copies:
+        copy.start()
     vector_steps[4]()
     drain()
     steps[9]()
+    for copy in copies:
+        copy.wait()
 
 
 def finish(index, messages, edge_grads, node_grads, vectors, node_part, weight, residual, collective):
@@ -930,14 +954,19 @@
         in_specs=[
             hold, across, across, across, hold, hold, pl.BlockSpec((width, width), lambda i: (2, 0)), hold,
         ],
-        out_specs=[hold] * 3,
+        out_specs=[hold] + [across] * 4 + [hold],
         out_shape=[
             jax.ShapeDtypeStruct(residual.shape, WIDE),
-            jax.ShapeDtypeStruct((sum(sources), width), LOW),
+            jax.ShapeDtypeStruct((3 * width, width), LOW),
+            jax.ShapeDtypeStruct((width, width), LOW),
+            jax.ShapeDtypeStruct((2 * width, width), LOW),
+            jax.ShapeDtypeStruct((width, width), LOW),
             jax.ShapeDtypeStruct(vectors.shape, WIDE),
         ],
         scratch_shapes=[
             pltpu.VMEM((rows, width), WIDE),
+            pltpu.VMEM((sum(sources), width), LOW),
+            pltpu.SemaphoreType.DMA((4,)),
             *collect_scratch(rows, width, edges),
             *reducers_scratch(sources, width, along),
             *vector_scratch(vectors.shape, along),
@@ -1231,25 +1260,25 @@
         edge_count, recv_list, send_local, edge_cotangent, edge_input, received, first_pre, second_pre,
         wide_grad, node_part, node_low, edge_w_one, edge_w_two, edge_gain[None],
     )
-    node_grad, summed, vectors = finish(
+    node_grad, *summed, vectors = finish(
         recv_list, messages, edge_grads, node_grads, jnp.concatenate([vectors[:4], node_vectors[:4]]), node_part,
         edge_w_one, node_cotangent, 3,
     )
-    summed = summed.astype(jnp.float32)
+    summed = [item.astype(jnp.float32) for item in summed]
     return (
         node_out,
         edge_result,
         node_grad,
         edge_grad,
-        summed[: 3 * width],
+        summed[0],
         vectors[0],
-        summed[3 * width : 4 * width],
+        summed[1],
         vectors[1],
         vectors[2],
         vectors[3],
-        summed[4 * width : 6 * width],
+        summed[2],
         vectors[4],
-        summed[6 * width : 7 * width],
+        summed[3],
         vectors[5],
         vectors[6],
         vectors[7],

time: 343 us -> 324 us (0.945)
  Pallas kernels: 324 us -> 304 us
  other arithmetic: 0.61 us -> 10 us
  local copies, waits for them, and re-layouts: 10.9 us -> 5.27 us
    convert_element_type x0 -> x4, other arithmetic: none -> 9.4 us  [shards(): summed = [item.astype(jnp.float32) for item in summed]]
    pallas_call x1, Pallas kernels: 36.8 us -> 27.6 us  [edge_forward(): pl.pallas_call(forward_kernel, grid=(steps,), in_specs=[scalar, scalar, h...]
    pallas_call x1, Pallas kernels: 49.5 us -> 41.2 us  [edge_backward(): pl.pallas_call(backward_kernel, grid=(steps,), in_specs=[scalar, scalar,...]
    slice x3 -> x0, local copies, waits for them, and re-layouts: 6.69 us -> none  [the longest x1 2.99 us: shards(): summed[4 * width:6 * width]]
  transfers between devices with their start and end apart: 1 -> 1, of which waited for: 0 -> 0; matrix products, arithmetic and copies ran while one was open for 0% -> 0% of each run, Pallas kernels for 11% -> 9%
where the time goes in v12:
time: 324 us
  Pallas kernels  304 us (94%)
  other arithmetic  10 us (3%)
  local copies, waits for them, and re-layouts  5.27 us (2%)
    pallas_call x1, Pallas kernels, middle(): pl.pallas_call(middle_kernel, in_specs=[hold, across] + [hold] * 9, out_s...  94 us
    pallas_call x1, Pallas kernels, finish(): pl.pallas_call(finish_kernel, grid=(1,), in_specs=[hold, across, across,...  85.6 us
    pallas_call x1, Pallas kernels, begin(): pl.pallas_call(begin_kernel, in_specs=[hold, across, hold, hold], out_spe...  55.9 us
    pallas_call x1, Pallas kernels, edge_backward(): pl.pallas_call(backward_kernel, grid=(steps,), in_specs=[scalar, scalar,...  41.2 us
    pallas_call x1, Pallas kernels, edge_forward(): pl.pallas_call(forward_kernel, grid=(steps,), in_specs=[scalar, scalar, h...  27.6 us
    convert_element_type x4, other arithmetic, shards(): summed = [item.astype(jnp.float32) for item in summed]  9.4 us
  transfers between devices with their start and end apart: 1, of which 0 were waited for; matrix products, arithmetic and copies ran while one was open for 0% of the time, Pallas kernels for 9%

profile of v12, /device:TPU:0, one launch (start us, length us, event | category | flops | bytes accessed | tf_op | source)
XLA Modules:
  0.0 323.7 jit_solution(4025427775119934251)
XLA Ops:
  0.6 55.9 %begin_rows.1 = (bf16[512,512]{1,0:T(8,128)(2,1)}, bf16[3,4,512,512]{3,2,1,0:T(8,128)(2,1)}, f32[32,16,512]{2,1,0:T(8,128)}, s32[36,128]{1,0:T(8,128)}, s32[36,128]{1,0:T(8,128)}) custom-call(f32[16,16384]{1,0:T(8,128)} %residual.2, f32[16,16384]{1,0:T(8,128)} %residual.3, s32[36,128]{1,0:T(8,128)} %bitcast.25, s32[36,128]{1,0:T(8,128)} %bitcast.26), custom_call_target="tpu_custom_call" | custom-call | tf_op jit(solution)/shard_map/begin_rows/pallas_call | solution.py:1193
  56.6 2.7 all-to-all-start
  59.9 27.6 %edge_forward.1 = (f32[4608,512]{1,0:T(8,128)}, f32[4608,512]{1,0:T(8,128)}, f32[4608,512]{1,0:T(8,128)}, bf16[4608,512]{1,0:T(8,128)(2,1)}, bf16[4608,512]{1,0:T(8,128)(2,1)}) custom-call(s32[1]{0:T(128)S(6)} %copy.37.count, s32[4608]{0:T(1024)} %bitcast.23, s32[36,128]{1,0:T(8,128)} %get-tuple-element.43.send, bf16[4608,512]{1,0:T(8,128)(2,1)} %edge.3, ...), custom_call_target="tpu_custom_call" | custom-call | flops 24159191040 | bytes 94371840 | tf_op jit(solution)/shard_map/edge_forward/pallas_call | solution.py:169
  87.4 0.0 all-to-all-done
  87.5 0.0 copy-start
  87.5 1.0 copy-done
  88.4 94.0 %middle_nodes.1 = (bf16[3,4,512,512]{3,2,1,0:T(8,128)(2,1)}, f32[512,512]{1,0:T(8,128)}, f32[16,16384]{1,0:T(8,128)}, f32[1536,512]{1,0:T(8,128)}, f32[8,512]{1,0:T(8,128)}) custom-call(s32[36,128]{1,0:T(8,128)} %get-tuple-element.42.index, bf16[4608,512]{1,0:T(8,128)(2,1)} %get-tuple-element.46.messages, bf16[512,512]{1,0:T(8,128)(2,1)} %get-tuple-element.45.nodes.node_low, ...), custom_call_target="tpu_custom_call" | custom-call | tf_op jit(solution)/shard_map/middle_nodes/pallas_call | solution.py:1038
  182.4 0.0 copy-start.4
  182.5 41.2 %edge_backward.1 = (f32[4608,512]{1,0:T(8,128)}, bf16[4608,512]{1,0:T(8,128)(2,1)}, f32[2048,512]{1,0:T(8,128)}, f32[8,512]{1,0:T(8,128)}, f32[512,512]{1,0:T(8,128)}) custom-call(s32[1]{0:T(128)S(6)} %copy.37.count, s32[4608]{0:T(1024)} %bitcast.24, s32[36,128]{1,0:T(8,128)} %get-tuple-element.43.send, bf16[4608,512]{1,0:T(8,128)(2,1)} %cotangent.1, ...), custom_call_target="tpu_custom_call" | custom-call | flops 28991029248 | bytes 94371840 | tf_op jit(solution)/shard_map/edge_backward/pallas_call | solution.py:278
  223.7 0.7 slice.30
  224.4 0.0 copy-done.4
  224.4 0.6 pad_maximum_fusion.vectors
  225.1 85.6 %finish_sums.1 = (f32[16,16384]{1,0:T(8,128)}, bf16[1536,512]{1,0:T(8,128)(2,1)}, bf16[512,512]{1,0:T(8,128)(2,1)}, bf16[1024,512]{1,0:T(8,128)(2,1)}, bf16[512,512]{1,0:T(8,128)(2,1)}, /*index=5*/f32[8,512]{1,0:T(8,128)}) custom-call(s32[36,128]{1,0:T(8,128)} %get-tuple-element.42.index, bf16[4608,512]{1,0:T(8,128)(2,1)} %get-tuple-element.55.messages, ...), custom_call_target="tpu_custom_call" | custom-call | tf_op jit(solution)/shard_map/finish_sums/pallas_call | solution.py:951
  310.7 0.0 copy-start.1
  310.7 1.6 fusion
  312.3 2.1 convert_element_type.13
  314.5 0.0 copy-start.2
  314.5 2.2 convert_element_type.15
  316.7 0.0 copy-start.3
  316.7 2.9 convert_element_type.14
  319.6 0.0 copy-done.1
  319.6 2.1 convert_element_type.12
  321.7 0.0 copy-done.2
  321.8 1.0 copy.38
  322.7 0.0 copy-done.3
  322.7 1.0 copy.39
  (1 shorter events, 0.0 us)
Async XLA Ops:
  56.6 30.9 %all-to-all-start = ((f32[32,16,512]{2,1,0:T(8,128)}), f32[32,16,512]{2,1,0:T(8,128)S(1)}, u32[]{:S(2)}, u32[]{:S(2)}) async-start(f32[32,16,512]{2,1,0:T(8,128)} %get-tuple-element.47), calls=%async_computation | async-start | bytes 2097152 | tf_op jit(solution)/shard_map/all_to_all | solution.py:1247
  87.5 1.0 copy-start
  182.4 42.0 %copy-start.4 = (f32[8,512]{1,0:T(8,128)S(1)}, f32[8,512]{1,0:T(8,128)}, u32[]{:S(2)}) copy-start(f32[8,512]{1,0:T(8,128)} %get-tuple-element.59) | copy-start | bytes 49156
  310.7 8.9 %copy-start.1 = (bf16[1536,512]{1,0:T(8,128)(2,1)S(1)}, bf16[1536,512]{1,0:T(8,128)(2,1)}, u32[]{:S(2)}) copy-start(bf16[1536,512]{1,0:T(8,128)(2,1)} %get-tuple-element.63) | copy-start | bytes 4718596
  314.5 7.3 %copy-start.2 = (f32[16,16384]{1,0:T(8,128)S(1)}, f32[16,16384]{1,0:T(8,128)}, u32[]{:S(2)}) copy-start(f32[16,16384]{1,0:T(8,128)} %get-tuple-element.92) | copy-start | bytes 3145732
  316.7 6.0 %copy-start.3 = (f32[16,16384]{1,0:T(8,128)S(1)}, f32[16,16384]{1,0:T(8,128)}, u32[]{:S(2)}) copy-start(f32[16,16384]{1,0:T(8,128)} %get-tuple-element.94) | copy-start | bytes 3145732

commit v13 on v12

--- a/solution.py
+++ b/solution.py
@@ -1,3 +1,4 @@
+import functools
 import math
 
 import jax
@@ -196,7 +197,7 @@
 
 
 def backward_kernel(
-    count, recv, send, cotangent, edge, received, first, second, wide, node_part, nodes, w_one, w_two, gain,
+    count, recv, send, cotangent, edge, received, first, second, wide, node_part, node_vectors, nodes, w_one, w_two, gain,
     grad, message, all_grads, vectors, sender_grad,
     table, rows, stage, sems, by_sender, grads, give_sem,
 ):
@@ -209,7 +210,7 @@
     def _():
         load_table(wide, table, stage, sems)
         grads[...] = jnp.zeros_like(grads)
-        vectors[...] = jnp.zeros_like(vectors)
+        vectors[...] = node_vectors[...]
         by_sender[...] = jnp.zeros_like(by_sender)
         gather_rows(recv, base, table, rows, parts)
 
@@ -260,7 +261,8 @@
 
 
 def edge_backward(
-    count, recv, send, cotangent, edge, received, first, second, wide, node_part, nodes, w_one, w_two, gain
+    count, recv, send, cotangent, edge, received, first, second, wide, node_part, node_vectors, nodes,
+    w_one, w_two, gain,
 ):
     edges, width = edge.shape
     steps = edges // TILE
@@ -280,7 +282,7 @@
         grid=(steps,),
         in_specs=[
             scalar, scalar, hold, tile, tile, tile, tile, tile,
-            across, hold, hold, hold, hold, hold,
+            across, hold, hold, hold, hold, hold, hold,
         ],
         out_specs=[
             tile, tile, across, whole(8), whole(per_device),
@@ -308,7 +310,7 @@
         name="edge_backward",
     )(
         count, recv, send, cotangent, edge, received, first, second, wide,
-        node_part, nodes, w_one, w_two, gain,
+        node_part, node_vectors, nodes, w_one, w_two, gain,
     )
 
 
@@ -621,6 +623,8 @@
             8: ((near, partner), (near, partner), to_sibling),
             9: ((far, sub), (far, sub), to_sibling),
             10: ((far, partner), (far, partner), to_sibling),
+            11: ((near, sub), (near, sub), to_partner),
+            12: ((far, sub), (far, sub), to_partner),
         }[kind]
         source = own if source is None else table.at[source[0], source[1]]
         rows = pl.ds(piece * size, size)
@@ -642,20 +646,31 @@
         for kind in kinds:
             move(kind, piece).start()
 
+    straight = range(PIECES - 1)
+
     def one(piece):
-        relay(0, (3, 4), piece)
-        relay(1, (5, 6), piece)
+        relay(0, (3, 4) if piece in straight else (4,), piece)
+        relay(1, (5, 6) if piece in straight else (5, 6, 11), piece)
 
     def two(piece):
-        relay(3, (7, 8), piece)
-        relay(5, (9,), piece)
+        if piece in straight:
+            relay(3, (7, 8), piece)
+            relay(5, (9,), piece)
+        else:
+            relay(5, (9, 12), piece)
+            relay(11, (8,), piece)
 
     def three(piece):
-        relay(7, (10,), piece)
+        if piece in straight:
+            relay(7, (10,), piece)
+        else:
+            relay(12, (10,), piece)
 
     def drain():
-        for kind in range(11):
+        for kind in range(13):
             for piece in range(PIECES):
+                if kind in ((11, 12) if piece in straight else (3, 7)):
+                    continue
                 if kind in (2, 4, 6, 8, 9, 10):
                     move(kind, piece).wait_recv()
                 move(kind, piece).wait_send()
@@ -667,8 +682,8 @@
 def spread_scratch():
     return [
         pltpu.SemaphoreType.DMA,
-        pltpu.SemaphoreType.DMA((11, PIECES)),
-        pltpu.SemaphoreType.DMA((11, PIECES)),
+        pltpu.SemaphoreType.DMA((13, PIECES)),
+        pltpu.SemaphoreType.DMA((13, PIECES)),
     ]
 
 
@@ -1013,10 +1028,10 @@
     grads[width : 2 * width] = dot_left(low, third_low)
     grads[2 * width : 3 * width] = dot_left(act, fourth_low)
     vectors[...] = jnp.zeros_like(vectors)
-    vectors[0:1] = jnp.sum(third_low.astype(WIDE), 0, keepdims=True)
-    vectors[1:2] = jnp.sum(fourth_low.astype(WIDE), 0, keepdims=True)
-    vectors[2:3] = jnp.sum(given * normal, 0, keepdims=True)
-    vectors[3:4] = jnp.sum(given, 0, keepdims=True)
+    vectors[4:5] = jnp.sum(third_low.astype(WIDE), 0, keepdims=True)
+    vectors[5:6] = jnp.sum(fourth_low.astype(WIDE), 0, keepdims=True)
+    vectors[6:7] = jnp.sum(given * normal, 0, keepdims=True)
+    vectors[7:8] = jnp.sum(given, 0, keepdims=True)
     node_part[...] = dot_right(third_low, w_one[:width])
     exchange(normal * gain[...] + shift[...])
 
@@ -1214,6 +1229,33 @@
         name="begin_rows",
     )(shard, later, senders.reshape(lines), receivers.reshape(lines))
     return own, table.reshape(12 * rows, width), later, send_local, recv_wide
+
+
+def release_kernel(count, *refs):
+    for source, target in zip(refs[:count], refs[count:]):
+        target[...] = source[...].astype(target.dtype)
+
+
+def release(whole, reduced):
+    arrays = [*whole, *reduced]
+    steps = 4
+
+    def spec(item, kept):
+        rows, columns = item.shape
+        if kept:
+            return pl.BlockSpec((rows, columns // steps), lambda i: (0, i))
+        return pl.BlockSpec((rows // steps, columns), lambda i: (i, 0))
+
+    specs = [spec(item, i < len(whole)) for i, item in enumerate(arrays)]
+    return pl.pallas_call(
+        functools.partial(release_kernel, len(arrays)),
+        grid=(steps,),
+        in_specs=specs,
+        out_specs=specs,
+        out_shape=[jax.ShapeDtypeStruct(item.shape, WIDE) for item in arrays],
+        compiler_params=pltpu.CompilerParams(vmem_limit_bytes=VMEM_BYTES),
+        name="release_results",
+    )(*arrays)
 
 
 def shards(
@@ -1258,13 +1300,12 @@
     )
     edge_grad, messages, edge_grads, vectors, node_part = edge_backward(
         edge_count, recv_list, send_local, edge_cotangent, edge_input, received, first_pre, second_pre,
-        wide_grad, node_part, node_low, edge_w_one, edge_w_two, edge_gain[None],
+        wide_grad, node_part, node_vectors, node_low, edge_w_one, edge_w_two, edge_gain[None],
     )
     node_grad, *summed, vectors = finish(
-        recv_list, messages, edge_grads, node_grads, jnp.concatenate([vectors[:4], node_vectors[:4]]), node_part,
-        edge_w_one, node_cotangent, 3,
-    )
-    summed = [item.astype(jnp.float32) for item in summed]
+        recv_list, messages, edge_grads, node_grads, vectors, node_part, edge_w_one, node_cotangent, 3
+    )
+    node_out, node_grad, *summed = release((node_out, node_grad), summed)
     return (
         node_out,
         edge_result,

time: 324 us -> 313 us (0.966)
  other arithmetic: 10 us -> 0 us
    convert_element_type x4 -> x0, other arithmetic: 9.4 us -> none  [shards(): summed = [item.astype(jnp.float32) for item in summed]]
    pallas_call x0 -> x1, Pallas kernels: none -> 6.46 us  [release(): pl.pallas_call(functools.partial(release_kernel, len(arrays)), grid=(step...]
where the time goes in v13:
time: 313 us; the launch traced here: 312 us
  Pallas kernels  306 us (98%)
    pallas_call x1, Pallas kernels, middle(): pl.pallas_call(middle_kernel, in_specs=[hold, across] + [hold] * 9, out_s...  91.5 us
    pallas_call x1, Pallas kernels, finish(): pl.pallas_call(finish_kernel, grid=(1,), in_specs=[hold, across, across,...  85.2 us
    pallas_call x1, Pallas kernels, begin(): pl.pallas_call(begin_kernel, in_specs=[hold, across, hold, hold], out_spe...  53.4 us
    pallas_call x1, Pallas kernels, edge_backward(): pl.pallas_call(backward_kernel, grid=(steps,), in_specs=[scalar, scalar,...  41.4 us
    pallas_call x1, Pallas kernels, edge_forward(): pl.pallas_call(forward_kernel, grid=(steps,), in_specs=[scalar, scalar, h...  27.6 us
    pallas_call x1, Pallas kernels, release(): pl.pallas_call(functools.partial(release_kernel, len(arrays)), grid=(step...  6.46 us
  transfers between devices with their start and end apart: 1, of which 0 were waited for; matrix products, arithmetic and copies ran while one was open for 0% of the time, Pallas kernels for 9%

profile of v13, /device:TPU:0, one launch (start us, length us, event | category | flops | bytes accessed | tf_op | source)
XLA Modules:
  0.0 312.3 jit_solution(14917970518066989174)
XLA Ops:
  0.6 53.4 %begin_rows.1 = (bf16[512,512]{1,0:T(8,128)(2,1)}, bf16[3,4,512,512]{3,2,1,0:T(8,128)(2,1)}, f32[32,16,512]{2,1,0:T(8,128)}, s32[36,128]{1,0:T(8,128)}, s32[36,128]{1,0:T(8,128)}) custom-call(f32[16,16384]{1,0:T(8,128)} %residual.2, f32[16,16384]{1,0:T(8,128)} %residual.3, s32[36,128]{1,0:T(8,128)} %bitcast.25, s32[36,128]{1,0:T(8,128)} %bitcast.26), custom_call_target="tpu_custom_call" | custom-call | tf_op jit(solution)/shard_map/begin_rows/pallas_call | solution.py:1208
  54.1 2.7 all-to-all-start
  57.4 27.6 %edge_forward.1 = (f32[4608,512]{1,0:T(8,128)}, f32[4608,512]{1,0:T(8,128)}, f32[4608,512]{1,0:T(8,128)}, bf16[4608,512]{1,0:T(8,128)(2,1)}, bf16[4608,512]{1,0:T(8,128)(2,1)}) custom-call(s32[1]{0:T(128)S(6)} %copy.35.count, s32[4608]{0:T(1024)} %bitcast.23, s32[36,128]{1,0:T(8,128)} %get-tuple-element.49.send, bf16[4608,512]{1,0:T(8,128)(2,1)} %edge.3, ...), custom_call_target="tpu_custom_call" | custom-call | flops 24159191040 | bytes 94371840 | tf_op jit(solution)/shard_map/edge_forward/pallas_call | solution.py:170
  84.9 0.0 all-to-all-done
  85.0 0.0 copy-start
  85.0 1.0 copy-done
  85.9 91.5 %middle_nodes.1 = (bf16[3,4,512,512]{3,2,1,0:T(8,128)(2,1)}, f32[512,512]{1,0:T(8,128)}, f32[16,16384]{1,0:T(8,128)}, f32[1536,512]{1,0:T(8,128)}, f32[8,512]{1,0:T(8,128)}) custom-call(s32[36,128]{1,0:T(8,128)} %get-tuple-element.48.index, bf16[4608,512]{1,0:T(8,128)(2,1)} %get-tuple-element.52.messages, bf16[512,512]{1,0:T(8,128)(2,1)} %get-tuple-element.51.nodes.node_low, ...), custom_call_target="tpu_custom_call" | custom-call | tf_op jit(solution)/shard_map/middle_nodes/pallas_call | solution.py:1053
  177.5 41.4 %edge_backward.1 = (f32[4608,512]{1,0:T(8,128)}, bf16[4608,512]{1,0:T(8,128)(2,1)}, f32[2048,512]{1,0:T(8,128)}, f32[8,512]{1,0:T(8,128)}, f32[512,512]{1,0:T(8,128)}) custom-call(s32[1]{0:T(128)S(6)} %copy.35.count, s32[4608]{0:T(1024)} %bitcast.24, s32[36,128]{1,0:T(8,128)} %get-tuple-element.49.send, bf16[4608,512]{1,0:T(8,128)(2,1)} %cotangent.1, ...), custom_call_target="tpu_custom_call" | custom-call | flops 28991029248 | bytes 94371840 | tf_op jit(solution)/shard_map/edge_backward/pallas_call | solution.py:280
  218.9 85.2 %finish_sums.1 = (f32[16,16384]{1,0:T(8,128)}, bf16[1536,512]{1,0:T(8,128)(2,1)}, bf16[512,512]{1,0:T(8,128)(2,1)}, bf16[1024,512]{1,0:T(8,128)(2,1)}, bf16[512,512]{1,0:T(8,128)(2,1)}, /*index=5*/f32[8,512]{1,0:T(8,128)}) custom-call(s32[36,128]{1,0:T(8,128)} %get-tuple-element.48.index, bf16[4608,512]{1,0:T(8,128)(2,1)} %get-tuple-element.61.messages, ...), custom_call_target="tpu_custom_call" | custom-call | tf_op jit(solution)/shard_map/finish_sums/pallas_call | solution.py:966
  304.1 1.6 fusion
  305.7 6.5 %release_results.1 = (f32[16,16384]{1,0:T(8,128)}, f32[16,16384]{1,0:T(8,128)}, f32[1536,512]{1,0:T(8,128)}, f32[512,512]{1,0:T(8,128)}, f32[1024,512]{1,0:T(8,128)}, /*index=5*/f32[512,512]{1,0:T(8,128)}) custom-call(f32[16,16384]{1,0:T(8,128)} %get-tuple-element.54.refs_0_, f32[16,16384]{1,0:T(8,128)} %get-tuple-element.66.refs_1_, ...), custom_call_target="tpu_custom_call" | custom-call | tf_op jit(solution)/shard_map/release_results/pallas_call | solution.py:1250
Async XLA Ops:
  54.1 30.9 %all-to-all-start = ((f32[32,16,512]{2,1,0:T(8,128)}), f32[32,16,512]{2,1,0:T(8,128)S(1)}, u32[]{:S(2)}, u32[]{:S(2)}) async-start(f32[32,16,512]{2,1,0:T(8,128)} %get-tuple-element.53), calls=%async_computation | async-start | bytes 2097152 | tf_op jit(solution)/shard_map/all_to_all | solution.py:1289
  85.0 1.0 copy-start

commit v14 on v13

--- a/solution.py
+++ b/solution.py
@@ -412,7 +412,7 @@
     for i, (which, start, rows) in enumerate(streams_of([source.shape[0] for source in sources])):
         first = start + sum(source.shape[0] for source in sources[:which])
         made.append(reducer(at, sources[which], start, reduced, first, rows, i % 2 > 0, refs[i * 13 : i * 13 + 13]))
-    return both(made), refs[len(made) * 13 :]
+    return made, refs[len(made) * 13 :]
 
 
 def reducer_scratch(rows, width, along):
@@ -597,10 +597,6 @@
             move(k).wait_send()
 
     return [start, turn(0), turn(1), turn(2), last]
-
-
-def both(streams):
-    return [lambda steps=steps: [step() for step in steps] for steps in zip(*streams)]
 
 
 def spread_moves(at, own, table, keep_sem, send_sems, recv_sems):
@@ -919,25 +915,35 @@
     load, run, drain = collect_moves(at, index, messages, total, refs[:count])
     load.start()
     meet_all()
-    steps, refs = reducers(at, (edge_grads, node_grads), reduced, refs[count:])
+    streams, refs = reducers(at, (edge_grads, node_grads), reduced, refs[count:])
     vector_steps = vector_reducer(at, vectors, reduced_vectors, refs[:4])
     exchange, receive = exchange_moves(residual, node_grad, refs[4:])
-    steps[0]()
+    for stream in streams:
+        stream[0]()
     vector_steps[0]()
     load.wait()
-    run({
-        1: [steps[1], vector_steps[1]],
-        4: [steps[2], vector_steps[2]],
-        7: [steps[3], vector_steps[3]],
-        10: [steps[4]],
-    })
-    steps[5]()
+    timetable = (
+        (0, 1, (0,)), (1, 1, (1, 2, 3)), (4, 2, (0, 1)), (6, 2, (3, 2)), (6, 3, (1,)), (7, 3, (0,)), (8, 3, (3, 2)),
+        (10, 4, (1, 0)), (11, 4, (3, 2)),
+    )
+    later = {1: [vector_steps[1]], 4: [vector_steps[2]], 7: [vector_steps[3]]}
+    for when, hop, which in timetable:
+        later.setdefault(when, []).extend(streams[i][hop] for i in which if i < len(streams))
+    run(later)
+
+    def hops(hop, which):
+        for i in which:
+            if i < len(streams):
+                streams[i][hop]()
+
+    hops(5, (1, 0))
     high, rest = split_low(total[...])
     exchange(node_part[...] + dot_right(high, weight[...]) + dot_right(rest, weight[...]))
-    steps[6]()
-    steps[7]()
+    hops(5, (3, 2))
+    hops(6, (1, 0, 3, 2))
+    hops(7, range(4))
     receive()
-    steps[8]()
+    hops(8, range(4))
     width = total.shape[1]
     nodes_at = edge_grads.shape[0]
     copies = [
@@ -950,7 +956,8 @@
         copy.start()
     vector_steps[4]()
     drain()
-    steps[9]()
+    for stream in streams:
+        stream[9]()
     for copy in copies:
         copy.wait()
 
@@ -1238,7 +1245,7 @@
 
 def release(whole, reduced):
     arrays = [*whole, *reduced]
-    steps = 4
+    steps = 8
 
     def spec(item, kept):
         rows, columns = item.shape

time: 313 us -> 313 us (level)
    pallas_call x1, Pallas kernels: 85.2 us -> 82 us  [finish(): pl.pallas_call(finish_kernel, grid=(1,), in_specs=[hold, across, across,...]
where the time goes in v14:
time: 313 us; the launch traced here: 311 us
  Pallas kernels  304 us (97%)
    pallas_call x1, Pallas kernels, middle(): pl.pallas_call(middle_kernel, in_specs=[hold, across] + [hold] * 9, out_s...  91.5 us
    pallas_call x1, Pallas kernels, finish(): pl.pallas_call(finish_kernel, grid=(1,), in_specs=[hold, across, across,...  82 us
    pallas_call x1, Pallas kernels, begin(): pl.pallas_call(begin_kernel, in_specs=[hold, across, hold, hold], out_spe...  53.4 us
    pallas_call x1, Pallas kernels, edge_backward(): pl.pallas_call(backward_kernel, grid=(steps,), in_specs=[scalar, scalar,...  41.4 us
    pallas_call x1, Pallas kernels, edge_forward(): pl.pallas_call(forward_kernel, grid=(steps,), in_specs=[scalar, scalar, h...  27.6 us
    pallas_call x1, Pallas kernels, release(): pl.pallas_call(functools.partial(release_kernel, len(arrays)), grid=(step...  7.92 us
  transfers between devices with their start and end apart: 1, of which 0 were waited for; matrix products, arithmetic and copies ran while one was open for 0% of the time, Pallas kernels for 9%

profile of v14, /device:TPU:0, one launch (start us, length us, event | category | flops | bytes accessed | tf_op | source)
XLA Modules:
  0.0 310.6 jit_solution(6079227106733717604)
XLA Ops:
  0.6 53.4 %begin_rows.1 = (bf16[512,512]{1,0:T(8,128)(2,1)}, bf16[3,4,512,512]{3,2,1,0:T(8,128)(2,1)}, f32[32,16,512]{2,1,0:T(8,128)}, s32[36,128]{1,0:T(8,128)}, s32[36,128]{1,0:T(8,128)}) custom-call(f32[16,16384]{1,0:T(8,128)} %residual.2, f32[16,16384]{1,0:T(8,128)} %residual.3, s32[36,128]{1,0:T(8,128)} %bitcast.25, s32[36,128]{1,0:T(8,128)} %bitcast.26), custom_call_target="tpu_custom_call" | custom-call | tf_op jit(solution)/shard_map/begin_rows/pallas_call | solution.py:1215
  54.1 2.7 all-to-all-start
  57.4 27.6 %edge_forward.1 = (f32[4608,512]{1,0:T(8,128)}, f32[4608,512]{1,0:T(8,128)}, f32[4608,512]{1,0:T(8,128)}, bf16[4608,512]{1,0:T(8,128)(2,1)}, bf16[4608,512]{1,0:T(8,128)(2,1)}) custom-call(s32[1]{0:T(128)S(6)} %copy.35.count, s32[4608]{0:T(1024)} %bitcast.23, s32[36,128]{1,0:T(8,128)} %get-tuple-element.49.send, bf16[4608,512]{1,0:T(8,128)(2,1)} %edge.3, ...), custom_call_target="tpu_custom_call" | custom-call | flops 24159191040 | bytes 94371840 | tf_op jit(solution)/shard_map/edge_forward/pallas_call | solution.py:170
  85.0 0.0 all-to-all-done
  85.0 0.0 copy-start
  85.0 1.0 copy-done
  86.0 91.5 %middle_nodes.1 = (bf16[3,4,512,512]{3,2,1,0:T(8,128)(2,1)}, f32[512,512]{1,0:T(8,128)}, f32[16,16384]{1,0:T(8,128)}, f32[1536,512]{1,0:T(8,128)}, f32[8,512]{1,0:T(8,128)}) custom-call(s32[36,128]{1,0:T(8,128)} %get-tuple-element.48.index, bf16[4608,512]{1,0:T(8,128)(2,1)} %get-tuple-element.52.messages, bf16[512,512]{1,0:T(8,128)(2,1)} %get-tuple-element.51.nodes.node_low, ...), custom_call_target="tpu_custom_call" | custom-call | tf_op jit(solution)/shard_map/middle_nodes/pallas_call | solution.py:1060
  177.5 41.4 %edge_backward.1 = (f32[4608,512]{1,0:T(8,128)}, bf16[4608,512]{1,0:T(8,128)(2,1)}, f32[2048,512]{1,0:T(8,128)}, f32[8,512]{1,0:T(8,128)}, f32[512,512]{1,0:T(8,128)}) custom-call(s32[1]{0:T(128)S(6)} %copy.35.count, s32[4608]{0:T(1024)} %bitcast.24, s32[36,128]{1,0:T(8,128)} %get-tuple-element.49.send, bf16[4608,512]{1,0:T(8,128)(2,1)} %cotangent.1, ...), custom_call_target="tpu_custom_call" | custom-call | flops 28991029248 | bytes 94371840 | tf_op jit(solution)/shard_map/edge_backward/pallas_call | solution.py:280
  218.9 82.0 %finish_sums.1 = (f32[16,16384]{1,0:T(8,128)}, bf16[1536,512]{1,0:T(8,128)(2,1)}, bf16[512,512]{1,0:T(8,128)(2,1)}, bf16[1024,512]{1,0:T(8,128)(2,1)}, bf16[512,512]{1,0:T(8,128)(2,1)}, /*index=5*/f32[8,512]{1,0:T(8,128)}) custom-call(s32[36,128]{1,0:T(8,128)} %get-tuple-element.48.index, bf16[4608,512]{1,0:T(8,128)(2,1)} %get-tuple-element.61.messages, ...), custom_call_target="tpu_custom_call" | custom-call | tf_op jit(solution)/shard_map/finish_sums/pallas_call | solution.py:973
  300.9 1.6 fusion
  302.5 7.9 %release_results.1 = (f32[16,16384]{1,0:T(8,128)}, f32[16,16384]{1,0:T(8,128)}, f32[1536,512]{1,0:T(8,128)}, f32[512,512]{1,0:T(8,128)}, f32[1024,512]{1,0:T(8,128)}, /*index=5*/f32[512,512]{1,0:T(8,128)}) custom-call(f32[16,16384]{1,0:T(8,128)} %get-tuple-element.54.refs_0_, f32[16,16384]{1,0:T(8,128)} %get-tuple-element.66.refs_1_, ...), custom_call_target="tpu_custom_call" | custom-call | tf_op jit(solution)/shard_map/release_results/pallas_call | solution.py:1257
Async XLA Ops:
  54.1 30.9 %all-to-all-start = ((f32[32,16,512]{2,1,0:T(8,128)}), f32[32,16,512]{2,1,0:T(8,128)S(1)}, u32[]{:S(2)}, u32[]{:S(2)}) async-start(f32[32,16,512]{2,1,0:T(8,128)} %get-tuple-element.53), calls=%async_computation | async-start | bytes 2097152 | tf_op jit(solution)/shard_map/all_to_all | solution.py:1296
  85.0 1.0 copy-start

commit v15 on v14

--- a/solution.py
+++ b/solution.py
@@ -642,7 +642,7 @@
         for kind in kinds:
             move(kind, piece).start()
 
-    straight = range(PIECES - 1)
+    straight = range(PIECES - 2)
 
     def one(piece):
         relay(0, (3, 4) if piece in straight else (4,), piece)
@@ -1245,7 +1245,7 @@
 
 def release(whole, reduced):
     arrays = [*whole, *reduced]
-    steps = 8
+    steps = 2
 
     def spec(item, kept):
         rows, columns = item.shape

time: 313 us -> 308 us (0.984)
  Pallas kernels: 304 us -> 299 us
where the time goes in v15:
time: 308 us; the launch traced here: 307 us
  Pallas kernels  299 us (97%)
  starting transfers between devices  4.36 us (1%)
    pallas_call x1, Pallas kernels, middle(): pl.pallas_call(middle_kernel, in_specs=[hold, across] + [hold] * 9, out_s...  89.1 us
    pallas_call x1, Pallas kernels, finish(): pl.pallas_call(finish_kernel, grid=(1,), in_specs=[hold, across, across,...  84.2 us
    pallas_call x1, Pallas kernels, begin(): pl.pallas_call(begin_kernel, in_specs=[hold, across, hold, hold], out_spe...  50.8 us
    pallas_call x1, Pallas kernels, edge_backward(): pl.pallas_call(backward_kernel, grid=(steps,), in_specs=[scalar, scalar,...  41.4 us
    pallas_call x1, Pallas kernels, edge_forward(): pl.pallas_call(forward_kernel, grid=(steps,), in_specs=[scalar, scalar, h...  27.6 us
  transfers between devices with their start and end apart: 1, of which 0 were waited for; matrix products, arithmetic and copies ran while one was open for 0% of the time, Pallas kernels for 9%

profile of v15, /device:TPU:0, one launch (start us, length us, event | category | flops | bytes accessed | tf_op | source)
XLA Modules:
  0.0 307.0 jit_solution(5814450989718282404)
XLA Ops:
  0.6 50.8 %begin_rows.1 = (bf16[512,512]{1,0:T(8,128)(2,1)}, bf16[3,4,512,512]{3,2,1,0:T(8,128)(2,1)}, f32[32,16,512]{2,1,0:T(8,128)}, s32[36,128]{1,0:T(8,128)}, s32[36,128]{1,0:T(8,128)}) custom-call(f32[16,16384]{1,0:T(8,128)} %residual.2, f32[16,16384]{1,0:T(8,128)} %residual.3, s32[36,128]{1,0:T(8,128)} %bitcast.25, s32[36,128]{1,0:T(8,128)} %bitcast.26), custom_call_target="tpu_custom_call" | custom-call | tf_op jit(solution)/shard_map/begin_rows/pallas_call | solution.py:1215
  51.5 4.4 %all-to-all-start = ((f32[32,16,512]{2,1,0:T(8,128)}), f32[32,16,512]{2,1,0:T(8,128)S(1)}, u32[]{:S(2)}, u32[]{:S(2)}) async-start(f32[32,16,512]{2,1,0:T(8,128)} %get-tuple-element.53), calls=%async_computation | async-start | bytes 2097152 | tf_op jit(solution)/shard_map/all_to_all | solution.py:1296
  56.5 27.6 %edge_forward.1 = (f32[4608,512]{1,0:T(8,128)}, f32[4608,512]{1,0:T(8,128)}, f32[4608,512]{1,0:T(8,128)}, bf16[4608,512]{1,0:T(8,128)(2,1)}, bf16[4608,512]{1,0:T(8,128)(2,1)}) custom-call(s32[1]{0:T(128)S(6)} %copy.35.count, s32[4608]{0:T(1024)} %bitcast.23, s32[36,128]{1,0:T(8,128)} %get-tuple-element.49.send, bf16[4608,512]{1,0:T(8,128)(2,1)} %edge.3, ...), custom_call_target="tpu_custom_call" | custom-call | flops 24159191040 | bytes 94371840 | tf_op jit(solution)/shard_map/edge_forward/pallas_call | solution.py:170
  84.0 0.0 all-to-all-done
  84.1 0.0 copy-start
  84.1 1.0 copy-done
  85.0 89.1 %middle_nodes.1 = (bf16[3,4,512,512]{3,2,1,0:T(8,128)(2,1)}, f32[512,512]{1,0:T(8,128)}, f32[16,16384]{1,0:T(8,128)}, f32[1536,512]{1,0:T(8,128)}, f32[8,512]{1,0:T(8,128)}) custom-call(s32[36,128]{1,0:T(8,128)} %get-tuple-element.48.index, bf16[4608,512]{1,0:T(8,128)(2,1)} %get-tuple-element.52.messages, bf16[512,512]{1,0:T(8,128)(2,1)} %get-tuple-element.51.nodes.node_low, ...), custom_call_target="tpu_custom_call" | custom-call | tf_op jit(solution)/shard_map/middle_nodes/pallas_call | solution.py:1060
  174.1 41.4 %edge_backward.1 = (f32[4608,512]{1,0:T(8,128)}, bf16[4608,512]{1,0:T(8,128)(2,1)}, f32[2048,512]{1,0:T(8,128)}, f32[8,512]{1,0:T(8,128)}, f32[512,512]{1,0:T(8,128)}) custom-call(s32[1]{0:T(128)S(6)} %copy.35.count, s32[4608]{0:T(1024)} %bitcast.24, s32[36,128]{1,0:T(8,128)} %get-tuple-element.49.send, bf16[4608,512]{1,0:T(8,128)(2,1)} %cotangent.1, ...), custom_call_target="tpu_custom_call" | custom-call | flops 28991029248 | bytes 94371840 | tf_op jit(solution)/shard_map/edge_backward/pallas_call | solution.py:280
  215.5 84.2 %finish_sums.1 = (f32[16,16384]{1,0:T(8,128)}, bf16[1536,512]{1,0:T(8,128)(2,1)}, bf16[512,512]{1,0:T(8,128)(2,1)}, bf16[1024,512]{1,0:T(8,128)(2,1)}, bf16[512,512]{1,0:T(8,128)(2,1)}, /*index=5*/f32[8,512]{1,0:T(8,128)}) custom-call(s32[36,128]{1,0:T(8,128)} %get-tuple-element.48.index, bf16[4608,512]{1,0:T(8,128)(2,1)} %get-tuple-element.61.messages, ...), custom_call_target="tpu_custom_call" | custom-call | tf_op jit(solution)/shard_map/finish_sums/pallas_call | solution.py:973
  299.7 1.6 fusion
  301.3 5.6 %release_results.1 = (f32[16,16384]{1,0:T(8,128)}, f32[16,16384]{1,0:T(8,128)}, f32[1536,512]{1,0:T(8,128)}, f32[512,512]{1,0:T(8,128)}, f32[1024,512]{1,0:T(8,128)}, /*index=5*/f32[512,512]{1,0:T(8,128)}) custom-call(f32[16,16384]{1,0:T(8,128)} %get-tuple-element.54.refs_0_, f32[16,16384]{1,0:T(8,128)} %get-tuple-element.66.refs_1_, ...), custom_call_target="tpu_custom_call" | custom-call | tf_op jit(solution)/shard_map/release_results/pallas_call | solution.py:1257
Async XLA Ops:
  51.5 32.6 %all-to-all-start = ((f32[32,16,512]{2,1,0:T(8,128)}), f32[32,16,512]{2,1,0:T(8,128)S(1)}, u32[]{:S(2)}, u32[]{:S(2)}) async-start(f32[32,16,512]{2,1,0:T(8,128)} %get-tuple-element.53), calls=%async_computation | async-start | bytes 2097152 | tf_op jit(solution)/shard_map/all_to_all | solution.py:1296
  84.1 1.0 copy-start

commit v16 on v15

--- a/solution.py
+++ b/solution.py
@@ -14,6 +14,7 @@
 TILE = 512
 CHUNK = 512
 LANES = 128
+SPARE = 8
 VMEM_BYTES = 60 * 2**20
 
 
@@ -80,8 +81,6 @@
 
 
 def gather_rows(index, base, table, rows, parts):
-    count = rows.shape[0] // parts
-
     def body(i, carry):
         for u in range(16):
             slot = i * 16 + u
@@ -91,11 +90,11 @@
             ]
         return carry
 
-    lax.fori_loop(0, count // 16, body, 0)
+    lax.fori_loop(0, TILE // 16, body, 0)
 
 
 def gather_inline(index, base, table, rows, parts):
-    for slot in range(rows.shape[0] // parts):
+    for slot in range(TILE):
         place = index[base + slot]
         rows[slot * parts : (slot + 1) * parts, :] = table[pl.ds(pl.multiple_of(place * parts, parts), parts), :]
 
@@ -183,8 +182,8 @@
             jax.ShapeDtypeStruct((edges, width), jnp.bfloat16),
         ],
         scratch_shapes=[
-            pltpu.VMEM((wide.shape[0] * parts, LANES), jnp.float32),
-            pltpu.VMEM((TILE * parts, LANES), jnp.float32),
+            pltpu.VMEM((wide.shape[0] * parts + SPARE, LANES), jnp.float32),
+            pltpu.VMEM((TILE * parts + SPARE, LANES), jnp.float32),
             pltpu.VMEM((4, CHUNK, width), jnp.bfloat16),
             pltpu.SemaphoreType.DMA((4,)),
         ],
@@ -235,7 +234,6 @@
     grad_first = dot_right(second_low, w_two[...]) * (logistic * (1.0 + pre * (1.0 - logistic)))
     first_low = grad_first.astype(jnp.bfloat16)
     message[...] = first_low
-    vectors[0:1, :] += jnp.sum(first_low.astype(jnp.float32), 0, keepdims=True)
     grads[:width] += dot_left(edge[...], first_low)
     grads[2 * width : 3 * width] += dot_left(received[...], first_low)
     node = lax.broadcasted_iota(jnp.int32, (nodes.shape[0], LANES), 0)
@@ -251,6 +249,7 @@
 
     @pl.when(step == pl.num_programs(0) - 1)
     def _():
+        vectors[0:1, :] = jnp.sum(by_sender[...], 0, keepdims=True)
         high, rest = split_low(by_sender[...])
         grads[width : 2 * width] = dot_left(nodes[...], high) + dot_left(nodes[...], rest)
         give = pltpu.make_async_copy(grads, all_grads, give_sem)
@@ -295,8 +294,8 @@
             jax.ShapeDtypeStruct((per_device, width), jnp.float32),
         ],
         scratch_shapes=[
-            pltpu.VMEM((wide.shape[0] * parts, LANES), jnp.float32),
-            pltpu.VMEM((TILE * parts, LANES), jnp.float32),
+            pltpu.VMEM((wide.shape[0] * parts + SPARE, LANES), jnp.float32),
+            pltpu.VMEM((TILE * parts + SPARE, LANES), jnp.float32),
             pltpu.VMEM((4, CHUNK, width), jnp.bfloat16),
             pltpu.SemaphoreType.DMA((4,)),
             pltpu.VMEM((per_device, width), jnp.float32),

time: 308 us -> 308 us (level)
  no operation moved by 1% of the time
where the time goes in v16:
time: 308 us; the launch traced here: 307 us
  Pallas kernels  299 us (97%)
  starting transfers between devices  4.36 us (1%)
    pallas_call x1, Pallas kernels, middle(): pl.pallas_call(middle_kernel, in_specs=[hold, across] + [hold] * 9, out_s...  89.1 us
    pallas_call x1, Pallas kernels, finish(): pl.pallas_call(finish_kernel, grid=(1,), in_specs=[hold, across, across,...  84.2 us
    pallas_call x1, Pallas kernels, begin(): pl.pallas_call(begin_kernel, in_specs=[hold, across, hold, hold], out_spe...  50.8 us
    pallas_call x1, Pallas kernels, edge_backward(): pl.pallas_call(backward_kernel, grid=(steps,), in_specs=[scalar, scalar,...  41.4 us
    pallas_call x1, Pallas kernels, edge_forward(): pl.pallas_call(forward_kernel, grid=(steps,), in_specs=[scalar, scalar, h...  27.6 us
  transfers between devices with their start and end apart: 1, of which 0 were waited for; matrix products, arithmetic and copies ran while one was open for 0% of the time, Pallas kernels for 9%

profile of v16, /device:TPU:0, one launch (start us, length us, event | category | flops | bytes accessed | tf_op | source)
XLA Modules:
  0.0 307.0 jit_solution(8310615630488424466)
XLA Ops:
  0.6 50.8 %begin_rows.1 = (bf16[512,512]{1,0:T(8,128)(2,1)}, bf16[3,4,512,512]{3,2,1,0:T(8,128)(2,1)}, f32[32,16,512]{2,1,0:T(8,128)}, s32[36,128]{1,0:T(8,128)}, s32[36,128]{1,0:T(8,128)}) custom-call(f32[16,16384]{1,0:T(8,128)} %residual.2, f32[16,16384]{1,0:T(8,128)} %residual.3, s32[36,128]{1,0:T(8,128)} %bitcast.25, s32[36,128]{1,0:T(8,128)} %bitcast.26), custom_call_target="tpu_custom_call" | custom-call | tf_op jit(solution)/shard_map/begin_rows/pallas_call | solution.py:1214
  51.5 4.4 %all-to-all-start = ((f32[32,16,512]{2,1,0:T(8,128)}), f32[32,16,512]{2,1,0:T(8,128)S(1)}, u32[]{:S(2)}, u32[]{:S(2)}) async-start(f32[32,16,512]{2,1,0:T(8,128)} %get-tuple-element.53), calls=%async_computation | async-start | bytes 2097152 | tf_op jit(solution)/shard_map/all_to_all | solution.py:1295
  56.5 27.6 %edge_forward.1 = (f32[4608,512]{1,0:T(8,128)}, f32[4608,512]{1,0:T(8,128)}, f32[4608,512]{1,0:T(8,128)}, bf16[4608,512]{1,0:T(8,128)(2,1)}, bf16[4608,512]{1,0:T(8,128)(2,1)}) custom-call(s32[1]{0:T(128)S(6)} %copy.35.count, s32[4608]{0:T(1024)} %bitcast.23, s32[36,128]{1,0:T(8,128)} %get-tuple-element.49.send, bf16[4608,512]{1,0:T(8,128)(2,1)} %edge.3, ...), custom_call_target="tpu_custom_call" | custom-call | flops 24159191040 | bytes 94371840 | tf_op jit(solution)/shard_map/edge_forward/pallas_call | solution.py:169
  84.0 0.0 all-to-all-done
  84.1 0.0 copy-start
  84.1 1.0 copy-done
  85.0 89.1 %middle_nodes.1 = (bf16[3,4,512,512]{3,2,1,0:T(8,128)(2,1)}, f32[512,512]{1,0:T(8,128)}, f32[16,16384]{1,0:T(8,128)}, f32[1536,512]{1,0:T(8,128)}, f32[8,512]{1,0:T(8,128)}) custom-call(s32[36,128]{1,0:T(8,128)} %get-tuple-element.48.index, bf16[4608,512]{1,0:T(8,128)(2,1)} %get-tuple-element.52.messages, bf16[512,512]{1,0:T(8,128)(2,1)} %get-tuple-element.51.nodes.node_low, ...), custom_call_target="tpu_custom_call" | custom-call | tf_op jit(solution)/shard_map/middle_nodes/pallas_call | solution.py:1059
  174.2 41.4 %edge_backward.1 = (f32[4608,512]{1,0:T(8,128)}, bf16[4608,512]{1,0:T(8,128)(2,1)}, f32[2048,512]{1,0:T(8,128)}, f32[8,512]{1,0:T(8,128)}, f32[512,512]{1,0:T(8,128)}) custom-call(s32[1]{0:T(128)S(6)} %copy.35.count, s32[4608]{0:T(1024)} %bitcast.24, s32[36,128]{1,0:T(8,128)} %get-tuple-element.49.send, bf16[4608,512]{1,0:T(8,128)(2,1)} %cotangent.1, ...), custom_call_target="tpu_custom_call" | custom-call | flops 28991029248 | bytes 94371840 | tf_op jit(solution)/shard_map/edge_backward/pallas_call | solution.py:279
  215.5 84.2 %finish_sums.1 = (f32[16,16384]{1,0:T(8,128)}, bf16[1536,512]{1,0:T(8,128)(2,1)}, bf16[512,512]{1,0:T(8,128)(2,1)}, bf16[1024,512]{1,0:T(8,128)(2,1)}, bf16[512,512]{1,0:T(8,128)(2,1)}, /*index=5*/f32[8,512]{1,0:T(8,128)}) custom-call(s32[36,128]{1,0:T(8,128)} %get-tuple-element.48.index, bf16[4608,512]{1,0:T(8,128)(2,1)} %get-tuple-element.61.messages, ...), custom_call_target="tpu_custom_call" | custom-call | tf_op jit(solution)/shard_map/finish_sums/pallas_call | solution.py:972
  299.7 1.6 fusion
  301.3 5.6 %release_results.1 = (f32[16,16384]{1,0:T(8,128)}, f32[16,16384]{1,0:T(8,128)}, f32[1536,512]{1,0:T(8,128)}, f32[512,512]{1,0:T(8,128)}, f32[1024,512]{1,0:T(8,128)}, /*index=5*/f32[512,512]{1,0:T(8,128)}) custom-call(f32[16,16384]{1,0:T(8,128)} %get-tuple-element.54.refs_0_, f32[16,16384]{1,0:T(8,128)} %get-tuple-element.66.refs_1_, ...), custom_call_target="tpu_custom_call" | custom-call | tf_op jit(solution)/shard_map/release_results/pallas_call | solution.py:1256
Async XLA Ops:
  51.5 32.6 %all-to-all-start = ((f32[32,16,512]{2,1,0:T(8,128)}), f32[32,16,512]{2,1,0:T(8,128)S(1)}, u32[]{:S(2)}, u32[]{:S(2)}) async-start(f32[32,16,512]{2,1,0:T(8,128)} %get-tuple-element.53), calls=%async_computation | async-start | bytes 2097152 | tf_op jit(solution)/shard_map/all_to_all | solution.py:1295
  84.1 1.0 copy-start

commit v17 on v16

--- a/solution.py
+++ b/solution.py
@@ -1237,12 +1237,17 @@
     return own, table.reshape(12 * rows, width), later, send_local, recv_wide
 
 
-def release_kernel(count, *refs):
-    for source, target in zip(refs[:count], refs[count:]):
+def release_kernel(count, vectors, *refs):
+    for source, target in zip(refs[:count], refs[count : 2 * count]):
         target[...] = source[...].astype(target.dtype)
 
-
-def release(whole, reduced):
+    @pl.when(pl.program_id(0) == 0)
+    def _():
+        for i, target in enumerate(refs[2 * count :]):
+            target[...] = vectors[i : i + 1, :]
+
+
+def release(whole, reduced, vectors):
     arrays = [*whole, *reduced]
     steps = 2
 
@@ -1256,12 +1261,13 @@
     return pl.pallas_call(
         functools.partial(release_kernel, len(arrays)),
         grid=(steps,),
-        in_specs=specs,
-        out_specs=specs,
-        out_shape=[jax.ShapeDtypeStruct(item.shape, WIDE) for item in arrays],
+        in_specs=[pl.BlockSpec(vectors.shape, lambda i: (0, 0))] + specs,
+        out_specs=specs + [pl.BlockSpec((1, vectors.shape[1]), lambda i: (0, 0))] * vectors.shape[0],
+        out_shape=[jax.ShapeDtypeStruct(item.shape, WIDE) for item in arrays]
+        + [jax.ShapeDtypeStruct((1, vectors.shape[1]), WIDE)] * vectors.shape[0],
         compiler_params=pltpu.CompilerParams(vmem_limit_bytes=VMEM_BYTES),
         name="release_results",
-    )(*arrays)
+    )(vectors, *arrays)
 
 
 def shards(
@@ -1311,7 +1317,8 @@
     node_grad, *summed, vectors = finish(
         recv_list, messages, edge_grads, node_grads, vectors, node_part, edge_w_one, node_cotangent, 3
     )
-    node_out, node_grad, *summed = release((node_out, node_grad), summed)
+    node_out, node_grad, *rest = release((node_out, node_grad), summed, vectors)
+    summed, vectors = rest[:4], [row.reshape(width) for row in rest[4:]]
     return (
         node_out,
         edge_result,

time: 308 us -> 307 us (level)
  no operation moved by 1% of the time
where the time goes in v17:
time: 307 us; the launch traced here: 306 us
  Pallas kernels  299 us (97%)
  starting transfers between devices  4.36 us (1%)
    pallas_call x1, Pallas kernels, middle(): pl.pallas_call(middle_kernel, in_specs=[hold, across] + [hold] * 9, out_s...  89.1 us
    pallas_call x1, Pallas kernels, finish(): pl.pallas_call(finish_kernel, grid=(1,), in_specs=[hold, across, across,...  84.1 us
    pallas_call x1, Pallas kernels, begin(): pl.pallas_call(begin_kernel, in_specs=[hold, across, hold, hold], out_spe...  50.8 us
    pallas_call x1, Pallas kernels, edge_backward(): pl.pallas_call(backward_kernel, grid=(steps,), in_specs=[scalar, scalar,...  41.4 us
    pallas_call x1, Pallas kernels, edge_forward(): pl.pallas_call(forward_kernel, grid=(steps,), in_specs=[scalar, scalar, h...  27.6 us
  transfers between devices with their start and end apart: 1, of which 0 were waited for; matrix products, arithmetic and copies ran while one was open for 0% of the time, Pallas kernels for 9%

profile of v17, /device:TPU:0, one launch (start us, length us, event | category | flops | bytes accessed | tf_op | source)
XLA Modules:
  0.0 305.8 jit_solution(13635482406981803514)
XLA Ops:
  0.6 50.8 %begin_rows.1 = (bf16[512,512]{1,0:T(8,128)(2,1)}, bf16[3,4,512,512]{3,2,1,0:T(8,128)(2,1)}, f32[32,16,512]{2,1,0:T(8,128)}, s32[36,128]{1,0:T(8,128)}, s32[36,128]{1,0:T(8,128)}) custom-call(f32[16,16384]{1,0:T(8,128)} %residual.2, f32[16,16384]{1,0:T(8,128)} %residual.3, s32[36,128]{1,0:T(8,128)} %bitcast.25, s32[36,128]{1,0:T(8,128)} %bitcast.26), custom_call_target="tpu_custom_call" | custom-call | tf_op jit(solution)/shard_map/begin_rows/pallas_call | solution.py:1214
  51.4 4.4 %all-to-all-start = ((f32[32,16,512]{2,1,0:T(8,128)}), f32[32,16,512]{2,1,0:T(8,128)S(1)}, u32[]{:S(2)}, u32[]{:S(2)}) async-start(f32[32,16,512]{2,1,0:T(8,128)} %get-tuple-element.64), calls=%async_computation | async-start | bytes 2097152 | tf_op jit(solution)/shard_map/all_to_all | solution.py:1301
  56.5 27.6 %edge_forward.1 = (f32[4608,512]{1,0:T(8,128)}, f32[4608,512]{1,0:T(8,128)}, f32[4608,512]{1,0:T(8,128)}, bf16[4608,512]{1,0:T(8,128)(2,1)}, bf16[4608,512]{1,0:T(8,128)(2,1)}) custom-call(s32[1]{0:T(128)S(6)} %copy.35.count, s32[4608]{0:T(1024)} %bitcast.23, s32[36,128]{1,0:T(8,128)} %get-tuple-element.57.send, bf16[4608,512]{1,0:T(8,128)(2,1)} %edge.3, ...), custom_call_target="tpu_custom_call" | custom-call | flops 24159191040 | bytes 94371840 | tf_op jit(solution)/shard_map/edge_forward/pallas_call | solution.py:169
  84.0 0.0 all-to-all-done
  84.1 0.0 copy-start
  84.1 1.0 copy-done
  85.0 89.1 %middle_nodes.1 = (bf16[3,4,512,512]{3,2,1,0:T(8,128)(2,1)}, f32[512,512]{1,0:T(8,128)}, f32[16,16384]{1,0:T(8,128)}, f32[1536,512]{1,0:T(8,128)}, f32[8,512]{1,0:T(8,128)}) custom-call(s32[36,128]{1,0:T(8,128)} %get-tuple-element.56.index, bf16[4608,512]{1,0:T(8,128)(2,1)} %get-tuple-element.63.messages, bf16[512,512]{1,0:T(8,128)(2,1)} %get-tuple-element.59.nodes.node_low, ...), custom_call_target="tpu_custom_call" | custom-call | tf_op jit(solution)/shard_map/middle_nodes/pallas_call | solution.py:1059
  174.2 41.4 %edge_backward.1 = (f32[4608,512]{1,0:T(8,128)}, bf16[4608,512]{1,0:T(8,128)(2,1)}, f32[2048,512]{1,0:T(8,128)}, f32[8,512]{1,0:T(8,128)}, f32[512,512]{1,0:T(8,128)}) custom-call(s32[1]{0:T(128)S(6)} %copy.35.count, s32[4608]{0:T(1024)} %bitcast.24, s32[36,128]{1,0:T(8,128)} %get-tuple-element.57.send, bf16[4608,512]{1,0:T(8,128)(2,1)} %cotangent.1, ...), custom_call_target="tpu_custom_call" | custom-call | flops 28991029248 | bytes 94371840 | tf_op jit(solution)/shard_map/edge_backward/pallas_call | solution.py:279
  215.6 84.1 %finish_sums.1 = (f32[16,16384]{1,0:T(8,128)}, bf16[1536,512]{1,0:T(8,128)(2,1)}, bf16[512,512]{1,0:T(8,128)(2,1)}, bf16[1024,512]{1,0:T(8,128)(2,1)}, bf16[512,512]{1,0:T(8,128)(2,1)}, /*index=5*/f32[8,512]{1,0:T(8,128)}) custom-call(s32[36,128]{1,0:T(8,128)} %get-tuple-element.56.index, bf16[4608,512]{1,0:T(8,128)(2,1)} %get-tuple-element.68.messages, ...), custom_call_target="tpu_custom_call" | custom-call | tf_op jit(solution)/shard_map/finish_sums/pallas_call | solution.py:972
  299.7 5.9 %release_results.1 = (f32[16,16384]{1,0:T(8,128)}, f32[16,16384]{1,0:T(8,128)}, f32[1536,512]{1,0:T(8,128)}, f32[512,512]{1,0:T(8,128)}, f32[1024,512]{1,0:T(8,1...) custom-call(f32[8,512]{1,0:T(8,128)} %get-tuple-element.73.vectors, ...), custom_call_target="tpu_custom_call" | custom-call | tf_op jit(solution)/shard_map/release_results/pallas_call | solution.py:1261
Async XLA Ops:
  51.4 32.6 %all-to-all-start = ((f32[32,16,512]{2,1,0:T(8,128)}), f32[32,16,512]{2,1,0:T(8,128)S(1)}, u32[]{:S(2)}, u32[]{:S(2)}) async-start(f32[32,16,512]{2,1,0:T(8,128)} %get-tuple-element.64), calls=%async_computation | async-start | bytes 2097152 | tf_op jit(solution)/shard_map/all_to_all | solution.py:1301
  84.1 1.0 copy-start
